TPU v7x, 32 devices: a whole 2x2x4 slice. The times are simulated.
32 devices in a mesh: dp: 2 (over y), ctx: 16 (over z, x, core).
Axes of the slice: x: 2, y: 2, z: 4, core: 2. Of those that a mesh axis runs over, the one named last changes fastest.
Arguments:
- tokens: bfloat16 [2, 2048, 896], P('dp', 'ctx'), may hold values from -6 to 6
- w_qkv: bfloat16 [896, 1152], P('dp'), may hold values from -0.1875 to 0.1875
- b_qkv: float32 [1152], replicated, may hold values from -3 to 3
- w_out: bfloat16 [896, 896], P('dp'), may hold values from -6 to 6
- gain_attn: float32 [896], replicated, may hold values from 0.5 to 1.5
- gain_mlp: float32 [896], replicated, may hold values from 0.5 to 1.5
- w_gate: bfloat16 [896, 4864], P(None, 'dp'), may hold values from -0.1875 to 0.1875
- w_up: bfloat16 [896, 4864], P(None, 'dp'), may hold values from -0.1875 to 0.1875
- w_down: bfloat16 [4864, 896], P('dp'), may hold values from -0.078125 to 0.078125
- cotangent: bfloat16 [2, 2048, 896], P('dp', 'ctx'), may hold values from -6 to 6
Outputs:
- output: bfloat16 [2, 2048, 896], P('dp', 'ctx')
- grad_tokens: float32 [2, 2048, 896], P('dp', 'ctx')
- grad_w_qkv: float32 [896, 1152], P('dp')
- grad_b_qkv: float32 [1152], replicated
- grad_w_out: float32 [896, 896], P('dp')
- grad_gain_attn: float32 [896], replicated
- grad_gain_mlp: float32 [896], replicated
- grad_w_gate: float32 [896, 4864], P(None, 'dp')
- grad_w_up: float32 [896, 4864], P(None, 'dp')
- grad_w_down: float32 [4864, 896], P('dp')
All inputs are finite; a program needn't handle non-finite values.
Results may differ from a plain program's by a relative error of at most 0.015.
Values may be sent and summed in bfloat16 or wider, within the bound.
No kernel may reach another device: no remote copies, remote signals or barrier semaphores. Data moves between devices by JAX's collectives and lax.ppermute only.
A program may use at most 192 MiB of HBM per device.

v0:
```python
import jax
import jax.numpy as jnp
from jax import lax
from jax.sharding import PartitionSpec as P

D = 896
QH = 14
KH = 2
HD = 64


EPS = 1e-06
ROPE_BASE = 1000000.0


def positions(index_rows, half_rows, ctx_count, first_device):
    block_no = index_rows // half_rows + 2 * first_device
    device = block_no // 2
    start = jnp.where(block_no % 2 == 0, device, 2 * ctx_count - 1 - device)
    return start * half_rows + index_rows % half_rows


def rotary_tables(place):
    freq = ROPE_BASE ** (-(jnp.arange(HD // 2).astype(jnp.float32) * (2.0 / HD)))
    angle = place.astype(jnp.float32)[:, None] * freq[None, :]
    angle = jnp.concatenate([angle, angle], 1)
    return (jnp.cos(angle), jnp.sin(angle))


def rotate_apply(heads, cosine, sine):
    first = heads[..., : HD // 2]
    second = heads[..., HD // 2 :]
    turned = jnp.concatenate([-second, first], -1)
    return heads * cosine[:, None, :] + turned * sine[:, None, :]


def rotate_back(grads, cosine, sine):
    scaled = grads * sine[:, None, :]
    first = scaled[..., : HD // 2]
    second = scaled[..., HD // 2 :]
    return grads * cosine[:, None, :] + jnp.concatenate([second, -first], -1)


def split_columns(values, groups, ctx_count):
    rows = values.shape[0]
    return values.reshape(rows, groups, ctx_count, values.shape[1] // (groups * ctx_count))


def local(tokens, w_qkv, b_qkv, w_out, gain_attn, gain_mlp, w_gate, w_up, w_down, cotangent):
    f32 = jnp.float32
    bf16 = jnp.bfloat16
    tok_rows = tokens.shape[1]
    half_rows = tok_rows // 2
    ctx_count = lax.axis_size("ctx")
    ctx_index = lax.axis_index("ctx")
    dp_count = lax.axis_size("dp")
    group_size = QH // KH
    width_q = QH * HD
    width_k = KH * HD
    score_scale = HD ** (-0.5)
    shards = (w_qkv, w_out, w_gate, w_up, w_down)
    w_qkv_full, w_out_full, w_gate_full, w_up_full, w_down_full = (
        lax.all_gather(shards[0], "dp", axis=0, tiled=True),
        lax.all_gather(shards[1], "dp", axis=0, tiled=True),
        lax.all_gather(shards[2], "dp", axis=1, tiled=True),
        lax.all_gather(shards[3], "dp", axis=1, tiled=True),
        lax.all_gather(shards[4], "dp", axis=0, tiled=True),
    )
    resid_in = tokens[0].astype(f32)
    query_place = positions(jnp.arange(tok_rows, dtype=jnp.int32), half_rows, ctx_count, ctx_index)
    cosine, sine = rotary_tables(query_place)
    inverse_one = lax.rsqrt(jnp.mean(resid_in * resid_in, -1, keepdims=True) + EPS)
    unit_one = resid_in * inverse_one
    normed_one = (unit_one * gain_attn).astype(bf16)
    joint = jnp.dot(normed_one, w_qkv_full, preferred_element_type=f32) + b_qkv
    queries = rotate_apply(joint[:, :width_q].reshape(tok_rows, QH, HD), cosine, sine).astype(bf16)
    queries = queries.reshape(tok_rows, KH, group_size, HD)
    keys_local = rotate_apply(
        joint[:, width_q : width_q + width_k].reshape(tok_rows, KH, HD), cosine, sine
    ).astype(bf16)
    values_local = joint[:, width_q + width_k :].astype(bf16)
    local_pairs = jnp.concatenate([keys_local.reshape(tok_rows, width_k), values_local], 1)
    all_pairs = lax.all_gather(local_pairs, "ctx", axis=0, tiled=True)
    total_keys = all_pairs.shape[0]
    key_block = min(1024, total_keys)
    block_count = total_keys // key_block
    key_place = positions(jnp.arange(total_keys, dtype=jnp.int32), half_rows, ctx_count, 0)
    pair_blocks = all_pairs.reshape(block_count, key_block, 2 * width_k)
    place_blocks = key_place.reshape(block_count, key_block)

    def block_scores(pair_block, place_block):
        key_heads = pair_block[:, :width_k].reshape(key_block, KH, HD)
        value_heads = pair_block[:, width_k:].reshape(key_block, KH, HD)
        scores = (
            jnp.einsum("qhgd,khd->hgqk", queries, key_heads, preferred_element_type=f32)
            * score_scale
        )
        allowed = place_block[None, None, None, :] <= query_place[None, None, :, None]
        return (jnp.where(allowed, scores, -1e30), key_heads, value_heads)

    def gather_stats(carry, pieces):
        run_max, run_sum = carry
        scores, key_heads, value_heads = block_scores(pieces[0], pieces[1])
        new_max = jnp.maximum(run_max, jnp.max(scores, -1, keepdims=True))
        run_sum = run_sum * jnp.exp(run_max - new_max) + jnp.sum(
            jnp.exp(scores - new_max), -1, keepdims=True
        )
        return ((new_max, run_sum), None)

    start_max = jnp.full((KH, group_size, tok_rows, 1), -1e30, f32)
    start_sum = jnp.zeros((KH, group_size, tok_rows, 1), f32)
    (run_max, run_sum), unused = lax.scan(
        gather_stats, (start_max, start_sum), (pair_blocks, place_blocks)
    )
    log_total = run_max + jnp.log(run_sum)

    def weighted_sum(acc, pieces):
        scores, key_heads, value_heads = block_scores(pieces[0], pieces[1])
        probs_low = jnp.exp(scores - log_total).astype(bf16)
        acc = acc + jnp.einsum("hgqk,khd->qhgd", probs_low, value_heads, preferred_element_type=f32)
        return (acc, None)

    attended, unused = lax.scan(
        weighted_sum, jnp.zeros((tok_rows, KH, group_size, HD), f32), (pair_blocks, place_blocks)
    )
    attended_low = attended.reshape(tok_rows, width_q).astype(bf16)
    hidden = resid_in + jnp.dot(attended_low, w_out_full, preferred_element_type=f32)
    inverse_two = lax.rsqrt(jnp.mean(hidden * hidden, -1, keepdims=True) + EPS)
    unit_two = hidden * inverse_two
    normed_two = (unit_two * gain_mlp).astype(bf16)
    gate = jnp.dot(normed_two, w_gate_full, preferred_element_type=f32)
    upper = jnp.dot(normed_two, w_up_full, preferred_element_type=f32)
    activated = jax.nn.silu(gate)
    middle = (activated * upper).astype(bf16)
    mlp_out = jnp.dot(middle, w_down_full, preferred_element_type=f32)
    output = (hidden + mlp_out).astype(bf16)
    grad_out = cotangent[0].astype(f32)
    grad_mlp_low = grad_out.astype(bf16)
    grad_middle = jnp.einsum("td,fd->tf", grad_mlp_low, w_down_full, preferred_element_type=f32)
    sigma = jax.nn.sigmoid(gate)
    slope = sigma * (1.0 + gate * (1.0 - sigma))
    grad_gate_low = (grad_middle * upper * slope).astype(bf16)
    grad_up_low = (grad_middle * activated).astype(bf16)
    grad_normed_two = jnp.einsum(
        "tf,df->td", grad_gate_low, w_gate_full, preferred_element_type=f32
    ) + jnp.einsum("tf,df->td", grad_up_low, w_up_full, preferred_element_type=f32)
    grad_gain_two = jnp.sum(grad_normed_two * unit_two, 0)
    scaled_two = grad_normed_two * gain_mlp
    grad_hidden = grad_out + inverse_two * (
        scaled_two - unit_two * jnp.mean(scaled_two * unit_two, -1, keepdims=True)
    )
    grad_attn_low = grad_hidden.astype(bf16)
    grad_heads = jnp.einsum(
        "td,cd->tc", grad_attn_low, w_out_full, preferred_element_type=f32
    ).astype(bf16)
    grad_heads = grad_heads.reshape(tok_rows, KH, group_size, HD)
    delta = jnp.sum(grad_heads.astype(f32) * attended, -1)
    delta = jnp.transpose(delta, (1, 2, 0))[..., None]

    def attention_back(grad_queries, pieces):
        scores, key_heads, value_heads = block_scores(pieces[0], pieces[1])
        probs = jnp.exp(scores - log_total)
        probs_low = probs.astype(bf16)
        grad_probs = jnp.einsum(
            "qhgd,khd->hgqk", grad_heads, value_heads, preferred_element_type=f32
        )
        grad_scores = (probs * (grad_probs - delta)).astype(bf16)
        grad_queries = grad_queries + jnp.einsum(
            "hgqk,khd->qhgd", grad_scores, key_heads, preferred_element_type=f32
        )
        grad_keys = (
            jnp.einsum("hgqk,qhgd->khd", grad_scores, queries, preferred_element_type=f32)
            * score_scale
        )
        grad_values = jnp.einsum(
            "hgqk,qhgd->khd", probs_low, grad_heads, preferred_element_type=f32
        )
        joined = jnp.concatenate(
            [grad_keys.reshape(key_block, width_k), grad_values.reshape(key_block, width_k)], 1
        )
        return (grad_queries, joined)

    grad_queries, pair_terms = lax.scan(
        attention_back, jnp.zeros((tok_rows, KH, group_size, HD), f32), (pair_blocks, place_blocks)
    )
    pair_terms = pair_terms.reshape(total_keys, 2 * width_k)
    grad_pairs = lax.psum_scatter(
        pair_terms.astype(jnp.bfloat16), "ctx", scatter_dimension=0, tiled=True
    ).astype(jnp.float32)
    grad_queries = rotate_back((grad_queries * score_scale).reshape(tok_rows, QH, HD), cosine, sine)
    grad_keys = rotate_back(grad_pairs[:, :width_k].reshape(tok_rows, KH, HD), cosine, sine)
    grad_joint_low = jnp.concatenate(
        [
            grad_queries.reshape(tok_rows, width_q),
            grad_keys.reshape(tok_rows, width_k),
            grad_pairs[:, width_k:],
        ],
        1,
    ).astype(bf16)
    grad_bias = jnp.sum(grad_joint_low.astype(f32), 0)
    grad_normed_one = jnp.einsum(
        "tc,dc->td", grad_joint_low, w_qkv_full, preferred_element_type=f32
    )
    grad_gain_one = jnp.sum(grad_normed_one * unit_one, 0)
    scaled_one = grad_normed_one * gain_attn
    grad_input = grad_hidden + inverse_one * (
        scaled_one - unit_one * jnp.mean(scaled_one * unit_one, -1, keepdims=True)
    )
    traded = (
        lax.all_to_all(
            split_columns(grad_joint_low, 1, ctx_count),
            "ctx",
            split_axis=2,
            concat_axis=0,
            tiled=True,
        ),
        lax.all_to_all(
            split_columns(grad_attn_low, 1, ctx_count),
            "ctx",
            split_axis=2,
            concat_axis=0,
            tiled=True,
        ),
        lax.all_to_all(
            split_columns(grad_gate_low, dp_count, ctx_count),
            "ctx",
            split_axis=2,
            concat_axis=0,
            tiled=True,
        ),
        lax.all_to_all(
            split_columns(grad_up_low, dp_count, ctx_count),
            "ctx",
            split_axis=2,
            concat_axis=0,
            tiled=True,
        ),
        lax.all_to_all(
            split_columns(middle, dp_count, ctx_count),
            "ctx",
            split_axis=2,
            concat_axis=0,
            tiled=True,
        ),
    )
    joint_part = traded[0][:, 0, 0, :]
    outproj_part = traded[1][:, 0, 0, :]
    gate_part = traded[2][:, :, 0, :]
    up_part = traded[3][:, :, 0, :]
    middle_part = traded[4][:, :, 0, :]
    normed_one_p = lax.all_gather(normed_one, "ctx", axis=0, tiled=True)
    attended_p = lax.all_gather(attended_low, "ctx", axis=0, tiled=True)
    normed_two_p = lax.all_gather(normed_two, "ctx", axis=0, tiled=True)
    grad_out_p = lax.all_gather(grad_mlp_low, "ctx", axis=0, tiled=True)
    term_joint = jnp.einsum("td,tc->dc", normed_one_p, joint_part, preferred_element_type=f32)
    term_out = jnp.einsum("tc,td->cd", attended_p, outproj_part, preferred_element_type=f32)
    term_gate = jnp.einsum("td,tgf->dgf", normed_two_p, gate_part, preferred_element_type=f32)
    term_up = jnp.einsum("td,tgf->dgf", normed_two_p, up_part, preferred_element_type=f32)
    term_down = jnp.einsum("tgf,td->gfd", middle_part, grad_out_p, preferred_element_type=f32)
    summed = (
        lax.psum_scatter(
            term_joint.astype(jnp.bfloat16), "dp", scatter_dimension=0, tiled=True
        ).astype(jnp.float32),
        lax.psum_scatter(
            term_out.astype(jnp.bfloat16), "dp", scatter_dimension=0, tiled=True
        ).astype(jnp.float32),
        lax.psum_scatter(
            term_gate.astype(jnp.bfloat16), "dp", scatter_dimension=1, tiled=True
        ).astype(jnp.float32),
        lax.psum_scatter(
            term_up.astype(jnp.bfloat16), "dp", scatter_dimension=1, tiled=True
        ).astype(jnp.float32),
        lax.psum_scatter(
            term_down.astype(jnp.bfloat16), "dp", scatter_dimension=0, tiled=True
        ).astype(jnp.float32),
    )
    owned = (
        lax.all_gather(summed[0].astype(jnp.bfloat16), "ctx", axis=1, tiled=True).astype(
            jnp.float32
        ),
        lax.all_gather(summed[1].astype(jnp.bfloat16), "ctx", axis=1, tiled=True).astype(
            jnp.float32
        ),
        lax.all_gather(summed[2].astype(jnp.bfloat16), "ctx", axis=2, tiled=True).astype(
            jnp.float32
        ),
        lax.all_gather(summed[3].astype(jnp.bfloat16), "ctx", axis=2, tiled=True).astype(
            jnp.float32
        ),
        lax.all_gather(summed[4].astype(jnp.bfloat16), "ctx", axis=1, tiled=True).astype(
            jnp.float32
        ),
    )
    grad_joint = owned[0]
    grad_outproj = owned[1]
    grad_gate = owned[2].reshape(D, owned[2].shape[2])
    grad_up = owned[3].reshape(D, owned[3].shape[2])
    grad_down = owned[4].reshape(owned[4].shape[1], D)
    small_sums = lax.psum((grad_gain_one, grad_gain_two, grad_bias), ("dp", "ctx"))
    return (
        output[None],
        grad_input[None],
        grad_joint,
        small_sums[2],
        grad_outproj,
        small_sums[0],
        small_sums[1],
        grad_gate,
        grad_up,
        grad_down,
    )


def solution(mesh):
    placed = (
        P("dp", "ctx", None),
        P("dp", None),
        P(),
        P("dp", None),
        P(),
        P(),
        P(None, "dp"),
        P(None, "dp"),
        P("dp", None),
        P("dp", "ctx", None),
    )
    return jax.shard_map(
        local,
        mesh=mesh,
        in_specs=placed,
        out_specs=(
            P("dp", "ctx", None),
            P("dp", "ctx", None),
            P("dp", None),
            P(),
            P("dp", None),
            P(),
            P(),
            P(None, "dp"),
            P(None, "dp"),
            P("dp", None),
        ),
        check_vma=False,
    )
```

profile of v0, /device:TPU:0, one launch (start us, length us, event | category | flops | bytes accessed | tf_op | source)
XLA Modules:
  0.0 1005.5 jit_solution(15075171275984046993)
XLA Ops:
  10.4 34.6 %all-gather.15.cloned.1.call-done = bf16[896,1152]{1,0:T(8,128)(2,1)} async-done(((bf16[448,1152]{1,0:T(8,128)(2,1)}), bf16[896,1152]{1,0:T(8,128)(2,1)}) %all-gather.15.cloned.1.call-update) | async-done | bytes 2064400 | tf_op jit(solution)/shard_map/all_gather | solution.py:63
  51.1 35.1 %all-gather.17.cloned.1.call-done = bf16[2048,256]{1,0:T(8,128)(2,1)} async-done(((bf16[128,256]{1,0:T(8,128)(2,1)}), bf16[2048,256]{1,0:T(8,128)(2,1)}) %all-gather.17.cloned.1.call-update) | async-done | bytes 1048592 | tf_op jit(solution)/shard_map/all_gather | solution.py:83
  87.7 18.8 %while.37 = (s32[]{:T(128)}, f32[2,7,128,1]{2,1,0,3:T(8,128)S(1)}, f32[2,7,128,1]{2,1,0,3:T(8,128)S(1)}, s32[2,1024]{1,0:T(2,128)S(1)}, bf16[2,1024,256]{1,2,0:T...) while((s32[]{:T(128)}, f32[2,7,128,1]{2,1,0,3:T(8,128)S(1)}, ...), condition=%wide.region_4.5_spmd.clone, body=%wide.region_1.4_spmd.clone.sunk | while | flops 247870848 | bytes 17244284 | solution.py:112
  117.3 108.5 %all-gather.21.cloned.1.call-done = bf16[896,4864]{1,0:T(8,128)(2,1)} async-done(((bf16[896,2432]{1,0:T(8,128)(2,1)}), bf16[896,4864]{1,0:T(8,128)(2,1)}) %all-gather.21.cloned.1.call-update) | async-done | bytes 8716304 | tf_op jit(solution)/shard_map/all_gather | solution.py:65
  232.3 105.0 %all-gather.23.cloned.1.call-done = bf16[896,4864]{1,0:T(8,128)(2,1)} async-done(((bf16[896,2432]{1,0:T(8,128)(2,1)}), bf16[896,4864]{1,0:T(8,128)(2,1)}) %all-gather.23.cloned.1.call-update) | async-done | bytes 8716304 | tf_op jit(solution)/shard_map/all_gather | solution.py:66
  343.7 105.2 %all-gather.25.cloned.1.call-done = bf16[4864,896]{1,0:T(8,128)(2,1)} async-done(((bf16[2432,896]{1,0:T(8,128)(2,1)}), bf16[4864,896]{1,0:T(8,128)(2,1)}) %all-gather.25.cloned.1.call-update) | async-done | bytes 8716304 | tf_op jit(solution)/shard_map/all_gather | solution.py:67
  471.1 32.2 %while.39 = (s32[]{:T(128)}, f32[128,2,7,64]{0,3,2,1:T(8,128)S(1)}, bf16[2,1024,256]{1,2,0:T(8,128)(2,1)}, bf16[2,1024,256]{1,2,0:T(8,128)(2,1)S(1)}, s32[2,1024...) while((s32[]{:T(128)}, f32[128,2,7,64]{0,3,2,1:T(8,128)S(1)}, ...), condition=%wide.region_11.12_spmd.clone, body=%wide.region_10.11_spmd.clone.sunk | while | flops 1194431104 | bytes 92178688 | solution.py:183
  522.0 24.5 %all-to-all-done.2 = bf16[128,2,16,152]{0,3,1,2:T(8,128)(2,1)} async-done(((bf16[128,2,16,152]{0,3,1,2:T(8,128)(2,1)}), bf16[128,2,16,152]{0,3,1,2:T(8,128)(2,1)}, u32[]{:S(2)}, u32[]{:S(2)}) %all-to-all-start.2) | async-done | bytes 1245216 | tf_op jit(solution)/shard_map/all_to_all | solution.py:224
  562.0 22.0 %all-to-all-done.3 = bf16[128,2,16,152]{0,3,1,2:T(8,128)(2,1)} async-done(((bf16[128,2,16,152]{0,3,1,2:T(8,128)(2,1)}), bf16[128,2,16,152]{0,3,1,2:T(8,128)(2,1)}, u32[]{:S(2)}, u32[]{:S(2)}) %all-to-all-start.3) | async-done | bytes 1245216 | tf_op jit(solution)/shard_map/all_to_all | solution.py:231
  605.2 22.7 %all-to-all-done.4 = bf16[128,2,16,152]{0,3,1,2:T(8,128)(2,1)} async-done(((bf16[128,2,16,152]{0,3,1,2:T(8,128)(2,1)}), bf16[128,2,16,152]{0,3,1,2:T(8,128)(2,1)}, u32[]{:S(2)}, u32[]{:S(2)}) %all-to-all-start.4) | async-done | bytes 1245216 | tf_op jit(solution)/shard_map/all_to_all | solution.py:238
  627.9 17.3 %all-to-all-start.1 = ((bf16[128,1,16,56]{0,3,1,2:T(8,128)(2,1)}), bf16[128,1,16,56]{0,3,1,2:T(8,128)(2,1)S(1)}, u32[]{:S(2)}, u32[]{:S(2)}) async-start(bf16[128,1,16,56]{0,3,1,2:T(8,128)(2,1)} %bitcast.28), calls=%async_computation.1 | async-start | bytes 458752 | tf_op jit(solution)/shard_map/all_to_all | solution.py:217
  663.0 10.5 %all-to-all-done = bf16[128,1,16,72]{0,3,1,2:T(8,128)(2,1)S(1)} async-done(((bf16[128,1,16,72]{0,3,1,2:T(8,128)(2,1)}), bf16[128,1,16,72]{0,3,1,2:T(8,128)(2,1)S(1)}, u32[]{:S(2)}, u32[]{:S(2)}) %all-to-all-start) | async-done | bytes 294944 | tf_op jit(solution)/shard_map/all_to_all | solution.py:210
  673.6 20.3 %all-gather.27.cloned.1.call-done = bf16[2048,896]{1,0:T(8,128)(2,1)} async-done(((bf16[128,896]{1,0:T(8,128)(2,1)}), bf16[2048,896]{1,0:T(8,128)(2,1)}) %all-gather.27.cloned.1.call-update) | async-done | bytes 3670032 | tf_op jit(solution)/shard_map/all_gather | solution.py:251
  697.5 47.8 %all-gather.29.cloned.1.call-done = bf16[2048,896]{0,1:T(8,128)(2,1)} async-done(((bf16[128,896]{0,1:T(8,128)(2,1)}), bf16[2048,896]{0,1:T(8,128)(2,1)}) %all-gather.29.cloned.1.call-update) | async-done | bytes 3670032 | tf_op jit(solution)/shard_map/all_gather | solution.py:252
  749.4 11.8 %reduce-scatter.25.cloned.1.call-done = bf16[896,1,152]{0,2,1:T(8,128)(2,1)} async-done(((bf16[896,2,152]{0,2,1:T(8,128)(2,1)}), bf16[896,1,152]{0,2,1:T(8,128)(2,1)}) %reduce-scatter.25.cloned.1.call-update) | async-done | bytes 272400
  761.2 17.8 %reduce-scatter.27.cloned.1.call-done = bf16[896,1,152]{0,2,1:T(8,128)(2,1)} async-done(((bf16[896,2,152]{0,2,1:T(8,128)(2,1)}), bf16[896,1,152]{0,2,1:T(8,128)(2,1)}) %reduce-scatter.27.cloned.1.call-update) | async-done | bytes 272400
  779.1 17.7 %reduce-scatter.29.cloned.1.call-done = bf16[1,152,896]{2,1,0:T(8,128)(2,1)} async-done(((bf16[2,152,896]{2,1,0:T(8,128)(2,1)}), bf16[1,152,896]{2,1,0:T(8,128)(2,1)}) %reduce-scatter.29.cloned.1.call-update) | async-done | bytes 272400
  804.5 39.6 %all-reduce.3 = (f32[1152]{0:T(1024)}, f32[896]{0:T(1024)}, f32[896]{0:T(1024)}) all-reduce(f32[1152]{0:T(1024)S(1)} %get-tuple-element.424, f32[896]{0:T(1024)S(1)} %get-tuple-element.371, f32[896]{0:T(1024)S(1)} %get-tuple-element.369), channel_id=1, replica_groups=mesh['dp'=2,'ctx'=16] {'dp','ctx'}, use_global_device_ids=true, to_apply=%region_16.17 | all-reduce | flops 2944 | bytes 23552 | tf_op jit(solution)/shard_map/psum | solution.py:299
  846.2 28.3 %all_gather.52 = bf16[448,1152]{0,1:T(8,128)(2,1)S(1)} all-gather(bf16[448,72]{0,1:T(8,128)(2,1)S(1)} %copy.143), channel_id=1, replica_groups=mesh['dp'=2,'ctx'=16] {'ctx'}, dimensions={1}, use_global_device_ids=true | all-gather | bytes 1096704 | tf_op jit(solution)/shard_map/all_gather | solution.py:278
  877.2 23.3 %all_gather.54 = bf16[448,896]{0,1:T(8,128)(2,1)S(1)} all-gather(bf16[448,56]{0,1:T(8,128)(2,1)S(1)} %copy.145), channel_id=1, replica_groups=mesh['dp'=2,'ctx'=16] {'ctx'}, dimensions={1}, use_global_device_ids=true | all-gather | bytes 852992 | tf_op jit(solution)/shard_map/all_gather | solution.py:281
  908.2 10.5 %copy.127 = f32[896,2432]{1,0:T(8,128)} copy(f32[896,2432]{0,1:T(8,128)} %bitcast_convert_fusion.2) | data formatting | bytes 17432576
  918.8 21.1 %all-gather.35.cloned.1.call-done = bf16[896,1,2432]{0,2,1:T(8,128)(2,1)} async-done(((bf16[896,1,152]{0,2,1:T(8,128)(2,1)}), bf16[896,1,2432]{0,2,1:T(8,128)(2,1)}) %all-gather.35.cloned.1.call-update) | async-done | bytes 4358160 | tf_op jit(solution)/shard_map/all_gather | solution.py:287
  946.2 10.6 %copy.128 = f32[896,2432]{1,0:T(8,128)} copy(f32[896,2432]{0,1:T(8,128)} %bitcast_convert_fusion.1) | data formatting | bytes 17432576
  956.7 35.5 %all-gather.37.cloned.1.call-done = bf16[1,2432,896]{2,1,0:T(8,128)(2,1)} async-done(((bf16[1,152,896]{2,1,0:T(8,128)(2,1)}), bf16[1,2432,896]{2,1,0:T(8,128)(2,1)}) %all-gather.37.cloned.1.call-update) | async-done | bytes 4358160 | tf_op jit(solution)/shard_map/all_gather | solution.py:290
  (261 shorter events, 225.9 us)
Async XLA Ops:
  7.2 37.9 %all-gather.15.cloned.1.call-start = ((), (), s32[]{:S(2)}) async-start(), calls=%async_computation.11 | async-start | bytes 3096576 | tf_op jit(solution)/shard_map/all_gather | solution.py:63
  7.9 78.3 %all-gather.17.cloned.1.call-start = ((), (), s32[]{:S(2)}) async-start(), calls=%async_computation.12 | async-start | bytes 1114112 | tf_op jit(solution)/shard_map/all_gather | solution.py:83
  48.1 66.2 %all-gather.19.cloned.1.call-start = ((), (), s32[]{:S(2)}) async-start(), calls=%async_computation.13 | async-start | bytes 2408448 | tf_op jit(solution)/shard_map/all_gather | solution.py:64
  48.8 176.9 %all-gather.21.cloned.1.call-start = ((), (), s32[]{:S(2)}) async-start(), calls=%async_computation.14 | async-start | bytes 13074432 | tf_op jit(solution)/shard_map/all_gather | solution.py:65
  49.4 287.9 %all-gather.23.cloned.1.call-start = ((), (), s32[]{:S(2)}) async-start(), calls=%async_computation.15 | async-start | bytes 13074432 | tf_op jit(solution)/shard_map/all_gather | solution.py:66
  50.0 398.8 %all-gather.25.cloned.1.call-start = ((), (), s32[]{:S(2)}) async-start(), calls=%async_computation.16 | async-start | bytes 13074432 | tf_op jit(solution)/shard_map/all_gather | solution.py:67
  50.6 541.4 %all-gather.31.cloned.1.call-start = ((), (), s32[]{:S(2)}) async-start(), calls=%async_computation.19 | async-start | bytes 3899392 | tf_op jit(solution)/shard_map/all_gather | solution.py:253
  117.1 487.1 %reduce-scatter.19.cloned.1.call-start = ((), (), s32[]{:S(2)}) async-start(), calls=%async_computation.24 | async-start | bytes 1114112
  505.6 145.7 %all-gather.39.cloned.1.call-start = ((), (), s32[]{:S(2)}) async-start(), calls=%async_computation.23 | async-start | bytes 3899392 | tf_op jit(solution)/shard_map/all_gather | solution.py:254
  506.4 187.5 %all-gather.27.cloned.1.call-start = ((), (), s32[]{:S(2)}) async-start(), calls=%async_computation.17 | async-start | bytes 3899392 | tf_op jit(solution)/shard_map/all_gather | solution.py:251
  507.0 238.3 %all-gather.29.cloned.1.call-start = ((), (), s32[]{:S(2)}) async-start(), calls=%async_computation.18 | async-start | bytes 3899392 | tf_op jit(solution)/shard_map/all_gather | solution.py:252
  511.5 34.9 %all-to-all-start.2 = ((bf16[128,2,16,152]{0,3,1,2:T(8,128)(2,1)}), bf16[128,2,16,152]{0,3,1,2:T(8,128)(2,1)}, u32[]{:S(2)}, u32[]{:S(2)}) async-start(bf16[128,2,16,152]{0,3,1,2:T(8,128)(2,1)} %copy.117), calls=%async_computation.2 | async-start | bytes 2490368 | tf_op jit(solution)/shard_map/all_to_all | solution.py:224
  546.4 37.6 %all-to-all-start.3 = ((bf16[128,2,16,152]{0,3,1,2:T(8,128)(2,1)}), bf16[128,2,16,152]{0,3,1,2:T(8,128)(2,1)}, u32[]{:S(2)}, u32[]{:S(2)}) async-start(bf16[128,2,16,152]{0,3,1,2:T(8,128)(2,1)} %copy.120), calls=%async_computation.3 | async-start | bytes 2490368 | tf_op jit(solution)/shard_map/all_to_all | solution.py:231
  584.0 43.8 %all-to-all-start.4 = ((bf16[128,2,16,152]{0,3,1,2:T(8,128)(2,1)}), bf16[128,2,16,152]{0,3,1,2:T(8,128)(2,1)}, u32[]{:S(2)}, u32[]{:S(2)}) async-start(bf16[128,2,16,152]{0,3,1,2:T(8,128)(2,1)} %copy.123), calls=%async_computation.4 | async-start | bytes 2490368 | tf_op jit(solution)/shard_map/all_to_all | solution.py:238
  591.9 169.3 %reduce-scatter.25.cloned.1.call-start = ((), (), s32[]{:S(2)}) async-start(), calls=%async_computation.27 | async-start | bytes 817152
  596.7 182.3 %reduce-scatter.27.cloned.1.call-start = ((), (), s32[]{:S(2)}) async-start(), calls=%async_computation.28 | async-start | bytes 817152
  627.9 29.1 %all-to-all-start.1 = ((bf16[128,1,16,56]{0,3,1,2:T(8,128)(2,1)}), bf16[128,1,16,56]{0,3,1,2:T(8,128)(2,1)S(1)}, u32[]{:S(2)}, u32[]{:S(2)}) async-start(bf16[128,1,16,56]{0,3,1,2:T(8,128)(2,1)} %bitcast.28), calls=%async_computation.1 | async-start | bytes 458752 | tf_op jit(solution)/shard_map/all_to_all | solution.py:217
  645.2 151.7 %reduce-scatter.29.cloned.1.call-start = ((), (), s32[]{:S(2)}) async-start(), calls=%async_computation.29 | async-start | bytes 817152
  656.9 16.6 %all-to-all-start = ((bf16[128,1,16,72]{0,3,1,2:T(8,128)(2,1)}), bf16[128,1,16,72]{0,3,1,2:T(8,128)(2,1)S(1)}, u32[]{:S(2)}, u32[]{:S(2)}) async-start(bf16[128,1,16,72]{0,3,1,2:T(8,128)(2,1)} %bitcast.24), calls=%async_computation | async-start | bytes 589824 | tf_op jit(solution)/shard_map/all_to_all | solution.py:210
  663.0 182.2 %reduce-scatter.21.cloned.1.call-start = ((), (), s32[]{:S(2)}) async-start(), calls=%async_computation.25 | async-start | bytes 344064
  697.4 178.8 %reduce-scatter.23.cloned.1.call-start = ((), (), s32[]{:S(2)}) async-start(), calls=%async_computation.26 | async-start | bytes 344064
  749.4 152.5 %all-gather.33.cloned.1.call-start = ((), (), s32[]{:S(2)}) async-start(), calls=%async_computation.20 | async-start | bytes 4630528 | tf_op jit(solution)/shard_map/all_gather | solution.py:284
  761.2 178.7 %all-gather.35.cloned.1.call-start = ((), (), s32[]{:S(2)}) async-start(), calls=%async_computation.21 | async-start | bytes 4630528 | tf_op jit(solution)/shard_map/all_gather | solution.py:287
  779.1 213.1 %all-gather.37.cloned.1.call-start = ((), (), s32[]{:S(2)}) async-start(), calls=%async_computation.22 | async-start | bytes 4630528 | tf_op jit(solution)/shard_map/all_gather | solution.py:290
  (32 other events, 866.3 us)
Sparse Core Ops, SparseCore 0:
  9.6 35.4 all-gather.14
  48.2 37.9 all-gather.16
  87.7 26.4 all-gather.18
  115.7 110.0 all-gather.20
  227.2 110.0 all-gather.22
  338.7 110.0 all-gather.24
  451.7 47.4 all-gather.30
  505.8 67.0 reduce-scatter.18
  575.4 68.8 all-gather.38
  646.7 47.0 all-gather.26
  696.2 48.9 all-gather.28
  748.0 13.0 reduce-scatter.24
  764.1 14.9 reduce-scatter.26
  781.9 14.9 reduce-scatter.28
  799.6 11.2 reduce-scatter.20
  813.6 11.6 reduce-scatter.22
  827.5 58.5 all-gather.32
  888.4 51.4 all-gather.34
  942.2 49.9 all-gather.36
where the time goes:
time: 1010 us
  waiting for transfers between devices  645 us (64%)
  matrix products  103 us (10%)
  blocking collectives  91.1 us (9%)
  local copies, waits for them, and re-layouts  63 us (6%)
  starting transfers between devices  46.6 us (5%)
  other arithmetic  40.6 us (4%)
  between operations  15.2 us (2%)
    all_gather x1, waiting for transfers between devices, local(): lax.all_gather(shards[2], 'dp', axis=1, tiled=True)  108 us
    all_gather x1, waiting for transfers between devices, local(): lax.all_gather(shards[4], 'dp', axis=0, tiled=True)  105 us
    all_gather x1, waiting for transfers between devices, local(): lax.all_gather(shards[3], 'dp', axis=1, tiled=True)  105 us
    unnamed x25, waiting for transfers between devices  52.3 us
    all_gather x1, waiting for transfers between devices, local(): attended_p = lax.all_gather(attended_low, 'ctx', axis=0, tiled=True)  47.8 us
    psum x1, blocking collectives, local(): lax.psum((grad_gain_one, grad_gain_two, grad_bias), ('dp', 'ctx'))  39.6 us
    all_gather x1, waiting for transfers between devices, local(): lax.all_gather(summed[4].astype(jnp.bfloat16), 'ctx', axis=1, tiled=True)  35.5 us
    all_gather x1, waiting for transfers between devices, local(): all_pairs = lax.all_gather(local_pairs, 'ctx', axis=0, tiled=True)  35.1 us
  transfers between devices with their start and end apart: 24, of which 17 were waited for; matrix products, arithmetic and copies ran while one was open for 19% of the time, Pallas kernels for 0%

commit v1 on v0

v1 whole, which is shorter than its diff:
```python
import jax
import jax.numpy as jnp
from jax import lax
from jax.sharding import PartitionSpec as P

D = 896
QH = 14
KH = 2
HD = 64
GROUP = QH // KH
WIDTH_Q = QH * HD
WIDTH_K = KH * HD

EPS = 1e-06
ROPE_BASE = 1000000.0

f32 = jnp.float32
bf16 = jnp.bfloat16


def rotary_tables(place):
    freq = ROPE_BASE ** (-(jnp.arange(HD // 2).astype(f32) * (2.0 / HD)))
    angle = place.astype(f32)[:, None] * freq[None, :]
    angle = jnp.concatenate([angle, angle], 1)
    return (jnp.cos(angle), jnp.sin(angle))


def rotate_apply(heads, cosine, sine):
    first = heads[..., : HD // 2]
    second = heads[..., HD // 2 :]
    turned = jnp.concatenate([-second, first], -1)
    return heads * cosine[:, None, :] + turned * sine[:, None, :]


def rotate_back(grads, cosine, sine):
    scaled = grads * sine[:, None, :]
    first = scaled[..., : HD // 2]
    second = scaled[..., HD // 2 :]
    return grads * cosine[:, None, :] + jnp.concatenate([second, -first], -1)


def ring_order(chips):
    if chips % 2:
        return list(range(chips))
    rows = chips // 2
    return [2 * i for i in range(rows)] + [2 * i + 1 for i in reversed(range(rows))]


def half_cut(rows):
    cut = (rows // 2 + 7) // 8 * 8
    return cut if cut < rows else rows // 2


class Net:
    def __init__(self):
        self.dp = lax.axis_size("dp")
        self.ctx = lax.axis_size("ctx")
        self.chips = self.ctx // 2
        self.order = ring_order(self.chips)
        self.d = lax.axis_index("dp")
        self.c = lax.axis_index("ctx")
        self.core = self.c % 2
        place = [0] * self.chips
        for spot, chip in enumerate(self.order):
            place[chip] = spot
        self.pos = jnp.array(place, jnp.int32)[self.c // 2]

    def swap(self, x):
        return lax.ppermute(x, "ctx", [(i, i ^ 1) for i in range(self.ctx)])

    def shift(self, x, step):
        n = self.dp
        return lax.ppermute(x, "dp", [(i, (i + step) % n) for i in range(n)])

    def hop(self, x, step):
        n = self.chips
        perm = []
        for spot in range(n):
            for core in range(2):
                perm.append((2 * self.order[spot] + core, 2 * self.order[(spot + step) % n] + core))
        return lax.ppermute(x, "ctx", perm)

    def owner(self, slot):
        return (self.pos - slot) % self.chips

    def group_gather(self, x):
        parts = [x] + [self.shift(x, s) for s in range(1, self.dp)]
        parts = parts + [self.swap(p) for p in parts]
        return jnp.concatenate(parts, 0)

    def group_scatter(self, x, rows):
        half = self.dp * rows
        mine = x[:half] + self.swap(x[half:].astype(bf16)).astype(f32)
        total = mine[:rows]
        for s in range(1, self.dp):
            got = self.shift(mine[s * rows : (s + 1) * rows].astype(bf16), self.dp - s)
            total = total + got.astype(f32)
        return total

    def ring_gather(self, x):
        n = self.chips
        half = n // 2
        cut = half_cut(x.shape[0])
        found = [x] + [None] * (n - 1)
        fwd, back = x, x
        for s in range(1, half):
            fwd = self.hop(fwd, 1)
            back = self.hop(back, -1)
            found[s] = fwd
            found[n - s] = back
        found[half] = jnp.concatenate([self.hop(fwd[:cut], 1), self.hop(back[cut:], -1)], 0)
        return found

    def ring_scatter(self, local):
        n = self.chips
        half = n // 2
        cut = half_cut(local[half].shape[0])

        def add(got, mine):
            return (got.astype(f32) + mine.astype(f32)).astype(bf16)

        fwd = self.hop(local[half][:cut], 1)
        back = self.hop(local[half][cut:], -1)
        for s in range(1, half):
            mine_f = local[half + s]
            mine_b = local[half - s]
            if s == 1:
                mine_f = jnp.concatenate([add(fwd, mine_f[:cut]), mine_f[cut:]], 0)
                mine_b = jnp.concatenate([mine_b[:cut], add(back, mine_b[cut:])], 0)
            else:
                mine_f = add(fwd, mine_f)
                mine_b = add(back, mine_b)
            fwd = self.hop(mine_f, 1)
            back = self.hop(mine_b, -1)
        return fwd.astype(f32) + back.astype(f32) + local[0].astype(f32)

    def full_rows(self, shard):
        rows = shard.shape[0]
        half = rows // 2
        full = jnp.zeros((rows * self.dp, shard.shape[1]), shard.dtype)
        full = lax.dynamic_update_slice(full, shard, (self.d * rows, 0))
        piece = lax.dynamic_slice(shard, (self.core * half, 0), (half, shard.shape[1]))
        for s in range(1, self.dp):
            got = self.shift(piece, s)
            other = self.swap(got)
            base = ((self.d - s) % self.dp) * rows
            full = lax.dynamic_update_slice(full, got, (base + self.core * half, 0))
            full = lax.dynamic_update_slice(full, other, (base + (1 - self.core) * half, 0))
        return full

    def total(self, x):
        x = x + self.swap(x)
        bit = 1
        while bit < self.chips:
            x = x + lax.ppermute(x, "ctx", [(i, i ^ (2 * bit)) for i in range(self.ctx)])
            bit *= 2
        bit = 1
        while bit < self.dp:
            x = x + lax.ppermute(x, "dp", [(i, i ^ bit) for i in range(self.dp)])
            bit *= 2
        return x


def local(tokens, w_qkv, b_qkv, w_out, gain_attn, gain_mlp, w_gate, w_up, w_down, cotangent):
    net = Net()
    rows = tokens.shape[1]
    half_rows = rows // 2
    ctx_count = net.ctx
    core = net.core
    chips = net.chips
    scale = HD ** (-0.5)

    w_qkv_full = net.full_rows(w_qkv)
    w_out_full = net.full_rows(w_out)
    grad_out_low = cotangent[0]
    grad_out_group = net.group_gather(grad_out_low)

    ff_loc = w_gate.shape[1]
    ff_half = ff_loc // 2
    main = (ff_half // 128) * 128
    rest = ff_half - main
    width = main + 2 * rest
    first = core * main
    own_cols = (jnp.arange(width) + first < ff_half) == (core == 0)
    wg = lax.dynamic_slice(w_gate, (0, first), (D, width))
    wu = lax.dynamic_slice(w_up, (0, first), (D, width))
    wd = lax.dynamic_slice(w_down, (first, 0), (width, D))

    resid_in = tokens[0].astype(f32)
    row_ids = jnp.arange(half_rows, dtype=jnp.int32)
    query_place = jnp.concatenate(
        [net.c * half_rows + row_ids, (2 * ctx_count - 1 - net.c) * half_rows + row_ids]
    )
    cosine, sine = rotary_tables(query_place)
    inverse_one = lax.rsqrt(jnp.mean(resid_in * resid_in, -1, keepdims=True) + EPS)
    unit_one = resid_in * inverse_one
    normed_one = (unit_one * gain_attn).astype(bf16)
    joint = jnp.dot(normed_one, w_qkv_full, preferred_element_type=f32) + b_qkv
    queries = rotate_apply(joint[:, :WIDTH_Q].reshape(rows, QH, HD), cosine, sine).astype(bf16)
    queries = queries.reshape(rows, KH, GROUP, HD)
    keys_local = rotate_apply(
        joint[:, WIDTH_Q : WIDTH_Q + WIDTH_K].reshape(rows, KH, HD), cosine, sine
    ).astype(bf16)
    values_local = joint[:, WIDTH_Q + WIDTH_K :].astype(bf16)
    local_pairs = jnp.concatenate([keys_local.reshape(rows, WIDTH_K), values_local], 1)

    slots = net.ring_gather(local_pairs)
    mine = jnp.concatenate(slots, 0)
    all_pairs = jnp.concatenate([mine, net.swap(mine)], 0)
    order = jnp.array(net.order, jnp.int32)
    chip_ids = order[(net.pos - jnp.arange(chips, dtype=jnp.int32)) % chips]
    slot_ids = jnp.concatenate([2 * chip_ids + core, 2 * chip_ids + 1 - core])
    key_place = jnp.concatenate(
        [
            slot_ids[:, None] * half_rows + row_ids[None],
            (2 * ctx_count - 1 - slot_ids)[:, None] * half_rows + row_ids[None],
        ],
        1,
    ).reshape(-1)

    total_keys = all_pairs.shape[0]
    key_block = min(1024, total_keys)
    block_count = total_keys // key_block
    pair_blocks = all_pairs.reshape(block_count, key_block, 2 * WIDTH_K)
    place_blocks = key_place.reshape(block_count, key_block)

    def block_scores(pair_block, place_block):
        key_heads = pair_block[:, :WIDTH_K].reshape(key_block, KH, HD)
        value_heads = pair_block[:, WIDTH_K:].reshape(key_block, KH, HD)
        scores = (
            jnp.einsum("qhgd,khd->hgqk", queries, key_heads, preferred_element_type=f32) * scale
        )
        allowed = place_block[None, None, None, :] <= query_place[None, None, :, None]
        return (jnp.where(allowed, scores, -1e30), key_heads, value_heads)

    def gather_stats(carry, pieces):
        run_max, run_sum = carry
        scores, key_heads, value_heads = block_scores(pieces[0], pieces[1])
        new_max = jnp.maximum(run_max, jnp.max(scores, -1, keepdims=True))
        run_sum = run_sum * jnp.exp(run_max - new_max) + jnp.sum(
            jnp.exp(scores - new_max), -1, keepdims=True
        )
        return ((new_max, run_sum), None)

    start_max = jnp.full((KH, GROUP, rows, 1), -1e30, f32)
    start_sum = jnp.zeros((KH, GROUP, rows, 1), f32)
    (run_max, run_sum), unused = lax.scan(
        gather_stats, (start_max, start_sum), (pair_blocks, place_blocks)
    )
    log_total = run_max + jnp.log(run_sum)

    def weighted_sum(acc, pieces):
        scores, key_heads, value_heads = block_scores(pieces[0], pieces[1])
        probs_low = jnp.exp(scores - log_total).astype(bf16)
        acc = acc + jnp.einsum("hgqk,khd->qhgd", probs_low, value_heads, preferred_element_type=f32)
        return (acc, None)

    attended, unused = lax.scan(
        weighted_sum, jnp.zeros((rows, KH, GROUP, HD), f32), (pair_blocks, place_blocks)
    )
    attended_low = attended.reshape(rows, WIDTH_Q).astype(bf16)
    hidden = resid_in + jnp.dot(attended_low, w_out_full, preferred_element_type=f32)
    inverse_two = lax.rsqrt(jnp.mean(hidden * hidden, -1, keepdims=True) + EPS)
    unit_two = hidden * inverse_two
    normed_two = (unit_two * gain_mlp).astype(bf16)

    normed_two_group = net.group_gather(normed_two)
    gate = jnp.dot(normed_two_group, wg, preferred_element_type=f32)
    upper = jnp.dot(normed_two_group, wu, preferred_element_type=f32)
    sigma = jax.nn.sigmoid(gate)
    activated = gate * sigma
    middle = jnp.where(own_cols, activated * upper, 0.0).astype(bf16)
    grad_middle = jnp.einsum("td,fd->tf", grad_out_group, wd, preferred_element_type=f32)
    slope = sigma * (1.0 + gate * (1.0 - sigma))
    grad_gate_low = jnp.where(own_cols, grad_middle * upper * slope, 0.0).astype(bf16)
    grad_up_low = jnp.where(own_cols, grad_middle * activated, 0.0).astype(bf16)

    part_down = jnp.einsum(
        "tf,td->fd", middle, grad_out_group, preferred_element_type=f32
    ).astype(bf16)
    part_down = lax.dynamic_slice(part_down, (core * rest, 0), (ff_half, D))
    down_rows = ff_half // chips

    def down_chunk(slot):
        return lax.dynamic_slice(part_down, (net.owner(slot) * down_rows, 0), (down_rows, D))

    sum_down = net.ring_scatter([down_chunk(s) for s in range(chips)]).astype(bf16)
    sum_down = lax.optimization_barrier(sum_down)

    def split_main(x):
        left = (x[:, :main], x[:, main:])
        right = (x[:, 2 * rest :], x[:, : 2 * rest])
        return (
            jnp.where(core == 0, left[0], right[0]),
            jnp.where(core == 0, left[1], right[1]),
        )

    gate_main, gate_tile = split_main(grad_gate_low)
    up_main, up_tile = split_main(grad_up_low)
    packed = jnp.concatenate(
        [gate_main, up_main, gate_tile + jnp.roll(up_tile, rest, 1)], 1
    )
    part_mlp = jnp.einsum(
        "td,tf->df", normed_two_group, packed, preferred_element_type=f32
    ).astype(bf16)
    mlp_rows = D // chips

    def mlp_chunk(slot):
        return lax.dynamic_slice(
            part_mlp, (net.owner(slot) * mlp_rows, 0), (mlp_rows, 2 * ff_half)
        )

    sum_mlp = net.ring_scatter([mlp_chunk(s) for s in range(chips)]).astype(bf16)
    sum_mlp = lax.optimization_barrier(sum_mlp)

    grad_normed_two = jnp.einsum(
        "tf,df->td", grad_gate_low, wg, preferred_element_type=f32
    ) + jnp.einsum("tf,df->td", grad_up_low, wu, preferred_element_type=f32)
    grad_normed_two = net.group_scatter(grad_normed_two, rows)
    mlp_out = jnp.dot(middle, wd, preferred_element_type=f32)
    output = (hidden + net.group_scatter(mlp_out, rows)).astype(bf16)
    grad_out = grad_out_low.astype(f32)
    grad_gain_two = jnp.sum(grad_normed_two * unit_two, 0)
    scaled_two = grad_normed_two * gain_mlp
    grad_hidden = grad_out + inverse_two * (
        scaled_two - unit_two * jnp.mean(scaled_two * unit_two, -1, keepdims=True)
    )
    grad_attn_low = grad_hidden.astype(bf16)
    grad_heads = jnp.einsum(
        "td,cd->tc", grad_attn_low, w_out_full, preferred_element_type=f32
    ).astype(bf16)
    grad_heads = grad_heads.reshape(rows, KH, GROUP, HD)
    delta = jnp.sum(grad_heads.astype(f32) * attended, -1)
    delta = jnp.transpose(delta, (1, 2, 0))[..., None]

    def attention_back(grad_queries, pieces):
        scores, key_heads, value_heads = block_scores(pieces[0], pieces[1])
        probs = jnp.exp(scores - log_total)
        probs_low = probs.astype(bf16)
        grad_probs = jnp.einsum(
            "qhgd,khd->hgqk", grad_heads, value_heads, preferred_element_type=f32
        )
        grad_scores = (probs * (grad_probs - delta)).astype(bf16)
        grad_queries = grad_queries + jnp.einsum(
            "hgqk,khd->qhgd", grad_scores, key_heads, preferred_element_type=f32
        )
        grad_keys = (
            jnp.einsum("hgqk,qhgd->khd", grad_scores, queries, preferred_element_type=f32) * scale
        )
        grad_values = jnp.einsum(
            "hgqk,qhgd->khd", probs_low, grad_heads, preferred_element_type=f32
        )
        joined = jnp.concatenate(
            [grad_keys.reshape(key_block, WIDTH_K), grad_values.reshape(key_block, WIDTH_K)], 1
        )
        return (grad_queries, joined)

    grad_queries, pair_terms = lax.scan(
        attention_back, jnp.zeros((rows, KH, GROUP, HD), f32), (pair_blocks, place_blocks)
    )
    pair_terms = pair_terms.reshape(2, chips, rows, 2 * WIDTH_K)
    pair_sums = pair_terms[0] + net.swap(pair_terms[1].astype(bf16)).astype(f32)
    pair_sums = pair_sums.astype(bf16)
    grad_pairs = net.ring_scatter([pair_sums[s] for s in range(chips)])
    grad_queries = rotate_back((grad_queries * scale).reshape(rows, QH, HD), cosine, sine)
    grad_keys = rotate_back(grad_pairs[:, :WIDTH_K].reshape(rows, KH, HD), cosine, sine)
    grad_joint_low = jnp.concatenate(
        [
            grad_queries.reshape(rows, WIDTH_Q),
            grad_keys.reshape(rows, WIDTH_K),
            grad_pairs[:, WIDTH_K:],
        ],
        1,
    ).astype(bf16)
    grad_bias = jnp.sum(grad_joint_low.astype(f32), 0)
    grad_normed_one = jnp.einsum(
        "tc,dc->td", grad_joint_low, w_qkv_full, preferred_element_type=f32
    )
    grad_gain_one = jnp.sum(grad_normed_one * unit_one, 0)
    scaled_one = grad_normed_one * gain_attn
    grad_input = grad_hidden + inverse_one * (
        scaled_one - unit_one * jnp.mean(scaled_one * unit_one, -1, keepdims=True)
    )
    small = net.total(jnp.concatenate([grad_gain_one, grad_gain_two, grad_bias]))

    q_rows = w_qkv.shape[0] // 2
    q_first = net.d * (2 * q_rows) + core * q_rows
    attended_group = lax.dynamic_slice(
        net.group_gather(attended_low), (0, q_first), (2 * net.dp * rows, q_rows)
    )
    normed_one_group = lax.dynamic_slice(
        net.group_gather(normed_one), (0, q_first), (2 * net.dp * rows, q_rows)
    )
    part_out = jnp.einsum(
        "tc,td->cd", attended_group, net.group_gather(grad_attn_low), preferred_element_type=f32
    )
    part_joint = jnp.einsum(
        "td,tc->dc", normed_one_group, net.group_gather(grad_joint_low), preferred_element_type=f32
    )
    part_small = jnp.concatenate([part_joint, part_out], 1).astype(bf16)
    small_cols = part_small.shape[1] // chips

    def small_chunk(slot):
        return lax.dynamic_slice(part_small, (0, net.owner(slot) * small_cols), (q_rows, small_cols))

    sum_small = net.ring_scatter([small_chunk(s) for s in range(chips)]).astype(bf16)
    sum_small = lax.optimization_barrier(sum_small)

    grad_down = jnp.zeros((ff_loc, D), f32)
    for s, got in enumerate(net.ring_gather(sum_down)):
        other = net.swap(got)
        base = net.owner(s) * down_rows
        grad_down = lax.dynamic_update_slice(
            grad_down, got.astype(f32), (core * ff_half + base, 0)
        )
        grad_down = lax.dynamic_update_slice(
            grad_down, other.astype(f32), ((1 - core) * ff_half + base, 0)
        )
    grad_gate = jnp.zeros((D, ff_loc), f32)
    grad_up = jnp.zeros((D, ff_loc), f32)
    left_lane = jnp.arange(2 * rest) < rest
    for s, got in enumerate(net.ring_gather(sum_mlp)):
        other = net.swap(got)
        zero = jnp.where(core == 0, got, other).astype(f32)
        one = jnp.where(core == 0, other, got).astype(f32)
        tile_zero, tile_one = zero[:, 2 * main :], one[:, 2 * main :]
        mid_gate = jnp.where(left_lane, tile_zero, tile_one)
        mid_up = jnp.roll(jnp.where(left_lane, tile_one, tile_zero), rest, 1)
        base = net.owner(s) * mlp_rows
        grad_gate = lax.dynamic_update_slice(
            grad_gate, jnp.concatenate([zero[:, :main], mid_gate, one[:, :main]], 1), (base, 0)
        )
        grad_up = lax.dynamic_update_slice(
            grad_up,
            jnp.concatenate([zero[:, main : 2 * main], mid_up, one[:, main : 2 * main]], 1),
            (base, 0),
        )
    grad_small = jnp.zeros((2 * q_rows, part_small.shape[1]), f32)
    for s, got in enumerate(net.ring_gather(sum_small)):
        other = net.swap(got)
        base = net.owner(s) * small_cols
        grad_small = lax.dynamic_update_slice(grad_small, got.astype(f32), (core * q_rows, base))
        grad_small = lax.dynamic_update_slice(
            grad_small, other.astype(f32), ((1 - core) * q_rows, base)
        )
    qkv_cols = w_qkv.shape[1]
    return (
        output[None],
        grad_input[None],
        grad_small[:, :qkv_cols],
        small[2 * D :],
        grad_small[:, qkv_cols:],
        small[:D],
        small[D : 2 * D],
        grad_gate,
        grad_up,
        grad_down,
    )


def solution(mesh):
    placed = (
        P("dp", "ctx", None),
        P("dp", None),
        P(),
        P("dp", None),
        P(),
        P(),
        P(None, "dp"),
        P(None, "dp"),
        P("dp", None),
        P("dp", "ctx", None),
    )
    return jax.shard_map(
        local,
        mesh=mesh,
        in_specs=placed,
        out_specs=(
            P("dp", "ctx", None),
            P("dp", "ctx", None),
            P("dp", None),
            P(),
            P("dp", None),
            P(),
            P(),
            P(None, "dp"),
            P(None, "dp"),
            P("dp", None),
        ),
        check_vma=False,
    )
```

time: 1010 us -> 514 us (0.51)
  waiting for transfers between devices: 645 us -> 183 us
  blocking collectives: 91.1 us -> 0 us
  starting transfers between devices: 46.6 us -> 103 us
  matrix products: 103 us -> 77.9 us
  local copies, waits for them, and re-layouts: 63 us -> 83.2 us
    all_gather x13 -> x0, waiting for transfers between devices: 513 us -> none  [the longest x1 108 us: local(): lax.all_gather(shards[2], 'dp', axis=1, tiled=True)]
    ppermute x0 -> x121, waiting for transfers between devices: none -> 183 us  [the longest x64 137 us: hop(): return lax.ppermute(x, 'ctx', perm)]
    ppermute x0 -> x121, starting transfers between devices: none -> 103 us  [the longest x64 76.5 us: hop(): return lax.ppermute(x, 'ctx', perm)]
    all_to_all x5 -> x0, waiting for transfers between devices: 79.6 us -> none  [the longest x1 24.5 us: local(): lax.all_to_all(split_columns(grad_gate_low, dp_count, ctx_count), 'ctx',...]
    unnamed x25 -> x0, waiting for transfers between devices: 52.3 us -> none
    all_gather x2 -> x0, blocking collectives: 51.6 us -> none  [the longest x1 28.3 us: local(): lax.all_gather(summed[0].astype(jnp.bfloat16), 'ctx', axis=1, tiled=True)]
    all_to_all x5 -> x0, starting transfers between devices: 45.7 us -> none  [the longest x1 17.3 us: local(): lax.all_to_all(split_columns(grad_attn_low, 1, ctx_count), 'ctx', split_a...]
    psum x1 -> x0, blocking collectives: 39.6 us -> none  [local(): lax.psum((grad_gain_one, grad_gain_two, grad_bias), ('dp', 'ctx'))]
  transfers between devices with their start and end apart: 24 -> 121, of which waited for: 17 -> 55; matrix products, arithmetic and copies ran while one was open for 19% -> 37% of each run, Pallas kernels for 0% -> 0%
where the time goes in v1:
time: 514 us; the launch traced here: 506 us
  waiting for transfers between devices  183 us (36%)
  starting transfers between devices  103 us (20%)
  local copies, waits for them, and re-layouts  83.2 us (16%)
  matrix products  77.9 us (15%)
  other arithmetic  49.1 us (10%)
  between operations  9.89 us (2%)
    ppermute x64, waiting for transfers between devices, hop(): return lax.ppermute(x, 'ctx', perm)  137 us
    ppermute x64, starting transfers between devices, hop(): return lax.ppermute(x, 'ctx', perm)  76.5 us
    ppermute x10, waiting for transfers between devices, shift(): return lax.ppermute(x, 'dp', [(i, (i + step) % n) for i in range(n)])  28.7 us
    ppermute x10, starting transfers between devices, shift(): return lax.ppermute(x, 'dp', [(i, (i + step) % n) for i in range(n)])  13.3 us
    ppermute x3, waiting for transfers between devices, total(): x = x + lax.ppermute(x, 'ctx', [(i, i ^ 2 * bit) for i in range(self.ctx)])  12.4 us
    dot_general x4, matrix products, block_scores(): jnp.einsum('qhgd,khd->hgqk', queries, key_heads, preferred_element_type=f32)  10.8 us
  transfers between devices with their start and end apart: 121, of which 55 were waited for; matrix products, arithmetic and copies ran while one was open for 37% of the time, Pallas kernels for 0%

profile of v1, /device:TPU:0, one launch (start us, length us, event | category | flops | bytes accessed | tf_op | source)
XLA Modules:
  0.0 506.1 jit_solution(4285551348390787953)
XLA Ops:
  18.8 8.4 %collective-permute-done.11 = bf16[224,896]{1,0:T(8,128)(2,1)} collective-permute-done((bf16[224,896]{1,0:T(8,128)(2,1)}, bf16[224,896]{1,0:T(8,128)(2,1)}, u32[]{:S(2)}, u32[]{:S(2)}) %collective-permute-start.11) | collective-permute-done | bytes 401440 | tf_op jit(solution)/shard_map/ppermute | solution.py:73
  56.4 18.3 %while.37 = (s32[]{:T(128)}, f32[2,7,128,1]{2,1,0,3:T(8,128)S(1)}, f32[2,7,128,1]{2,1,0,3:T(8,128)S(1)}, s32[2,1024]{1,0:T(2,128)S(1)}, s32[128]{0:T(128)S(1)}, ...) while((s32[]{:T(128)}, f32[2,7,128,1]{2,1,0,3:T(8,128)S(1)}, ...), condition=%wide.region_4.5_spmd.clone, body=%wide.region_1.4_spmd.clone.sunk | while | flops 247866112 | bytes 17243768 | solution.py:247
  60.9 4.6 exponential_reduce_fusion.2
  70.1 4.6 exponential_reduce_fusion.2
  75.3 9.0 %while.38 = (s32[]{:T(128)}, f32[128,2,7,64]{0,3,2,1:T(8,128)}, bf16[2,1024,256]{1,2,0:T(8,128)(2,1)S(1)}, s32[2,1024]{1,0:T(2,128)S(1)}, s32[128]{0:T(128)S(1)}...) while((s32[]{:T(128)}, f32[128,2,7,64]{0,3,2,1:T(8,128)}, ...), condition=%wide.region_6.7_spmd.clone, body=%wide.region_5.6_spmd.clone.sunk | while | flops 477462528 | bytes 4050551 | solution.py:258
  91.2 6.1 %collective-permute-done.13 = bf16[128,896]{1,0:T(8,128)(2,1)} collective-permute-done((bf16[128,896]{1,0:T(8,128)(2,1)}, bf16[128,896]{1,0:T(8,128)(2,1)}, u32[]{:S(2)}, u32[]{:S(2)}) %collective-permute-start.13) | collective-permute-done | bytes 229408 | tf_op jit(solution)/shard_map/ppermute | solution.py:73
  133.6 8.4 %collective-permute-done.97 = bf16[80,896]{1,0:T(8,128)(2,1)S(1)} collective-permute-done((bf16[80,896]{1,0:T(8,128)(2,1)S(1)}, bf16[80,896]{1,0:T(8,128)(2,1)S(1)}, u32[]{:S(2)}, u32[]{:S(2)}) %collective-permute-start.97) | collective-permute-done | bytes 143392 | tf_op jit(solution)/shard_map/ppermute | solution.py:81
  144.9 6.5 %collective-permute-done.77 = bf16[56,2432]{1,0:T(8,128)(2,1)S(1)} collective-permute-done((bf16[56,2432]{1,0:T(8,128)(2,1)S(1)}, bf16[56,2432]{1,0:T(8,128)(2,1)S(1)}, u32[]{:S(2)}, u32[]{:S(2)}) %collective-permute-start.77) | collective-permute-done | bytes 272416 | tf_op jit(solution)/shard_map/ppermute | solution.py:81
  160.3 9.1 %collective-permute-start.103 = (bf16[152,896]{1,0:T(8,128)(2,1)}, bf16[152,896]{1,0:T(8,128)(2,1)}, u32[]{:S(2)}, u32[]{:S(2)}) collective-permute-start(bf16[152,896]{1,0:T(8,128)(2,1)} %get-tuple-element.376), channel_id=1, source_target_pairs={{0,2},{1,3},{4,0},{5,1},{8,4},{9,5},{12,8},{13,9},{14,12},{15,13},... | collective-permute-start | bytes 817160 | tf_op jit(solution)/shard_map/ppermute | solution.py:81
  171.0 5.5 %collective-permute-done.22 = bf16[128,896]{1,0:T(8,128)(2,1)S(1)} collective-permute-done((bf16[128,896]{1,0:T(8,128)(2,1)S(1)}, bf16[128,896]{1,0:T(8,128)(2,1)S(1)}, u32[]{:S(2)}, u32[]{:S(2)}) %collective-permute-start.22) | collective-permute-done | bytes 229408 | tf_op jit(solution)/shard_map/ppermute | solution.py:73
  187.9 35.8 %while.39 = (s32[]{:T(128)}, f32[128,2,7,64]{0,3,2,1:T(8,128)}, f32[2,1024,256]{2,1,0:T(8,128)}, bf16[2,1024,256]{1,2,0:T(8,128)(2,1)S(1)}, s32[2,1024]{1,0:T(2,...) while((s32[]{:T(128)}, f32[128,2,7,64]{0,3,2,1:T(8,128)}, ...), condition=%wide.region_11.12_spmd.clone, body=%wide.region_10.11_spmd.clone.sunk | while | flops 1193508864 | bytes 89556680 | solution.py:358
  189.4 5.0 fusion.235
  198.0 5.0 fusion.237
  207.2 5.0 fusion.235
  215.9 5.0 fusion.237
  235.1 7.2 %collective-permute-done.74 = bf16[112,2432]{1,0:T(8,128)(2,1)} collective-permute-done((bf16[112,2432]{1,0:T(8,128)(2,1)}, bf16[112,2432]{1,0:T(8,128)(2,1)}, u32[]{:S(2)}, u32[]{:S(2)}) %collective-permute-start.74) | collective-permute-done | bytes 544800 | tf_op jit(solution)/shard_map/ppermute | solution.py:81
  275.2 7.8 %collective-permute-done.31 = bf16[128,256]{0,1:T(8,128)(2,1)S(1)} collective-permute-done((bf16[128,256]{0,1:T(8,128)(2,1)S(1)}, bf16[128,256]{0,1:T(8,128)(2,1)S(1)}, u32[]{:S(2)}, u32[]{:S(2)}) %collective-permute-start.31) | collective-permute-done | bytes 65568 | tf_op jit(solution)/shard_map/ppermute | solution.py:81
  304.6 8.7 %collective-permute-done.71 = f32[2944]{0:T(1024)S(1)} collective-permute-done((f32[2944]{0:T(1024)S(1)}, f32[2944]{0:T(1024)S(1)}, u32[]{:S(2)}, u32[]{:S(2)}) %collective-permute-start.71) | collective-permute-done | bytes 11808 | tf_op jit(solution)/shard_map/ppermute | solution.py:155
  331.7 6.7 %collective-permute-done.76 = bf16[112,2432]{1,0:T(8,128)(2,1)S(1)} collective-permute-done((bf16[112,2432]{1,0:T(8,128)(2,1)S(1)}, bf16[112,2432]{1,0:T(8,128)(2,1)S(1)}, u32[]{:S(2)}, u32[]{:S(2)}) %collective-permute-start.76) | collective-permute-done | bytes 544800 | tf_op jit(solution)/shard_map/ppermute | solution.py:81
  363.0 9.6 %collective-permute-done.49 = bf16[224,256]{1,0:T(8,128)(2,1)S(1)} collective-permute-done((bf16[224,256]{1,0:T(8,128)(2,1)S(1)}, bf16[224,256]{1,0:T(8,128)(2,1)S(1)}, u32[]{:S(2)}, u32[]{:S(2)}) %collective-permute-start.49) | collective-permute-done | bytes 114720 | tf_op jit(solution)/shard_map/ppermute | solution.py:81
  382.0 5.4 %collective-permute-done.82 = bf16[112,2432]{1,0:T(8,128)(2,1)S(1)} collective-permute-done((bf16[112,2432]{1,0:T(8,128)(2,1)S(1)}, bf16[112,2432]{1,0:T(8,128)(2,1)S(1)}, u32[]{:S(2)}, u32[]{:S(2)}) %collective-permute-start.82) | collective-permute-done | bytes 544800 | tf_op jit(solution)/shard_map/ppermute | solution.py:81
  411.2 7.1 %collective-permute-done.59 = bf16[112,256]{1,0:T(8,128)(2,1)S(1)} collective-permute-done((bf16[112,256]{1,0:T(8,128)(2,1)S(1)}, bf16[112,256]{1,0:T(8,128)(2,1)S(1)}, u32[]{:S(2)}, u32[]{:S(2)}) %collective-permute-start.59) | collective-permute-done | bytes 57376 | tf_op jit(solution)/shard_map/ppermute | solution.py:81
  419.0 5.7 %collective-permute-done.63 = bf16[112,256]{1,0:T(8,128)(2,1)S(1)} collective-permute-done((bf16[112,256]{1,0:T(8,128)(2,1)S(1)}, bf16[112,256]{1,0:T(8,128)(2,1)S(1)}, u32[]{:S(2)}, u32[]{:S(2)}) %collective-permute-start.63) | collective-permute-done | bytes 57376 | tf_op jit(solution)/shard_map/ppermute | solution.py:81
  436.8 9.4 %collective-permute-done.86 = bf16[112,2432]{1,0:T(8,128)(2,1)S(1)} collective-permute-done((bf16[112,2432]{1,0:T(8,128)(2,1)S(1)}, bf16[112,2432]{1,0:T(8,128)(2,1)S(1)}, u32[]{:S(2)}, u32[]{:S(2)}) %collective-permute-start.86) | collective-permute-done | bytes 544800 | tf_op jit(solution)/shard_map/ppermute | solution.py:81
  (674 shorter events, 354.9 us)
Async XLA Ops:
  7.4 19.7 %collective-permute-start.11 = (bf16[224,896]{1,0:T(8,128)(2,1)}, bf16[224,896]{1,0:T(8,128)(2,1)}, u32[]{:S(2)}, u32[]{:S(2)}) collective-permute-start(bf16[224,896]{1,0:T(8,128)(2,1)} %constant_dynamic-slice_fusion.11), channel_id=1, source_target_pairs={{0,16},{16,0},{1,17},{17,1},{2,18},{18,2},{3,19},{19,3},{4,20},{20... | collective-permute-start | bytes 1204232 | tf_op jit(solution)/shard_map/ppermute | solution.py:73
  7.5 82.4 %collective-permute-start.18 = (bf16[128,896]{1,0:T(8,128)(2,1)}, bf16[128,896]{1,0:T(8,128)(2,1)}, u32[]{:S(2)}, u32[]{:S(2)}) collective-permute-start(bf16[128,896]{1,0:T(8,128)(2,1)} %bitcast.14), channel_id=1, source_target_pairs={{0,16},{16,0},{1,17},{17,1},{2,18},{18,2},{3,19},{19,3},{4,20},{20... | collective-permute-start | bytes 688136 | tf_op jit(solution)/shard_map/ppermute | solution.py:73
  27.1 24.8 %collective-permute-start.12 = (bf16[224,896]{1,0:T(8,128)(2,1)}, bf16[224,896]{1,0:T(8,128)(2,1)}, u32[]{:S(2)}, u32[]{:S(2)}) collective-permute-start(bf16[224,896]{1,0:T(8,128)(2,1)} %collective-permute-done.11), channel_id=1, source_target_pairs={{0,1},{1,0},{2,3},{3,2},{4,5},{5,4},{6,7},{7,6},{8,9},{9,8},{10,11... | collective-permute-start | bytes 1204232 | tf_op jit(solution)/shard_map/ppermute | solution.py:69
  108.1 159.1 %collective-permute-start.39 = (bf16[128,896]{0,1:T(8,128)(2,1)}, bf16[128,896]{0,1:T(8,128)(2,1)}, u32[]{:S(2)}, u32[]{:S(2)}) collective-permute-start(bf16[128,896]{0,1:T(8,128)(2,1)} %bitcast.12), channel_id=1, source_target_pairs={{0,1},{1,0},{2,3},{3,2},{4,5},{5,4},{6,7},{7,6},{8,9},{9,8},{10,11... | collective-permute-start | bytes 688136 | tf_op jit(solution)/shard_map/ppermute | solution.py:69
  108.6 160.5 %collective-permute-start.40 = (bf16[128,896]{0,1:T(8,128)(2,1)}, bf16[128,896]{0,1:T(8,128)(2,1)}, u32[]{:S(2)}, u32[]{:S(2)}) collective-permute-start(bf16[128,896]{0,1:T(8,128)(2,1)} %collective-permute-done.38), channel_id=1, source_target_pairs={{0,1},{1,0},{2,3},{3,2},{4,5},{5,4},{6,7},{7,6},{8,9},{9,8},{10,11... | collective-permute-start | bytes 688136 | tf_op jit(solution)/shard_map/ppermute | solution.py:69
  120.2 40.0 %collective-permute-start.21 = (bf16[256,896]{1,0:T(8,128)(2,1)S(1)}, bf16[256,896]{1,0:T(8,128)(2,1)S(1)}, u32[]{:S(2)}, u32[]{:S(2)}) collective-permute-start(bf16[256,896]{1,0:T(8,128)(2,1)S(1)} %slice.848), channel_id=1, source_target_pairs={{0,1},{1,0},{2,3},{3,2},{4,5},{5,4},{6,7},{7,6},{8,9},{9,8},{10,11... | collective-permute-start | bytes 1376264 | tf_op jit(solution)/shard_map/ppermute | solution.py:69
  158.9 68.2 %collective-permute-start.99 = (bf16[152,896]{1,0:T(8,128)(2,1)}, bf16[152,896]{1,0:T(8,128)(2,1)}, u32[]{:S(2)}, u32[]{:S(2)}) collective-permute-start(bf16[152,896]{1,0:T(8,128)(2,1)} %get-tuple-element.375), channel_id=1, source_target_pairs={{0,4},{1,5},{4,8},{5,9},{8,12},{9,13},{12,14},{13,15},{14,10},{15,... | collective-permute-start | bytes 817160 | tf_op jit(solution)/shard_map/ppermute | solution.py:81
  160.3 68.4 %collective-permute-start.103 = (bf16[152,896]{1,0:T(8,128)(2,1)}, bf16[152,896]{1,0:T(8,128)(2,1)}, u32[]{:S(2)}, u32[]{:S(2)}) collective-permute-start(bf16[152,896]{1,0:T(8,128)(2,1)} %get-tuple-element.376), channel_id=1, source_target_pairs={{0,2},{1,3},{4,0},{5,1},{8,4},{9,5},{12,8},{13,9},{14,12},{15,13},... | collective-permute-start | bytes 817160 | tf_op jit(solution)/shard_map/ppermute | solution.py:81
  232.4 30.2 %collective-permute-start.41 = (bf16[128,896]{1,0:T(8,128)(2,1)S(1)}, bf16[128,896]{1,0:T(8,128)(2,1)S(1)}, u32[]{:S(2)}, u32[]{:S(2)}) collective-permute-start(bf16[128,896]{1,0:T(8,128)(2,1)S(1)} %copy-done.41), channel_id=1, source_target_pairs={{0,16},{16,0},{1,17},{17,1},{2,18},{18,2},{3,19},{19,3},{4,20},{20... | collective-permute-start | bytes 688136 | tf_op jit(solution)/shard_map/ppermute | solution.py:73
  267.2 26.7 %collective-permute-start.75 = (bf16[112,2432]{1,0:T(8,128)(2,1)S(1)}, bf16[112,2432]{1,0:T(8,128)(2,1)S(1)}, u32[]{:S(2)}, u32[]{:S(2)}) collective-permute-start(bf16[112,2432]{1,0:T(8,128)(2,1)S(1)} %get-tuple-element.365), channel_id=1, source_target_pairs={{0,4},{1,5},{4,8},{5,9},{8,12},{9,13},{12,14},{13,15},{14,10},{15,... | collective-permute-start | bytes 1634312 | tf_op jit(solution)/shard_map/ppermute | solution.py:81
  269.1 25.5 %collective-permute-start.79 = (bf16[112,2432]{1,0:T(8,128)(2,1)S(1)}, bf16[112,2432]{1,0:T(8,128)(2,1)S(1)}, u32[]{:S(2)}, u32[]{:S(2)}) collective-permute-start(bf16[112,2432]{1,0:T(8,128)(2,1)S(1)} %get-tuple-element.366), channel_id=1, source_target_pairs={{0,2},{1,3},{4,0},{5,1},{8,4},{9,5},{12,8},{13,9},{14,12},{15,13},... | collective-permute-start | bytes 1634312 | tf_op jit(solution)/shard_map/ppermute | solution.py:81
  286.2 35.2 %collective-permute-start.107 = (bf16[152,896]{1,0:T(8,128)(2,1)S(1)}, bf16[152,896]{1,0:T(8,128)(2,1)S(1)}, u32[]{:S(2)}, u32[]{:S(2)}) collective-permute-start(bf16[152,896]{1,0:T(8,128)(2,1)S(1)} %collective-permute-done.106), channel_id=1, source_target_pairs={{0,1},{1,0},{2,3},{3,2},{4,5},{5,4},{6,7},{7,6},{8,9},{9,8},{10,11... | collective-permute-start | bytes 817160 | tf_op jit(solution)/shard_map/ppermute | solution.py:69
  290.6 28.1 %collective-permute-start.108 = (bf16[152,896]{1,0:T(8,128)(2,1)S(1)}, bf16[152,896]{1,0:T(8,128)(2,1)S(1)}, u32[]{:S(2)}, u32[]{:S(2)}) collective-permute-start(bf16[152,896]{1,0:T(8,128)(2,1)S(1)} %collective-permute-done.106), channel_id=1, source_target_pairs={{0,4},{1,5},{4,8},{5,9},{8,12},{9,13},{12,14},{13,15},{14,10},{15,... | collective-permute-start | bytes 817160 | tf_op jit(solution)/shard_map/ppermute | solution.py:81
  292.6 28.8 %collective-permute-start.114 = (bf16[152,896]{1,0:T(8,128)(2,1)S(1)}, bf16[152,896]{1,0:T(8,128)(2,1)S(1)}, u32[]{:S(2)}, u32[]{:S(2)}) collective-permute-start(bf16[152,896]{1,0:T(8,128)(2,1)S(1)} %collective-permute-done.113), channel_id=1, source_target_pairs={{0,2},{1,3},{4,0},{5,1},{8,4},{9,5},{12,8},{13,9},{14,12},{15,13},... | collective-permute-start | bytes 817160 | tf_op jit(solution)/shard_map/ppermute | solution.py:81
  296.2 35.4 %collective-permute-start.80 = (bf16[112,2432]{1,0:T(8,128)(2,1)S(1)}, bf16[112,2432]{1,0:T(8,128)(2,1)S(1)}, u32[]{:S(2)}, u32[]{:S(2)}) collective-permute-start(bf16[112,2432]{1,0:T(8,128)(2,1)S(1)} %get-tuple-element.364), channel_id=1, source_target_pairs={{0,2},{1,3},{4,0},{5,1},{8,4},{9,5},{12,8},{13,9},{14,12},{15,13},... | collective-permute-start | bytes 1634312 | tf_op jit(solution)/shard_map/ppermute | solution.py:81
  343.3 31.5 %collective-permute-start.120 = (bf16[152,896]{1,0:T(8,128)(2,1)S(1)}, bf16[152,896]{1,0:T(8,128)(2,1)S(1)}, u32[]{:S(2)}, u32[]{:S(2)}) collective-permute-start(bf16[152,896]{1,0:T(8,128)(2,1)S(1)} %collective-permute-done.113), channel_id=1, source_target_pairs={{0,1},{1,0},{2,3},{3,2},{4,5},{5,4},{6,7},{7,6},{8,9},{9,8},{10,11... | collective-permute-start | bytes 817160 | tf_op jit(solution)/shard_map/ppermute | solution.py:69
  344.4 35.3 %collective-permute-start.81 = (bf16[112,2432]{1,0:T(8,128)(2,1)S(1)}, bf16[112,2432]{1,0:T(8,128)(2,1)S(1)}, u32[]{:S(2)}, u32[]{:S(2)}) collective-permute-start(bf16[112,2432]{1,0:T(8,128)(2,1)S(1)} %add_convert_fusion), channel_id=1, source_target_pairs={{0,1},{1,0},{2,3},{3,2},{4,5},{5,4},{6,7},{7,6},{8,9},{9,8},{10,11... | collective-permute-start | bytes 1634312 | tf_op jit(solution)/shard_map/ppermute | solution.py:69
  355.7 45.8 %collective-permute-start.89 = (bf16[112,2432]{1,0:T(8,128)(2,1)S(1)}, bf16[112,2432]{1,0:T(8,128)(2,1)S(1)}, u32[]{:S(2)}, u32[]{:S(2)}) collective-permute-start(bf16[112,2432]{1,0:T(8,128)(2,1)S(1)} %add_convert_fusion), channel_id=1, source_target_pairs={{0,2},{1,3},{4,0},{5,1},{8,4},{9,5},{12,8},{13,9},{14,12},{15,13},... | collective-permute-start | bytes 1634312 | tf_op jit(solution)/shard_map/ppermute | solution.py:81
  387.4 37.2 %collective-permute-start.83 = (bf16[112,2432]{1,0:T(8,128)(2,1)S(1)}, bf16[112,2432]{1,0:T(8,128)(2,1)S(1)}, u32[]{:S(2)}, u32[]{:S(2)}) collective-permute-start(bf16[112,2432]{1,0:T(8,128)(2,1)S(1)} %collective-permute-done.82), channel_id=1, source_target_pairs={{0,1},{1,0},{2,3},{3,2},{4,5},{5,4},{6,7},{7,6},{8,9},{9,8},{10,11... | collective-permute-start | bytes 1634312 | tf_op jit(solution)/shard_map/ppermute | solution.py:69
  401.5 28.9 %collective-permute-start.84 = (bf16[112,2432]{1,0:T(8,128)(2,1)S(1)}, bf16[112,2432]{1,0:T(8,128)(2,1)S(1)}, u32[]{:S(2)}, u32[]{:S(2)}) collective-permute-start(bf16[112,2432]{1,0:T(8,128)(2,1)S(1)} %collective-permute-done.82), channel_id=1, source_target_pairs={{0,4},{1,5},{4,8},{5,9},{8,12},{9,13},{12,14},{13,15},{14,10},{15,... | collective-permute-start | bytes 1634312 | tf_op jit(solution)/shard_map/ppermute | solution.py:81
  401.9 25.7 %collective-permute-start.96 = (bf16[112,2432]{1,0:T(8,128)(2,1)S(1)}, bf16[112,2432]{1,0:T(8,128)(2,1)S(1)}, u32[]{:S(2)}, u32[]{:S(2)}) collective-permute-start(bf16[112,2432]{1,0:T(8,128)(2,1)S(1)} %collective-permute-done.89), channel_id=1, source_target_pairs={{0,1},{1,0},{2,3},{3,2},{4,5},{5,4},{6,7},{7,6},{8,9},{9,8},{10,11... | collective-permute-start | bytes 1634312 | tf_op jit(solution)/shard_map/ppermute | solution.py:69
  410.6 21.1 %collective-permute-start.90 = (bf16[112,2432]{1,0:T(8,128)(2,1)S(1)}, bf16[112,2432]{1,0:T(8,128)(2,1)S(1)}, u32[]{:S(2)}, u32[]{:S(2)}) collective-permute-start(bf16[112,2432]{1,0:T(8,128)(2,1)S(1)} %collective-permute-done.89), channel_id=1, source_target_pairs={{0,2},{1,3},{4,0},{5,1},{8,4},{9,5},{12,8},{13,9},{14,12},{15,13},... | collective-permute-start | bytes 1634312 | tf_op jit(solution)/shard_map/ppermute | solution.py:81
  447.0 33.6 %collective-permute-start.88 = (bf16[56,2432]{1,0:T(8,128)(2,1)}, bf16[56,2432]{1,0:T(8,128)(2,1)S(1)}, u32[]{:S(2)}, u32[]{:S(2)}) collective-permute-start(bf16[56,2432]{1,0:T(8,128)(2,1)} %slice.697), channel_id=1, source_target_pairs={{0,4},{1,5},{4,8},{5,9},{8,12},{9,13},{12,14},{13,15},{14,10},{15,... | collective-permute-start | bytes 817160 | tf_op jit(solution)/shard_map/ppermute | solution.py:81
  450.5 30.1 %collective-permute-start.92 = (bf16[56,2432]{1,0:T(8,128)(2,1)}, bf16[56,2432]{1,0:T(8,128)(2,1)}, u32[]{:S(2)}, u32[]{:S(2)}) collective-permute-start(bf16[56,2432]{1,0:T(8,128)(2,1)} %slice.698), channel_id=1, source_target_pairs={{0,2},{1,3},{4,0},{5,1},{8,4},{9,5},{12,8},{13,9},{14,12},{15,13},... | collective-permute-start | bytes 817160 | tf_op jit(solution)/shard_map/ppermute | solution.py:81
  (164 other events, 1368.5 us)

commit v2 on v1

v2 whole, which is shorter than its diff:
```python
import jax
import jax.numpy as jnp
from jax import lax
from jax.experimental import pallas as pl
from jax.experimental.pallas import tpu as pltpu
from jax.sharding import PartitionSpec as P

D = 896
QH = 14
KH = 2
HD = 64
GROUP = QH // KH
WIDTH_Q = QH * HD
WIDTH_K = KH * HD

EPS = 1e-06
ROPE_BASE = 1000000.0

f32 = jnp.float32
bf16 = jnp.bfloat16


def ring_order(chips):
    if chips % 2:
        return list(range(chips))
    rows = chips // 2
    return [2 * i for i in range(rows)] + [2 * i + 1 for i in reversed(range(rows))]


def half_cut(rows):
    cut = (rows // 2 + 7) // 8 * 8
    return cut if cut < rows else rows // 2


class Net:
    def __init__(self):
        self.dp = lax.axis_size("dp")
        self.ctx = lax.axis_size("ctx")
        self.chips = self.ctx // 2
        self.order = ring_order(self.chips)
        self.d = lax.axis_index("dp")
        self.c = lax.axis_index("ctx")
        self.core = self.c % 2
        place = [0] * self.chips
        for spot, chip in enumerate(self.order):
            place[chip] = spot
        self.pos = jnp.array(place, jnp.int32)[self.c // 2]

    def swap(self, x):
        return lax.ppermute(x, "ctx", [(i, i ^ 1) for i in range(self.ctx)])

    def shift(self, x, step):
        n = self.dp
        return lax.ppermute(x, "dp", [(i, (i + step) % n) for i in range(n)])

    def hop(self, x, step):
        n = self.chips
        perm = []
        for spot in range(n):
            for core in range(2):
                perm.append((2 * self.order[spot] + core, 2 * self.order[(spot + step) % n] + core))
        return lax.ppermute(x, "ctx", perm)

    def owner(self, slot):
        return (self.pos - slot) % self.chips

    def group_gather(self, x):
        chip = jnp.concatenate([x] + [self.shift(x, s) for s in range(1, self.dp)], 0)
        return jnp.concatenate([chip, self.swap(chip)], 0)

    def ring_gather(self, x):
        n = self.chips
        half = n // 2
        cut = half_cut(x.shape[0])
        found = [x] + [None] * (n - 1)
        fwd, back = x, x
        for s in range(1, half):
            fwd = self.hop(fwd, 1)
            back = self.hop(back, -1)
            found[s] = fwd
            found[n - s] = back
        found[half] = jnp.concatenate([self.hop(fwd[:cut], 1), self.hop(back[cut:], -1)], 0)
        return found

    def ring_scatter(self, local):
        n = self.chips
        half = n // 2
        cut = half_cut(local[half].shape[0])

        def add(got, mine):
            return (got.astype(f32) + mine.astype(f32)).astype(bf16)

        fwd = self.hop(local[half][:cut], 1)
        back = self.hop(local[half][cut:], -1)
        for s in range(1, half):
            mine_f = local[half + s]
            mine_b = local[half - s]
            if s == 1:
                mine_f = jnp.concatenate([add(fwd, mine_f[:cut]), mine_f[cut:]], 0)
                mine_b = jnp.concatenate([mine_b[:cut], add(back, mine_b[cut:])], 0)
            else:
                mine_f = add(fwd, mine_f)
                mine_b = add(back, mine_b)
            fwd = self.hop(mine_f, 1)
            back = self.hop(mine_b, -1)
        return fwd.astype(f32) + back.astype(f32) + local[0].astype(f32)

    def full_rows(self, shard):
        rows = shard.shape[0]
        half = rows // 2
        piece = lax.dynamic_slice(shard, (self.core * half, 0), (half, shard.shape[1]))
        blocks = [shard]
        for s in range(1, self.dp):
            got = self.shift(piece, s)
            other = self.swap(got)
            low = jnp.where(self.core == 0, got, other)
            high = jnp.where(self.core == 0, other, got)
            blocks.append(jnp.concatenate([low, high], 0))
        if self.dp == 2:
            first = jnp.where(self.d == 0, blocks[0], blocks[1])
            second = jnp.where(self.d == 0, blocks[1], blocks[0])
            return jnp.concatenate([first, second], 0)
        ranked = jnp.stack(blocks)[(self.d - jnp.arange(self.dp)) % self.dp]
        return ranked.reshape(self.dp * rows, shard.shape[1])

    def total(self, x):
        x = x + self.swap(x)
        bit = 1
        while bit < self.chips:
            x = x + lax.ppermute(x, "ctx", [(i, i ^ (2 * bit)) for i in range(self.ctx)])
            bit *= 2
        bit = 1
        while bit < self.dp:
            x = x + lax.ppermute(x, "dp", [(i, i ^ bit) for i in range(self.dp)])
            bit *= 2
        return x


VMEM_BYTES = 56 * 1024 * 1024
KEYS = 256


def full_spec(shape):
    return pl.BlockSpec(shape, lambda: (0,) * len(shape))


def call(kernel, outs, args, smem=0, scratch=(), flops=0):
    specs = [pl.BlockSpec(memory_space=pltpu.SMEM)] * smem
    specs += [pl.BlockSpec(memory_space=pltpu.VMEM)] * (len(args) - smem)
    moved = sum(x.size * x.dtype.itemsize for x in list(args) + list(outs))
    return pl.pallas_call(
        kernel,
        out_shape=list(outs),
        in_specs=specs,
        out_specs=[pl.BlockSpec(memory_space=pltpu.VMEM)] * len(outs),
        scratch_shapes=list(scratch),
        compiler_params=pltpu.CompilerParams(vmem_limit_bytes=VMEM_BYTES),
        cost_estimate=pl.CostEstimate(flops=flops, bytes_accessed=moved, transcendentals=0),
    )(*args)


def lanes(shape):
    return lax.broadcasted_iota(jnp.int32, shape, len(shape) - 1)


def dot_nt(a, b, precision=None):
    return lax.dot_general(
        a, b, (((1,), (1,)), ((), ())), preferred_element_type=f32, precision=precision
    )


def dot_tn(a, b):
    return lax.dot_general(a, b, (((0,), (0,)), ((), ())), preferred_element_type=f32)


def qkv_kernel(x_ref, gain_ref, w_ref, b_ref, cos_ref, sin_ref, norm_ref, q_ref, pair_ref):
    x = x_ref[...].astype(f32)
    inverse = lax.rsqrt(jnp.mean(x * x, -1, keepdims=True) + EPS)
    normed = (x * inverse * gain_ref[...]).astype(bf16)
    norm_ref[...] = normed
    joint = jnp.dot(normed, w_ref[...], preferred_element_type=f32) + b_ref[...]
    cosine = cos_ref[...]
    sine = sin_ref[...]
    early = lanes(cosine.shape) % HD < HD // 2
    for i in range((WIDTH_Q + WIDTH_K) // 128):
        tile = joint[:, i * 128 : (i + 1) * 128]
        turned = jnp.where(early, -pltpu.roll(tile, 96, 1), pltpu.roll(tile, 32, 1))
        turned = tile * cosine + turned * sine
        if i * 128 < WIDTH_Q:
            q_ref[:, i * 128 : (i + 1) * 128] = turned.astype(bf16)
        else:
            pair_ref[:, :WIDTH_K] = turned.astype(bf16)
    pair_ref[:, WIDTH_K:] = joint[:, WIDTH_Q + WIDTH_K :].astype(bf16)


def spread_heads(x, out_ref, factor):
    rows = x.shape[0]
    half = rows // 2
    for head in range(QH):
        kh, g = divmod(head, GROUP)
        tile = x[:, (head // 2) * 128 : (head // 2 + 1) * 128].astype(f32)
        if head % 2 != kh:
            tile = pltpu.roll(tile, HD, 1)
        tile = jnp.where(lanes(tile.shape) // HD == kh, tile * factor, 0.0).astype(out_ref.dtype)
        for part in range(2):
            start = (part * GROUP + g) * half
            out_ref[kh, start : start + half, :] = tile[part * half : (part + 1) * half]


def join_heads(src_ref, half, tile):
    sides = []
    for side in range(2):
        kh, g = divmod(2 * tile + side, GROUP)
        parts = [
            src_ref[kh, (part * GROUP + g) * half : (part * GROUP + g + 1) * half, :]
            for part in range(2)
        ]
        both = jnp.concatenate(parts, 0)
        sides.append(both if side == kh else pltpu.roll(both, HD, 1))
    return jnp.where(lanes(sides[0].shape) < HD, sides[0], sides[1])


def forward_kernel(
    ctx, meta_ref, q_ref, mine_ref, other_ref, x_ref, w_ref, gain_ref,
    low_ref, o_ref, lse_ref, spread_ref, k_ref, v_ref, hidden_ref, normed_ref,
    s_ref, max_ref, sum_ref,
):
    rows = q_ref.shape[0]
    half = rows // 2
    part_rows = GROUP * half
    me = meta_ref[0]
    chips = ctx // 2
    for j in range(ctx):
        src = mine_ref if j < chips else other_ref
        at = (j % chips) * rows
        owner = meta_ref[1 + j]
        for part in range(2):
            place = owner if part == 0 else 2 * ctx - 1 - owner
            to = pl.ds(pl.multiple_of(place * half, half), half)
            block = src[at + part * half : at + (part + 1) * half, :]
            k_ref[to, :] = block[:, :WIDTH_K]
            v_ref[to, :] = block[:, WIDTH_K:]
    spread_heads(q_ref[...], spread_ref, HD ** (-0.5))
    for kh in range(KH):
        for part in range(2):
            span = slice(part * part_rows, (part + 1) * part_rows)
            start = (me if part == 0 else 2 * ctx - 1 - me) * half
            last = start // KEYS
            queries = spread_ref[kh, span, :]

            def keys_of(ref, i):
                return ref[pl.ds(pl.multiple_of(i * KEYS, KEYS), KEYS), :]

            scores = dot_nt(queries, keys_of(k_ref, last))
            row = lax.broadcasted_iota(jnp.int32, scores.shape, 0) % half + start
            scores = jnp.where(lanes(scores.shape) + last * KEYS <= row, scores, -1e30)
            s_ref[last] = scores
            max_ref[...] = jnp.maximum(scores[:, :128], scores[:, 128:])

            def score(i, carry):
                s = dot_nt(queries, keys_of(k_ref, i))
                s_ref[i] = s
                max_ref[...] = jnp.maximum(max_ref[...], jnp.maximum(s[:, :128], s[:, 128:]))
                return carry

            lax.fori_loop(0, last, score, 0)
            top = jnp.max(max_ref[...], -1, keepdims=True)
            sum_ref[...] = jnp.zeros_like(sum_ref)
            o_ref[kh, span, :] = jnp.zeros((part_rows, 128), f32)

            def weigh(i, carry):
                p = jnp.exp(s_ref[i] - top)
                sum_ref[...] += p[:, :128] + p[:, 128:]
                o_ref[kh, span, :] += jnp.dot(
                    p.astype(bf16), keys_of(v_ref, i), preferred_element_type=f32
                )
                return carry

            lax.fori_loop(0, last + 1, weigh, 0)
            total = jnp.sum(sum_ref[...], -1, keepdims=True)
            o_ref[kh, span, :] = o_ref[kh, span, :] / total
            lse = jnp.broadcast_to(top + jnp.log(total), (part_rows, 128))
            lse_ref[kh, part] = dot_nt(
                jnp.full((8, 128), 1.0 / 128, f32), lse, lax.Precision.HIGHEST
            )
    for tile in range(WIDTH_Q // 128):
        low_ref[:, tile * 128 : (tile + 1) * 128] = join_heads(o_ref, half, tile).astype(bf16)
    hidden = x_ref[...].astype(f32) + jnp.dot(low_ref[...], w_ref[...], preferred_element_type=f32)
    hidden_ref[...] = hidden
    inverse = lax.rsqrt(jnp.mean(hidden * hidden, -1, keepdims=True) + EPS)
    normed_ref[...] = (hidden * inverse * gain_ref[...]).astype(bf16)


def backward_kernel(
    ctx, meta_ref, gn_ref, hidden_ref, gout_ref, gain_ref, w_ref, spread_ref, k_ref, v_ref, lse_ref,
    o_ref,
    gh_ref, ga_ref, gain_grad_ref, gq_ref, mine_ref, other_ref,
    go_ref, gqs_ref, gk_ref, gv_ref,
):
    rows = gn_ref.shape[0]
    half = rows // 2
    part_rows = GROUP * half
    me = meta_ref[0]
    chips = ctx // 2
    hidden = hidden_ref[...]
    inverse = lax.rsqrt(jnp.mean(hidden * hidden, -1, keepdims=True) + EPS)
    unit = hidden * inverse
    grad = gn_ref[...]
    gain_grad_ref[...] = jnp.sum(grad * unit, 0, keepdims=True)
    scaled = grad * gain_ref[...]
    gh = gout_ref[...].astype(f32) + inverse * (
        scaled - unit * jnp.mean(scaled * unit, -1, keepdims=True)
    )
    gh_ref[...] = gh
    ga = gh.astype(bf16)
    ga_ref[...] = ga
    spread_heads(dot_nt(ga, w_ref[...]).astype(bf16), go_ref, 1.0)
    gqs_ref[...] = jnp.zeros_like(gqs_ref)
    gk_ref[...] = jnp.zeros_like(gk_ref)
    gv_ref[...] = jnp.zeros_like(gv_ref)
    for kh in range(KH):
        for part in range(2):
            span = slice(part * part_rows, (part + 1) * part_rows)
            start = (me if part == 0 else 2 * ctx - 1 - me) * half
            last = start // KEYS
            queries = spread_ref[kh, span, :]
            heads = go_ref[kh, span, :]
            lse = lse_ref[kh, part][:1]
            delta = dot_nt(
                jnp.ones((8, 128), f32), heads.astype(f32) * o_ref[kh, span, :],
                lax.Precision.HIGHEST,
            )[:1]

            def step(i, masked):
                at = pl.ds(pl.multiple_of(i * KEYS, KEYS), KEYS)
                keys = k_ref[at, :]
                p = jnp.exp(dot_nt(keys, queries) - lse)
                if masked:
                    row = lanes(p.shape) % half + start
                    key = lax.broadcasted_iota(jnp.int32, p.shape, 0) + i * KEYS
                    p = jnp.where(key <= row, p, 0.0)
                gs = (p * (dot_nt(v_ref[at, :], heads) - delta)).astype(bf16)
                gv_ref[at, :] += jnp.dot(p.astype(bf16), heads, preferred_element_type=f32)
                gk_ref[at, :] += jnp.dot(gs, queries, preferred_element_type=f32)
                gqs_ref[kh, span, :] += dot_tn(gs, keys)

            def body(i, carry):
                step(i, False)
                return carry

            lax.fori_loop(0, last, body, 0)
            step(last, True)
    for tile in range(WIDTH_Q // 128):
        gq_ref[:, tile * 128 : (tile + 1) * 128] = join_heads(gqs_ref, half, tile) * HD ** (-0.5)
    for j in range(ctx):
        dst = mine_ref if j < chips else other_ref
        at = (j % chips) * rows
        owner = meta_ref[1 + j]
        for part in range(2):
            place = owner if part == 0 else 2 * ctx - 1 - owner
            frm = pl.ds(pl.multiple_of(place * half, half), half)
            to = slice(at + part * half, at + (part + 1) * half)
            dst[to, :WIDTH_K] = gk_ref[frm, :].astype(dst.dtype)
            dst[to, WIDTH_K:] = gv_ref[frm, :].astype(dst.dtype)


def finish_kernel(
    gq_ref, pair_ref, x_ref, gain_ref, w_ref, cos_ref, sin_ref, gh_ref,
    joint_ref, gx_ref, gain_grad_ref, bias_ref,
):
    cosine = cos_ref[...]
    sine = sin_ref[...]
    early = lanes(cosine.shape) % HD < HD // 2
    for i in range((WIDTH_Q + WIDTH_K) // 128):
        at = slice(i * 128, (i + 1) * 128)
        grad = gq_ref[:, at] if i * 128 < WIDTH_Q else pair_ref[:, :WIDTH_K]
        scaled = grad * sine
        turned = jnp.where(early, pltpu.roll(scaled, 96, 1), -pltpu.roll(scaled, 32, 1))
        joint_ref[:, at] = (grad * cosine + turned).astype(bf16)
    joint_ref[:, WIDTH_Q + WIDTH_K :] = pair_ref[:, WIDTH_K:].astype(bf16)
    joint = joint_ref[...]
    bias_ref[...] = jnp.sum(joint.astype(f32), 0, keepdims=True)
    grad = dot_nt(joint, w_ref[...])
    x = x_ref[...].astype(f32)
    inverse = lax.rsqrt(jnp.mean(x * x, -1, keepdims=True) + EPS)
    unit = x * inverse
    gain_grad_ref[...] = jnp.sum(grad * unit, 0, keepdims=True)
    scaled = grad * gain_ref[...]
    gx_ref[...] = gh_ref[...] + inverse * (
        scaled - unit * jnp.mean(scaled * unit, -1, keepdims=True)
    )


def place_blocks(blocks, spots, out_shape, old=None):
    shape = blocks[0].shape
    count = len(blocks)
    if shape[0] % 8 or shape[1] % 128:
        out = jnp.zeros(out_shape, f32) if old is None else old
        for block, (i, j) in zip(blocks, spots):
            out = lax.dynamic_update_slice(
                out, block.astype(f32), (i * shape[0], j * shape[1])
            )
        return out

    def kernel(spots_ref, *refs):
        step = pl.program_id(0)
        out_ref = refs[-1]
        for i in range(count):

            @pl.when(step == i)
            def write(i=i):
                out_ref[...] = refs[i][...].astype(f32)

    keep = [] if old is None else [old]
    return pl.pallas_call(
        kernel,
        out_shape=jax.ShapeDtypeStruct(out_shape, f32),
        grid_spec=pltpu.PrefetchScalarGridSpec(
            num_scalar_prefetch=1,
            grid=(count,),
            in_specs=[pl.BlockSpec(shape, lambda i, spots: (0, 0))] * count
            + [pl.BlockSpec(memory_space=pl.ANY)] * len(keep),
            out_specs=pl.BlockSpec(shape, lambda i, spots: (spots[i, 0], spots[i, 1])),
        ),
        input_output_aliases={} if old is None else {count + 1: 0},
        compiler_params=pltpu.CompilerParams(vmem_limit_bytes=VMEM_BYTES),
    )(jnp.stack([jnp.stack(s) for s in spots]).astype(jnp.int32), *blocks, *keep)


def place_mlp(pairs, owners, core, main, out_shape, old=None):
    count = len(pairs)
    rows = pairs[0][0].shape[0]
    columns = pairs[0][0].shape[1]
    blocks = [x for pair in pairs for x in pair]

    def kernel(spots_ref, *refs):
        step = pl.program_id(0)
        gate_ref, up_ref = refs[-2:]
        core_zero = spots_ref[count] == 0
        for i in range(count):

            @pl.when(step == i)
            def write(i=i):
                got = refs[2 * i][...].astype(f32)
                other = refs[2 * i + 1][...].astype(f32)
                zero = jnp.where(core_zero, got, other)
                one = jnp.where(core_zero, other, got)
                tile_zero, tile_one = zero[:, 2 * main :], one[:, 2 * main :]
                left = lanes(tile_zero.shape) < 64
                gate_ref[:, :main] = zero[:, :main]
                gate_ref[:, main : main + 128] = jnp.where(left, tile_zero, tile_one)
                gate_ref[:, main + 128 :] = one[:, :main]
                up_ref[:, :main] = zero[:, main : 2 * main]
                up_ref[:, main : main + 128] = pltpu.roll(
                    jnp.where(left, tile_one, tile_zero), 64, 1
                )
                up_ref[:, main + 128 :] = one[:, main : 2 * main]

    keep = [] if old is None else list(old)
    out_spec = pl.BlockSpec((rows, out_shape[1]), lambda i, spots: (spots[i], 0))
    return pl.pallas_call(
        kernel,
        out_shape=[jax.ShapeDtypeStruct(out_shape, f32)] * 2,
        grid_spec=pltpu.PrefetchScalarGridSpec(
            num_scalar_prefetch=1,
            grid=(count,),
            in_specs=[pl.BlockSpec((rows, columns), lambda i, spots: (0, 0))] * (2 * count)
            + [pl.BlockSpec(memory_space=pl.ANY)] * len(keep),
            out_specs=[out_spec, out_spec],
        ),
        input_output_aliases={} if old is None else {2 * count + 1: 0, 2 * count + 2: 1},
        compiler_params=pltpu.CompilerParams(vmem_limit_bytes=VMEM_BYTES),
    )(jnp.stack(list(owners) + [core]).astype(jnp.int32), *blocks, *keep)


def local(tokens, w_qkv, b_qkv, w_out, gain_attn, gain_mlp, w_gate, w_up, w_down, cotangent):
    net = Net()
    rows = tokens.shape[1]
    half_rows = rows // 2
    ctx_count = net.ctx
    core = net.core
    chips = net.chips
    part_rows = GROUP * half_rows
    x = tokens[0]
    gain_one = gain_attn[None]
    gain_two = gain_mlp[None]

    w_qkv_full = net.full_rows(w_qkv)

    ff_loc = w_gate.shape[1]
    ff_half = ff_loc // 2
    main = (ff_half // 128) * 128
    rest = ff_half - main
    width = main + 2 * rest
    first = core * main
    own_cols = (jnp.arange(width) + first < ff_half) == (core == 0)
    wg = lax.dynamic_slice(w_gate, (0, first), (D, width))
    wu = lax.dynamic_slice(w_up, (0, first), (D, width))
    wd = lax.dynamic_slice(w_down, (first, 0), (width, D))

    row_ids = jnp.arange(half_rows, dtype=jnp.int32)
    place = jnp.concatenate(
        [net.c * half_rows + row_ids, (2 * ctx_count - 1 - net.c) * half_rows + row_ids]
    )
    freq = ROPE_BASE ** (-((jnp.arange(128) % (HD // 2)).astype(f32) * (2.0 / HD)))
    angle = place.astype(f32)[:, None] * freq[None, :]
    cosine, sine = jnp.cos(angle), jnp.sin(angle)
    normed_one, queries, pairs = call(
        qkv_kernel,
        [
            jax.ShapeDtypeStruct((rows, D), bf16),
            jax.ShapeDtypeStruct((rows, WIDTH_Q), bf16),
            jax.ShapeDtypeStruct((rows, 2 * WIDTH_K), bf16),
        ],
        [x, gain_one, w_qkv_full, b_qkv[None], cosine, sine],
        flops=2 * rows * D * 1152,
    )

    slots = net.ring_gather(pairs)
    mine = jnp.concatenate(slots, 0)
    other = net.swap(mine)
    order = jnp.array(net.order, jnp.int32)
    chip_ids = order[(net.pos - jnp.arange(chips, dtype=jnp.int32)) % chips]
    meta = jnp.concatenate([net.c[None], 2 * chip_ids + core, 2 * chip_ids + 1 - core])
    meta = meta.astype(jnp.int32)

    late_w, late_g, late_n, unused = lax.optimization_barrier((w_out, cotangent[0], normed_one, pairs))
    w_out_full = net.full_rows(late_w)
    early_group = net.group_gather(jnp.concatenate([late_g, late_n], 1))
    grad_out_group = early_group[:, :D]
    normed_one_group = early_group[:, D:]

    total_keys = rows * ctx_count
    padded = (KH, 2 * part_rows, 128)
    attended_low, attended, lse, spread, keys, values, hidden, normed_two = call(
        lambda *refs: forward_kernel(ctx_count, *refs),
        [
            jax.ShapeDtypeStruct((rows, WIDTH_Q), bf16),
            jax.ShapeDtypeStruct(padded, f32),
            jax.ShapeDtypeStruct((KH, 2, 8, part_rows), f32),
            jax.ShapeDtypeStruct(padded, bf16),
            jax.ShapeDtypeStruct((total_keys, WIDTH_K), bf16),
            jax.ShapeDtypeStruct((total_keys, WIDTH_K), bf16),
            jax.ShapeDtypeStruct((rows, D), f32),
            jax.ShapeDtypeStruct((rows, D), bf16),
        ],
        [meta, queries, mine, other, x, w_out_full, gain_two],
        smem=1,
        scratch=[
            pltpu.VMEM((total_keys // KEYS, part_rows, KEYS), f32),
            pltpu.VMEM((part_rows, 128), f32),
            pltpu.VMEM((part_rows, 128), f32),
        ],
        flops=8 * KH * part_rows * total_keys * 128,
    )

    normed_two_group = net.group_gather(normed_two)
    gate = jnp.dot(normed_two_group, wg, preferred_element_type=f32)
    upper = jnp.dot(normed_two_group, wu, preferred_element_type=f32)
    sigma = jax.nn.sigmoid(gate)
    activated = gate * sigma
    middle = jnp.where(own_cols, activated * upper, 0.0).astype(bf16)
    grad_middle = jnp.einsum("td,fd->tf", grad_out_group, wd, preferred_element_type=f32)
    slope = sigma * (1.0 + gate * (1.0 - sigma))
    grad_gate_low = jnp.where(own_cols, grad_middle * upper * slope, 0.0).astype(bf16)
    grad_up_low = jnp.where(own_cols, grad_middle * activated, 0.0).astype(bf16)

    grad_normed_two = jnp.einsum(
        "tf,df->td", grad_gate_low, wg, preferred_element_type=f32
    ) + jnp.einsum("tf,df->td", grad_up_low, wu, preferred_element_type=f32)
    mlp_out = jnp.dot(middle, wd, preferred_element_type=f32)
    chip_rows = net.dp * rows
    swapped = net.swap(
        jnp.concatenate([grad_normed_two[chip_rows:], mlp_out[chip_rows:]], 0).astype(bf16)
    ).astype(f32)
    grad_chip = grad_normed_two[:chip_rows] + swapped[:chip_rows]
    mlp_chip = mlp_out[:chip_rows] + swapped[chip_rows:]
    grad_two = grad_chip[:rows]
    for s in range(1, net.dp):
        sent = grad_chip[s * rows : (s + 1) * rows].astype(bf16)
        grad_two = grad_two + net.shift(sent, net.dp - s).astype(f32)

    part_down = jnp.einsum(
        "tf,td->fd", middle, grad_out_group, preferred_element_type=f32
    ).astype(bf16)
    part_down = lax.dynamic_slice(part_down, (core * rest, 0), (ff_half, D))
    down_rows = ff_half // chips

    def down_chunk(slot):
        return lax.dynamic_slice(part_down, (net.owner(slot) * down_rows, 0), (down_rows, D))

    sum_down = net.ring_scatter([down_chunk(s) for s in range(chips)]).astype(bf16)

    def split_main(x):
        left = (x[:, :main], x[:, main:])
        right = (x[:, 2 * rest :], x[:, : 2 * rest])
        return (
            jnp.where(core == 0, left[0], right[0]),
            jnp.where(core == 0, left[1], right[1]),
        )

    gate_main, gate_tile = split_main(grad_gate_low)
    up_main, up_tile = split_main(grad_up_low)
    packed = jnp.concatenate(
        [gate_main, up_main, gate_tile + jnp.roll(up_tile, rest, 1)], 1
    )
    part_mlp = jnp.einsum(
        "td,tf->df", normed_two_group, packed, preferred_element_type=f32
    ).astype(bf16)
    mlp_rows = D // chips

    def mlp_chunk(slot):
        return lax.dynamic_slice(
            part_mlp, (net.owner(slot) * mlp_rows, 0), (mlp_rows, 2 * ff_half)
        )

    sum_mlp = net.ring_scatter([mlp_chunk(s) for s in range(chips)]).astype(bf16)
    sum_mlp = lax.optimization_barrier(sum_mlp)

    grad_hidden, grad_attn_low, grad_gain_two, grad_queries, terms_mine, terms_other = call(
        lambda *refs: backward_kernel(ctx_count, *refs),
        [
            jax.ShapeDtypeStruct((rows, D), f32),
            jax.ShapeDtypeStruct((rows, D), bf16),
            jax.ShapeDtypeStruct((1, D), f32),
            jax.ShapeDtypeStruct((rows, WIDTH_Q), f32),
            jax.ShapeDtypeStruct((chips * rows, 2 * WIDTH_K), f32),
            jax.ShapeDtypeStruct((chips * rows, 2 * WIDTH_K), bf16),
        ],
        [
            meta, grad_two, hidden, cotangent[0], gain_two, w_out_full, spread, keys, values, lse,
            attended,
        ],
        smem=1,
        scratch=[
            pltpu.VMEM(padded, bf16),
            pltpu.VMEM(padded, f32),
            pltpu.VMEM((total_keys, WIDTH_K), f32),
            pltpu.VMEM((total_keys, WIDTH_K), f32),
        ],
        flops=20 * KH * part_rows * total_keys * 128,
    )
    pair_sums = (terms_mine + net.swap(terms_other).astype(f32)).astype(bf16)
    grad_pairs = net.ring_scatter(
        [pair_sums[s * rows : (s + 1) * rows] for s in range(chips)]
    )
    grad_joint_low, grad_input, grad_gain_one, grad_bias = call(
        finish_kernel,
        [
            jax.ShapeDtypeStruct((rows, 1152), bf16),
            jax.ShapeDtypeStruct((rows, D), f32),
            jax.ShapeDtypeStruct((1, D), f32),
            jax.ShapeDtypeStruct((1, 1152), f32),
        ],
        [grad_queries, grad_pairs, x, gain_one, w_qkv_full, cosine, sine, grad_hidden],
        flops=2 * rows * D * 1152,
    )

    out_sum = mlp_chip[:rows]
    sent = jnp.concatenate([attended_low, grad_attn_low], 0)
    gathered = [sent]
    for s in range(1, net.dp):
        got = net.shift(
            jnp.concatenate([mlp_chip[s * rows : (s + 1) * rows].astype(bf16), sent], 0),
            net.dp - s,
        )
        out_sum = out_sum + got[:rows].astype(f32)
        gathered.append(got[rows:])
    output = (hidden + out_sum).astype(bf16)
    gathered = jnp.concatenate(gathered, 0)
    gathered = jnp.concatenate([gathered, net.swap(gathered)], 0).reshape(2 * net.dp, 2, rows, D)
    attended_group = gathered[:, 0].reshape(2 * net.dp * rows, D)
    grad_attn_group = gathered[:, 1].reshape(2 * net.dp * rows, D)

    q_rows = w_qkv.shape[0] // 2
    q_first = net.d * (2 * q_rows) + core * q_rows
    group_rows = 2 * net.dp * rows
    part_out = jnp.einsum(
        "tc,td->cd",
        lax.dynamic_slice(attended_group, (0, q_first), (group_rows, q_rows)),
        grad_attn_group,
        preferred_element_type=f32,
    )
    part_joint = jnp.einsum(
        "td,tc->dc",
        lax.dynamic_slice(normed_one_group, (0, q_first), (group_rows, q_rows)),
        net.group_gather(grad_joint_low),
        preferred_element_type=f32,
    )
    part_small = jnp.concatenate([part_joint, part_out], 1).astype(bf16)
    small_cols = part_small.shape[1] // chips

    def small_chunk(slot):
        return lax.dynamic_slice(part_small, (0, net.owner(slot) * small_cols), (q_rows, small_cols))

    sum_small = net.ring_scatter([small_chunk(s) for s in range(chips)]).astype(bf16)

    tall = jnp.concatenate(
        [sum_small[:, i * 128 : (i + 1) * 128] for i in range(small_cols // 128)], 0
    )
    piece = tall.shape[0] // (D // 128)
    wide = jnp.concatenate([tall[i * piece : (i + 1) * piece] for i in range(D // 128)], 1)
    both = lax.optimization_barrier(jnp.concatenate([sum_down, wide], 0))

    owners = [net.owner(s) for s in range(chips)]
    got_mlp = net.ring_gather(sum_mlp)
    got_both = net.ring_gather(both)
    pairs_mlp = [(got, net.swap(got)) for got in got_mlp]
    pairs_both = [(got, net.swap(got)) for got in got_both]

    down_blocks, down_spots, small_blocks, small_spots = [], [], [], []
    for owner, pair in zip(owners, pairs_both):
        for which, got in zip((core, 1 - core), pair):
            down_blocks.append(got[:down_rows])
            down_spots.append((which * chips + owner, jnp.int32(0)))
            wide = got[down_rows:]
            tall = jnp.concatenate([wide[:, i * 128 : (i + 1) * 128] for i in range(D // 128)], 0)
            small_blocks.append(
                jnp.concatenate(
                    [tall[i * q_rows : (i + 1) * q_rows] for i in range(small_cols // 128)], 1
                )
            )
            small_spots.append((which, owner))
    grad_down = place_blocks(down_blocks, down_spots, (ff_loc, D))
    grad_small = place_blocks(small_blocks, small_spots, (2 * q_rows, part_small.shape[1]))
    half = chips // 2
    if 2 * rest == 128:
        first_slots = [s for s in range(chips) if s != half]
        grad_mlp = place_mlp(
            [pairs_mlp[s] for s in first_slots], [owners[s] for s in first_slots], core, main,
            (D, ff_loc),
        )
        grad_gate, grad_up = place_mlp(
            [pairs_mlp[half]], [owners[half]], core, main, (D, ff_loc), grad_mlp
        )
    else:
        grad_gate = jnp.zeros((D, ff_loc), f32)
        grad_up = jnp.zeros((D, ff_loc), f32)
        left_lane = jnp.arange(2 * rest) < rest
        for owner, (got, swapped) in zip(owners, pairs_mlp):
            zero = jnp.where(core == 0, got, swapped).astype(f32)
            one = jnp.where(core == 0, swapped, got).astype(f32)
            tile_zero, tile_one = zero[:, 2 * main :], one[:, 2 * main :]
            mid_gate = jnp.where(left_lane, tile_zero, tile_one)
            mid_up = jnp.roll(jnp.where(left_lane, tile_one, tile_zero), rest, 1)
            base = owner * mlp_rows
            grad_gate = lax.dynamic_update_slice(
                grad_gate, jnp.concatenate([zero[:, :main], mid_gate, one[:, :main]], 1), (base, 0)
            )
            grad_up = lax.dynamic_update_slice(
                grad_up,
                jnp.concatenate([zero[:, main : 2 * main], mid_up, one[:, main : 2 * main]], 1),
                (base, 0),
            )

    small = net.total(jnp.concatenate([grad_gain_one, grad_gain_two, grad_bias], 1))[0]
    qkv_cols = w_qkv.shape[1]
    return (
        output[None],
        grad_input[None],
        grad_small[:, :qkv_cols],
        small[2 * D :],
        grad_small[:, qkv_cols:],
        small[:D],
        small[D : 2 * D],
        grad_gate,
        grad_up,
        grad_down,
    )


def solution(mesh):
    placed = (
        P("dp", "ctx", None),
        P("dp", None),
        P(),
        P("dp", None),
        P(),
        P(),
        P(None, "dp"),
        P(None, "dp"),
        P("dp", None),
        P("dp", "ctx", None),
    )
    return jax.shard_map(
        local,
        mesh=mesh,
        in_specs=placed,
        out_specs=(
            P("dp", "ctx", None),
            P("dp", "ctx", None),
            P("dp", None),
            P(),
            P("dp", None),
            P(),
            P(),
            P(None, "dp"),
            P(None, "dp"),
            P("dp", None),
        ),
        check_vma=False,
    )
```

time: 514 us -> 390 us (0.76)
  Pallas kernels: 0 us -> 70.1 us
  matrix products: 77.9 us -> 18.1 us
  waiting for transfers between devices: 183 us -> 127 us
  local copies, waits for them, and re-layouts: 83.2 us -> 41.3 us
  starting transfers between devices: 103 us -> 77.1 us
  other arithmetic: 49.1 us -> 40.8 us
    pallas_call x0 -> x8, Pallas kernels: none -> 70.1 us  [the longest x4 37.5 us: call(): pl.pallas_call(kernel, out_shape=list(outs), in_specs=specs, out_specs=[p...]
    dot_general x20 -> x2, matrix products: 54.5 us -> 1.09 us  [the longest x1 0.57 us: local(): jnp.einsum('td,tc->dc', lax.dynamic_slice(normed_one_group, (0, q_first),...]
    ppermute x64 -> x56, waiting for transfers between devices: 137 us -> 99.4 us  [hop(): return lax.ppermute(x, 'ctx', perm)]
    ppermute x64 -> x56, starting transfers between devices: 76.5 us -> 59.6 us  [hop(): return lax.ppermute(x, 'ctx', perm)]
    dynamic_update_slice x18 -> x0, local copies, waits for them, and re-layouts: 14 us -> none  [the longest x8 8.44 us: local(): lax.dynamic_update_slice(grad_up, jnp.concatenate([zero[:, main:2 * main]...]
    reduce_sum x6 -> x0, other arithmetic: 11.8 us -> none  [the longest x2 9.13 us: gather_stats(): jnp.sum(jnp.exp(scores - new_max), -1, keepdims=True)]
    concatenate x4 -> x20, other arithmetic: 0.12 us -> 11.8 us  [the longest x8 5.93 us: local(): jnp.concatenate([tall[i * q_rows:(i + 1) * q_rows] for i in range(small_c...]
    ppermute x3, waiting for transfers between devices: 12.4 us -> 1.37 us  [total(): x = x + lax.ppermute(x, 'ctx', [(i, i ^ 2 * bit) for i in range(self.ctx)])]
  transfers between devices with their start and end apart: 121 -> 93, of which waited for: 55 -> 34; matrix products, arithmetic and copies ran while one was open for 37% -> 20% of each run, Pallas kernels for 0% -> 13%
where the time goes in v2:
time: 390 us; the launch traced here: 383 us
  waiting for transfers between devices  127 us (33%)
  starting transfers between devices  77.1 us (20%)
  Pallas kernels  70.1 us (18%)
  local copies, waits for them, and re-layouts  41.3 us (11%)
  other arithmetic  40.8 us (10%)
  matrix products  18.1 us (5%)
  between operations  9.03 us (2%)
    ppermute x56, waiting for transfers between devices, hop(): return lax.ppermute(x, 'ctx', perm)  99.4 us
    ppermute x56, starting transfers between devices, hop(): return lax.ppermute(x, 'ctx', perm)  59.6 us
    pallas_call x4, Pallas kernels, call(): pl.pallas_call(kernel, out_shape=list(outs), in_specs=specs, out_specs=[p...  37.5 us
    ppermute x7, waiting for transfers between devices, shift(): return lax.ppermute(x, 'dp', [(i, (i + step) % n) for i in range(n)])  24.7 us
    pallas_call x2, Pallas kernels, place_blocks(): pl.pallas_call(kernel, out_shape=jax.ShapeDtypeStruct(out_shape, f32), gr...  18.7 us
    pallas_call x2, Pallas kernels, place_mlp(): pl.pallas_call(kernel, out_shape=[jax.ShapeDtypeStruct(out_shape, f32)] *...  13.8 us
    slice x16, local copies, waits for them, and re-layouts, local(): down_blocks.append(got[:down_rows])  12.7 us
    another operation x18, other arithmetic, place_blocks(): jnp.stack([jnp.stack(s) for s in spots]).astype(jnp.int32)  9.88 us
  transfers between devices with their start and end apart: 93, of which 34 were waited for; matrix products, arithmetic and copies ran while one was open for 20% of the time, Pallas kernels for 13%

profile of v2, /device:TPU:0, one launch (start us, length us, event | category | flops | bytes accessed | tf_op | source)
XLA Modules:
  0.0 383.1 jit_solution(9715512163703078883)
XLA Ops:
  1.8 3.0 collective-permute-start
  31.7 3.2 shard_map.195
  60.7 13.7 %shard_map.196 = (bf16[128,896]{1,0:T(8,128)(2,1)}, f32[2,896,128]{2,1,0:T(8,128)}, f32[2,2,8,448]{3,2,1,0:T(8,128)}, bf16[2,896,128]{2,1,0:T(8,128)(2,1)}, bf16...) custom-call(s32[17]{0:T(128)} %pad_add_fusion.16.refs_0_, ...), custom_call_target="tpu_custom_call" | custom-call | flops 1879048192 | bytes 6516292 | tf_op jit(solution)/shard_map/pallas_call | solution.py:151
  76.3 6.2 %collective-permute-done.13 = bf16[128,896]{1,0:T(8,128)(2,1)S(1)} collective-permute-done((bf16[128,896]{1,0:T(8,128)(2,1)}, bf16[128,896]{1,0:T(8,128)(2,1)S(1)}, u32[]{:S(2)}, u32[]{:S(2)}) %collective-permute-start.13) | collective-permute-done | bytes 229408 | tf_op jit(solution)/shard_map/ppermute | solution.py:54
  83.8 3.9 %fusion.6 = f32[512,1280]{1,0:T(8,128)S(1)} fusion(bf16[2432,896]{1,0:T(8,128)(2,1)} %param.20, s32[]{:T(128)S(6)} %select_n.334, bf16[512,1792]{1,0:T(8,128)(2,1)S(1)} %pad_maximum_fusion.1), kind=kOutput, calls=%fused_computation.15 | convolution fusion | flops 1174405120 | bytes 5832708 | tf_op jit(solution)/shard_map/td,fd->tf/dot_general | solution.py:563
  110.3 4.4 %collective-permute-done.69 = bf16[56,2432]{1,0:T(8,128)(2,1)S(1)} collective-permute-done((bf16[56,2432]{1,0:T(8,128)(2,1)S(1)}, bf16[56,2432]{1,0:T(8,128)(2,1)S(1)}, u32[]{:S(2)}, u32[]{:S(2)}) %collective-permute-start.69) | collective-permute-done | bytes 272416 | tf_op jit(solution)/shard_map/ppermute | solution.py:62
  119.0 3.9 %collective-permute-done.18 = bf16[128,896]{1,0:T(8,128)(2,1)S(1)} collective-permute-done((bf16[128,896]{1,0:T(8,128)(2,1)S(1)}, bf16[128,896]{1,0:T(8,128)(2,1)S(1)}, u32[]{:S(2)}, u32[]{:S(2)}) %collective-permute-start.18) | collective-permute-done | bytes 229408 | tf_op jit(solution)/shard_map/ppermute | solution.py:54
  123.8 16.8 %shard_map.197 = (f32[128,896]{1,0:T(8,128)}, bf16[128,896]{1,0:T(8,128)(2,1)}, f32[1,896]{1,0:T(1,128)}, f32[128,896]{1,0:T(8,128)}, f32[1024,256]{1,0:T(8,128)}, /*index=5*/bf16[1024,256]{1,0:T(8,128)(2,1)}) custom-call(s32[17]{0:T(128)} %pad_add_fusion.16.refs_0_, f32[128,896]{1,0:T(8,128)} %slice_add_fusion.2.refs_1_, ...), custom_call_target="tpu_custom_call" | custom-call | flops 4697620480 | bytes 7961668 | tf_op jit(solution)/shard_map/pallas_call | solution.py:151
  146.5 5.1 %collective-permute-done.31 = bf16[152,896]{1,0:T(8,128)(2,1)S(1)} collective-permute-done((bf16[152,896]{1,0:T(8,128)(2,1)S(1)}, bf16[152,896]{1,0:T(8,128)(2,1)S(1)}, u32[]{:S(2)}, u32[]{:S(2)}) %collective-permute-start.31) | collective-permute-done | bytes 272416 | tf_op jit(solution)/shard_map/ppermute | solution.py:62
  153.1 8.6 %collective-permute-done.35 = bf16[152,896]{1,0:T(8,128)(2,1)S(1)} collective-permute-done((bf16[152,896]{1,0:T(8,128)(2,1)S(1)}, bf16[152,896]{1,0:T(8,128)(2,1)S(1)}, u32[]{:S(2)}, u32[]{:S(2)}) %collective-permute-start.35) | collective-permute-done | bytes 272416 | tf_op jit(solution)/shard_map/ppermute | solution.py:62
  180.1 8.9 %collective-permute-done.19 = bf16[384,896]{1,0:T(8,128)(2,1)S(1)} collective-permute-done((bf16[384,896]{1,0:T(8,128)(2,1)S(1)}, bf16[384,896]{1,0:T(8,128)(2,1)S(1)}, u32[]{:S(2)}, u32[]{:S(2)}) %collective-permute-start.19) | collective-permute-done | bytes 688160 | tf_op jit(solution)/shard_map/ppermute | solution.py:54
  194.3 3.8 shard_map.198
  200.0 3.9 %collective-permute-done.75 = bf16[112,2432]{1,0:T(8,128)(2,1)} collective-permute-done((bf16[112,2432]{1,0:T(8,128)(2,1)}, bf16[112,2432]{1,0:T(8,128)(2,1)}, u32[]{:S(2)}, u32[]{:S(2)}) %collective-permute-start.75) | collective-permute-done | bytes 544800 | tf_op jit(solution)/shard_map/ppermute | solution.py:62
  205.8 3.4 collective-permute-done.37
  214.1 6.0 %collective-permute-done.76 = bf16[112,2432]{1,0:T(8,128)(2,1)S(1)} collective-permute-done((bf16[112,2432]{1,0:T(8,128)(2,1)S(1)}, bf16[112,2432]{1,0:T(8,128)(2,1)S(1)}, u32[]{:S(2)}, u32[]{:S(2)}) %collective-permute-start.76) | collective-permute-done | bytes 544800 | tf_op jit(solution)/shard_map/ppermute | solution.py:62
  226.6 12.5 %collective-permute-done.44 = bf16[112,256]{1,0:T(8,128)(2,1)S(1)} collective-permute-done((bf16[112,256]{1,0:T(8,128)(2,1)S(1)}, bf16[112,256]{1,0:T(8,128)(2,1)S(1)}, u32[]{:S(2)}, u32[]{:S(2)}) %collective-permute-start.44) | collective-permute-done | bytes 57376 | tf_op jit(solution)/shard_map/ppermute | solution.py:62
  265.7 5.4 %collective-permute-done.46 = bf16[224,256]{1,0:T(8,128)(2,1)S(1)} collective-permute-done((bf16[224,256]{1,0:T(8,128)(2,1)S(1)}, bf16[224,256]{1,0:T(8,128)(2,1)S(1)}, u32[]{:S(2)}, u32[]{:S(2)}) %collective-permute-start.46) | collective-permute-done | bytes 114720 | tf_op jit(solution)/shard_map/ppermute | solution.py:62
  279.4 10.2 %collective-permute-done.79.refs_6_ = bf16[112,2432]{1,0:T(8,128)(2,1)S(1)} collective-permute-done((bf16[112,2432]{1,0:T(8,128)(2,1)S(1)}, bf16[112,2432]{1,0:T(8,128)(2,1)S(1)}, u32[]{:S(2)}, u32[]{:S(2)}) %collective-permute-start.79) | collective-permute-done | bytes 544800 | tf_op jit(solution)/shard_map/ppermute | solution.py:62
  291.1 6.4 %collective-permute-done.49 = bf16[216,896]{1,0:T(8,128)(2,1)S(1)} collective-permute-done((bf16[216,896]{1,0:T(8,128)(2,1)S(1)}, bf16[216,896]{1,0:T(8,128)(2,1)S(1)}, u32[]{:S(2)}, u32[]{:S(2)}) %collective-permute-start.49) | collective-permute-done | bytes 387104 | tf_op jit(solution)/shard_map/ppermute | solution.py:62
  311.6 7.1 %collective-permute-done.51 = bf16[216,896]{1,0:T(8,128)(2,1)} collective-permute-done((bf16[216,896]{1,0:T(8,128)(2,1)S(1)}, bf16[216,896]{1,0:T(8,128)(2,1)}, u32[]{:S(2)}, u32[]{:S(2)}) %collective-permute-start.51) | collective-permute-done | bytes 387104 | tf_op jit(solution)/shard_map/ppermute | solution.py:62
  329.3 10.3 %shard_map.200 = (f32[896,2432]{1,0:T(8,128)}, f32[896,2432]{1,0:T(8,128)}) custom-call(s32[8]{0:T(128)} %stack.358.spots_ref, bf16[112,2432]{1,0:T(8,128)(2,1)} %copy-done.2, bf16[112,2432]{1,0:T(8,128)(2,1)} %copy-done.16, bf16[112,2432]{1,0:T(8,128)(2,1)} %copy-done.12, bf16[112,2432]{1,0:T(8,128)(2,1)} %copy-done.17, bf16[112,2432]{1,0:T(8,128)(2,1)} %copy-done.14, ...), custom_call_target="tpu_custom_call" | custom-call | tf_op jit(solution)/shard_map/pallas_call | solution.py:461
  340.5 3.5 shard_map.201
  357.8 8.5 %shard_map.199 = f32[448,2048]{1,0:T(8,128)} custom-call(s32[16,2]{1,0:T(8,128)} %stack.356.spots_ref, bf16[224,256]{1,0:T(8,128)(2,1)} %get-tuple-element.283.refs_0_, bf16[224,256]{1,0:T(8,128)(2,1)} %get-tuple-element.282.refs_1_, bf16[224,256]{1,0:T(8,128)(2,1)} %get-tuple-element.281.refs_2_, bf16[224,256]{1,0:T(8,128)(2,1)} %get-tuple-element.280.refs_3_, ...), custom_call_target="tpu_custom_call" | custom-call | tf_op jit(solution)/shard_map/pallas_call | solution.py:415
  372.7 10.2 %shard_map.202 = f32[2432,896]{1,0:T(8,128)} custom-call(s32[16,2]{1,0:T(8,128)} %stack.407.spots_ref, bf16[152,896]{1,0:T(8,128)(2,1)} %slice.1309.refs_0_, bf16[152,896]{1,0:T(8,128)(2,1)} %slice.1310.refs_1_, bf16[152,896]{1,0:T(8,128)(2,1)} %slice.1311.refs_2_, bf16[152,896]{1,0:T(8,128)(2,1)} %slice.1312.refs_3_, bf16[152,896]{1,0:T(8,128)(2,1)} %slice.1313.refs_4_, ...), custom_call_target="tpu_custom_call" | custom-call | tf_op jit(solution)/shard_map/pallas_call | solution.py:415
  (461 shorter events, 205.1 us)
Async XLA Ops:
  1.8 25.6 %collective-permute-start = (bf16[224,1152]{1,0:T(8,128)(2,1)S(1)}, bf16[224,1152]{1,0:T(8,128)(2,1)S(1)}, u32[]{:S(2)}, u32[]{:S(2)}) collective-permute-start(bf16[224,1152]{1,0:T(8,128)(2,1)S(1)} %constant_dynamic-slice_fusion.9), channel_id=1, source_target_pairs={{0,16},{16,0},{1,17},{17,1},{2,18},{18,2},{3,19},{19,3},{4,20},{20... | collective-permute-start | bytes 1548296 | tf_op jit(solution)/shard_map/ppermute | solution.py:54
  37.0 18.1 %collective-permute-start.11 = (bf16[224,896]{1,0:T(8,128)(2,1)S(1)}, bf16[224,896]{1,0:T(8,128)(2,1)S(1)}, u32[]{:S(2)}, u32[]{:S(2)}) collective-permute-start(bf16[224,896]{1,0:T(8,128)(2,1)S(1)} %constant_dynamic-slice_fusion.8), channel_id=1, source_target_pairs={{0,16},{16,0},{1,17},{17,1},{2,18},{18,2},{3,19},{19,3},{4,20},{20... | collective-permute-start | bytes 1204232 | tf_op jit(solution)/shard_map/ppermute | solution.py:54
  38.1 19.9 %collective-permute-start.15 = (bf16[128,1792]{1,0:T(8,128)(2,1)S(1)}, bf16[128,1792]{1,0:T(8,128)(2,1)S(1)}, u32[]{:S(2)}, u32[]{:S(2)}) collective-permute-start(bf16[128,1792]{1,0:T(8,128)(2,1)S(1)} %constant_dynamic-update-slice_fusion.12), channel_id=1, source_target_pairs={{0,16},{16,0},{1,17},{17,1},{2,18},{18,2},{3,19},{19,3},{4,20},{20... | collective-permute-start | bytes 1376264 | tf_op jit(solution)/shard_map/ppermute | solution.py:54
  58.1 25.6 %collective-permute-start.16 = (bf16[256,1792]{1,0:T(8,128)(2,1)S(1)}, bf16[256,1792]{1,0:T(8,128)(2,1)S(1)}, u32[]{:S(2)}, u32[]{:S(2)}) collective-permute-start(bf16[256,1792]{1,0:T(8,128)(2,1)S(1)} %pad_maximum_fusion.5), channel_id=1, source_target_pairs={{0,1},{1,0},{2,3},{3,2},{4,5},{5,4},{6,7},{7,6},{8,9},{9,8},{10,11... | collective-permute-start | bytes 2752520 | tf_op jit(solution)/shard_map/ppermute | solution.py:50
  107.3 33.8 %collective-permute-start.34 = (bf16[152,896]{1,0:T(8,128)(2,1)S(1)}, bf16[152,896]{1,0:T(8,128)(2,1)}, u32[]{:S(2)}, u32[]{:S(2)}) collective-permute-start(bf16[152,896]{1,0:T(8,128)(2,1)S(1)} %pad_maximum_fusion.16), channel_id=1, source_target_pairs={{0,2},{1,3},{4,0},{5,1},{8,4},{9,5},{12,8},{13,9},{14,12},{15,13},... | collective-permute-start | bytes 817160 | tf_op jit(solution)/shard_map/ppermute | solution.py:62
  109.7 31.4 %collective-permute-start.30 = (bf16[152,896]{1,0:T(8,128)(2,1)}, bf16[152,896]{1,0:T(8,128)(2,1)}, u32[]{:S(2)}, u32[]{:S(2)}) collective-permute-start(bf16[152,896]{1,0:T(8,128)(2,1)} %pad_maximum_fusion.15), channel_id=1, source_target_pairs={{0,4},{1,5},{4,8},{5,9},{8,12},{9,13},{12,14},{13,15},{14,10},{15,... | collective-permute-start | bytes 817160 | tf_op jit(solution)/shard_map/ppermute | solution.py:62
  117.4 56.3 %collective-permute-start.70 = (bf16[112,2432]{1,0:T(8,128)(2,1)S(1)}, bf16[112,2432]{1,0:T(8,128)(2,1)S(1)}, u32[]{:S(2)}, u32[]{:S(2)}) collective-permute-start(bf16[112,2432]{1,0:T(8,128)(2,1)S(1)} %pad_maximum_fusion.11), channel_id=1, source_target_pairs={{0,4},{1,5},{4,8},{5,9},{8,12},{9,13},{12,14},{13,15},{14,10},{15,... | collective-permute-start | bytes 1634312 | tf_op jit(solution)/shard_map/ppermute | solution.py:62
  140.7 34.6 %collective-permute-start.74 = (bf16[112,2432]{1,0:T(8,128)(2,1)S(1)}, bf16[112,2432]{1,0:T(8,128)(2,1)S(1)}, u32[]{:S(2)}, u32[]{:S(2)}) collective-permute-start(bf16[112,2432]{1,0:T(8,128)(2,1)S(1)} %pad_maximum_fusion.12), channel_id=1, source_target_pairs={{0,2},{1,3},{4,0},{5,1},{8,4},{9,5},{12,8},{13,9},{14,12},{15,13},... | collective-permute-start | bytes 1634312 | tf_op jit(solution)/shard_map/ppermute | solution.py:62
  144.3 17.4 %collective-permute-start.35 = (bf16[152,896]{1,0:T(8,128)(2,1)S(1)}, bf16[152,896]{1,0:T(8,128)(2,1)S(1)}, u32[]{:S(2)}, u32[]{:S(2)}) collective-permute-start(bf16[152,896]{1,0:T(8,128)(2,1)S(1)} %get-tuple-element.84), channel_id=1, source_target_pairs={{0,2},{1,3},{4,0},{5,1},{8,4},{9,5},{12,8},{13,9},{14,12},{15,13},... | collective-permute-start | bytes 817160 | tf_op jit(solution)/shard_map/ppermute | solution.py:62
  144.8 19.4 %collective-permute-start.21 = (bf16[64,256]{1,0:T(8,128)(2,1)S(1)}, bf16[64,256]{1,0:T(8,128)(2,1)S(1)}, u32[]{:S(2)}, u32[]{:S(2)}) collective-permute-start(bf16[64,256]{1,0:T(8,128)(2,1)S(1)} %get-tuple-element.112), channel_id=1, source_target_pairs={{0,4},{1,5},{4,8},{5,9},{8,12},{9,13},{12,14},{13,15},{14,10},{15,... | collective-permute-start | bytes 98312 | tf_op jit(solution)/shard_map/ppermute | solution.py:62
  163.8 98.0 %collective-permute-start.36 = (bf16[152,896]{1,0:T(8,128)(2,1)}, bf16[152,896]{1,0:T(8,128)(2,1)}, u32[]{:S(2)}, u32[]{:S(2)}) collective-permute-start(bf16[152,896]{1,0:T(8,128)(2,1)} %get-tuple-element.82), channel_id=1, source_target_pairs={{0,2},{1,3},{4,0},{5,1},{8,4},{9,5},{12,8},{13,9},{14,12},{15,13},... | collective-permute-start | bytes 817160 | tf_op jit(solution)/shard_map/ppermute | solution.py:62
  168.6 93.2 %collective-permute-start.32 = (bf16[152,896]{1,0:T(8,128)(2,1)}, bf16[152,896]{1,0:T(8,128)(2,1)}, u32[]{:S(2)}, u32[]{:S(2)}) collective-permute-start(bf16[152,896]{1,0:T(8,128)(2,1)} %get-tuple-element.81), channel_id=1, source_target_pairs={{0,4},{1,5},{4,8},{5,9},{8,12},{9,13},{12,14},{13,15},{14,10},{15,... | collective-permute-start | bytes 817160 | tf_op jit(solution)/shard_map/ppermute | solution.py:62
  178.0 21.5 %collective-permute-start.71 = (bf16[112,2432]{1,0:T(8,128)(2,1)}, bf16[112,2432]{1,0:T(8,128)(2,1)S(1)}, u32[]{:S(2)}, u32[]{:S(2)}) collective-permute-start(bf16[112,2432]{1,0:T(8,128)(2,1)} %get-tuple-element.73), channel_id=1, source_target_pairs={{0,4},{1,5},{4,8},{5,9},{8,12},{9,13},{12,14},{13,15},{14,10},{15,... | collective-permute-start | bytes 1634312 | tf_op jit(solution)/shard_map/ppermute | solution.py:62
  224.1 23.9 %collective-permute-start.77 = (bf16[112,2432]{1,0:T(8,128)(2,1)S(1)}, bf16[112,2432]{1,0:T(8,128)(2,1)S(1)}, u32[]{:S(2)}, u32[]{:S(2)}) collective-permute-start(bf16[112,2432]{1,0:T(8,128)(2,1)S(1)} %add_convert_fusion.refs_0_), channel_id=1, source_target_pairs={{0,4},{1,5},{4,8},{5,9},{8,12},{9,13},{12,14},{13,15},{14,10},{15,... | collective-permute-start | bytes 1634312 | tf_op jit(solution)/shard_map/ppermute | solution.py:62
  225.5 30.5 %collective-permute-start.81 = (bf16[112,2432]{1,0:T(8,128)(2,1)S(1)}, bf16[112,2432]{1,0:T(8,128)(2,1)S(1)}, u32[]{:S(2)}, u32[]{:S(2)}) collective-permute-start(bf16[112,2432]{1,0:T(8,128)(2,1)S(1)} %add_convert_fusion.refs_0_), channel_id=1, source_target_pairs={{0,2},{1,3},{4,0},{5,1},{8,4},{9,5},{12,8},{13,9},{14,12},{15,13},... | collective-permute-start | bytes 1634312 | tf_op jit(solution)/shard_map/ppermute | solution.py:62
  274.4 31.3 %collective-permute-start.86 = (bf16[112,2432]{1,0:T(8,128)(2,1)S(1)}, bf16[112,2432]{1,0:T(8,128)(2,1)S(1)}, u32[]{:S(2)}, u32[]{:S(2)}) collective-permute-start(bf16[112,2432]{1,0:T(8,128)(2,1)S(1)} %add_convert_fusion.refs_0_), channel_id=1, source_target_pairs={{0,1},{1,0},{2,3},{3,2},{4,5},{5,4},{6,7},{7,6},{8,9},{9,8},{10,11... | collective-permute-start | bytes 1634312 | tf_op jit(solution)/shard_map/ppermute | solution.py:50
  278.1 19.5 %collective-permute-start.49 = (bf16[216,896]{1,0:T(8,128)(2,1)S(1)}, bf16[216,896]{1,0:T(8,128)(2,1)S(1)}, u32[]{:S(2)}, u32[]{:S(2)}) collective-permute-start(bf16[216,896]{1,0:T(8,128)(2,1)S(1)} %pad_maximum_fusion.14), channel_id=1, source_target_pairs={{0,4},{1,5},{4,8},{5,9},{8,12},{9,13},{12,14},{13,15},{14,10},{15,... | collective-permute-start | bytes 1161224 | tf_op jit(solution)/shard_map/ppermute | solution.py:62
  289.6 19.9 %collective-permute-start.87 = (bf16[112,2432]{1,0:T(8,128)(2,1)S(1)}, bf16[112,2432]{1,0:T(8,128)(2,1)S(1)}, u32[]{:S(2)}, u32[]{:S(2)}) collective-permute-start(bf16[112,2432]{1,0:T(8,128)(2,1)S(1)} %collective-permute-done.77.refs_2_), channel_id=1, source_target_pairs={{0,1},{1,0},{2,3},{3,2},{4,5},{5,4},{6,7},{7,6},{8,9},{9,8},{10,11... | collective-permute-start | bytes 1634312 | tf_op jit(solution)/shard_map/ppermute | solution.py:50
  289.7 19.9 %collective-permute-start.92 = (bf16[112,2432]{1,0:T(8,128)(2,1)S(1)}, bf16[112,2432]{1,0:T(8,128)(2,1)S(1)}, u32[]{:S(2)}, u32[]{:S(2)}) collective-permute-start(bf16[112,2432]{1,0:T(8,128)(2,1)S(1)} %collective-permute-done.81.refs_12_), channel_id=1, source_target_pairs={{0,1},{1,0},{2,3},{3,2},{4,5},{5,4},{6,7},{7,6},{8,9},{9,8},{10,11... | collective-permute-start | bytes 1634312 | tf_op jit(solution)/shard_map/ppermute | solution.py:50
  321.1 18.6 %collective-permute-start.85 = (bf16[112,2432]{1,0:T(8,128)(2,1)S(1)}, bf16[112,2432]{1,0:T(8,128)(2,1)S(1)}, u32[]{:S(2)}, u32[]{:S(2)}) collective-permute-start(bf16[112,2432]{1,0:T(8,128)(2,1)S(1)} %constant_dynamic-update-slice_fusion.26.refs_0_), channel_id=1, source_target_pairs={{0,1},{1,0},{2,3},{3,2},{4,5},{5,4},{6,7},{7,6},{8,9},{9,8},{10,11... | collective-permute-start | bytes 1634312 | tf_op jit(solution)/shard_map/ppermute | solution.py:50
  321.2 25.5 %collective-permute-start.52 = (bf16[216,896]{1,0:T(8,128)(2,1)}, bf16[216,896]{1,0:T(8,128)(2,1)S(1)}, u32[]{:S(2)}, u32[]{:S(2)}) collective-permute-start(bf16[216,896]{1,0:T(8,128)(2,1)} %collective-permute-done.51), channel_id=1, source_target_pairs={{0,1},{1,0},{2,3},{3,2},{4,5},{5,4},{6,7},{7,6},{8,9},{9,8},{10,11... | collective-permute-start | bytes 1161224 | tf_op jit(solution)/shard_map/ppermute | solution.py:50
  321.7 22.2 %collective-permute-start.53 = (bf16[216,896]{1,0:T(8,128)(2,1)}, bf16[216,896]{1,0:T(8,128)(2,1)S(1)}, u32[]{:S(2)}, u32[]{:S(2)}) collective-permute-start(bf16[216,896]{1,0:T(8,128)(2,1)} %collective-permute-done.51), channel_id=1, source_target_pairs={{0,4},{1,5},{4,8},{5,9},{8,12},{9,13},{12,14},{13,15},{14,10},{15,... | collective-permute-start | bytes 1161224 | tf_op jit(solution)/shard_map/ppermute | solution.py:62
  323.5 22.3 %collective-permute-start.57 = (bf16[216,896]{1,0:T(8,128)(2,1)S(1)}, bf16[216,896]{1,0:T(8,128)(2,1)S(1)}, u32[]{:S(2)}, u32[]{:S(2)}) collective-permute-start(bf16[216,896]{1,0:T(8,128)(2,1)S(1)} %collective-permute-done.56), channel_id=1, source_target_pairs={{0,2},{1,3},{4,0},{5,1},{8,4},{9,5},{12,8},{13,9},{14,12},{15,13},... | collective-permute-start | bytes 1161224 | tf_op jit(solution)/shard_map/ppermute | solution.py:62
  324.6 22.8 %collective-permute-start.62 = (bf16[216,896]{1,0:T(8,128)(2,1)S(1)}, bf16[216,896]{1,0:T(8,128)(2,1)S(1)}, u32[]{:S(2)}, u32[]{:S(2)}) collective-permute-start(bf16[216,896]{1,0:T(8,128)(2,1)S(1)} %collective-permute-done.56), channel_id=1, source_target_pairs={{0,1},{1,0},{2,3},{3,2},{4,5},{5,4},{6,7},{7,6},{8,9},{9,8},{10,11... | collective-permute-start | bytes 1161224 | tf_op jit(solution)/shard_map/ppermute | solution.py:50
  (114 other events, 1381.7 us)

commit v3 on v2

--- a/solution.py
+++ b/solution.py
@@ -134,6 +134,34 @@
             x = x + lax.ppermute(x, "dp", [(i, i ^ bit) for i in range(self.dp)])
             bit *= 2
         return x
+
+    def gather_both(self, a, b, place_a, place_b):
+        n = self.chips
+        half = n // 2
+        streams = [[a, a, a, place_a, None, None], [b, b, b, place_b, None, None]]
+        waiting = [([0], [x]) for x in (a, b)]
+        for s in range(1, half + 1):
+            for k, stream in enumerate(streams):
+                own, fwd, back, place, placed, token = stream
+                if token is not None:
+                    fwd, back, token = lax.optimization_barrier((fwd, back, token))
+                if s < half:
+                    fwd, back = self.hop(fwd, 1), self.hop(back, -1)
+                    arrived = ([s, n - s], [fwd, back])
+                else:
+                    cut = half_cut(own.shape[0])
+                    far = jnp.concatenate([self.hop(fwd[:cut], 1), self.hop(back[cut:], -1)], 0)
+                    arrived = ([half], [far])
+                slots, blocks = waiting[k]
+                out = place(slots, [(x, self.swap(x)) for x in blocks], placed)
+                waiting[k] = arrived
+                streams[k] = [own, fwd, back, place, out[:2], out[2]]
+        results = []
+        for k, stream in enumerate(streams):
+            slots, blocks = waiting[k]
+            out = stream[3](slots, [(x, self.swap(x)) for x in blocks], stream[4])
+            results.append(out[:2])
+        return results
 
 
 VMEM_BYTES = 56 * 1024 * 1024
@@ -241,47 +269,57 @@
             k_ref[to, :] = block[:, :WIDTH_K]
             v_ref[to, :] = block[:, WIDTH_K:]
     spread_heads(q_ref[...], spread_ref, HD ** (-0.5))
-    for kh in range(KH):
-        for part in range(2):
-            span = slice(part * part_rows, (part + 1) * part_rows)
-            start = (me if part == 0 else 2 * ctx - 1 - me) * half
-            last = start // KEYS
-            queries = spread_ref[kh, span, :]
-
-            def keys_of(ref, i):
-                return ref[pl.ds(pl.multiple_of(i * KEYS, KEYS), KEYS), :]
-
-            scores = dot_nt(queries, keys_of(k_ref, last))
+    for part in range(2):
+        span = slice(part * part_rows, (part + 1) * part_rows)
+        start = (me if part == 0 else 2 * ctx - 1 - me) * half
+        last = start // KEYS
+
+        def keys_of(ref, i):
+            return ref[pl.ds(pl.multiple_of(i * KEYS, KEYS), KEYS), :]
+
+        for kh in range(KH):
+            scores = dot_nt(spread_ref[kh, span, :], keys_of(k_ref, last))
             row = lax.broadcasted_iota(jnp.int32, scores.shape, 0) % half + start
             scores = jnp.where(lanes(scores.shape) + last * KEYS <= row, scores, -1e30)
-            s_ref[last] = scores
-            max_ref[...] = jnp.maximum(scores[:, :128], scores[:, 128:])
-
-            def score(i, carry):
-                s = dot_nt(queries, keys_of(k_ref, i))
-                s_ref[i] = s
-                max_ref[...] = jnp.maximum(max_ref[...], jnp.maximum(s[:, :128], s[:, 128:]))
-                return carry
-
-            lax.fori_loop(0, last, score, 0)
-            top = jnp.max(max_ref[...], -1, keepdims=True)
-            sum_ref[...] = jnp.zeros_like(sum_ref)
+            s_ref[kh, last] = scores
+            max_ref[kh] = jnp.maximum(scores[:, :128], scores[:, 128:])
+
+        def score(i, carry):
+            for kh in range(KH):
+                s = dot_nt(spread_ref[kh, span, :], keys_of(k_ref, i))
+                s_ref[kh, i] = s
+                max_ref[kh] = jnp.maximum(max_ref[kh], jnp.maximum(s[:, :128], s[:, 128:]))
+            return carry
+
+        lax.fori_loop(0, last, score, 0)
+        for kh in range(KH):
+            top = jnp.max(max_ref[kh], -1, keepdims=True)
+            max_ref[kh] = jnp.broadcast_to(top, (part_rows, 128))
+            sum_ref[kh] = jnp.zeros((part_rows, 128), f32)
             o_ref[kh, span, :] = jnp.zeros((part_rows, 128), f32)
 
-            def weigh(i, carry):
-                p = jnp.exp(s_ref[i] - top)
-                sum_ref[...] += p[:, :128] + p[:, 128:]
+        def weigh(i, carry):
+            for kh in range(KH):
+                s = s_ref[kh, i]
+                top = max_ref[kh]
+                left = jnp.exp(s[:, :128] - top)
+                right = jnp.exp(s[:, 128:] - top)
+                sum_ref[kh] += left + right
                 o_ref[kh, span, :] += jnp.dot(
-                    p.astype(bf16), keys_of(v_ref, i), preferred_element_type=f32
+                    jnp.concatenate([left, right], 1).astype(bf16),
+                    keys_of(v_ref, i),
+                    preferred_element_type=f32,
                 )
-                return carry
-
-            lax.fori_loop(0, last + 1, weigh, 0)
-            total = jnp.sum(sum_ref[...], -1, keepdims=True)
+            return carry
+
+        lax.fori_loop(0, last + 1, weigh, 0)
+        for kh in range(KH):
+            total = jnp.sum(sum_ref[kh], -1, keepdims=True)
             o_ref[kh, span, :] = o_ref[kh, span, :] / total
-            lse = jnp.broadcast_to(top + jnp.log(total), (part_rows, 128))
             lse_ref[kh, part] = dot_nt(
-                jnp.full((8, 128), 1.0 / 128, f32), lse, lax.Precision.HIGHEST
+                jnp.full((8, 128), 1.0 / 128, f32),
+                max_ref[kh] + jnp.log(total),
+                lax.Precision.HIGHEST,
             )
     for tile in range(WIDTH_Q // 128):
         low_ref[:, tile * 128 : (tile + 1) * 128] = join_heads(o_ref, half, tile).astype(bf16)
@@ -318,38 +356,45 @@
     gqs_ref[...] = jnp.zeros_like(gqs_ref)
     gk_ref[...] = jnp.zeros_like(gk_ref)
     gv_ref[...] = jnp.zeros_like(gv_ref)
-    for kh in range(KH):
-        for part in range(2):
-            span = slice(part * part_rows, (part + 1) * part_rows)
-            start = (me if part == 0 else 2 * ctx - 1 - me) * half
-            last = start // KEYS
-            queries = spread_ref[kh, span, :]
-            heads = go_ref[kh, span, :]
-            lse = lse_ref[kh, part][:1]
-            delta = dot_nt(
-                jnp.ones((8, 128), f32), heads.astype(f32) * o_ref[kh, span, :],
+    for part in range(2):
+        span = slice(part * part_rows, (part + 1) * part_rows)
+        start = (me if part == 0 else 2 * ctx - 1 - me) * half
+        last = start // KEYS
+        deltas = [
+            dot_nt(
+                jnp.ones((8, 128), f32),
+                go_ref[kh, span, :].astype(f32) * o_ref[kh, span, :],
                 lax.Precision.HIGHEST,
             )[:1]
-
-            def step(i, masked):
-                at = pl.ds(pl.multiple_of(i * KEYS, KEYS), KEYS)
-                keys = k_ref[at, :]
-                p = jnp.exp(dot_nt(keys, queries) - lse)
+            for kh in range(KH)
+        ]
+
+        def step(i, masked):
+            at = pl.ds(pl.multiple_of(i * KEYS, KEYS), KEYS)
+            keys = k_ref[at, :]
+            grad_k = gk_ref[at, :]
+            grad_v = gv_ref[at, :]
+            for kh in range(KH):
+                queries = spread_ref[kh, span, :]
+                heads = go_ref[kh, span, :]
+                p = jnp.exp(dot_nt(keys, queries) - lse_ref[kh, part][:1])
                 if masked:
                     row = lanes(p.shape) % half + start
                     key = lax.broadcasted_iota(jnp.int32, p.shape, 0) + i * KEYS
                     p = jnp.where(key <= row, p, 0.0)
-                gs = (p * (dot_nt(v_ref[at, :], heads) - delta)).astype(bf16)
-                gv_ref[at, :] += jnp.dot(p.astype(bf16), heads, preferred_element_type=f32)
-                gk_ref[at, :] += jnp.dot(gs, queries, preferred_element_type=f32)
+                gs = (p * (dot_nt(v_ref[at, :], heads) - deltas[kh])).astype(bf16)
+                grad_v += jnp.dot(p.astype(bf16), heads, preferred_element_type=f32)
+                grad_k += jnp.dot(gs, queries, preferred_element_type=f32)
                 gqs_ref[kh, span, :] += dot_tn(gs, keys)
-
-            def body(i, carry):
-                step(i, False)
-                return carry
-
-            lax.fori_loop(0, last, body, 0)
-            step(last, True)
+            gk_ref[at, :] = grad_k
+            gv_ref[at, :] = grad_v
+
+        def body(i, carry):
+            step(i, False)
+            return carry
+
+        lax.fori_loop(0, last, body, 0)
+        step(last, True)
     for tile in range(WIDTH_Q // 128):
         gq_ref[:, tile * 128 : (tile + 1) * 128] = join_heads(gqs_ref, half, tile) * HD ** (-0.5)
     for j in range(ctx):
@@ -391,6 +436,285 @@
     )
 
 
+def mlp_kernel(
+    half_rows, spots_ref, x_ref, gy_ref, gate_a, gate_b, up_a, up_b, down_a, down_b,
+    mid_ref, gg_ref, gu_ref, gx_ref, out_ref, send_ref, gx_acc, out_acc,
+):
+    step = pl.program_id(0)
+    x = x_ref[...]
+    gy = gy_ref[...]
+    wg = jnp.concatenate([gate_a[...], gate_b[...]], 1)
+    wu = jnp.concatenate([up_a[...], up_b[...]], 1)
+    wd = jnp.concatenate([down_a[...], down_b[...]], 0)
+    gate = jnp.dot(x, wg, preferred_element_type=f32)
+    up = jnp.dot(x, wu, preferred_element_type=f32)
+    grad = dot_nt(gy, wd)
+    core = spots_ref[1]
+    column = lanes((1, gate.shape[1])) + (step * 256 + spots_ref[2])
+    own = (column < spots_ref[3]) == (core == 0)
+    sigma = jax.nn.sigmoid(gate)
+    active = gate * sigma
+    middle = jnp.where(own, active * up, 0.0).astype(bf16)
+    grad_gate = jnp.where(
+        own, grad * up * (sigma * (1.0 + gate * (1.0 - sigma))), 0.0
+    ).astype(bf16)
+    grad_up = jnp.where(own, grad * active, 0.0).astype(bf16)
+    mid_ref[...] = middle
+    gg_ref[...] = grad_gate
+    gu_ref[...] = grad_up
+    gx = dot_nt(grad_gate, wg) + dot_nt(grad_up, wu)
+    out = jnp.dot(middle, wd, preferred_element_type=f32)
+
+    @pl.when(step == 0)
+    def start():
+        gx_acc[...] = gx
+        out_acc[...] = out
+
+    @pl.when(step > 0)
+    def add():
+        gx_acc[...] += gx
+        out_acc[...] += out
+
+    @pl.when(step == pl.num_programs(0) - 1)
+    def end():
+        gx_ref[...] = gx_acc[:half_rows]
+        out_ref[...] = out_acc[:half_rows]
+        send_ref[:half_rows] = gx_acc[half_rows:].astype(bf16)
+        send_ref[half_rows:] = out_acc[half_rows:].astype(bf16)
+
+
+def feed_forward(meta, x, gy, w_gate, w_up, w_down, width):
+    tokens = x.shape[0]
+    half = tokens // 2
+    steps = width // 256
+    tiles = width // 128 - 1
+
+    def columns(j):
+        return pl.BlockSpec((D, 128), lambda i, m: (0, m[1] * tiles + 2 * i + j))
+
+    def rows(j):
+        return pl.BlockSpec((128, D), lambda i, m: (m[1] * tiles + 2 * i + j, 0))
+
+    whole = pl.BlockSpec((tokens, D), lambda i, m: (0, 0))
+    halves = pl.BlockSpec((half, D), lambda i, m: (0, 0))
+    tile = pl.BlockSpec((tokens, 256), lambda i, m: (0, i))
+    hidden = jax.ShapeDtypeStruct((tokens, width), bf16)
+    return pl.pallas_call(
+        lambda *refs: mlp_kernel(half, *refs),
+        out_shape=[hidden] * 3
+        + [jax.ShapeDtypeStruct((half, D), f32)] * 2
+        + [jax.ShapeDtypeStruct((tokens, D), bf16)],
+        grid_spec=pltpu.PrefetchScalarGridSpec(
+            num_scalar_prefetch=1,
+            grid=(steps,),
+            in_specs=[whole, whole, columns(0), columns(1), columns(0), columns(1), rows(0), rows(1)],
+            out_specs=[tile, tile, tile, halves, halves, whole],
+            scratch_shapes=[pltpu.VMEM((tokens, D), f32)] * 2,
+        ),
+        compiler_params=pltpu.CompilerParams(vmem_limit_bytes=VMEM_BYTES),
+        cost_estimate=pl.CostEstimate(
+            flops=12 * tokens * width * D, bytes_accessed=6 * width * D, transcendentals=0
+        ),
+    )(meta, x, gy, w_gate, w_gate, w_up, w_up, w_down, w_down)
+
+
+def mlp_grad_kernel(
+    down_rows, main, meta_ref, x_ref, gy_ref, mid_ref, gg_ref, gu_ref, out_ref, mlp_acc, down_acc
+):
+    step = pl.program_id(0)
+    core = meta_ref[1]
+    at_main = pl.ds(pl.multiple_of(core * 128, 128), main)
+    at_tile = pl.ds(pl.multiple_of((1 - core) * main, 128), 128)
+
+    @pl.when(step == 0)
+    def products():
+        x = x_ref[...]
+        mlp_acc[:, :main] = dot_tn(x, gg_ref[:, at_main])
+        mlp_acc[:, main : 2 * main] = dot_tn(x, gu_ref[:, at_main])
+        mixed = gg_ref[:, at_tile].astype(f32) + pltpu.roll(gu_ref[:, at_tile].astype(f32), 64, 1)
+        mlp_acc[:, 2 * main :] = dot_tn(x, mixed.astype(bf16))
+        down_acc[...] = dot_tn(mid_ref[...], gy_ref[...])
+
+    mlp_rows = mlp_acc.shape[0] // pl.num_programs(0)
+    columns = mlp_acc.shape[1] // 128
+    block = mlp_acc[pl.ds(pl.multiple_of(step * mlp_rows, 16), mlp_rows), :].astype(bf16)
+    for j in range(columns):
+        for i in range(mlp_rows // 16):
+            out_ref[0, j * 16 : (j + 1) * 16, i * 128 : (i + 1) * 128] = block[
+                i * 16 : (i + 1) * 16, j * 128 : (j + 1) * 128
+            ]
+    first = pl.multiple_of(core * 64 + step * down_rows, 8)
+    out_ref[0, columns * 16 :, :] = down_acc[pl.ds(first, down_rows), :].astype(bf16)
+
+
+def mlp_gradients(meta, x, gy, mid, gg, gu, chips, down_rows, main):
+    tokens = x.shape[0]
+    columns = (2 * main + 128) // 128
+    rows = columns * 16 + down_rows
+    wide = pl.BlockSpec((tokens, D), lambda i, m: (0, 0))
+    tall = pl.BlockSpec((tokens, mid.shape[1]), lambda i, m: (0, 0))
+    return pl.pallas_call(
+        lambda *refs: mlp_grad_kernel(down_rows, main, *refs),
+        out_shape=jax.ShapeDtypeStruct((chips, rows, D), bf16),
+        grid_spec=pltpu.PrefetchScalarGridSpec(
+            num_scalar_prefetch=1,
+            grid=(chips,),
+            in_specs=[wide, wide, tall, tall, tall],
+            out_specs=pl.BlockSpec((1, rows, D), lambda i, m: (m[4 + i], 0, 0)),
+            scratch_shapes=[
+                pltpu.VMEM((D, columns * 128), f32),
+                pltpu.VMEM((mid.shape[1], D), f32),
+            ],
+        ),
+        compiler_params=pltpu.CompilerParams(vmem_limit_bytes=VMEM_BYTES),
+        cost_estimate=pl.CostEstimate(
+            flops=6 * tokens * mid.shape[1] * D, bytes_accessed=4 * chips * rows * D,
+            transcendentals=0,
+        ),
+    )(meta, x, gy, mid, gg, gu)
+
+
+def small_grad_kernel(chips, q_rows, meta_ref, norm_ref, joint_ref, att_ref, ga_ref, out_ref, acc):
+    cols = joint_ref.shape[1]
+    acc[:, :cols] = dot_tn(norm_ref[...], joint_ref[...])
+    acc[:, cols:] = dot_tn(att_ref[...], ga_ref[...])
+    first = (2 * meta_ref[0] + meta_ref[1]) * q_rows
+    rows = acc[pl.ds(pl.multiple_of(first, 16), q_rows), :]
+    count = acc.shape[1] // 128 // chips
+    lanes_out = D // 128
+    piece = q_rows * count // lanes_out
+    for owner in range(chips):
+        tall = jnp.concatenate(
+            [rows[:, (owner * count + i) * 128 : (owner * count + i + 1) * 128] for i in range(count)],
+            0,
+        ).astype(bf16)
+        slot = meta_ref[4 + owner]
+        for i in range(lanes_out):
+            out_ref[slot, :, i * 128 : (i + 1) * 128] = tall[i * piece : (i + 1) * piece]
+
+
+def place_pairs(meta, slots, pairs, main, ff_loc, old=None):
+    count = len(pairs)
+    mlp_rows = D // 8
+    columns = pairs[0][0].shape[0] // 16
+    tiles = main // 128
+    blocks = [x for pair in pairs for x in pair]
+
+    def kernel(meta_ref, *refs):
+        step = pl.program_id(0)
+        gate_ref, up_ref, token_ref = refs[-3:]
+        token_ref[...] = jnp.zeros(token_ref.shape, f32)
+        core_zero = meta_ref[1] == 0
+
+        def column(ref, j):
+            parts = [
+                ref[j * 16 : (j + 1) * 16, i * 128 : (i + 1) * 128] for i in range(mlp_rows // 16)
+            ]
+            return jnp.concatenate(parts, 0).astype(f32)
+
+        for k in range(count):
+
+            @pl.when(step == k)
+            def write(k=k):
+                for j in range(columns):
+                    got = column(refs[2 * k], j)
+                    other = column(refs[2 * k + 1], j)
+                    zero = jnp.where(core_zero, got, other)
+                    one = jnp.where(core_zero, other, got)
+                    if j < 2 * tiles:
+                        ref = gate_ref if j < tiles else up_ref
+                        at = (j % tiles) * 128
+                        ref[:, at : at + 128] = zero
+                        ref[:, at + main + 128 : at + main + 256] = one
+                    else:
+                        left = lanes(zero.shape) < 64
+                        gate_ref[:, main : main + 128] = jnp.where(left, zero, one)
+                        up_ref[:, main : main + 128] = pltpu.roll(jnp.where(left, one, zero), 64, 1)
+
+    keep = [] if old is None else list(old)
+    out_spec = pl.BlockSpec((mlp_rows, ff_loc), lambda i, m: (m[12 + pick(slots, i)], 0))
+    return pl.pallas_call(
+        kernel,
+        out_shape=[jax.ShapeDtypeStruct((D, ff_loc), f32)] * 2
+        + [jax.ShapeDtypeStruct((8, 128), f32)],
+        grid_spec=pltpu.PrefetchScalarGridSpec(
+            num_scalar_prefetch=1,
+            grid=(count,),
+            in_specs=[pl.BlockSpec(blocks[0].shape, lambda i, m: (0, 0))] * (2 * count)
+            + [pl.BlockSpec(memory_space=pl.ANY)] * len(keep),
+            out_specs=[out_spec, out_spec, pl.BlockSpec((8, 128), lambda i, m: (0, 0))],
+        ),
+        input_output_aliases={} if old is None else {2 * count + 1: 0, 2 * count + 2: 1},
+        compiler_params=pltpu.CompilerParams(vmem_limit_bytes=VMEM_BYTES),
+        cost_estimate=pl.CostEstimate(
+            flops=0, bytes_accessed=count * mlp_rows * ff_loc * 16, transcendentals=0
+        ),
+    )(meta, *blocks, *keep)
+
+
+def pick(values, i):
+    out = values[0]
+    for k in range(1, len(values)):
+        out = jnp.where(i == k, values[k], out)
+    return out
+
+
+def place_rest(meta, slots, pairs, down_rows, q_rows, ff_loc, cols, chips, old=None):
+    count = len(pairs)
+    blocks = [x for pair in pairs for x in pair]
+    lanes_out = D // 128
+    piece = blocks[0].shape[0] - down_rows
+
+    def kernel(meta_ref, *refs):
+        step = pl.program_id(0)
+        down_ref, small_ref, token_ref = refs[-3:]
+        token_ref[...] = jnp.zeros(token_ref.shape, f32)
+        for k in range(2 * count):
+
+            @pl.when(step == k)
+            def write(k=k):
+                ref = refs[k]
+                down_ref[...] = ref[piece:, :].astype(f32)
+                tall = jnp.concatenate(
+                    [ref[:piece, i * 128 : (i + 1) * 128] for i in range(lanes_out)], 0
+                ).astype(f32)
+                for i in range(tall.shape[0] // q_rows):
+                    small_ref[:, i * 128 : (i + 1) * 128] = tall[i * q_rows : (i + 1) * q_rows]
+
+    keep = [] if old is None else list(old)
+
+    def side(i, m):
+        return jnp.where(i % 2 == 0, m[1], 1 - m[1])
+
+    def owner(i, m):
+        return m[12 + pick(slots, i // 2)]
+
+    return pl.pallas_call(
+        kernel,
+        out_shape=[
+            jax.ShapeDtypeStruct((ff_loc, D), f32),
+            jax.ShapeDtypeStruct((2 * q_rows, cols), f32),
+            jax.ShapeDtypeStruct((8, 128), f32),
+        ],
+        grid_spec=pltpu.PrefetchScalarGridSpec(
+            num_scalar_prefetch=1,
+            grid=(2 * count,),
+            in_specs=[pl.BlockSpec(blocks[0].shape, lambda i, m: (0, 0))] * (2 * count)
+            + [pl.BlockSpec(memory_space=pl.ANY)] * len(keep),
+            out_specs=[
+                pl.BlockSpec((down_rows, D), lambda i, m: (side(i, m) * chips + owner(i, m), 0)),
+                pl.BlockSpec((q_rows, cols // chips), lambda i, m: (side(i, m), owner(i, m))),
+                pl.BlockSpec((8, 128), lambda i, m: (0, 0)),
+            ],
+        ),
+        input_output_aliases={} if old is None else {2 * count + 1: 0, 2 * count + 2: 1},
+        compiler_params=pltpu.CompilerParams(vmem_limit_bytes=VMEM_BYTES),
+        cost_estimate=pl.CostEstimate(
+            flops=0, bytes_accessed=count * down_rows * D * 16, transcendentals=0
+        ),
+    )(meta, *blocks, *keep)
+
+
 def place_blocks(blocks, spots, out_shape, old=None):
     shape = blocks[0].shape
     count = len(blocks)
@@ -427,52 +751,6 @@
     )(jnp.stack([jnp.stack(s) for s in spots]).astype(jnp.int32), *blocks, *keep)
 
 
-def place_mlp(pairs, owners, core, main, out_shape, old=None):
-    count = len(pairs)
-    rows = pairs[0][0].shape[0]
-    columns = pairs[0][0].shape[1]
-    blocks = [x for pair in pairs for x in pair]
-
-    def kernel(spots_ref, *refs):
-        step = pl.program_id(0)
-        gate_ref, up_ref = refs[-2:]
-        core_zero = spots_ref[count] == 0
-        for i in range(count):
-
-            @pl.when(step == i)
-            def write(i=i):
-                got = refs[2 * i][...].astype(f32)
-                other = refs[2 * i + 1][...].astype(f32)
-                zero = jnp.where(core_zero, got, other)
-                one = jnp.where(core_zero, other, got)
-                tile_zero, tile_one = zero[:, 2 * main :], one[:, 2 * main :]
-                left = lanes(tile_zero.shape) < 64
-                gate_ref[:, :main] = zero[:, :main]
-                gate_ref[:, main : main + 128] = jnp.where(left, tile_zero, tile_one)
-                gate_ref[:, main + 128 :] = one[:, :main]
-                up_ref[:, :main] = zero[:, main : 2 * main]
-                up_ref[:, main : main + 128] = pltpu.roll(
-                    jnp.where(left, tile_one, tile_zero), 64, 1
-                )
-                up_ref[:, main + 128 :] = one[:, main : 2 * main]
-
-    keep = [] if old is None else list(old)
-    out_spec = pl.BlockSpec((rows, out_shape[1]), lambda i, spots: (spots[i], 0))
-    return pl.pallas_call(
-        kernel,
-        out_shape=[jax.ShapeDtypeStruct(out_shape, f32)] * 2,
-        grid_spec=pltpu.PrefetchScalarGridSpec(
-            num_scalar_prefetch=1,
-            grid=(count,),
-            in_specs=[pl.BlockSpec((rows, columns), lambda i, spots: (0, 0))] * (2 * count)
-            + [pl.BlockSpec(memory_space=pl.ANY)] * len(keep),
-            out_specs=[out_spec, out_spec],
-        ),
-        input_output_aliases={} if old is None else {2 * count + 1: 0, 2 * count + 2: 1},
-        compiler_params=pltpu.CompilerParams(vmem_limit_bytes=VMEM_BYTES),
-    )(jnp.stack(list(owners) + [core]).astype(jnp.int32), *blocks, *keep)
-
-
 def local(tokens, w_qkv, b_qkv, w_out, gain_attn, gain_mlp, w_gate, w_up, w_down, cotangent):
     net = Net()
     rows = tokens.shape[1]
@@ -493,10 +771,12 @@
     rest = ff_half - main
     width = main + 2 * rest
     first = core * main
-    own_cols = (jnp.arange(width) + first < ff_half) == (core == 0)
-    wg = lax.dynamic_slice(w_gate, (0, first), (D, width))
-    wu = lax.dynamic_slice(w_up, (0, first), (D, width))
-    wd = lax.dynamic_slice(w_down, (first, 0), (width, D))
+    tiled = 2 * rest == 128 and width % 256 == 0 and chips == 8 and (ff_half // chips) % 8 == 0
+    ring = jnp.arange(chips, dtype=jnp.int32)
+    owners_of = (net.pos - ring) % chips
+    spots = jnp.concatenate(
+        [jnp.stack([net.d, core, first, jnp.int32(ff_half)]), owners_of, owners_of]
+    ).astype(jnp.int32)
 
     row_ids = jnp.arange(half_rows, dtype=jnp.int32)
     place = jnp.concatenate(
@@ -547,75 +827,92 @@
         [meta, queries, mine, other, x, w_out_full, gain_two],
         smem=1,
         scratch=[
-            pltpu.VMEM((total_keys // KEYS, part_rows, KEYS), f32),
-            pltpu.VMEM((part_rows, 128), f32),
-            pltpu.VMEM((part_rows, 128), f32),
+            pltpu.VMEM((KH, total_keys // KEYS, part_rows, KEYS), f32),
+            pltpu.VMEM((KH, part_rows, 128), f32),
+            pltpu.VMEM((KH, part_rows, 128), f32),
         ],
         flops=8 * KH * part_rows * total_keys * 128,
     )
 
     normed_two_group = net.group_gather(normed_two)
-    gate = jnp.dot(normed_two_group, wg, preferred_element_type=f32)
-    upper = jnp.dot(normed_two_group, wu, preferred_element_type=f32)
-    sigma = jax.nn.sigmoid(gate)
-    activated = gate * sigma
-    middle = jnp.where(own_cols, activated * upper, 0.0).astype(bf16)
-    grad_middle = jnp.einsum("td,fd->tf", grad_out_group, wd, preferred_element_type=f32)
-    slope = sigma * (1.0 + gate * (1.0 - sigma))
-    grad_gate_low = jnp.where(own_cols, grad_middle * upper * slope, 0.0).astype(bf16)
-    grad_up_low = jnp.where(own_cols, grad_middle * activated, 0.0).astype(bf16)
-
-    grad_normed_two = jnp.einsum(
-        "tf,df->td", grad_gate_low, wg, preferred_element_type=f32
-    ) + jnp.einsum("tf,df->td", grad_up_low, wu, preferred_element_type=f32)
-    mlp_out = jnp.dot(middle, wd, preferred_element_type=f32)
     chip_rows = net.dp * rows
-    swapped = net.swap(
-        jnp.concatenate([grad_normed_two[chip_rows:], mlp_out[chip_rows:]], 0).astype(bf16)
-    ).astype(f32)
-    grad_chip = grad_normed_two[:chip_rows] + swapped[:chip_rows]
-    mlp_chip = mlp_out[:chip_rows] + swapped[chip_rows:]
+    down_rows = ff_half // chips
+    mlp_rows = D // chips
+    if tiled:
+        mid, gate_low, up_low, grad_mine, out_mine, sent = feed_forward(
+            spots, normed_two_group, grad_out_group, w_gate, w_up, w_down, width
+        )
+    else:
+        own_cols = (jnp.arange(width) + first < ff_half) == (core == 0)
+        wg = lax.dynamic_slice(w_gate, (0, first), (D, width))
+        wu = lax.dynamic_slice(w_up, (0, first), (D, width))
+        wd = lax.dynamic_slice(w_down, (first, 0), (width, D))
+        gate = jnp.dot(normed_two_group, wg, preferred_element_type=f32)
+        upper = jnp.dot(normed_two_group, wu, preferred_element_type=f32)
+        sigma = jax.nn.sigmoid(gate)
+        activated = gate * sigma
+        middle = jnp.where(own_cols, activated * upper, 0.0).astype(bf16)
+        grad_middle = jnp.einsum("td,fd->tf", grad_out_group, wd, preferred_element_type=f32)
+        slope = sigma * (1.0 + gate * (1.0 - sigma))
+        grad_gate_low = jnp.where(own_cols, grad_middle * upper * slope, 0.0).astype(bf16)
+        grad_up_low = jnp.where(own_cols, grad_middle * activated, 0.0).astype(bf16)
+
+        grad_normed_two = jnp.einsum(
+            "tf,df->td", grad_gate_low, wg, preferred_element_type=f32
+        ) + jnp.einsum("tf,df->td", grad_up_low, wu, preferred_element_type=f32)
+        mlp_out = jnp.dot(middle, wd, preferred_element_type=f32)
+        grad_mine, out_mine = grad_normed_two[:chip_rows], mlp_out[:chip_rows]
+        sent = jnp.concatenate([grad_normed_two[chip_rows:], mlp_out[chip_rows:]], 0).astype(bf16)
+    swapped = net.swap(sent)
+    grad_chip = grad_mine + swapped[:chip_rows].astype(f32)
+    mlp_chip = out_mine + swapped[chip_rows:].astype(f32)
     grad_two = grad_chip[:rows]
     for s in range(1, net.dp):
-        sent = grad_chip[s * rows : (s + 1) * rows].astype(bf16)
-        grad_two = grad_two + net.shift(sent, net.dp - s).astype(f32)
-
-    part_down = jnp.einsum(
-        "tf,td->fd", middle, grad_out_group, preferred_element_type=f32
-    ).astype(bf16)
-    part_down = lax.dynamic_slice(part_down, (core * rest, 0), (ff_half, D))
-    down_rows = ff_half // chips
-
-    def down_chunk(slot):
-        return lax.dynamic_slice(part_down, (net.owner(slot) * down_rows, 0), (down_rows, D))
-
-    sum_down = net.ring_scatter([down_chunk(s) for s in range(chips)]).astype(bf16)
-
-    def split_main(x):
-        left = (x[:, :main], x[:, main:])
-        right = (x[:, 2 * rest :], x[:, : 2 * rest])
-        return (
-            jnp.where(core == 0, left[0], right[0]),
-            jnp.where(core == 0, left[1], right[1]),
+        piece = grad_chip[s * rows : (s + 1) * rows].astype(bf16)
+        grad_two = grad_two + net.shift(piece, net.dp - s).astype(f32)
+
+    if tiled:
+        terms = mlp_gradients(
+            spots, normed_two_group, grad_out_group, mid, gate_low, up_low, chips, down_rows, main
         )
-
-    gate_main, gate_tile = split_main(grad_gate_low)
-    up_main, up_tile = split_main(grad_up_low)
-    packed = jnp.concatenate(
-        [gate_main, up_main, gate_tile + jnp.roll(up_tile, rest, 1)], 1
-    )
-    part_mlp = jnp.einsum(
-        "td,tf->df", normed_two_group, packed, preferred_element_type=f32
-    ).astype(bf16)
-    mlp_rows = D // chips
-
-    def mlp_chunk(slot):
-        return lax.dynamic_slice(
-            part_mlp, (net.owner(slot) * mlp_rows, 0), (mlp_rows, 2 * ff_half)
+        summed = net.ring_scatter([terms[s] for s in range(chips)]).astype(bf16)
+        sum_mlp = summed[: terms.shape[1] - down_rows]
+        sum_down = summed[terms.shape[1] - down_rows :]
+    else:
+        part_down = jnp.einsum(
+            "tf,td->fd", middle, grad_out_group, preferred_element_type=f32
+        ).astype(bf16)
+        part_down = lax.dynamic_slice(part_down, (core * rest, 0), (ff_half, D))
+
+        def down_chunk(slot):
+            return lax.dynamic_slice(part_down, (net.owner(slot) * down_rows, 0), (down_rows, D))
+
+        sum_down = net.ring_scatter([down_chunk(s) for s in range(chips)]).astype(bf16)
+
+        def split_main(x):
+            left = (x[:, :main], x[:, main:])
+            right = (x[:, 2 * rest :], x[:, : 2 * rest])
+            return (
+                jnp.where(core == 0, left[0], right[0]),
+                jnp.where(core == 0, left[1], right[1]),
+            )
+
+        gate_main, gate_tile = split_main(grad_gate_low)
+        up_main, up_tile = split_main(grad_up_low)
+        packed = jnp.concatenate(
+            [gate_main, up_main, gate_tile + jnp.roll(up_tile, rest, 1)], 1
         )
-
-    sum_mlp = net.ring_scatter([mlp_chunk(s) for s in range(chips)]).astype(bf16)
-    sum_mlp = lax.optimization_barrier(sum_mlp)
+        part_mlp = jnp.einsum(
+            "td,tf->df", normed_two_group, packed, preferred_element_type=f32
+        ).astype(bf16)
+
+        def mlp_chunk(slot):
+            return lax.dynamic_slice(
+                part_mlp, (net.owner(slot) * mlp_rows, 0), (mlp_rows, 2 * ff_half)
+            )
+
+        sum_mlp = net.ring_scatter([mlp_chunk(s) for s in range(chips)]).astype(bf16)
+        sum_mlp = lax.optimization_barrier(sum_mlp)
 
     grad_hidden, grad_attn_low, grad_gain_two, grad_queries, terms_mine, terms_other = call(
         lambda *refs: backward_kernel(ctx_count, *refs),
@@ -673,67 +970,79 @@
     grad_attn_group = gathered[:, 1].reshape(2 * net.dp * rows, D)
 
     q_rows = w_qkv.shape[0] // 2
-    q_first = net.d * (2 * q_rows) + core * q_rows
-    group_rows = 2 * net.dp * rows
-    part_out = jnp.einsum(
-        "tc,td->cd",
-        lax.dynamic_slice(attended_group, (0, q_first), (group_rows, q_rows)),
-        grad_attn_group,
-        preferred_element_type=f32,
-    )
-    part_joint = jnp.einsum(
-        "td,tc->dc",
-        lax.dynamic_slice(normed_one_group, (0, q_first), (group_rows, q_rows)),
-        net.group_gather(grad_joint_low),
-        preferred_element_type=f32,
-    )
-    part_small = jnp.concatenate([part_joint, part_out], 1).astype(bf16)
-    small_cols = part_small.shape[1] // chips
-
-    def small_chunk(slot):
-        return lax.dynamic_slice(part_small, (0, net.owner(slot) * small_cols), (q_rows, small_cols))
-
-    sum_small = net.ring_scatter([small_chunk(s) for s in range(chips)]).astype(bf16)
-
-    tall = jnp.concatenate(
-        [sum_small[:, i * 128 : (i + 1) * 128] for i in range(small_cols // 128)], 0
-    )
-    piece = tall.shape[0] // (D // 128)
-    wide = jnp.concatenate([tall[i * piece : (i + 1) * piece] for i in range(D // 128)], 1)
-    both = lax.optimization_barrier(jnp.concatenate([sum_down, wide], 0))
-
-    owners = [net.owner(s) for s in range(chips)]
-    got_mlp = net.ring_gather(sum_mlp)
-    got_both = net.ring_gather(both)
-    pairs_mlp = [(got, net.swap(got)) for got in got_mlp]
-    pairs_both = [(got, net.swap(got)) for got in got_both]
-
-    down_blocks, down_spots, small_blocks, small_spots = [], [], [], []
-    for owner, pair in zip(owners, pairs_both):
-        for which, got in zip((core, 1 - core), pair):
-            down_blocks.append(got[:down_rows])
-            down_spots.append((which * chips + owner, jnp.int32(0)))
-            wide = got[down_rows:]
-            tall = jnp.concatenate([wide[:, i * 128 : (i + 1) * 128] for i in range(D // 128)], 0)
-            small_blocks.append(
-                jnp.concatenate(
-                    [tall[i * q_rows : (i + 1) * q_rows] for i in range(small_cols // 128)], 1
-                )
-            )
-            small_spots.append((which, owner))
-    grad_down = place_blocks(down_blocks, down_spots, (ff_loc, D))
-    grad_small = place_blocks(small_blocks, small_spots, (2 * q_rows, part_small.shape[1]))
-    half = chips // 2
-    if 2 * rest == 128:
-        first_slots = [s for s in range(chips) if s != half]
-        grad_mlp = place_mlp(
-            [pairs_mlp[s] for s in first_slots], [owners[s] for s in first_slots], core, main,
-            (D, ff_loc),
-        )
-        grad_gate, grad_up = place_mlp(
-            [pairs_mlp[half]], [owners[half]], core, main, (D, ff_loc), grad_mlp
+    qkv_cols = w_qkv.shape[1]
+    joint_group = net.group_gather(grad_joint_low)
+    if tiled:
+        piece = q_rows * (qkv_cols + D) // chips // D
+        terms_small = call(
+            lambda *refs: small_grad_kernel(chips, q_rows, *refs),
+            [jax.ShapeDtypeStruct((chips, piece, D), bf16)],
+            [spots, normed_one_group, joint_group, attended_group, grad_attn_group],
+            smem=1,
+            scratch=[pltpu.VMEM((D, qkv_cols + D), f32)],
+            flops=4 * chip_rows * D * (qkv_cols + D),
+        )[0]
+        sum_small = net.ring_scatter([terms_small[s] for s in range(chips)]).astype(bf16)
+        rest_block = jnp.concatenate([sum_small, sum_down], 0)
+        (grad_gate, grad_up), (grad_down, grad_small) = net.gather_both(
+            sum_mlp,
+            rest_block,
+            lambda slots, pairs, old: place_pairs(spots, slots, pairs, main, ff_loc, old),
+            lambda slots, pairs, old: place_rest(
+                spots, slots, pairs, down_rows, q_rows, ff_loc, qkv_cols + D, chips, old
+            ),
         )
     else:
+        q_first = net.d * (2 * q_rows) + core * q_rows
+        group_rows = 2 * net.dp * rows
+        part_out = jnp.einsum(
+            "tc,td->cd",
+            lax.dynamic_slice(attended_group, (0, q_first), (group_rows, q_rows)),
+            grad_attn_group,
+            preferred_element_type=f32,
+        )
+        part_joint = jnp.einsum(
+            "td,tc->dc",
+            lax.dynamic_slice(normed_one_group, (0, q_first), (group_rows, q_rows)),
+            joint_group,
+            preferred_element_type=f32,
+        )
+        part_small = jnp.concatenate([part_joint, part_out], 1).astype(bf16)
+        small_cols = part_small.shape[1] // chips
+
+        def small_chunk(slot):
+            return lax.dynamic_slice(part_small, (0, net.owner(slot) * small_cols), (q_rows, small_cols))
+
+        sum_small = net.ring_scatter([small_chunk(s) for s in range(chips)]).astype(bf16)
+
+        tall = jnp.concatenate(
+            [sum_small[:, i * 128 : (i + 1) * 128] for i in range(small_cols // 128)], 0
+        )
+        piece = tall.shape[0] // (D // 128)
+        wide = jnp.concatenate([tall[i * piece : (i + 1) * piece] for i in range(D // 128)], 1)
+        both = lax.optimization_barrier(jnp.concatenate([sum_down, wide], 0))
+
+        owners = [net.owner(s) for s in range(chips)]
+        got_mlp = net.ring_gather(sum_mlp)
+        got_both = net.ring_gather(both)
+        pairs_mlp = [(got, net.swap(got)) for got in got_mlp]
+        pairs_both = [(got, net.swap(got)) for got in got_both]
+
+        down_blocks, down_spots, small_blocks, small_spots = [], [], [], []
+        for owner, pair in zip(owners, pairs_both):
+            for which, got in zip((core, 1 - core), pair):
+                down_blocks.append(got[:down_rows])
+                down_spots.append((which * chips + owner, jnp.int32(0)))
+                wide = got[down_rows:]
+                tall = jnp.concatenate([wide[:, i * 128 : (i + 1) * 128] for i in range(D // 128)], 0)
+                small_blocks.append(
+                    jnp.concatenate(
+                        [tall[i * q_rows : (i + 1) * q_rows] for i in range(small_cols // 128)], 1
+                    )
+                )
+                small_spots.append((which, owner))
+        grad_down = place_blocks(down_blocks, down_spots, (ff_loc, D))
+        grad_small = place_blocks(small_blocks, small_spots, (2 * q_rows, part_small.shape[1]))
         grad_gate = jnp.zeros((D, ff_loc), f32)
         grad_up = jnp.zeros((D, ff_loc), f32)
         left_lane = jnp.arange(2 * rest) < rest
@@ -754,7 +1063,6 @@
             )
 
     small = net.total(jnp.concatenate([grad_gain_one, grad_gain_two, grad_bias], 1))[0]
-    qkv_cols = w_qkv.shape[1]
     return (
         output[None],
         grad_input[None],

time: 390 us -> 409 us (1.049)
  waiting for transfers between devices: 127 us -> 170 us
  Pallas kernels: 70.1 us -> 109 us
  matrix products: 18.1 us -> 0 us
  other arithmetic: 40.8 us -> 23.3 us
  local copies, waits for them, and re-layouts: 41.3 us -> 30.4 us
  starting transfers between devices: 77.1 us -> 69.2 us
  between operations: 9.03 us -> 2.1 us
    pallas_call x4 -> x12, Pallas kernels: 32.5 us -> 70.3 us  [the longest x5 20.5 us: place_pairs(): pl.pallas_call(kernel, out_shape=[jax.ShapeDtypeStruct((D, ff_loc), f32)]...]
    ppermute x56 -> x48, waiting for transfers between devices: 99.4 us -> 126 us  [hop(): return lax.ppermute(x, 'ctx', perm)]
    dot_general x10 -> x0, matrix products: 18.1 us -> none  [the longest x1 3.88 us: local(): jnp.einsum('td,fd->tf', grad_out_group, wd, preferred_element_type=f32)]
    ppermute x3, waiting for transfers between devices: 1.37 us -> 18.6 us  [total(): x = x + lax.ppermute(x, 'ctx', [(i, i ^ 2 * bit) for i in range(self.ctx)])]
    slice x39 -> x8, local copies, waits for them, and re-layouts: 14.2 us -> 1.59 us  [the longest x1 1.42 us: local(): grad_attn_group = gathered[:, 1].reshape(2 * net.dp * rows, D)]
    another operation x19 -> x0, other arithmetic: 10.5 us -> none  [the longest x18 9.88 us: place_blocks(): jnp.stack([jnp.stack(s) for s in spots]).astype(jnp.int32)]
    ppermute x56 -> x48, starting transfers between devices: 59.6 us -> 49.4 us  [hop(): return lax.ppermute(x, 'ctx', perm)]
    concatenate x11 -> x1, other arithmetic: 6.19 us -> 0.04 us  [local(): rest_block = jnp.concatenate([sum_small, sum_down], 0)]
  transfers between devices with their start and end apart: 93 -> 85, of which waited for: 34 -> 42; matrix products, arithmetic and copies ran while one was open for 20% -> 11% of each run, Pallas kernels for 13% -> 21%
where the time goes in v3:
time: 409 us; the launch traced here: 403 us
  waiting for transfers between devices  170 us (42%)
  Pallas kernels  109 us (27%)
  starting transfers between devices  69.2 us (17%)
  local copies, waits for them, and re-layouts  30.4 us (7%)
  other arithmetic  23.3 us (6%)
    ppermute x48, waiting for transfers between devices, hop(): return lax.ppermute(x, 'ctx', perm)  126 us
    ppermute x48, starting transfers between devices, hop(): return lax.ppermute(x, 'ctx', perm)  49.4 us
    pallas_call x5, Pallas kernels, call(): pl.pallas_call(kernel, out_shape=list(outs), in_specs=specs, out_specs=[p...  38.4 us
    pallas_call x5, Pallas kernels, place_pairs(): pl.pallas_call(kernel, out_shape=[jax.ShapeDtypeStruct((D, ff_loc), f32)]...  20.5 us
    ppermute x7, waiting for transfers between devices, shift(): return lax.ppermute(x, 'dp', [(i, (i + step) % n) for i in range(n)])  19.9 us
    pallas_call x5, Pallas kernels, place_rest(): pl.pallas_call(kernel, out_shape=[jax.ShapeDtypeStruct((ff_loc, D), f32),...  19 us
    pallas_call x1, Pallas kernels, feed_forward(): pl.pallas_call(lambda *refs: mlp_kernel(half, *refs), out_shape=[hidden]...  19 us
    ppermute x3, waiting for transfers between devices, total(): x = x + lax.ppermute(x, 'ctx', [(i, i ^ 2 * bit) for i in range(self.ctx)])  18.6 us
  transfers between devices with their start and end apart: 85, of which 42 were waited for; matrix products, arithmetic and copies ran while one was open for 11% of the time, Pallas kernels for 21%

profile of v3, /device:TPU:0, one launch (start us, length us, event | category | flops | bytes accessed | tf_op | source)
XLA Modules:
  0.0 403.3 jit_solution(18043224489761683612)
XLA Ops:
  11.9 4.7 %collective-permute-done = bf16[224,1152]{1,0:T(8,128)(2,1)S(1)} collective-permute-done((bf16[224,1152]{1,0:T(8,128)(2,1)S(1)}, bf16[224,1152]{1,0:T(8,128)(2,1)S(1)}, u32[]{:S(2)}, u32[]{:S(2)}) %collective-permute-start) | collective-permute-done | bytes 516128 | tf_op jit(solution)/shard_map/ppermute | solution.py:54
  51.8 10.3 %shard_map.196 = (bf16[128,896]{1,0:T(8,128)(2,1)}, f32[2,896,128]{2,1,0:T(8,128)}, f32[2,2,8,448]{3,2,1,0:T(8,128)}, bf16[2,896,128]{2,1,0:T(8,128)(2,1)}, bf16...) custom-call(s32[17]{0:T(128)} %pad_add_fusion.refs_0_, ...), custom_call_target="tpu_custom_call" | custom-call | flops 1879048192 | bytes 6516292 | tf_op jit(solution)/shard_map/pallas_call | solution.py:179
  73.9 19.0 %shard_map.197 = (bf16[512,1280]{1,0:T(8,128)(2,1)}, bf16[512,1280]{1,0:T(8,128)(2,1)}, bf16[512,1280]{1,0:T(8,128)(2,1)}, f32[256,896]{1,0:T(8,128)}, f32[256,896]{1,0:T(8,128)}, /*index=5*/bf16[512,896]{1,0:T(8,128)(2,1)}) custom-call(s32[20]{0:T(128)} %concatenate.102.refs_0_.meta_ref, bf16[512,896]{1,0:T(8,128)(2,1)} %copy-done.8, ...), custom_call_target="tpu_custom_call" | custom-call | flops 7046430720 | bytes 6881280 | tf_op jit(solution)/shard_map/pallas_call | solution.py:502
  93.2 11.8 %shard_map.201 = bf16[8,456,896]{2,1,0:T(8,128)(2,1)} custom-call(s32[20]{0:T(128)} %concatenate.102.refs_0_.meta_ref, bf16[512,896]{1,0:T(8,128)(2,1)} %copy-done.8, bf16[512,896]{1,0:T(8,128)(2,1)} %get-tuple-element.149.refs_2_, bf16[512,1280]{1,0:T(8,128)(2,1)} %get-tuple-element.96.refs_3_, bf16[512,1280]{1,0:T(8,128)(2,1)} %get-tuple-element.97.refs_4_, ...), custom_call_target="tpu_custom_call" | custom-call | flops 3523215360 | bytes 13074432 | tf_op jit(solution)/shard_map/pallas_call | solution.py:556
  113.8 15.5 %shard_map.198 = (f32[128,896]{1,0:T(8,128)}, bf16[128,896]{1,0:T(8,128)(2,1)}, f32[1,896]{1,0:T(1,128)}, f32[128,896]{1,0:T(8,128)}, f32[1024,256]{1,0:T(8,128)}, /*index=5*/bf16[1024,256]{1,0:T(8,128)(2,1)}) custom-call(s32[17]{0:T(128)} %pad_add_fusion.refs_0_, f32[128,896]{1,0:T(8,128)} %slice_add_fusion.refs_1_, f32[128,896]{1,0:T(8,128)} %get-tuple-element.76.refs_2_, ...), custom_call_target="tpu_custom_call" | custom-call | flops 4697620480 | bytes 7961668 | tf_op jit(solution)/shard_map/pallas_call | solution.py:179
  136.7 5.4 %collective-permute-done.21 = bf16[64,256]{1,0:T(8,128)(2,1)S(1)} collective-permute-done((bf16[64,256]{1,0:T(8,128)(2,1)S(1)}, bf16[64,256]{1,0:T(8,128)(2,1)S(1)}, u32[]{:S(2)}, u32[]{:S(2)}) %collective-permute-start.21) | collective-permute-done | bytes 32800 | tf_op jit(solution)/shard_map/ppermute | solution.py:62
  142.2 11.4 %collective-permute-done.25 = bf16[64,256]{1,0:T(8,128)(2,1)S(1)} collective-permute-done((bf16[64,256]{1,0:T(8,128)(2,1)S(1)}, bf16[64,256]{1,0:T(8,128)(2,1)S(1)}, u32[]{:S(2)}, u32[]{:S(2)}) %collective-permute-start.25) | collective-permute-done | bytes 32800 | tf_op jit(solution)/shard_map/ppermute | solution.py:62
  168.4 13.1 %collective-permute-done.24 = bf16[128,256]{1,0:T(8,128)(2,1)S(1)} collective-permute-done((bf16[128,256]{1,0:T(8,128)(2,1)S(1)}, bf16[128,256]{1,0:T(8,128)(2,1)S(1)}, u32[]{:S(2)}, u32[]{:S(2)}) %collective-permute-start.24) | collective-permute-done | bytes 65568 | tf_op jit(solution)/shard_map/ppermute | solution.py:62
  187.4 5.5 %collective-permute-done.29 = bf16[128,1152]{1,0:T(8,128)(2,1)S(1)} collective-permute-done((bf16[128,1152]{1,0:T(8,128)(2,1)}, bf16[128,1152]{1,0:T(8,128)(2,1)S(1)}, u32[]{:S(2)}, u32[]{:S(2)}) %collective-permute-start.29) | collective-permute-done | bytes 294944 | tf_op jit(solution)/shard_map/ppermute | solution.py:54
  202.8 5.6 %shard_map.200 = bf16[8,64,896]{2,1,0:T(8,128)(2,1)} custom-call(s32[20]{0:T(128)} %concatenate.102.refs_0_.meta_ref, bf16[512,896]{1,0:T(8,128)(2,1)} %get-tuple-element.148.refs_1_, bf16[512,1152]{1,0:T(8,128)(2,1)} %pad_maximum_fusion.4.refs_2_, bf16[512,896]{1,0:T(8,128)(2,1)} %bitcast.112, bf16[512,896]{1,0:T(8,128)(2,1)} %bitcast.111), custom_call_target="tpu_custom_call" | custom-call | flops 1879048192 | bytes 4849744 | tf_op jit(solution)/shard_map/pallas_call | solution.py:179
  211.4 6.8 %collective-permute-done.42 = bf16[456,896]{1,0:T(8,128)(2,1)} collective-permute-done((bf16[456,896]{1,0:T(8,128)(2,1)}, bf16[456,896]{1,0:T(8,128)(2,1)}, u32[]{:S(2)}, u32[]{:S(2)}) %collective-permute-start.42) | collective-permute-done | bytes 817184 | tf_op jit(solution)/shard_map/ppermute | solution.py:62
  225.7 18.4 %collective-permute-done.37 = bf16[64,896]{1,0:T(8,128)(2,1)S(1)} collective-permute-done((bf16[64,896]{1,0:T(8,128)(2,1)S(1)}, bf16[64,896]{1,0:T(8,128)(2,1)S(1)}, u32[]{:S(2)}, u32[]{:S(2)}) %collective-permute-start.37) | collective-permute-done | bytes 114720 | tf_op jit(solution)/shard_map/ppermute | solution.py:62
  261.5 7.5 %collective-permute-done.69.refs_0_ = bf16[304,896]{1,0:T(8,128)(2,1)S(1)} collective-permute-done((bf16[304,896]{1,0:T(8,128)(2,1)S(1)}, bf16[304,896]{1,0:T(8,128)(2,1)S(1)}, u32[]{:S(2)}, u32[]{:S(2)}) %collective-permute-start.69) | collective-permute-done | bytes 544800 | tf_op jit(solution)/shard_map/ppermute | solution.py:62
  282.6 10.2 %collective-permute-done.65 = f32[1,2944]{1,0:T(1,128)S(1)} collective-permute-done((f32[1,2944]{1,0:T(1,128)S(1)}, f32[1,2944]{1,0:T(1,128)S(1)}, u32[]{:S(2)}, u32[]{:S(2)}) %collective-permute-start.65) | collective-permute-done | bytes 11808 | tf_op jit(solution)/shard_map/ppermute | solution.py:130
  296.7 4.7 %collective-permute-done.67 = f32[1,2944]{1,0:T(1,128)S(1)} collective-permute-done((f32[1,2944]{1,0:T(1,128)S(1)}, f32[1,2944]{1,0:T(1,128)S(1)}, u32[]{:S(2)}, u32[]{:S(2)}) %collective-permute-start.67) | collective-permute-done | bytes 11808 | tf_op jit(solution)/shard_map/ppermute | solution.py:130
  308.0 7.8 %collective-permute-done.51.refs_2_ = bf16[216,896]{1,0:T(8,128)(2,1)S(1)} collective-permute-done((bf16[216,896]{1,0:T(8,128)(2,1)S(1)}, bf16[216,896]{1,0:T(8,128)(2,1)S(1)}, u32[]{:S(2)}, u32[]{:S(2)}) %collective-permute-start.51) | collective-permute-done | bytes 387104 | tf_op jit(solution)/shard_map/ppermute | solution.py:62
  318.0 10.7 %collective-permute-done.52.refs_0_ = bf16[216,896]{1,0:T(8,128)(2,1)S(1)} collective-permute-done((bf16[216,896]{1,0:T(8,128)(2,1)S(1)}, bf16[216,896]{1,0:T(8,128)(2,1)S(1)}, u32[]{:S(2)}, u32[]{:S(2)}) %collective-permute-start.52) | collective-permute-done | bytes 387104 | tf_op jit(solution)/shard_map/ppermute | solution.py:62
  336.1 6.6 %collective-permute-done.54 = bf16[112,896]{1,0:T(8,128)(2,1)S(1)} collective-permute-done((bf16[112,896]{1,0:T(8,128)(2,1)S(1)}, bf16[112,896]{1,0:T(8,128)(2,1)S(1)}, u32[]{:S(2)}, u32[]{:S(2)}) %collective-permute-start.54) | collective-permute-done | bytes 200736 | tf_op jit(solution)/shard_map/ppermute | solution.py:62
  345.5 4.6 %collective-permute-done.55 = bf16[104,896]{1,0:T(8,128)(2,1)S(1)} collective-permute-done((bf16[104,896]{1,0:T(8,128)(2,1)S(1)}, bf16[104,896]{1,0:T(8,128)(2,1)S(1)}, u32[]{:S(2)}, u32[]{:S(2)}) %collective-permute-start.55) | collective-permute-done | bytes 186400 | tf_op jit(solution)/shard_map/ppermute | solution.py:62
  361.7 4.6 %shard_map.208 = (f32[896,2432]{1,0:T(8,128)}, f32[896,2432]{1,0:T(8,128)}, f32[8,128]{1,0:T(8,128)}) custom-call(s32[20]{0:T(128)} %concatenate.102.refs_0_.meta_ref, bf16[304,896]{1,0:T(8,128)(2,1)} %copy-done.21, bf16[304,896]{1,0:T(8,128)(2,1)} %copy-done.25, bf16[304,896]{1,0:T(8,128)(2,1)} %copy-done.22, ...), custom_call_target="tpu_custom_call", output_to_operand_aliasing={{0}: (5, {}), {1}: (6, {})} | custom-call | bytes 8716288 | tf_op jit(solution)/shard_map/pallas_call | solution.py:636
  370.6 4.3 %shard_map.204 = (f32[2432,896]{1,0:T(8,128)}, f32[448,2048]{1,0:T(8,128)}, f32[8,128]{1,0:T(8,128)}) custom-call(s32[20]{0:T(128)} %concatenate.102.refs_0_.meta_ref, bf16[216,896]{1,0:T(8,128)(2,1)} %copy-done.35, bf16[216,896]{1,0:T(8,128)(2,1)} %copy-done.38, bf16[216,896]{1,0:T(8,128)(2,1)} %copy-done.36, ...), custom_call_target="tpu_custom_call", output_to_operand_aliasing={{0}: (5, {}), {1}: (6, {})} | custom-call | bytes 4358144 | tf_op jit(solution)/shard_map/pallas_call | solution.py:692
  374.9 4.6 %shard_map.209 = (f32[896,2432]{1,0:T(8,128)}, f32[896,2432]{1,0:T(8,128)}, f32[8,128]{1,0:T(8,128)}) custom-call(s32[20]{0:T(128)} %concatenate.102.refs_0_.meta_ref, bf16[304,896]{1,0:T(8,128)(2,1)} %copy-done.23, bf16[304,896]{1,0:T(8,128)(2,1)} %copy-done.27, bf16[304,896]{1,0:T(8,128)(2,1)} %copy-done.24, ...), custom_call_target="tpu_custom_call", output_to_operand_aliasing={{0}: (5, {}), {1}: (6, {})} | custom-call | bytes 8716288 | tf_op jit(solution)/shard_map/pallas_call | solution.py:636
  380.3 4.3 %shard_map.205 = (f32[2432,896]{1,0:T(8,128)}, f32[448,2048]{1,0:T(8,128)}, f32[8,128]{1,0:T(8,128)}) custom-call(s32[20]{0:T(128)} %concatenate.102.refs_0_.meta_ref, bf16[216,896]{1,0:T(8,128)(2,1)} %copy-done.17, bf16[216,896]{1,0:T(8,128)(2,1)} %copy-done.40, bf16[216,896]{1,0:T(8,128)(2,1)} %copy-done.19, ...), custom_call_target="tpu_custom_call", output_to_operand_aliasing={{0}: (5, {}), {1}: (6, {})} | custom-call | bytes 4358144 | tf_op jit(solution)/shard_map/pallas_call | solution.py:692
  394.9 4.6 %shard_map.210 = (f32[896,2432]{1,0:T(8,128)}, f32[896,2432]{1,0:T(8,128)}, f32[8,128]{1,0:T(8,128)}) custom-call(s32[20]{0:T(128)} %concatenate.102.refs_0_.meta_ref, bf16[304,896]{1,0:T(8,128)(2,1)} %copy-done.9, bf16[304,896]{1,0:T(8,128)(2,1)} %copy-done.28, bf16[304,896]{1,0:T(8,128)(2,1)} %copy-done.10, ...), custom_call_target="tpu_custom_call", output_to_operand_aliasing={{0}: (5, {}), {1}: (6, {})} | custom-call | bytes 8716288 | tf_op jit(solution)/shard_map/pallas_call | solution.py:636
  (370 shorter events, 199.2 us)
Async XLA Ops:
  26.7 21.4 %collective-permute-start.15 = (bf16[128,1792]{1,0:T(8,128)(2,1)S(1)}, bf16[128,1792]{1,0:T(8,128)(2,1)S(1)}, u32[]{:S(2)}, u32[]{:S(2)}) collective-permute-start(bf16[128,1792]{1,0:T(8,128)(2,1)S(1)} %constant_dynamic-update-slice_fusion.12), channel_id=1, source_target_pairs={{0,16},{16,0},{1,17},{17,1},{2,18},{18,2},{3,19},{19,3},{4,20},{20... | collective-permute-start | bytes 1376264 | tf_op jit(solution)/shard_map/ppermute | solution.py:54
  48.2 22.8 %collective-permute-start.16 = (bf16[256,1792]{1,0:T(8,128)(2,1)S(1)}, bf16[256,1792]{1,0:T(8,128)(2,1)S(1)}, u32[]{:S(2)}, u32[]{:S(2)}) collective-permute-start(bf16[256,1792]{1,0:T(8,128)(2,1)S(1)} %pad_maximum_fusion.6), channel_id=1, source_target_pairs={{0,1},{1,0},{2,3},{3,2},{4,5},{5,4},{6,7},{7,6},{8,9},{9,8},{10,11... | collective-permute-start | bytes 2752520 | tf_op jit(solution)/shard_map/ppermute | solution.py:50
  108.9 22.3 %collective-permute-start.44 = (bf16[224,896]{1,0:T(8,128)(2,1)S(1)}, bf16[224,896]{1,0:T(8,128)(2,1)S(1)}, u32[]{:S(2)}, u32[]{:S(2)}) collective-permute-start(bf16[224,896]{1,0:T(8,128)(2,1)S(1)} %get-tuple-element.143), channel_id=1, source_target_pairs={{0,2},{1,3},{4,0},{5,1},{8,4},{9,5},{12,8},{13,9},{14,12},{15,13},... | collective-permute-start | bytes 1204232 | tf_op jit(solution)/shard_map/ppermute | solution.py:62
  129.4 26.2 %collective-permute-start.40 = (bf16[232,896]{1,0:T(8,128)(2,1)S(1)}, bf16[232,896]{1,0:T(8,128)(2,1)S(1)}, u32[]{:S(2)}, u32[]{:S(2)}) collective-permute-start(bf16[232,896]{1,0:T(8,128)(2,1)S(1)} %get-tuple-element.140), channel_id=1, source_target_pairs={{0,4},{1,5},{4,8},{5,9},{8,12},{9,13},{12,14},{13,15},{14,10},{15,... | collective-permute-start | bytes 1247240 | tf_op jit(solution)/shard_map/ppermute | solution.py:62
  132.3 61.6 %collective-permute-start.45 = (bf16[456,896]{1,0:T(8,128)(2,1)}, bf16[456,896]{1,0:T(8,128)(2,1)}, u32[]{:S(2)}, u32[]{:S(2)}) collective-permute-start(bf16[456,896]{1,0:T(8,128)(2,1)} %pad_maximum_fusion.9), channel_id=1, source_target_pairs={{0,2},{1,3},{4,0},{5,1},{8,4},{9,5},{12,8},{13,9},{14,12},{15,13},... | collective-permute-start | bytes 2451464 | tf_op jit(solution)/shard_map/ppermute | solution.py:62
  135.0 31.4 %collective-permute-start.19 = (bf16[384,896]{1,0:T(8,128)(2,1)S(1)}, bf16[384,896]{1,0:T(8,128)(2,1)S(1)}, u32[]{:S(2)}, u32[]{:S(2)}) collective-permute-start(bf16[384,896]{1,0:T(8,128)(2,1)S(1)} %pad_maximum_fusion.11), channel_id=1, source_target_pairs={{0,16},{16,0},{1,17},{17,1},{2,18},{18,2},{3,19},{19,3},{4,20},{20... | collective-permute-start | bytes 2064392 | tf_op jit(solution)/shard_map/ppermute | solution.py:54
  161.3 32.7 %collective-permute-start.41 = (bf16[456,896]{1,0:T(8,128)(2,1)}, bf16[456,896]{1,0:T(8,128)(2,1)}, u32[]{:S(2)}, u32[]{:S(2)}) collective-permute-start(bf16[456,896]{1,0:T(8,128)(2,1)} %pad_maximum_fusion.8), channel_id=1, source_target_pairs={{0,4},{1,5},{4,8},{5,9},{8,12},{9,13},{12,14},{13,15},{14,10},{15,... | collective-permute-start | bytes 2451464 | tf_op jit(solution)/shard_map/ppermute | solution.py:62
  168.4 30.6 %collective-permute-start.31 = (bf16[512,896]{1,0:T(8,128)(2,1)}, bf16[512,896]{1,0:T(8,128)(2,1)}, u32[]{:S(2)}, u32[]{:S(2)}) collective-permute-start(bf16[512,896]{1,0:T(8,128)(2,1)} %pad_maximum_fusion.7), channel_id=1, source_target_pairs={{0,1},{1,0},{2,3},{3,2},{4,5},{5,4},{6,7},{7,6},{8,9},{9,8},{10,11... | collective-permute-start | bytes 2752520 | tf_op jit(solution)/shard_map/ppermute | solution.py:50
  196.9 21.3 %collective-permute-start.42 = (bf16[456,896]{1,0:T(8,128)(2,1)}, bf16[456,896]{1,0:T(8,128)(2,1)}, u32[]{:S(2)}, u32[]{:S(2)}) collective-permute-start(bf16[456,896]{1,0:T(8,128)(2,1)} %get-tuple-element.138), channel_id=1, source_target_pairs={{0,4},{1,5},{4,8},{5,9},{8,12},{9,13},{12,14},{13,15},{14,10},{15,... | collective-permute-start | bytes 2451464 | tf_op jit(solution)/shard_map/ppermute | solution.py:62
  198.4 21.2 %collective-permute-start.46 = (bf16[456,896]{1,0:T(8,128)(2,1)}, bf16[456,896]{1,0:T(8,128)(2,1)}, u32[]{:S(2)}, u32[]{:S(2)}) collective-permute-start(bf16[456,896]{1,0:T(8,128)(2,1)} %get-tuple-element.139), channel_id=1, source_target_pairs={{0,2},{1,3},{4,0},{5,1},{8,4},{9,5},{12,8},{13,9},{14,12},{15,13},... | collective-permute-start | bytes 2451464 | tf_op jit(solution)/shard_map/ppermute | solution.py:62
  221.4 31.8 %collective-permute-start.43 = (bf16[456,896]{1,0:T(8,128)(2,1)S(1)}, bf16[456,896]{1,0:T(8,128)(2,1)S(1)}, u32[]{:S(2)}, u32[]{:S(2)}) collective-permute-start(bf16[456,896]{1,0:T(8,128)(2,1)S(1)} %get-tuple-element.136), channel_id=1, source_target_pairs={{0,4},{1,5},{4,8},{5,9},{8,12},{9,13},{12,14},{13,15},{14,10},{15,... | collective-permute-start | bytes 2451464 | tf_op jit(solution)/shard_map/ppermute | solution.py:62
  223.0 30.2 %collective-permute-start.47 = (bf16[456,896]{1,0:T(8,128)(2,1)S(1)}, bf16[456,896]{1,0:T(8,128)(2,1)S(1)}, u32[]{:S(2)}, u32[]{:S(2)}) collective-permute-start(bf16[456,896]{1,0:T(8,128)(2,1)S(1)} %get-tuple-element.137), channel_id=1, source_target_pairs={{0,2},{1,3},{4,0},{5,1},{8,4},{9,5},{12,8},{13,9},{14,12},{15,13},... | collective-permute-start | bytes 2451464 | tf_op jit(solution)/shard_map/ppermute | solution.py:62
  223.6 20.5 %collective-permute-start.37 = (bf16[64,896]{1,0:T(8,128)(2,1)S(1)}, bf16[64,896]{1,0:T(8,128)(2,1)S(1)}, u32[]{:S(2)}, u32[]{:S(2)}) collective-permute-start(bf16[64,896]{1,0:T(8,128)(2,1)S(1)} %pad_maximum_fusion.16), channel_id=1, source_target_pairs={{0,2},{1,3},{4,0},{5,1},{8,4},{9,5},{12,8},{13,9},{14,12},{15,13},... | collective-permute-start | bytes 344072 | tf_op jit(solution)/shard_map/ppermute | solution.py:62
  224.2 19.9 %collective-permute-start.33 = (bf16[64,896]{1,0:T(8,128)(2,1)S(1)}, bf16[64,896]{1,0:T(8,128)(2,1)S(1)}, u32[]{:S(2)}, u32[]{:S(2)}) collective-permute-start(bf16[64,896]{1,0:T(8,128)(2,1)S(1)} %pad_maximum_fusion.15), channel_id=1, source_target_pairs={{0,4},{1,5},{4,8},{5,9},{8,12},{9,13},{12,14},{13,15},{14,10},{15,... | collective-permute-start | bytes 344072 | tf_op jit(solution)/shard_map/ppermute | solution.py:62
  271.0 34.4 %collective-permute-start.71 = (bf16[304,896]{1,0:T(8,128)(2,1)S(1)}, bf16[304,896]{1,0:T(8,128)(2,1)S(1)}, u32[]{:S(2)}, u32[]{:S(2)}) collective-permute-start(bf16[304,896]{1,0:T(8,128)(2,1)S(1)} %collective-permute-done.69.refs_0_), channel_id=1, source_target_pairs={{0,4},{1,5},{4,8},{5,9},{8,12},{9,13},{12,14},{13,15},{14,10},{15,... | collective-permute-start | bytes 1634312 | tf_op jit(solution)/shard_map/ppermute | solution.py:62
  271.7 33.9 %collective-permute-start.72 = (bf16[304,896]{1,0:T(8,128)(2,1)S(1)}, bf16[304,896]{1,0:T(8,128)(2,1)S(1)}, u32[]{:S(2)}, u32[]{:S(2)}) collective-permute-start(bf16[304,896]{1,0:T(8,128)(2,1)S(1)} %collective-permute-done.70.refs_2_), channel_id=1, source_target_pairs={{0,2},{1,3},{4,0},{5,1},{8,4},{9,5},{12,8},{13,9},{14,12},{15,13},... | collective-permute-start | bytes 1634312 | tf_op jit(solution)/shard_map/ppermute | solution.py:62
  273.0 42.8 %collective-permute-start.84 = (bf16[304,896]{1,0:T(8,128)(2,1)S(1)}, bf16[304,896]{1,0:T(8,128)(2,1)S(1)}, u32[]{:S(2)}, u32[]{:S(2)}) collective-permute-start(bf16[304,896]{1,0:T(8,128)(2,1)S(1)} %slice.362.refs_0_), channel_id=1, source_target_pairs={{0,1},{1,0},{2,3},{3,2},{4,5},{5,4},{6,7},{7,6},{8,9},{9,8},{10,11... | collective-permute-start | bytes 1634312 | tf_op jit(solution)/shard_map/ppermute | solution.py:50
  279.3 26.7 %collective-permute-start.50 = (bf16[216,896]{1,0:T(8,128)(2,1)S(1)}, bf16[216,896]{1,0:T(8,128)(2,1)S(1)}, u32[]{:S(2)}, u32[]{:S(2)}) collective-permute-start(bf16[216,896]{1,0:T(8,128)(2,1)S(1)} %collective-permute-done.48.refs_0_), channel_id=1, source_target_pairs={{0,4},{1,5},{4,8},{5,9},{8,12},{9,13},{12,14},{13,15},{14,10},{15,... | collective-permute-start | bytes 1161224 | tf_op jit(solution)/shard_map/ppermute | solution.py:62
  306.0 22.7 %collective-permute-start.73 = (bf16[304,896]{1,0:T(8,128)(2,1)S(1)}, bf16[304,896]{1,0:T(8,128)(2,1)S(1)}, u32[]{:S(2)}, u32[]{:S(2)}) collective-permute-start(bf16[304,896]{1,0:T(8,128)(2,1)S(1)} %collective-permute-done.71.refs_0_), channel_id=1, source_target_pairs={{0,4},{1,5},{4,8},{5,9},{8,12},{9,13},{12,14},{13,15},{14,10},{15,... | collective-permute-start | bytes 1634312 | tf_op jit(solution)/shard_map/ppermute | solution.py:62
  344.9 49.2 %collective-permute-start.78 = (bf16[304,896]{1,0:T(8,128)(2,1)S(1)}, bf16[304,896]{1,0:T(8,128)(2,1)S(1)}, u32[]{:S(2)}, u32[]{:S(2)}) collective-permute-start(bf16[304,896]{1,0:T(8,128)(2,1)S(1)} %collective-permute-done.73.refs_0_), channel_id=1, source_target_pairs={{0,1},{1,0},{2,3},{3,2},{4,5},{5,4},{6,7},{7,6},{8,9},{9,8},{10,11... | collective-permute-start | bytes 1634312 | tf_op jit(solution)/shard_map/ppermute | solution.py:50
  345.0 49.1 %collective-permute-start.79 = (bf16[304,896]{1,0:T(8,128)(2,1)S(1)}, bf16[304,896]{1,0:T(8,128)(2,1)}, u32[]{:S(2)}, u32[]{:S(2)}) collective-permute-start(bf16[304,896]{1,0:T(8,128)(2,1)S(1)} %collective-permute-done.74.refs_2_), channel_id=1, source_target_pairs={{0,1},{1,0},{2,3},{3,2},{4,5},{5,4},{6,7},{7,6},{8,9},{9,8},{10,11... | collective-permute-start | bytes 1634312 | tf_op jit(solution)/shard_map/ppermute | solution.py:50
  350.1 49.5 %collective-permute-start.77 = (bf16[304,896]{1,0:T(8,128)(2,1)S(1)}, bf16[304,896]{1,0:T(8,128)(2,1)}, u32[]{:S(2)}, u32[]{:S(2)}) collective-permute-start(bf16[304,896]{1,0:T(8,128)(2,1)S(1)} %constant_dynamic-update-slice_fusion.19.refs_0_), channel_id=1, source_target_pairs={{0,1},{1,0},{2,3},{3,2},{4,5},{5,4},{6,7},{7,6},{8,9},{9,8},{10,11... | collective-permute-start | bytes 1634312 | tf_op jit(solution)/shard_map/ppermute | solution.py:50
  350.2 29.3 %collective-permute-start.58 = (bf16[216,896]{1,0:T(8,128)(2,1)S(1)}, bf16[216,896]{1,0:T(8,128)(2,1)S(1)}, u32[]{:S(2)}, u32[]{:S(2)}) collective-permute-start(bf16[216,896]{1,0:T(8,128)(2,1)S(1)} %collective-permute-done.53.refs_2_), channel_id=1, source_target_pairs={{0,1},{1,0},{2,3},{3,2},{4,5},{5,4},{6,7},{7,6},{8,9},{9,8},{10,11... | collective-permute-start | bytes 1161224 | tf_op jit(solution)/shard_map/ppermute | solution.py:50
  351.8 32.8 %collective-permute-start.56 = (bf16[216,896]{1,0:T(8,128)(2,1)S(1)}, bf16[216,896]{1,0:T(8,128)(2,1)S(1)}, u32[]{:S(2)}, u32[]{:S(2)}) collective-permute-start(bf16[216,896]{1,0:T(8,128)(2,1)S(1)} %constant_dynamic-update-slice_fusion.14.refs_0_), channel_id=1, source_target_pairs={{0,1},{1,0},{2,3},{3,2},{4,5},{5,4},{6,7},{7,6},{8,9},{9,8},{10,11... | collective-permute-start | bytes 1161224 | tf_op jit(solution)/shard_map/ppermute | solution.py:50
  (113 other events, 1766.2 us)

commit v4 on v3

--- a/solution.py
+++ b/solution.py
@@ -135,32 +135,45 @@
             bit *= 2
         return x
 
+    def send_gather(self, x):
+        return [x] + [self.hop(x, s) for s in range(1, self.chips)]
+
+    def send_scatter(self, local):
+        return [self.hop(local[s], -s) for s in range(1, self.chips)]
+
+    def ring_sum(self, head, tail, terms, split):
+        n = self.chips
+        half = n // 2
+        fwd, back = self.hop(head, 1), self.hop(tail, -1)
+        for s in range(1, half):
+            fwd = self.hop(ring_add(fwd, terms, half + s, 0), 1)
+            back = self.hop(ring_add(back, terms, half - s, 1), -1)
+        return ring_end(fwd, back, terms, split)
+
     def gather_both(self, a, b, place_a, place_b):
         n = self.chips
         half = n // 2
-        streams = [[a, a, a, place_a, None, None], [b, b, b, place_b, None, None]]
-        waiting = [([0], [x]) for x in (a, b)]
+        streams = [
+            [x, x, None, ([0], [(x, self.swap(x))]), place] for x, place in ((a, place_a), (b, place_b))
+        ]
         for s in range(1, half + 1):
-            for k, stream in enumerate(streams):
-                own, fwd, back, place, placed, token = stream
-                if token is not None:
-                    fwd, back, token = lax.optimization_barrier((fwd, back, token))
+            for stream in streams:
+                fwd, back, placed, waiting, place = stream
+                if s > 1:
+                    placed, fwd = place(*waiting, placed, fwd)
+                    pairs = [(fwd, self.swap(fwd)), (back, self.swap(back))]
+                    waiting = ([s - 1, n - s + 1], pairs)
                 if s < half:
                     fwd, back = self.hop(fwd, 1), self.hop(back, -1)
-                    arrived = ([s, n - s], [fwd, back])
                 else:
-                    cut = half_cut(own.shape[0])
-                    far = jnp.concatenate([self.hop(fwd[:cut], 1), self.hop(back[cut:], -1)], 0)
-                    arrived = ([half], [far])
-                slots, blocks = waiting[k]
-                out = place(slots, [(x, self.swap(x)) for x in blocks], placed)
-                waiting[k] = arrived
-                streams[k] = [own, fwd, back, place, out[:2], out[2]]
+                    cut = half_cut(fwd.shape[0])
+                    fwd, back = self.hop(fwd[:cut], 1), self.hop(back[cut:], -1)
+                stream[:4] = [fwd, back, placed, waiting]
         results = []
-        for k, stream in enumerate(streams):
-            slots, blocks = waiting[k]
-            out = stream[3](slots, [(x, self.swap(x)) for x in blocks], stream[4])
-            results.append(out[:2])
+        for fwd, back, placed, waiting, place in streams:
+            far = jnp.concatenate([fwd, back], 0)
+            placed, far = place(*waiting, placed, far)
+            results.append(place([half], [(far, self.swap(far))], placed, None)[0])
         return results
 
 
@@ -199,6 +212,78 @@
 
 def dot_tn(a, b):
     return lax.dot_general(a, b, (((0,), (0,)), ((), ())), preferred_element_type=f32)
+
+
+def ring_add(got, terms, slot, side):
+    rows, columns = terms.shape[1:]
+    some = got.shape[0]
+
+    def kernel(got_ref, term_ref, out_ref):
+        first = 0 if side == 0 else rows - some
+        out_ref[...] = term_ref[0]
+        here = slice(first, first + some)
+        total = got_ref[...].astype(f32) + term_ref[0, here, :].astype(f32)
+        out_ref[here, :] = total.astype(bf16)
+
+    return pl.pallas_call(
+        kernel,
+        out_shape=jax.ShapeDtypeStruct((rows, columns), bf16),
+        grid=(1,),
+        in_specs=[
+            pl.BlockSpec(got.shape, lambda i: (0, 0)),
+            pl.BlockSpec((1, rows, columns), lambda i: (slot, 0, 0)),
+        ],
+        out_specs=pl.BlockSpec((rows, columns), lambda i: (0, 0)),
+        compiler_params=pltpu.CompilerParams(vmem_limit_bytes=VMEM_BYTES),
+        cost_estimate=pl.CostEstimate(
+            flops=0, bytes_accessed=6 * rows * columns, transcendentals=0
+        ),
+    )(got, terms)
+
+
+def ring_end(fwd, back, terms, split):
+    rows, columns = terms.shape[1:]
+
+    def kernel(fwd_ref, back_ref, term_ref, first_ref, rest_ref):
+        for ref, here in ((first_ref, slice(0, split)), (rest_ref, slice(split, rows))):
+            total = fwd_ref[here, :].astype(f32) + back_ref[here, :].astype(f32)
+            ref[...] = (total + term_ref[0, here, :].astype(f32)).astype(bf16)
+
+    whole = pl.BlockSpec((rows, columns), lambda i: (0, 0))
+    return pl.pallas_call(
+        kernel,
+        out_shape=[
+            jax.ShapeDtypeStruct((split, columns), bf16),
+            jax.ShapeDtypeStruct((rows - split, columns), bf16),
+        ],
+        grid=(1,),
+        in_specs=[whole, whole, pl.BlockSpec((1, rows, columns), lambda i: (0, 0, 0))],
+        out_specs=[
+            pl.BlockSpec((split, columns), lambda i: (0, 0)),
+            pl.BlockSpec((rows - split, columns), lambda i: (0, 0)),
+        ],
+        compiler_params=pltpu.CompilerParams(vmem_limit_bytes=VMEM_BYTES),
+        cost_estimate=pl.CostEstimate(
+            flops=0, bytes_accessed=8 * rows * columns, transcendentals=0
+        ),
+    )(fwd, back, terms)
+
+
+def pair_kernel(mine_ref, got_ref, *out_refs):
+    rows = out_refs[0].shape[0]
+    for s, out_ref in enumerate(out_refs):
+        here = slice(s * rows, (s + 1) * rows)
+        out_ref[...] = (mine_ref[here, :] + got_ref[here, :].astype(f32)).astype(out_ref.dtype)
+
+
+def rest_kernel(*refs):
+    small = refs[0][...].astype(f32)
+    for ref in refs[1:-2]:
+        small = small + ref[...].astype(f32)
+    out_ref = refs[-1]
+    piece = small.shape[0]
+    out_ref[:piece, :] = small.astype(bf16)
+    out_ref[piece:, :] = refs[-2][...]
 
 
 def qkv_kernel(x_ref, gain_ref, w_ref, b_ref, cos_ref, sin_ref, norm_ref, q_ref, pair_ref):
@@ -410,19 +495,22 @@
 
 
 def finish_kernel(
-    gq_ref, pair_ref, x_ref, gain_ref, w_ref, cos_ref, sin_ref, gh_ref,
-    joint_ref, gx_ref, gain_grad_ref, bias_ref,
+    gq_ref, x_ref, gain_ref, w_ref, cos_ref, sin_ref, gh_ref, *refs
 ):
+    joint_ref, gx_ref, gain_grad_ref, bias_ref = refs[-4:]
+    pair = refs[0][...]
+    for ref in refs[1:-4]:
+        pair = pair + ref[...].astype(f32)
     cosine = cos_ref[...]
     sine = sin_ref[...]
     early = lanes(cosine.shape) % HD < HD // 2
     for i in range((WIDTH_Q + WIDTH_K) // 128):
         at = slice(i * 128, (i + 1) * 128)
-        grad = gq_ref[:, at] if i * 128 < WIDTH_Q else pair_ref[:, :WIDTH_K]
+        grad = gq_ref[:, at] if i * 128 < WIDTH_Q else pair[:, :WIDTH_K]
         scaled = grad * sine
         turned = jnp.where(early, pltpu.roll(scaled, 96, 1), -pltpu.roll(scaled, 32, 1))
         joint_ref[:, at] = (grad * cosine + turned).astype(bf16)
-    joint_ref[:, WIDTH_Q + WIDTH_K :] = pair_ref[:, WIDTH_K:].astype(bf16)
+    joint_ref[:, WIDTH_Q + WIDTH_K :] = pair[:, WIDTH_K:].astype(bf16)
     joint = joint_ref[...]
     bias_ref[...] = jnp.sum(joint.astype(f32), 0, keepdims=True)
     grad = dot_nt(joint, w_ref[...])
@@ -519,7 +607,8 @@
 
 
 def mlp_grad_kernel(
-    down_rows, main, meta_ref, x_ref, gy_ref, mid_ref, gg_ref, gu_ref, out_ref, mlp_acc, down_acc
+    down_rows, main, meta_ref, x_ref, gy_ref, mid_ref, gg_ref, gu_ref,
+    out_ref, head_ref, tail_ref, mlp_acc, down_acc,
 ):
     step = pl.program_id(0)
     core = meta_ref[1]
@@ -546,21 +635,35 @@
     first = pl.multiple_of(core * 64 + step * down_rows, 8)
     out_ref[0, columns * 16 :, :] = down_acc[pl.ds(first, down_rows), :].astype(bf16)
 
+    @pl.when(meta_ref[4 + step] == pl.num_programs(0) // 2)
+    def far():
+        head_ref[...] = out_ref[0, : head_ref.shape[0], :]
+        tail_ref[...] = out_ref[0, head_ref.shape[0] :, :]
+
 
 def mlp_gradients(meta, x, gy, mid, gg, gu, chips, down_rows, main):
     tokens = x.shape[0]
     columns = (2 * main + 128) // 128
     rows = columns * 16 + down_rows
+    cut = (rows // 2 + 15) // 16 * 16
     wide = pl.BlockSpec((tokens, D), lambda i, m: (0, 0))
     tall = pl.BlockSpec((tokens, mid.shape[1]), lambda i, m: (0, 0))
     return pl.pallas_call(
         lambda *refs: mlp_grad_kernel(down_rows, main, *refs),
-        out_shape=jax.ShapeDtypeStruct((chips, rows, D), bf16),
+        out_shape=[
+            jax.ShapeDtypeStruct((chips, rows, D), bf16),
+            jax.ShapeDtypeStruct((cut, D), bf16),
+            jax.ShapeDtypeStruct((rows - cut, D), bf16),
+        ],
         grid_spec=pltpu.PrefetchScalarGridSpec(
             num_scalar_prefetch=1,
             grid=(chips,),
             in_specs=[wide, wide, tall, tall, tall],
-            out_specs=pl.BlockSpec((1, rows, D), lambda i, m: (m[4 + i], 0, 0)),
+            out_specs=[
+                pl.BlockSpec((1, rows, D), lambda i, m: (m[4 + i], 0, 0)),
+                pl.BlockSpec((cut, D), lambda i, m: (0, 0)),
+                pl.BlockSpec((rows - cut, D), lambda i, m: (0, 0)),
+            ],
             scratch_shapes=[
                 pltpu.VMEM((D, columns * 128), f32),
                 pltpu.VMEM((mid.shape[1], D), f32),
@@ -574,36 +677,66 @@
     )(meta, x, gy, mid, gg, gu)
 
 
-def small_grad_kernel(chips, q_rows, meta_ref, norm_ref, joint_ref, att_ref, ga_ref, out_ref, acc):
+def small_grad_kernel(chips, q_rows, meta_ref, norm_ref, joint_ref, att_ref, ga_ref, *refs):
+    out_refs, acc = refs[:-1], refs[-1]
     cols = joint_ref.shape[1]
     acc[:, :cols] = dot_tn(norm_ref[...], joint_ref[...])
     acc[:, cols:] = dot_tn(att_ref[...], ga_ref[...])
-    first = (2 * meta_ref[0] + meta_ref[1]) * q_rows
-    rows = acc[pl.ds(pl.multiple_of(first, 16), q_rows), :]
-    count = acc.shape[1] // 128 // chips
-    lanes_out = D // 128
-    piece = q_rows * count // lanes_out
-    for owner in range(chips):
+    first = pl.multiple_of((2 * meta_ref[0] + meta_ref[1]) * q_rows, 16)
+    width = acc.shape[1] // chips
+    for out_ref, slot in zip(out_refs, range(chips)):
+        column = pl.multiple_of(meta_ref[12 + slot] * width, 128)
+        block = acc[pl.ds(first, q_rows), pl.ds(column, width)]
         tall = jnp.concatenate(
-            [rows[:, (owner * count + i) * 128 : (owner * count + i + 1) * 128] for i in range(count)],
-            0,
+            [block[:, i * 128 : (i + 1) * 128] for i in range(width // 128)], 0
         ).astype(bf16)
-        slot = meta_ref[4 + owner]
-        for i in range(lanes_out):
-            out_ref[slot, :, i * 128 : (i + 1) * 128] = tall[i * piece : (i + 1) * piece]
-
-
-def place_pairs(meta, slots, pairs, main, ff_loc, old=None):
-    count = len(pairs)
+        piece = out_ref.shape[0]
+        for i in range(D // 128):
+            out_ref[:, i * 128 : (i + 1) * 128] = tall[i * piece : (i + 1) * piece]
+
+
+def place_call(kernel, outs, meta, pairs, scratch, copies, old, through):
+    blocks = [x for pair in pairs for x in pair]
+    keep = [] if old is None else list(old)
+    outs = list(outs)
+    aliases = {1 + len(blocks) + i: i for i in range(len(keep))}
+    if through is not None:
+        aliases[1 + len(blocks) + len(keep)] = len(outs)
+        keep = keep + [through]
+        outs = outs + [jax.ShapeDtypeStruct(through.shape, through.dtype)]
+    count = len(blocks)
+    n_out = len(outs)
+    n_old = len(keep)
+
+    def body(meta_ref, *refs):
+        outs_at = count + n_old
+        kernel(meta_ref, refs[:count], refs[outs_at : outs_at + n_out], refs[outs_at + n_out :])
+
+    moved = 8 * sum(x.size for x in blocks)
+    result = pl.pallas_call(
+        body,
+        out_shape=outs,
+        in_specs=[pl.BlockSpec(memory_space=pltpu.SMEM)]
+        + [pl.BlockSpec(memory_space=pltpu.VMEM)] * count
+        + [pl.BlockSpec(memory_space=pl.ANY)] * n_old,
+        out_specs=[pl.BlockSpec(memory_space=pl.ANY)] * n_out,
+        scratch_shapes=list(scratch) + [pltpu.SemaphoreType.DMA((copies,))],
+        input_output_aliases=aliases,
+        compiler_params=pltpu.CompilerParams(vmem_limit_bytes=VMEM_BYTES),
+        cost_estimate=pl.CostEstimate(flops=0, bytes_accessed=moved, transcendentals=0),
+    )(meta, *blocks, *keep)
+    if through is None:
+        return list(result), None
+    return list(result[:-1]), result[-1]
+
+
+def place_pairs(meta, slots, pairs, main, ff_loc, old, through):
     mlp_rows = D // 8
     columns = pairs[0][0].shape[0] // 16
     tiles = main // 128
-    blocks = [x for pair in pairs for x in pair]
-
-    def kernel(meta_ref, *refs):
-        step = pl.program_id(0)
-        gate_ref, up_ref, token_ref = refs[-3:]
-        token_ref[...] = jnp.zeros(token_ref.shape, f32)
+
+    def kernel(meta_ref, refs, outs, scratch):
+        gate_buf, up_buf, sems = scratch
         core_zero = meta_ref[1] == 0
 
         def column(ref, j):
@@ -612,107 +745,112 @@
             ]
             return jnp.concatenate(parts, 0).astype(f32)
 
-        for k in range(count):
-
-            @pl.when(step == k)
-            def write(k=k):
-                for j in range(columns):
-                    got = column(refs[2 * k], j)
-                    other = column(refs[2 * k + 1], j)
-                    zero = jnp.where(core_zero, got, other)
-                    one = jnp.where(core_zero, other, got)
-                    if j < 2 * tiles:
-                        ref = gate_ref if j < tiles else up_ref
-                        at = (j % tiles) * 128
-                        ref[:, at : at + 128] = zero
-                        ref[:, at + main + 128 : at + main + 256] = one
-                    else:
-                        left = lanes(zero.shape) < 64
-                        gate_ref[:, main : main + 128] = jnp.where(left, zero, one)
-                        up_ref[:, main : main + 128] = pltpu.roll(jnp.where(left, one, zero), 64, 1)
-
-    keep = [] if old is None else list(old)
-    out_spec = pl.BlockSpec((mlp_rows, ff_loc), lambda i, m: (m[12 + pick(slots, i)], 0))
-    return pl.pallas_call(
+        copies = []
+        for k, slot in enumerate(slots):
+            for j in range(columns):
+                got = column(refs[2 * k], j)
+                other = column(refs[2 * k + 1], j)
+                zero = jnp.where(core_zero, got, other)
+                one = jnp.where(core_zero, other, got)
+                if j < 2 * tiles:
+                    buf = gate_buf if j < tiles else up_buf
+                    at = (j % tiles) * 128
+                    buf[k, :, at : at + 128] = zero
+                    buf[k, :, at + main + 128 : at + main + 256] = one
+                else:
+                    left = lanes(zero.shape) < 64
+                    gate_buf[k, :, main : main + 128] = jnp.where(left, zero, one)
+                    up_buf[k, :, main : main + 128] = pltpu.roll(jnp.where(left, one, zero), 64, 1)
+            here = pl.ds(pl.multiple_of(meta_ref[12 + slot] * mlp_rows, 8), mlp_rows)
+            for side, buf in enumerate((gate_buf, up_buf)):
+                copy = pltpu.make_async_copy(
+                    buf.at[k], outs[side].at[here, :], sems.at[2 * k + side]
+                )
+                copy.start()
+                copies.append(copy)
+        for copy in copies:
+            copy.wait()
+
+    count = len(slots)
+    return place_call(
         kernel,
-        out_shape=[jax.ShapeDtypeStruct((D, ff_loc), f32)] * 2
-        + [jax.ShapeDtypeStruct((8, 128), f32)],
-        grid_spec=pltpu.PrefetchScalarGridSpec(
-            num_scalar_prefetch=1,
-            grid=(count,),
-            in_specs=[pl.BlockSpec(blocks[0].shape, lambda i, m: (0, 0))] * (2 * count)
-            + [pl.BlockSpec(memory_space=pl.ANY)] * len(keep),
-            out_specs=[out_spec, out_spec, pl.BlockSpec((8, 128), lambda i, m: (0, 0))],
-        ),
-        input_output_aliases={} if old is None else {2 * count + 1: 0, 2 * count + 2: 1},
-        compiler_params=pltpu.CompilerParams(vmem_limit_bytes=VMEM_BYTES),
-        cost_estimate=pl.CostEstimate(
-            flops=0, bytes_accessed=count * mlp_rows * ff_loc * 16, transcendentals=0
-        ),
-    )(meta, *blocks, *keep)
-
-
-def pick(values, i):
-    out = values[0]
-    for k in range(1, len(values)):
-        out = jnp.where(i == k, values[k], out)
-    return out
-
-
-def place_rest(meta, slots, pairs, down_rows, q_rows, ff_loc, cols, chips, old=None):
-    count = len(pairs)
-    blocks = [x for pair in pairs for x in pair]
+        [jax.ShapeDtypeStruct((D, ff_loc), f32)] * 2,
+        meta,
+        pairs,
+        [pltpu.VMEM((count, mlp_rows, ff_loc), f32)] * 2,
+        2 * count,
+        old,
+        through,
+    )
+
+
+def place_rest(meta, slots, pairs, down_rows, q_rows, ff_loc, cols, chips, old, through):
     lanes_out = D // 128
-    piece = blocks[0].shape[0] - down_rows
-
-    def kernel(meta_ref, *refs):
-        step = pl.program_id(0)
-        down_ref, small_ref, token_ref = refs[-3:]
-        token_ref[...] = jnp.zeros(token_ref.shape, f32)
-        for k in range(2 * count):
-
-            @pl.when(step == k)
-            def write(k=k):
-                ref = refs[k]
-                down_ref[...] = ref[piece:, :].astype(f32)
-                tall = jnp.concatenate(
-                    [ref[:piece, i * 128 : (i + 1) * 128] for i in range(lanes_out)], 0
-                ).astype(f32)
-                for i in range(tall.shape[0] // q_rows):
-                    small_ref[:, i * 128 : (i + 1) * 128] = tall[i * q_rows : (i + 1) * q_rows]
-
-    keep = [] if old is None else list(old)
-
-    def side(i, m):
-        return jnp.where(i % 2 == 0, m[1], 1 - m[1])
-
-    def owner(i, m):
-        return m[12 + pick(slots, i // 2)]
-
-    return pl.pallas_call(
+    piece = pairs[0][0].shape[0] - down_rows
+    width = (cols + D) // chips
+
+    def kernel(meta_ref, refs, outs, scratch):
+        down_buf, small_buf, sems = scratch
+        down_ref, joint_ref, out_ref = outs[:3]
+        copies = []
+        for k in range(2 * len(slots)):
+            ref = refs[k]
+            core = meta_ref[1] if k % 2 == 0 else 1 - meta_ref[1]
+            owner = meta_ref[12 + slots[k // 2]]
+            down_buf[k] = ref[piece:, :].astype(f32)
+            here = pl.ds(pl.multiple_of((core * chips + owner) * down_rows, 8), down_rows)
+            copy = pltpu.make_async_copy(down_buf.at[k], down_ref.at[here, :], sems.at[each * k])
+            copy.start()
+            copies.append(copy)
+            tall = jnp.concatenate(
+                [ref[:piece, i * 128 : (i + 1) * 128] for i in range(lanes_out)], 0
+            ).astype(f32)
+            rows = pl.ds(pl.multiple_of(core * q_rows, 8), q_rows)
+            for i in range(width // 128):
+                small_buf[k, i] = tall[i * q_rows : (i + 1) * q_rows]
+                block = owner * (width // 128) + i
+
+                @pl.when(block < cols // 128)
+                def joint(k=k, i=i, rows=rows, block=block):
+                    at = pl.ds(pl.multiple_of(block * 128, 128), 128)
+                    pltpu.make_async_copy(
+                        small_buf.at[k, i], joint_ref.at[rows, at], sems.at[each * k + 1 + i]
+                    ).start()
+
+                @pl.when(block >= cols // 128)
+                def out(k=k, i=i, rows=rows, block=block):
+                    at = pl.ds(pl.multiple_of((block - cols // 128) * 128, 128), 128)
+                    pltpu.make_async_copy(
+                        small_buf.at[k, i], out_ref.at[rows, at], sems.at[each * k + 1 + i]
+                    ).start()
+
+        for copy in copies:
+            copy.wait()
+        for k in range(2 * len(slots)):
+            for i in range(width // 128):
+                pltpu.make_async_copy(
+                    small_buf.at[k, i], out_ref.at[pl.ds(0, q_rows), pl.ds(0, 128)], sems.at[each * k + 1 + i]
+                ).wait()
+
+    count = 2 * len(slots)
+    each = 1 + width // 128
+    return place_call(
         kernel,
-        out_shape=[
+        [
             jax.ShapeDtypeStruct((ff_loc, D), f32),
             jax.ShapeDtypeStruct((2 * q_rows, cols), f32),
-            jax.ShapeDtypeStruct((8, 128), f32),
+            jax.ShapeDtypeStruct((2 * q_rows, D), f32),
         ],
-        grid_spec=pltpu.PrefetchScalarGridSpec(
-            num_scalar_prefetch=1,
-            grid=(2 * count,),
-            in_specs=[pl.BlockSpec(blocks[0].shape, lambda i, m: (0, 0))] * (2 * count)
-            + [pl.BlockSpec(memory_space=pl.ANY)] * len(keep),
-            out_specs=[
-                pl.BlockSpec((down_rows, D), lambda i, m: (side(i, m) * chips + owner(i, m), 0)),
-                pl.BlockSpec((q_rows, cols // chips), lambda i, m: (side(i, m), owner(i, m))),
-                pl.BlockSpec((8, 128), lambda i, m: (0, 0)),
-            ],
-        ),
-        input_output_aliases={} if old is None else {2 * count + 1: 0, 2 * count + 2: 1},
-        compiler_params=pltpu.CompilerParams(vmem_limit_bytes=VMEM_BYTES),
-        cost_estimate=pl.CostEstimate(
-            flops=0, bytes_accessed=count * down_rows * D * 16, transcendentals=0
-        ),
-    )(meta, *blocks, *keep)
+        meta,
+        pairs,
+        [
+            pltpu.VMEM((count, down_rows, D), f32),
+            pltpu.VMEM((count, width // 128, q_rows, 128), f32),
+        ],
+        each * count,
+        old,
+        through,
+    )
 
 
 def place_blocks(blocks, spots, out_shape, old=None):
@@ -796,7 +934,7 @@
         flops=2 * rows * D * 1152,
     )
 
-    slots = net.ring_gather(pairs)
+    slots = net.send_gather(pairs)
     mine = jnp.concatenate(slots, 0)
     other = net.swap(mine)
     order = jnp.array(net.order, jnp.int32)
@@ -872,12 +1010,10 @@
         grad_two = grad_two + net.shift(piece, net.dp - s).astype(f32)
 
     if tiled:
-        terms = mlp_gradients(
+        terms, head, tail = mlp_gradients(
             spots, normed_two_group, grad_out_group, mid, gate_low, up_low, chips, down_rows, main
         )
-        summed = net.ring_scatter([terms[s] for s in range(chips)]).astype(bf16)
-        sum_mlp = summed[: terms.shape[1] - down_rows]
-        sum_down = summed[terms.shape[1] - down_rows :]
+        sum_mlp, sum_down = net.ring_sum(head, tail, terms, terms.shape[1] - down_rows)
     else:
         part_down = jnp.einsum(
             "tf,td->fd", middle, grad_out_group, preferred_element_type=f32
@@ -937,10 +1073,13 @@
         ],
         flops=20 * KH * part_rows * total_keys * 128,
     )
-    pair_sums = (terms_mine + net.swap(terms_other).astype(f32)).astype(bf16)
-    grad_pairs = net.ring_scatter(
-        [pair_sums[s * rows : (s + 1) * rows] for s in range(chips)]
-    )
+    pair_sums = call(
+        pair_kernel,
+        [jax.ShapeDtypeStruct((rows, 2 * WIDTH_K), f32)]
+        + [jax.ShapeDtypeStruct((rows, 2 * WIDTH_K), bf16)] * (chips - 1),
+        [terms_mine, net.swap(terms_other)],
+    )
+    grad_pairs = [pair_sums[0]] + net.send_scatter(pair_sums)
     grad_joint_low, grad_input, grad_gain_one, grad_bias = call(
         finish_kernel,
         [
@@ -949,7 +1088,7 @@
             jax.ShapeDtypeStruct((1, D), f32),
             jax.ShapeDtypeStruct((1, 1152), f32),
         ],
-        [grad_queries, grad_pairs, x, gain_one, w_qkv_full, cosine, sine, grad_hidden],
+        [grad_queries, x, gain_one, w_qkv_full, cosine, sine, grad_hidden] + grad_pairs,
         flops=2 * rows * D * 1152,
     )
 
@@ -976,20 +1115,23 @@
         piece = q_rows * (qkv_cols + D) // chips // D
         terms_small = call(
             lambda *refs: small_grad_kernel(chips, q_rows, *refs),
-            [jax.ShapeDtypeStruct((chips, piece, D), bf16)],
+            [jax.ShapeDtypeStruct((piece, D), bf16)] * chips,
             [spots, normed_one_group, joint_group, attended_group, grad_attn_group],
             smem=1,
             scratch=[pltpu.VMEM((D, qkv_cols + D), f32)],
             flops=4 * chip_rows * D * (qkv_cols + D),
+        )
+        rest_block = call(
+            rest_kernel,
+            [jax.ShapeDtypeStruct((piece + down_rows, D), bf16)],
+            [terms_small[0]] + net.send_scatter(terms_small) + [sum_down],
         )[0]
-        sum_small = net.ring_scatter([terms_small[s] for s in range(chips)]).astype(bf16)
-        rest_block = jnp.concatenate([sum_small, sum_down], 0)
-        (grad_gate, grad_up), (grad_down, grad_small) = net.gather_both(
+        (grad_gate, grad_up), (grad_down, grad_joint, grad_out_proj) = net.gather_both(
             sum_mlp,
             rest_block,
-            lambda slots, pairs, old: place_pairs(spots, slots, pairs, main, ff_loc, old),
-            lambda slots, pairs, old: place_rest(
-                spots, slots, pairs, down_rows, q_rows, ff_loc, qkv_cols + D, chips, old
+            lambda *args: place_pairs(spots, *args[:2], main, ff_loc, *args[2:]),
+            lambda *args: place_rest(
+                spots, *args[:2], down_rows, q_rows, ff_loc, qkv_cols, chips, *args[2:]
             ),
         )
     else:
@@ -1062,13 +1204,15 @@
                 (base, 0),
             )
 
+        grad_joint, grad_out_proj = grad_small[:, :qkv_cols], grad_small[:, qkv_cols:]
+
     small = net.total(jnp.concatenate([grad_gain_one, grad_gain_two, grad_bias], 1))[0]
     return (
         output[None],
         grad_input[None],
-        grad_small[:, :qkv_cols],
+        grad_joint,
         small[2 * D :],
-        grad_small[:, qkv_cols:],
+        grad_out_proj,
         small[:D],
         small[D : 2 * D],
         grad_gate,

time: 409 us -> 378 us (0.924); the launches traced: 403 us -> 377 us
  waiting for transfers between devices: 170 us -> 119 us
  starting transfers between devices: 69.2 us -> 86.6 us
  Pallas kernels: 109 us -> 121 us
  other arithmetic: 23.3 us -> 15.1 us
    ppermute x48 -> x45, waiting for transfers between devices: 126 us -> 78.1 us  [hop(): return lax.ppermute(x, 'ctx', perm)]
    ppermute x48 -> x45, starting transfers between devices: 49.4 us -> 67.5 us  [hop(): return lax.ppermute(x, 'ctx', perm)]
    unnamed x119 -> x144, local copies, waits for them, and re-layouts: 8.17 us -> 17.3 us
    pallas_call x10 -> x17, Pallas kernels: 39.5 us -> 48.3 us  [the longest x10 31 us: place_call(): pl.pallas_call(body, out_shape=outs, in_specs=[pl.BlockSpec(memory_space=...]
    ppermute x3, waiting for transfers between devices: 18.6 us -> 11.2 us  [total(): x = x + lax.ppermute(x, 'ctx', [(i, i ^ 2 * bit) for i in range(self.ctx)])]
    slice x14 -> x4, local copies, waits for them, and re-layouts: 8.77 us -> 2.15 us  [gather_both(): fwd, back = (self.hop(fwd[:cut], 1), self.hop(back[cut:], -1))]
    convert_element_type x13 -> x0, other arithmetic: 5.74 us -> none  [the longest x10 5.25 us: add(): return (got.astype(f32) + mine.astype(f32)).astype(bf16)]
    ppermute x7, waiting for transfers between devices: 19.9 us -> 25 us  [shift(): return lax.ppermute(x, 'dp', [(i, (i + step) % n) for i in range(n)])]
  transfers between devices with their start and end apart: 85 -> 82, of which waited for: 42 -> 28; matrix products, arithmetic and copies ran while one was open for 11% -> 7% of each run, Pallas kernels for 21% -> 25%
where the time goes in v4:
time: 378 us; the launch traced here: 377 us
  Pallas kernels  121 us (32%)
  waiting for transfers between devices  119 us (31%)
  starting transfers between devices  86.6 us (23%)
  local copies, waits for them, and re-layouts  32.8 us (9%)
  other arithmetic  15.1 us (4%)
    ppermute x45, waiting for transfers between devices, hop(): return lax.ppermute(x, 'ctx', perm)  78.1 us
    ppermute x45, starting transfers between devices, hop(): return lax.ppermute(x, 'ctx', perm)  67.5 us
    pallas_call x7, Pallas kernels, call(): pl.pallas_call(kernel, out_shape=list(outs), in_specs=specs, out_specs=[p...  42 us
    pallas_call x10, Pallas kernels, place_call(): pl.pallas_call(body, out_shape=outs, in_specs=[pl.BlockSpec(memory_space=...  31 us
    ppermute x7, waiting for transfers between devices, shift(): return lax.ppermute(x, 'dp', [(i, (i + step) % n) for i in range(n)])  25 us
    pallas_call x1, Pallas kernels, feed_forward(): pl.pallas_call(lambda *refs: mlp_kernel(half, *refs), out_shape=[hidden]...  19.1 us
    unnamed x144, local copies, waits for them, and re-layouts  17.3 us
    pallas_call x6, Pallas kernels, ring_add(): pl.pallas_call(kernel, out_shape=jax.ShapeDtypeStruct((rows, columns), bf...  14.6 us
  transfers between devices with their start and end apart: 82, of which 28 were waited for; matrix products, arithmetic and copies ran while one was open for 7% of the time, Pallas kernels for 25%

profile of v4, /device:TPU:0, one launch (start us, length us, event | category | flops | bytes accessed | tf_op | source)
XLA Modules:
  0.0 376.6 jit_solution(14301355072122151687)
XLA Ops:
  12.0 4.6 %collective-permute-done = bf16[224,1152]{1,0:T(8,128)(2,1)S(1)} collective-permute-done((bf16[224,1152]{1,0:T(8,128)(2,1)S(1)}, bf16[224,1152]{1,0:T(8,128)(2,1)S(1)}, u32[]{:S(2)}, u32[]{:S(2)}) %collective-permute-start) | collective-permute-done | bytes 516128 | tf_op jit(solution)/shard_map/ppermute | solution.py:54
  40.7 9.2 %collective-permute-done.10 = bf16[224,896]{1,0:T(8,128)(2,1)S(1)} collective-permute-done((bf16[224,896]{1,0:T(8,128)(2,1)S(1)}, bf16[224,896]{1,0:T(8,128)(2,1)S(1)}, u32[]{:S(2)}, u32[]{:S(2)}) %collective-permute-start.10) | collective-permute-done | bytes 401440 | tf_op jit(solution)/shard_map/ppermute | solution.py:54
  50.5 6.7 %collective-permute-done.14 = bf16[128,1792]{1,0:T(8,128)(2,1)S(1)} collective-permute-done((bf16[128,1792]{1,0:T(8,128)(2,1)S(1)}, bf16[128,1792]{1,0:T(8,128)(2,1)S(1)}, u32[]{:S(2)}, u32[]{:S(2)}) %collective-permute-start.14) | collective-permute-done | bytes 458784 | tf_op jit(solution)/shard_map/ppermute | solution.py:54
  59.8 10.3 %shard_map.196 = (bf16[128,896]{1,0:T(8,128)(2,1)}, f32[2,896,128]{2,1,0:T(8,128)}, f32[2,2,8,448]{3,2,1,0:T(8,128)}, bf16[2,896,128]{2,1,0:T(8,128)(2,1)}, bf16...) custom-call(s32[17]{0:T(128)} %pad_add_fusion.refs_0_, ...), custom_call_target="tpu_custom_call" | custom-call | flops 1879048192 | bytes 6516292 | tf_op jit(solution)/shard_map/pallas_call | solution.py:192
  73.9 4.5 %collective-permute-done.12 = bf16[128,896]{1,0:T(8,128)(2,1)S(1)} collective-permute-done((bf16[128,896]{1,0:T(8,128)(2,1)}, bf16[128,896]{1,0:T(8,128)(2,1)S(1)}, u32[]{:S(2)}, u32[]{:S(2)}) %collective-permute-start.12) | collective-permute-done | bytes 229408 | tf_op jit(solution)/shard_map/ppermute | solution.py:54
  82.2 19.1 %shard_map.197 = (bf16[512,1280]{1,0:T(8,128)(2,1)}, bf16[512,1280]{1,0:T(8,128)(2,1)}, bf16[512,1280]{1,0:T(8,128)(2,1)}, f32[256,896]{1,0:T(8,128)}, f32[256,896]{1,0:T(8,128)}, /*index=5*/bf16[512,896]{1,0:T(8,128)(2,1)}) custom-call(s32[20]{0:T(128)} %concatenate.81.refs_0_.meta_ref, bf16[512,896]{1,0:T(8,128)(2,1)} %copy-done.10, ...), custom_call_target="tpu_custom_call" | custom-call | flops 7046430720 | bytes 6881280 | tf_op jit(solution)/shard_map/pallas_call | solution.py:590
  107.3 12.0 %shard_map.202 = (bf16[8,456,896]{2,1,0:T(8,128)(2,1)}, bf16[240,896]{1,0:T(8,128)(2,1)}, bf16[216,896]{1,0:T(8,128)(2,1)}) custom-call(s32[20]{0:T(128)} %concatenate.81.refs_0_.meta_ref, bf16[512,896]{1,0:T(8,128)(2,1)} %copy-done.10, bf16[512,896]{1,0:T(8,128)(2,1)} %get-tuple-element.185.refs_2_, bf16[512,1280]{1,0:T(8,128)(2,1)} %get-tuple-element.134.refs_3_, ...), custom_call_target="tpu_custom_call" | custom-call | flops 3523215360 | bytes 13074432 | tf_op jit(solution)/shard_map/pallas_call | solution.py:651
  122.1 14.9 %shard_map.198 = (f32[128,896]{1,0:T(8,128)}, bf16[128,896]{1,0:T(8,128)(2,1)}, f32[1,896]{1,0:T(1,128)}, f32[128,896]{1,0:T(8,128)}, f32[1024,256]{1,0:T(8,128)}, /*index=5*/bf16[1024,256]{1,0:T(8,128)(2,1)}) custom-call(s32[17]{0:T(128)} %pad_add_fusion.refs_0_, f32[128,896]{1,0:T(8,128)} %slice_add_fusion.refs_1_, f32[128,896]{1,0:T(8,128)} %get-tuple-element.98.refs_2_, ...), custom_call_target="tpu_custom_call" | custom-call | flops 4697620480 | bytes 7961668 | tf_op jit(solution)/shard_map/pallas_call | solution.py:192
  150.8 13.3 %collective-permute-done.20.refs_1_ = bf16[128,256]{1,0:T(8,128)(2,1)S(1)} collective-permute-done((bf16[128,256]{1,0:T(8,128)(2,1)}, bf16[128,256]{1,0:T(8,128)(2,1)S(1)}, u32[]{:S(2)}, u32[]{:S(2)}) %collective-permute-start.20) | collective-permute-done | bytes 65568 | tf_op jit(solution)/shard_map/ppermute | solution.py:62
  183.2 3.8 %shard_map.200 = (bf16[128,1152]{1,0:T(8,128)(2,1)}, f32[128,896]{1,0:T(8,128)}, f32[1,896]{1,0:T(1,128)}, f32[1,1152]{1,0:T(1,128)}) custom-call(f32[128,896]{1,0:T(8,128)} %get-tuple-element.112.gq_ref, bf16[128,896]{1,0:T(8,128)(2,1)} %bitcast.24, f32[1,896]{1,0:T(1,128)} %broadcast_in_dim.22.gain_ref, bf16[896,1152]{1,0:T(8,128)(2,1)} %pad_maximum_fusion.w_ref, ...), custom_call_target="tpu_custom_call" | custom-call | flops 264241152 | bytes 4697600 | tf_op jit(solution)/shard_map/pallas_call | solution.py:192
  197.1 9.1 %collective-permute-done.43.got_ref = bf16[456,896]{1,0:T(8,128)(2,1)S(1)} collective-permute-done((bf16[456,896]{1,0:T(8,128)(2,1)}, bf16[456,896]{1,0:T(8,128)(2,1)S(1)}, u32[]{:S(2)}, u32[]{:S(2)}) %collective-permute-start.43) | collective-permute-done | bytes 817184 | tf_op jit(solution)/shard_map/ppermute | solution.py:62
  218.8 5.2 %collective-permute-done.44.back_ref = bf16[456,896]{1,0:T(8,128)(2,1)S(1)} collective-permute-done((bf16[456,896]{1,0:T(8,128)(2,1)}, bf16[456,896]{1,0:T(8,128)(2,1)S(1)}, u32[]{:S(2)}, u32[]{:S(2)}) %collective-permute-start.44) | collective-permute-done | bytes 817184 | tf_op jit(solution)/shard_map/ppermute | solution.py:62
  224.0 4.6 %collective-permute-done.40.fwd_ref = bf16[456,896]{1,0:T(8,128)(2,1)S(1)} collective-permute-done((bf16[456,896]{1,0:T(8,128)(2,1)}, bf16[456,896]{1,0:T(8,128)(2,1)S(1)}, u32[]{:S(2)}, u32[]{:S(2)}) %collective-permute-start.40) | collective-permute-done | bytes 817184 | tf_op jit(solution)/shard_map/ppermute | solution.py:62
  232.7 5.4 %shard_map.201 = (bf16[64,896]{1,0:T(8,128)(2,1)}, bf16[64,896]{1,0:T(8,128)(2,1)}, bf16[64,896]{1,0:T(8,128)(2,1)}, bf16[64,896]{1,0:T(8,128)(2,1)}, bf16[64,89...) custom-call(s32[20]{0:T(128)} %concatenate.81.refs_0_.meta_ref, ...), custom_call_target="tpu_custom_call" | custom-call | flops 1879048192 | bytes 4849744 | tf_op jit(solution)/shard_map/pallas_call | solution.py:192
  244.5 4.6 %collective-permute-start.33 = (bf16[64,896]{1,0:T(8,128)(2,1)}, bf16[64,896]{1,0:T(8,128)(2,1)S(1)}, u32[]{:S(2)}, u32[]{:S(2)}) collective-permute-start(bf16[64,896]{1,0:T(8,128)(2,1)} %get-tuple-element.130), channel_id=1, source_target_pairs={{0,14},{1,15},{4,10},{5,11},{8,6},{9,7},{12,2},{13,3},{14,0},{15,1... | collective-permute-start | bytes 344072 | tf_op jit(solution)/shard_map/ppermute | solution.py:62
  249.1 6.7 %collective-permute-done.31.refs_2_ = bf16[64,896]{1,0:T(8,128)(2,1)S(1)} collective-permute-done((bf16[64,896]{1,0:T(8,128)(2,1)}, bf16[64,896]{1,0:T(8,128)(2,1)S(1)}, u32[]{:S(2)}, u32[]{:S(2)}) %collective-permute-start.31) | collective-permute-done | bytes 114720 | tf_op jit(solution)/shard_map/ppermute | solution.py:62
  262.1 3.8 collective-permute-done.34.refs_5_
  282.7 7.2 %collective-permute-done.63 = f32[1,2944]{1,0:T(1,128)S(1)} collective-permute-done((f32[1,2944]{1,0:T(1,128)S(1)}, f32[1,2944]{1,0:T(1,128)S(1)}, u32[]{:S(2)}, u32[]{:S(2)}) %collective-permute-start.63) | collective-permute-done | bytes 11808 | tf_op jit(solution)/shard_map/ppermute | solution.py:130
  296.8 5.7 %collective-permute-done.48.refs_2_ = bf16[216,896]{1,0:T(8,128)(2,1)S(1)} collective-permute-done((bf16[216,896]{1,0:T(8,128)(2,1)}, bf16[216,896]{1,0:T(8,128)(2,1)S(1)}, u32[]{:S(2)}, u32[]{:S(2)}) %collective-permute-start.48) | collective-permute-done | bytes 387104 | tf_op jit(solution)/shard_map/ppermute | solution.py:62
  308.1 3.8 %shard_map.217 = (f32[896,2432]{1,0:T(8,128)}, f32[896,2432]{1,0:T(8,128)}, bf16[304,896]{1,0:T(8,128)(2,1)}) custom-call(s32[20]{0:T(128)} %concatenate.81.refs_0_.meta_ref, bf16[304,896]{1,0:T(8,128)(2,1)} %get-tuple-element.163.refs_0_, bf16[304,896]{1,0:T(8,128)(2,1)} %copy-done.22, ...), custom_call_target="tpu_custom_call", output_to_operand_aliasing={{0}: (5, {}), {1}: (6, {}), {2}: (7, {})} | custom-call | bytes 8716288 | tf_op jit(solution)/shard_map/pallas_call | solution.py:716
  321.6 4.6 %collective-permute-done.52.refs_2_ = bf16[216,896]{1,0:T(8,128)(2,1)S(1)} collective-permute-done((bf16[216,896]{1,0:T(8,128)(2,1)S(1)}, bf16[216,896]{1,0:T(8,128)(2,1)S(1)}, u32[]{:S(2)}, u32[]{:S(2)}) %collective-permute-start.52) | collective-permute-done | bytes 387104 | tf_op jit(solution)/shard_map/ppermute | solution.py:62
  327.9 3.9 %collective-permute-done.75.refs_6_ = bf16[304,896]{1,0:T(8,128)(2,1)S(1)} collective-permute-done((bf16[304,896]{1,0:T(8,128)(2,1)}, bf16[304,896]{1,0:T(8,128)(2,1)S(1)}, u32[]{:S(2)}, u32[]{:S(2)}) %collective-permute-start.75) | collective-permute-done | bytes 544800 | tf_op jit(solution)/shard_map/ppermute | solution.py:62
  333.4 3.8 %shard_map.218 = (f32[896,2432]{1,0:T(8,128)}, f32[896,2432]{1,0:T(8,128)}, bf16[304,896]{1,0:T(8,128)(2,1)}) custom-call(s32[20]{0:T(128)} %concatenate.81.refs_0_.meta_ref, bf16[304,896]{1,0:T(8,128)(2,1)} %get-tuple-element.166.refs_0_, bf16[304,896]{1,0:T(8,128)(2,1)} %copy-done.24, ...), custom_call_target="tpu_custom_call", output_to_operand_aliasing={{0}: (5, {}), {1}: (6, {}), {2}: (7, {})} | custom-call | bytes 8716288 | tf_op jit(solution)/shard_map/pallas_call | solution.py:716
  358.4 3.8 %shard_map.219 = (f32[896,2432]{1,0:T(8,128)}, f32[896,2432]{1,0:T(8,128)}, bf16[304,896]{1,0:T(8,128)(2,1)}) custom-call(s32[20]{0:T(128)} %concatenate.81.refs_0_.meta_ref, bf16[304,896]{1,0:T(8,128)(2,1)} %get-tuple-element.169.refs_0_, bf16[304,896]{1,0:T(8,128)(2,1)} %copy-done.23, ...), custom_call_target="tpu_custom_call", output_to_operand_aliasing={{0}: (5, {}), {1}: (6, {}), {2}: (7, {})} | custom-call | bytes 8716288 | tf_op jit(solution)/shard_map/pallas_call | solution.py:716
  (366 shorter events, 204.1 us)
Async XLA Ops:
  34.1 15.8 %collective-permute-start.7 = (bf16[128,256]{1,0:T(8,128)(2,1)}, bf16[128,256]{1,0:T(8,128)(2,1)S(1)}, u32[]{:S(2)}, u32[]{:S(2)}) collective-permute-start(bf16[128,256]{1,0:T(8,128)(2,1)} %get-tuple-element.95), channel_id=1, source_target_pairs={{0,6},{1,7},{4,2},{5,3},{8,0},{9,1},{12,4},{13,5},{14,8},{15,9},{1... | collective-permute-start | bytes 196616 | tf_op jit(solution)/shard_map/ppermute | solution.py:62
  39.2 18.0 %collective-permute-start.14 = (bf16[128,1792]{1,0:T(8,128)(2,1)S(1)}, bf16[128,1792]{1,0:T(8,128)(2,1)S(1)}, u32[]{:S(2)}, u32[]{:S(2)}) collective-permute-start(bf16[128,1792]{1,0:T(8,128)(2,1)S(1)} %constant_dynamic-update-slice_fusion.11), channel_id=1, source_target_pairs={{0,16},{16,0},{1,17},{17,1},{2,18},{18,2},{3,19},{19,3},{4,20},{20... | collective-permute-start | bytes 1376264 | tf_op jit(solution)/shard_map/ppermute | solution.py:54
  57.2 22.2 %collective-permute-start.15 = (bf16[256,1792]{1,0:T(8,128)(2,1)S(1)}, bf16[256,1792]{1,0:T(8,128)(2,1)S(1)}, u32[]{:S(2)}, u32[]{:S(2)}) collective-permute-start(bf16[256,1792]{1,0:T(8,128)(2,1)S(1)} %pad_maximum_fusion.6), channel_id=1, source_target_pairs={{0,1},{1,0},{2,3},{3,2},{4,5},{5,4},{6,7},{7,6},{8,9},{9,8},{10,11... | collective-permute-start | bytes 2752520 | tf_op jit(solution)/shard_map/ppermute | solution.py:50
  105.7 15.6 %collective-permute-start.17 = (bf16[128,896]{1,0:T(8,128)(2,1)S(1)}, bf16[128,896]{1,0:T(8,128)(2,1)S(1)}, u32[]{:S(2)}, u32[]{:S(2)}) collective-permute-start(bf16[128,896]{1,0:T(8,128)(2,1)S(1)} %slice.125), channel_id=1, source_target_pairs={{0,16},{16,0},{1,17},{17,1},{2,18},{18,2},{3,19},{19,3},{4,20},{20... | collective-permute-start | bytes 688136 | tf_op jit(solution)/shard_map/ppermute | solution.py:54
  119.3 17.8 %collective-permute-start.41 = (bf16[216,896]{1,0:T(8,128)(2,1)}, bf16[216,896]{1,0:T(8,128)(2,1)S(1)}, u32[]{:S(2)}, u32[]{:S(2)}) collective-permute-start(bf16[216,896]{1,0:T(8,128)(2,1)} %get-tuple-element.139), channel_id=1, source_target_pairs={{0,2},{1,3},{4,0},{5,1},{8,4},{9,5},{12,8},{13,9},{14,12},{15,13},... | collective-permute-start | bytes 1161224 | tf_op jit(solution)/shard_map/ppermute | solution.py:62
  119.3 20.8 %collective-permute-start.37 = (bf16[240,896]{1,0:T(8,128)(2,1)}, bf16[240,896]{1,0:T(8,128)(2,1)S(1)}, u32[]{:S(2)}, u32[]{:S(2)}) collective-permute-start(bf16[240,896]{1,0:T(8,128)(2,1)} %get-tuple-element.137), channel_id=1, source_target_pairs={{0,4},{1,5},{4,8},{5,9},{8,12},{9,13},{12,14},{13,15},{14,10},{15,... | collective-permute-start | bytes 1290248 | tf_op jit(solution)/shard_map/ppermute | solution.py:62
  140.1 47.4 %collective-permute-start.42 = (bf16[456,896]{1,0:T(8,128)(2,1)}, bf16[456,896]{1,0:T(8,128)(2,1)S(1)}, u32[]{:S(2)}, u32[]{:S(2)}) collective-permute-start(bf16[456,896]{1,0:T(8,128)(2,1)} %shard_map.206), channel_id=1, source_target_pairs={{0,2},{1,3},{4,0},{5,1},{8,4},{9,5},{12,8},{13,9},{14,12},{15,13},... | collective-permute-start | bytes 2451464 | tf_op jit(solution)/shard_map/ppermute | solution.py:62
  143.2 47.7 %collective-permute-start.38 = (bf16[456,896]{1,0:T(8,128)(2,1)}, bf16[456,896]{1,0:T(8,128)(2,1)S(1)}, u32[]{:S(2)}, u32[]{:S(2)}) collective-permute-start(bf16[456,896]{1,0:T(8,128)(2,1)} %shard_map.203), channel_id=1, source_target_pairs={{0,4},{1,5},{4,8},{5,9},{8,12},{9,13},{12,14},{13,15},{14,10},{15,... | collective-permute-start | bytes 2451464 | tf_op jit(solution)/shard_map/ppermute | solution.py:62
  145.3 51.0 %collective-permute-start.18 = (bf16[384,896]{1,0:T(8,128)(2,1)S(1)}, bf16[384,896]{1,0:T(8,128)(2,1)S(1)}, u32[]{:S(2)}, u32[]{:S(2)}) collective-permute-start(bf16[384,896]{1,0:T(8,128)(2,1)S(1)} %pad_maximum_fusion.9), channel_id=1, source_target_pairs={{0,16},{16,0},{1,17},{17,1},{2,18},{18,2},{3,19},{19,3},{4,20},{20... | collective-permute-start | bytes 2064392 | tf_op jit(solution)/shard_map/ppermute | solution.py:54
  148.8 16.7 %collective-permute-start.21 = (bf16[128,256]{1,0:T(8,128)(2,1)}, bf16[128,256]{1,0:T(8,128)(2,1)S(1)}, u32[]{:S(2)}, u32[]{:S(2)}) collective-permute-start(bf16[128,256]{1,0:T(8,128)(2,1)} %get-tuple-element.118), channel_id=1, source_target_pairs={{0,6},{1,7},{4,2},{5,3},{8,0},{9,1},{12,4},{13,5},{14,8},{15,9},{1... | collective-permute-start | bytes 196616 | tf_op jit(solution)/shard_map/ppermute | solution.py:62
  194.3 15.6 %collective-permute-start.39 = (bf16[456,896]{1,0:T(8,128)(2,1)}, bf16[456,896]{1,0:T(8,128)(2,1)S(1)}, u32[]{:S(2)}, u32[]{:S(2)}) collective-permute-start(bf16[456,896]{1,0:T(8,128)(2,1)} %shard_map.204), channel_id=1, source_target_pairs={{0,4},{1,5},{4,8},{5,9},{8,12},{9,13},{12,14},{13,15},{14,10},{15,... | collective-permute-start | bytes 2451464 | tf_op jit(solution)/shard_map/ppermute | solution.py:62
  196.4 20.8 %collective-permute-start.29 = (bf16[512,896]{1,0:T(8,128)(2,1)S(1)}, bf16[512,896]{1,0:T(8,128)(2,1)S(1)}, u32[]{:S(2)}, u32[]{:S(2)}) collective-permute-start(bf16[512,896]{1,0:T(8,128)(2,1)S(1)} %pad_maximum_fusion.7), channel_id=1, source_target_pairs={{0,1},{1,0},{2,3},{3,2},{4,5},{5,4},{6,7},{7,6},{8,9},{9,8},{10,11... | collective-permute-start | bytes 2752520 | tf_op jit(solution)/shard_map/ppermute | solution.py:50
  196.6 18.4 %collective-permute-start.28 = (bf16[256,1152]{1,0:T(8,128)(2,1)S(1)}, bf16[256,1152]{1,0:T(8,128)(2,1)}, u32[]{:S(2)}, u32[]{:S(2)}) collective-permute-start(bf16[256,1152]{1,0:T(8,128)(2,1)S(1)} %pad_maximum_fusion.10), channel_id=1, source_target_pairs={{0,1},{1,0},{2,3},{3,2},{4,5},{5,4},{6,7},{7,6},{8,9},{9,8},{10,11... | collective-permute-start | bytes 1769480 | tf_op jit(solution)/shard_map/ppermute | solution.py:50
  232.2 39.9 %collective-permute-start.66 = (bf16[304,896]{1,0:T(8,128)(2,1)}, bf16[304,896]{1,0:T(8,128)(2,1)S(1)}, u32[]{:S(2)}, u32[]{:S(2)}) collective-permute-start(bf16[304,896]{1,0:T(8,128)(2,1)} %get-tuple-element.162.refs_0_), channel_id=1, source_target_pairs={{0,1},{1,0},{2,3},{3,2},{4,5},{5,4},{6,7},{7,6},{8,9},{9,8},{10,11... | collective-permute-start | bytes 1634312 | tf_op jit(solution)/shard_map/ppermute | solution.py:50
  232.2 40.0 %collective-permute-start.67 = (bf16[304,896]{1,0:T(8,128)(2,1)}, bf16[304,896]{1,0:T(8,128)(2,1)S(1)}, u32[]{:S(2)}, u32[]{:S(2)}) collective-permute-start(bf16[304,896]{1,0:T(8,128)(2,1)} %get-tuple-element.162.refs_0_), channel_id=1, source_target_pairs={{0,4},{1,5},{4,8},{5,9},{8,12},{9,13},{12,14},{13,15},{14,10},{15,... | collective-permute-start | bytes 1634312 | tf_op jit(solution)/shard_map/ppermute | solution.py:62
  239.7 16.1 %collective-permute-start.31 = (bf16[64,896]{1,0:T(8,128)(2,1)}, bf16[64,896]{1,0:T(8,128)(2,1)S(1)}, u32[]{:S(2)}, u32[]{:S(2)}) collective-permute-start(bf16[64,896]{1,0:T(8,128)(2,1)} %get-tuple-element.128), channel_id=1, source_target_pairs={{0,6},{1,7},{4,2},{5,3},{8,0},{9,1},{12,4},{13,5},{14,8},{15,9},{1... | collective-permute-start | bytes 344072 | tf_op jit(solution)/shard_map/ppermute | solution.py:62
  241.5 18.0 %collective-permute-start.32 = (bf16[64,896]{1,0:T(8,128)(2,1)}, bf16[64,896]{1,0:T(8,128)(2,1)S(1)}, u32[]{:S(2)}, u32[]{:S(2)}) collective-permute-start(bf16[64,896]{1,0:T(8,128)(2,1)} %get-tuple-element.129), channel_id=1, source_target_pairs={{0,10},{1,11},{4,6},{5,7},{8,2},{9,3},{12,0},{13,1},{14,4},{15,5},... | collective-permute-start | bytes 344072 | tf_op jit(solution)/shard_map/ppermute | solution.py:62
  265.9 26.6 %collective-permute-start.69 = (bf16[304,896]{1,0:T(8,128)(2,1)S(1)}, bf16[304,896]{1,0:T(8,128)(2,1)S(1)}, u32[]{:S(2)}, u32[]{:S(2)}) collective-permute-start(bf16[304,896]{1,0:T(8,128)(2,1)S(1)} %copy-done.29), channel_id=1, source_target_pairs={{0,2},{1,3},{4,0},{5,1},{8,4},{9,5},{12,8},{13,9},{14,12},{15,13},... | collective-permute-start | bytes 1634312 | tf_op jit(solution)/shard_map/ppermute | solution.py:62
  272.2 20.2 %collective-permute-start.45 = (bf16[216,896]{1,0:T(8,128)(2,1)}, bf16[216,896]{1,0:T(8,128)(2,1)S(1)}, u32[]{:S(2)}, u32[]{:S(2)}) collective-permute-start(bf16[216,896]{1,0:T(8,128)(2,1)} %shard_map.210.refs_0_), channel_id=1, source_target_pairs={{0,1},{1,0},{2,3},{3,2},{4,5},{5,4},{6,7},{7,6},{8,9},{9,8},{10,11... | collective-permute-start | bytes 1161224 | tf_op jit(solution)/shard_map/ppermute | solution.py:50
  276.6 25.9 %collective-permute-start.68 = (bf16[304,896]{1,0:T(8,128)(2,1)}, bf16[304,896]{1,0:T(8,128)(2,1)S(1)}, u32[]{:S(2)}, u32[]{:S(2)}) collective-permute-start(bf16[304,896]{1,0:T(8,128)(2,1)} %get-tuple-element.163.refs_0_), channel_id=1, source_target_pairs={{0,1},{1,0},{2,3},{3,2},{4,5},{5,4},{6,7},{7,6},{8,9},{9,8},{10,11... | collective-permute-start | bytes 1634312 | tf_op jit(solution)/shard_map/ppermute | solution.py:50
  292.5 24.0 %collective-permute-start.73 = (bf16[304,896]{1,0:T(8,128)(2,1)S(1)}, bf16[304,896]{1,0:T(8,128)(2,1)S(1)}, u32[]{:S(2)}, u32[]{:S(2)}) collective-permute-start(bf16[304,896]{1,0:T(8,128)(2,1)S(1)} %collective-permute-done.69.refs_2_), channel_id=1, source_target_pairs={{0,2},{1,3},{4,0},{5,1},{8,4},{9,5},{12,8},{13,9},{14,12},{15,13},... | collective-permute-start | bytes 1634312 | tf_op jit(solution)/shard_map/ppermute | solution.py:62
  316.7 22.6 %collective-permute-start.77 = (bf16[304,896]{1,0:T(8,128)(2,1)S(1)}, bf16[304,896]{1,0:T(8,128)(2,1)S(1)}, u32[]{:S(2)}, u32[]{:S(2)}) collective-permute-start(bf16[304,896]{1,0:T(8,128)(2,1)S(1)} %collective-permute-done.73.refs_2_), channel_id=1, source_target_pairs={{0,2},{1,3},{4,0},{5,1},{8,4},{9,5},{12,8},{13,9},{14,12},{15,13},... | collective-permute-start | bytes 1634312 | tf_op jit(solution)/shard_map/ppermute | solution.py:62
  337.3 17.4 %collective-permute-start.76 = (bf16[304,896]{1,0:T(8,128)(2,1)}, bf16[304,896]{1,0:T(8,128)(2,1)S(1)}, u32[]{:S(2)}, u32[]{:S(2)}) collective-permute-start(bf16[304,896]{1,0:T(8,128)(2,1)} %get-tuple-element.169.refs_0_), channel_id=1, source_target_pairs={{0,1},{1,0},{2,3},{3,2},{4,5},{5,4},{6,7},{7,6},{8,9},{9,8},{10,11... | collective-permute-start | bytes 1634312 | tf_op jit(solution)/shard_map/ppermute | solution.py:50
  339.3 18.4 %collective-permute-start.78 = (bf16[304,896]{1,0:T(8,128)(2,1)S(1)}, bf16[304,896]{1,0:T(8,128)(2,1)S(1)}, u32[]{:S(2)}, u32[]{:S(2)}) collective-permute-start(bf16[304,896]{1,0:T(8,128)(2,1)S(1)} %collective-permute-done.77.refs_2_), channel_id=1, source_target_pairs={{0,1},{1,0},{2,3},{3,2},{4,5},{5,4},{6,7},{7,6},{8,9},{9,8},{10,11... | collective-permute-start | bytes 1634312 | tf_op jit(solution)/shard_map/ppermute | solution.py:50
  (124 other events, 1045.6 us)

commit v5 on v4

--- a/solution.py
+++ b/solution.py
@@ -1,3 +1,5 @@
+import math
+
 import jax
 import jax.numpy as jnp
 from jax import lax
@@ -135,62 +137,81 @@
             bit *= 2
         return x
 
-    def send_gather(self, x):
-        return [x] + [self.hop(x, s) for s in range(1, self.chips)]
-
-    def send_scatter(self, local):
-        return [self.hop(local[s], -s) for s in range(1, self.chips)]
-
-    def ring_sum(self, head, tail, terms, split):
+    def ring_parts(self, local):
+        n = self.chips
+        half = n // 2
+        cut = half_cut(local[half].shape[0])
+
+        def add(got, mine):
+            return (got.astype(f32) + mine.astype(f32)).astype(bf16)
+
+        fwd, back = self.hop(local[half][:cut], 1), self.hop(local[half][cut:], -1)
+        for s in range(1, half):
+            mine_f, mine_b = local[half + s], local[half - s]
+            if s == 1:
+                mine_f = jnp.concatenate([add(fwd, mine_f[:cut]), mine_f[cut:]], 0)
+                mine_b = jnp.concatenate([mine_b[:cut], add(back, mine_b[cut:])], 0)
+            else:
+                mine_f, mine_b = add(fwd, mine_f), add(back, mine_b)
+            fwd, back = self.hop(mine_f, 1), self.hop(mine_b, -1)
+        return [local[0], fwd, back]
+
+    def ring_sum(self, head, tail, terms, split, middle):
         n = self.chips
         half = n // 2
         fwd, back = self.hop(head, 1), self.hop(tail, -1)
+        token = None
         for s in range(1, half):
-            fwd = self.hop(ring_add(fwd, terms, half + s, 0), 1)
-            back = self.hop(ring_add(back, terms, half - s, 1), -1)
+            after = token if s == half - 1 else None
+            fwd_sum = ring_add(fwd, terms, half + s, 0, after)
+            back_sum = ring_add(back, terms, half - s, 1, after)
+            if s == 1:
+                token = middle(fwd_sum, back_sum)
+            fwd, back = self.hop(fwd_sum, 1), self.hop(back_sum, -1)
         return ring_end(fwd, back, terms, split)
 
-    def gather_both(self, a, b, place_a, place_b):
+    def gather_placed(self, x, place):
         n = self.chips
         half = n // 2
-        streams = [
-            [x, x, None, ([0], [(x, self.swap(x))]), place] for x, place in ((a, place_a), (b, place_b))
-        ]
+        fwd = back = x
+        placed = None
+        waiting = ([0], [(x, self.swap(x))])
         for s in range(1, half + 1):
-            for stream in streams:
-                fwd, back, placed, waiting, place = stream
-                if s > 1:
-                    placed, fwd = place(*waiting, placed, fwd)
-                    pairs = [(fwd, self.swap(fwd)), (back, self.swap(back))]
-                    waiting = ([s - 1, n - s + 1], pairs)
-                if s < half:
-                    fwd, back = self.hop(fwd, 1), self.hop(back, -1)
-                else:
-                    cut = half_cut(fwd.shape[0])
-                    fwd, back = self.hop(fwd[:cut], 1), self.hop(back[cut:], -1)
-                stream[:4] = [fwd, back, placed, waiting]
-        results = []
-        for fwd, back, placed, waiting, place in streams:
-            far = jnp.concatenate([fwd, back], 0)
-            placed, far = place(*waiting, placed, far)
-            results.append(place([half], [(far, self.swap(far))], placed, None)[0])
-        return results
+            if s > 1:
+                placed, token = place(*waiting, placed)
+                fwd, back = gate(token, fwd, back)
+                waiting = ([s - 1, n - s + 1], [(fwd, self.swap(fwd)), (back, self.swap(back))])
+            if s < half:
+                fwd, back = self.hop(fwd, 1), self.hop(back, -1)
+            else:
+                cut = half_cut(fwd.shape[0])
+                fwd, back = self.hop(fwd[:cut], 1), self.hop(back[cut:], -1)
+        far = jnp.concatenate([fwd, back], 0)
+        placed, token = place(*waiting, placed)
+        return place([half], [(far, self.swap(far))], placed)[0]
 
 
 VMEM_BYTES = 56 * 1024 * 1024
 KEYS = 256
+RING_ROWS = 152
 
 
 def full_spec(shape):
     return pl.BlockSpec(shape, lambda: (0,) * len(shape))
 
 
-def call(kernel, outs, args, smem=0, scratch=(), flops=0):
+def call(kernel, outs, args, smem=0, scratch=(), flops=0, loose=0):
+    tight = len(args) - loose
     specs = [pl.BlockSpec(memory_space=pltpu.SMEM)] * smem
-    specs += [pl.BlockSpec(memory_space=pltpu.VMEM)] * (len(args) - smem)
+    specs += [pl.BlockSpec(memory_space=pltpu.VMEM)] * (tight - smem)
+    specs += [pl.BlockSpec(memory_space=pl.ANY)] * loose
+
+    def body(*refs):
+        kernel(*refs[:tight], *refs[tight + loose :])
+
     moved = sum(x.size * x.dtype.itemsize for x in list(args) + list(outs))
     return pl.pallas_call(
-        kernel,
+        body,
         out_shape=list(outs),
         in_specs=specs,
         out_specs=[pl.BlockSpec(memory_space=pltpu.VMEM)] * len(outs),
@@ -214,31 +235,59 @@
     return lax.dot_general(a, b, (((0,), (0,)), ((), ())), preferred_element_type=f32)
 
 
-def ring_add(got, terms, slot, side):
+def gate(token, *blocks):
+    count = len(blocks)
+    anywhere = pl.BlockSpec(memory_space=pl.ANY)
+
+    def kernel(*refs):
+        return None
+
+    return pl.pallas_call(
+        kernel,
+        out_shape=[jax.ShapeDtypeStruct(x.shape, x.dtype) for x in blocks],
+        in_specs=[anywhere] * (count + 1),
+        out_specs=[anywhere] * count,
+        input_output_aliases={i + 1: i for i in range(count)},
+        cost_estimate=pl.CostEstimate(flops=0, bytes_accessed=1024, transcendentals=0),
+    )(token, *blocks)
+
+
+def ring_add(got, terms, slot, side, after=None):
     rows, columns = terms.shape[1:]
     some = got.shape[0]
-
-    def kernel(got_ref, term_ref, out_ref):
-        first = 0 if side == 0 else rows - some
-        out_ref[...] = term_ref[0]
-        here = slice(first, first + some)
-        total = got_ref[...].astype(f32) + term_ref[0, here, :].astype(f32)
-        out_ref[here, :] = total.astype(bf16)
-
+    step = math.gcd(rows, RING_ROWS)
+    steps, here = rows // step, some // step
+    first = 0 if side == 0 else steps - here
+
+    def kernel(*refs):
+        got_ref, term_ref, out_ref = refs[0], refs[1], refs[-1]
+        i = pl.program_id(0)
+        inside = (i >= first) & (i < first + here)
+
+        @pl.when(inside)
+        def add():
+            out_ref[...] = (got_ref[...].astype(f32) + term_ref[0].astype(f32)).astype(bf16)
+
+        @pl.when(jnp.logical_not(inside))
+        def keep():
+            out_ref[...] = term_ref[0]
+
+    extra = [] if after is None else [after]
     return pl.pallas_call(
         kernel,
         out_shape=jax.ShapeDtypeStruct((rows, columns), bf16),
-        grid=(1,),
+        grid=(steps,),
         in_specs=[
-            pl.BlockSpec(got.shape, lambda i: (0, 0)),
-            pl.BlockSpec((1, rows, columns), lambda i: (slot, 0, 0)),
-        ],
-        out_specs=pl.BlockSpec((rows, columns), lambda i: (0, 0)),
+            pl.BlockSpec((step, columns), lambda i: (jnp.clip(i - first, 0, here - 1), 0)),
+            pl.BlockSpec((1, step, columns), lambda i: (slot, i, 0)),
+        ]
+        + [pl.BlockSpec(memory_space=pl.ANY)] * len(extra),
+        out_specs=pl.BlockSpec((step, columns), lambda i: (i, 0)),
         compiler_params=pltpu.CompilerParams(vmem_limit_bytes=VMEM_BYTES),
         cost_estimate=pl.CostEstimate(
             flops=0, bytes_accessed=6 * rows * columns, transcendentals=0
         ),
-    )(got, terms)
+    )(got, terms, *extra)
 
 
 def ring_end(fwd, back, terms, split):
@@ -276,14 +325,16 @@
         out_ref[...] = (mine_ref[here, :] + got_ref[here, :].astype(f32)).astype(out_ref.dtype)
 
 
-def rest_kernel(*refs):
+def block_kernel(mlp_ref, down_ref, *refs):
     small = refs[0][...].astype(f32)
-    for ref in refs[1:-2]:
+    for ref in refs[1:-1]:
         small = small + ref[...].astype(f32)
     out_ref = refs[-1]
+    top = mlp_ref.shape[0]
     piece = small.shape[0]
-    out_ref[:piece, :] = small.astype(bf16)
-    out_ref[piece:, :] = refs[-2][...]
+    out_ref[:top, :] = mlp_ref[...]
+    out_ref[top : top + piece, :] = small.astype(bf16)
+    out_ref[top + piece :, :] = down_ref[...]
 
 
 def qkv_kernel(x_ref, gain_ref, w_ref, b_ref, cos_ref, sin_ref, norm_ref, q_ref, pair_ref):
@@ -526,49 +577,51 @@
 
 def mlp_kernel(
     half_rows, spots_ref, x_ref, gy_ref, gate_a, gate_b, up_a, up_b, down_a, down_b,
-    mid_ref, gg_ref, gu_ref, gx_ref, out_ref, send_ref, gx_acc, out_acc,
+    xt_ref, midt_ref, gg_ref, gu_ref, gx_ref, out_ref, send_ref,
+    wg_all, wu_all, wd_all, mid_all, gg_all, gu_all,
 ):
     step = pl.program_id(0)
-    x = x_ref[...]
-    gy = gy_ref[...]
+    here = pl.ds(pl.multiple_of(step * 256, 256), 256)
     wg = jnp.concatenate([gate_a[...], gate_b[...]], 1)
     wu = jnp.concatenate([up_a[...], up_b[...]], 1)
     wd = jnp.concatenate([down_a[...], down_b[...]], 0)
-    gate = jnp.dot(x, wg, preferred_element_type=f32)
-    up = jnp.dot(x, wu, preferred_element_type=f32)
-    grad = dot_nt(gy, wd)
+    wg_all[:, here] = wg
+    wu_all[:, here] = wu
+    wd_all[here, :] = wd
     core = spots_ref[1]
-    column = lanes((1, gate.shape[1])) + (step * 256 + spots_ref[2])
+    column = lanes((1, 256)) + (step * 256 + spots_ref[2])
     own = (column < spots_ref[3]) == (core == 0)
-    sigma = jax.nn.sigmoid(gate)
-    active = gate * sigma
-    middle = jnp.where(own, active * up, 0.0).astype(bf16)
-    grad_gate = jnp.where(
-        own, grad * up * (sigma * (1.0 + gate * (1.0 - sigma))), 0.0
-    ).astype(bf16)
-    grad_up = jnp.where(own, grad * active, 0.0).astype(bf16)
-    mid_ref[...] = middle
-    gg_ref[...] = grad_gate
-    gu_ref[...] = grad_up
-    gx = dot_nt(grad_gate, wg) + dot_nt(grad_up, wu)
-    out = jnp.dot(middle, wd, preferred_element_type=f32)
+    tokens = x_ref.shape[0]
+    for r in range(0, tokens, 256):
+        rows = slice(r, r + 256)
+        x = x_ref[rows, :]
+        gate = jnp.dot(x, wg, preferred_element_type=f32)
+        up = jnp.dot(x, wu, preferred_element_type=f32)
+        grad = jnp.where(own, dot_nt(gy_ref[rows, :], wd), 0.0)
+        sigma = jax.nn.sigmoid(gate)
+        active = gate * sigma
+        middle = jnp.where(own, active * up, 0.0).astype(bf16)
+        grad_gate = (grad * up * (sigma + active * (1.0 - sigma))).astype(bf16)
+        grad_up = (grad * active).astype(bf16)
+        midt_ref[:, rows] = middle.T
+        gg_ref[rows, :] = grad_gate
+        gu_ref[rows, :] = grad_up
+        mid_all[rows, here] = middle
+        gg_all[rows, here] = grad_gate
+        gu_all[rows, here] = grad_up
 
     @pl.when(step == 0)
-    def start():
-        gx_acc[...] = gx
-        out_acc[...] = out
-
-    @pl.when(step > 0)
-    def add():
-        gx_acc[...] += gx
-        out_acc[...] += out
+    def transpose():
+        xt_ref[...] = x_ref[...].T
 
     @pl.when(step == pl.num_programs(0) - 1)
     def end():
-        gx_ref[...] = gx_acc[:half_rows]
-        out_ref[...] = out_acc[:half_rows]
-        send_ref[:half_rows] = gx_acc[half_rows:].astype(bf16)
-        send_ref[half_rows:] = out_acc[half_rows:].astype(bf16)
+        gx = dot_nt(gg_all[...], wg_all[...]) + dot_nt(gu_all[...], wu_all[...])
+        gx_ref[...] = gx[:half_rows]
+        send_ref[:half_rows] = gx[half_rows:].astype(bf16)
+        out = jnp.dot(mid_all[...], wd_all[...], preferred_element_type=f32)
+        out_ref[...] = out[:half_rows]
+        send_ref[half_rows:] = out[half_rows:].astype(bf16)
 
 
 def feed_forward(meta, x, gy, w_gate, w_up, w_down, width):
@@ -589,15 +642,31 @@
     hidden = jax.ShapeDtypeStruct((tokens, width), bf16)
     return pl.pallas_call(
         lambda *refs: mlp_kernel(half, *refs),
-        out_shape=[hidden] * 3
-        + [jax.ShapeDtypeStruct((half, D), f32)] * 2
-        + [jax.ShapeDtypeStruct((tokens, D), bf16)],
+        out_shape=[
+            jax.ShapeDtypeStruct((D, tokens), bf16),
+            jax.ShapeDtypeStruct((width, tokens), bf16),
+            hidden,
+            hidden,
+            jax.ShapeDtypeStruct((half, D), f32),
+            jax.ShapeDtypeStruct((half, D), f32),
+            jax.ShapeDtypeStruct((tokens, D), bf16),
+        ],
         grid_spec=pltpu.PrefetchScalarGridSpec(
             num_scalar_prefetch=1,
             grid=(steps,),
             in_specs=[whole, whole, columns(0), columns(1), columns(0), columns(1), rows(0), rows(1)],
-            out_specs=[tile, tile, tile, halves, halves, whole],
-            scratch_shapes=[pltpu.VMEM((tokens, D), f32)] * 2,
+            out_specs=[
+                pl.BlockSpec((D, tokens), lambda i, m: (0, 0)),
+                pl.BlockSpec((256, tokens), lambda i, m: (i, 0)),
+                tile,
+                tile,
+                halves,
+                halves,
+                whole,
+            ],
+            scratch_shapes=[pltpu.VMEM((D, width), bf16)] * 2
+            + [pltpu.VMEM((width, D), bf16)]
+            + [pltpu.VMEM((tokens, width), bf16)] * 3,
         ),
         compiler_params=pltpu.CompilerParams(vmem_limit_bytes=VMEM_BYTES),
         cost_estimate=pl.CostEstimate(
@@ -607,7 +676,7 @@
 
 
 def mlp_grad_kernel(
-    down_rows, main, meta_ref, x_ref, gy_ref, mid_ref, gg_ref, gu_ref,
+    down_rows, main, meta_ref, xt_ref, gy_ref, midt_ref, gg_ref, gu_ref,
     out_ref, head_ref, tail_ref, mlp_acc, down_acc,
 ):
     step = pl.program_id(0)
@@ -617,16 +686,22 @@
 
     @pl.when(step == 0)
     def products():
-        x = x_ref[...]
-        mlp_acc[:, :main] = dot_tn(x, gg_ref[:, at_main])
-        mlp_acc[:, main : 2 * main] = dot_tn(x, gu_ref[:, at_main])
+        xt = xt_ref[...]
+        mlp_acc[:, :main] = jnp.dot(
+            xt, gg_ref[:, at_main], preferred_element_type=f32
+        ).astype(bf16)
+        mlp_acc[:, main : 2 * main] = jnp.dot(
+            xt, gu_ref[:, at_main], preferred_element_type=f32
+        ).astype(bf16)
         mixed = gg_ref[:, at_tile].astype(f32) + pltpu.roll(gu_ref[:, at_tile].astype(f32), 64, 1)
-        mlp_acc[:, 2 * main :] = dot_tn(x, mixed.astype(bf16))
-        down_acc[...] = dot_tn(mid_ref[...], gy_ref[...])
+        mlp_acc[:, 2 * main :] = jnp.dot(
+            xt, mixed.astype(bf16), preferred_element_type=f32
+        ).astype(bf16)
+        down_acc[...] = jnp.dot(midt_ref[...], gy_ref[...], preferred_element_type=f32)
 
     mlp_rows = mlp_acc.shape[0] // pl.num_programs(0)
     columns = mlp_acc.shape[1] // 128
-    block = mlp_acc[pl.ds(pl.multiple_of(step * mlp_rows, 16), mlp_rows), :].astype(bf16)
+    block = mlp_acc[pl.ds(pl.multiple_of(step * mlp_rows, 16), mlp_rows), :]
     for j in range(columns):
         for i in range(mlp_rows // 16):
             out_ref[0, j * 16 : (j + 1) * 16, i * 128 : (i + 1) * 128] = block[
@@ -641,13 +716,15 @@
         tail_ref[...] = out_ref[0, head_ref.shape[0] :, :]
 
 
-def mlp_gradients(meta, x, gy, mid, gg, gu, chips, down_rows, main):
-    tokens = x.shape[0]
+def mlp_gradients(meta, xt, gy, midt, gg, gu, chips, down_rows, main):
+    tokens = gy.shape[0]
     columns = (2 * main + 128) // 128
-    rows = columns * 16 + down_rows
-    cut = (rows // 2 + 15) // 16 * 16
-    wide = pl.BlockSpec((tokens, D), lambda i, m: (0, 0))
-    tall = pl.BlockSpec((tokens, mid.shape[1]), lambda i, m: (0, 0))
+    cut = columns * 16
+    rows = cut + down_rows
+
+    def whole(x):
+        return pl.BlockSpec(x.shape, lambda i, m: (0, 0))
+
     return pl.pallas_call(
         lambda *refs: mlp_grad_kernel(down_rows, main, *refs),
         out_shape=[
@@ -658,23 +735,23 @@
         grid_spec=pltpu.PrefetchScalarGridSpec(
             num_scalar_prefetch=1,
             grid=(chips,),
-            in_specs=[wide, wide, tall, tall, tall],
+            in_specs=[whole(x) for x in (xt, gy, midt, gg, gu)],
             out_specs=[
                 pl.BlockSpec((1, rows, D), lambda i, m: (m[4 + i], 0, 0)),
                 pl.BlockSpec((cut, D), lambda i, m: (0, 0)),
                 pl.BlockSpec((rows - cut, D), lambda i, m: (0, 0)),
             ],
             scratch_shapes=[
-                pltpu.VMEM((D, columns * 128), f32),
-                pltpu.VMEM((mid.shape[1], D), f32),
+                pltpu.VMEM((D, columns * 128), bf16),
+                pltpu.VMEM((midt.shape[0], D), f32),
             ],
         ),
         compiler_params=pltpu.CompilerParams(vmem_limit_bytes=VMEM_BYTES),
         cost_estimate=pl.CostEstimate(
-            flops=6 * tokens * mid.shape[1] * D, bytes_accessed=4 * chips * rows * D,
+            flops=6 * tokens * midt.shape[0] * D, bytes_accessed=4 * chips * rows * D,
             transcendentals=0,
         ),
-    )(meta, x, gy, mid, gg, gu)
+    )(meta, xt, gy, midt, gg, gu)
 
 
 def small_grad_kernel(chips, q_rows, meta_ref, norm_ref, joint_ref, att_ref, ga_ref, *refs):
@@ -695,61 +772,43 @@
             out_ref[:, i * 128 : (i + 1) * 128] = tall[i * piece : (i + 1) * piece]
 
 
-def place_call(kernel, outs, meta, pairs, scratch, copies, old, through):
+def place_all(meta, slots, pairs, old, sizes):
+    main, ff_loc, q_rows, cols, down_rows, chips = sizes
+    mlp_rows = D // chips
+    columns = (2 * main + 128) // 128
+    tiles = main // 128
+    lanes_out = D // 128
+    top = columns * 16
     blocks = [x for pair in pairs for x in pair]
+    count = len(blocks)
+    piece = blocks[0].shape[0] - top - down_rows
+    parts = (cols + D) // chips // 128
     keep = [] if old is None else list(old)
-    outs = list(outs)
-    aliases = {1 + len(blocks) + i: i for i in range(len(keep))}
-    if through is not None:
-        aliases[1 + len(blocks) + len(keep)] = len(outs)
-        keep = keep + [through]
-        outs = outs + [jax.ShapeDtypeStruct(through.shape, through.dtype)]
-    count = len(blocks)
-    n_out = len(outs)
-    n_old = len(keep)
-
-    def body(meta_ref, *refs):
-        outs_at = count + n_old
-        kernel(meta_ref, refs[:count], refs[outs_at : outs_at + n_out], refs[outs_at + n_out :])
-
-    moved = 8 * sum(x.size for x in blocks)
-    result = pl.pallas_call(
-        body,
-        out_shape=outs,
-        in_specs=[pl.BlockSpec(memory_space=pltpu.SMEM)]
-        + [pl.BlockSpec(memory_space=pltpu.VMEM)] * count
-        + [pl.BlockSpec(memory_space=pl.ANY)] * n_old,
-        out_specs=[pl.BlockSpec(memory_space=pl.ANY)] * n_out,
-        scratch_shapes=list(scratch) + [pltpu.SemaphoreType.DMA((copies,))],
-        input_output_aliases=aliases,
-        compiler_params=pltpu.CompilerParams(vmem_limit_bytes=VMEM_BYTES),
-        cost_estimate=pl.CostEstimate(flops=0, bytes_accessed=moved, transcendentals=0),
-    )(meta, *blocks, *keep)
-    if through is None:
-        return list(result), None
-    return list(result[:-1]), result[-1]
-
-
-def place_pairs(meta, slots, pairs, main, ff_loc, old, through):
-    mlp_rows = D // 8
-    columns = pairs[0][0].shape[0] // 16
-    tiles = main // 128
-
-    def kernel(meta_ref, refs, outs, scratch):
-        gate_buf, up_buf, sems = scratch
+
+    def kernel(meta_ref, *refs):
+        ins = refs[:count]
+        gate_out, up_out, down_out, joint_out, proj_out, token_ref = refs[
+            count + len(keep) : count + len(keep) + 6
+        ]
+        gate_buf, up_buf, down_buf, small_buf, sems, small_sems = refs[count + len(keep) + 6 :]
         core_zero = meta_ref[1] == 0
+        copies = []
+
+        def send(src, dst, sem):
+            copy = pltpu.make_async_copy(src, dst, sem)
+            copy.start()
+            copies.append(copy)
 
         def column(ref, j):
-            parts = [
+            found = [
                 ref[j * 16 : (j + 1) * 16, i * 128 : (i + 1) * 128] for i in range(mlp_rows // 16)
             ]
-            return jnp.concatenate(parts, 0).astype(f32)
-
-        copies = []
+            return jnp.concatenate(found, 0).astype(f32)
+
         for k, slot in enumerate(slots):
             for j in range(columns):
-                got = column(refs[2 * k], j)
-                other = column(refs[2 * k + 1], j)
+                got = column(ins[2 * k], j)
+                other = column(ins[2 * k + 1], j)
                 zero = jnp.where(core_zero, got, other)
                 one = jnp.where(core_zero, other, got)
                 if j < 2 * tiles:
@@ -761,96 +820,79 @@
                     left = lanes(zero.shape) < 64
                     gate_buf[k, :, main : main + 128] = jnp.where(left, zero, one)
                     up_buf[k, :, main : main + 128] = pltpu.roll(jnp.where(left, one, zero), 64, 1)
-            here = pl.ds(pl.multiple_of(meta_ref[12 + slot] * mlp_rows, 8), mlp_rows)
-            for side, buf in enumerate((gate_buf, up_buf)):
-                copy = pltpu.make_async_copy(
-                    buf.at[k], outs[side].at[here, :], sems.at[2 * k + side]
-                )
-                copy.start()
-                copies.append(copy)
+            owner = meta_ref[12 + slot]
+            here = pl.ds(pl.multiple_of(owner * mlp_rows, 8), mlp_rows)
+            send(gate_buf.at[k], gate_out.at[here, :], sems.at[4 * k])
+            send(up_buf.at[k], up_out.at[here, :], sems.at[4 * k + 1])
+            for side in range(2):
+                b = 2 * k + side
+                core = meta_ref[1] if side == 0 else 1 - meta_ref[1]
+                down_buf[b] = ins[b][top + piece :, :].astype(f32)
+                here = pl.ds(pl.multiple_of((core * chips + owner) * down_rows, 8), down_rows)
+                send(down_buf.at[b], down_out.at[here, :], sems.at[4 * k + 2 + side])
+                tall = jnp.concatenate(
+                    [ins[b][top : top + piece, i * 128 : (i + 1) * 128] for i in range(lanes_out)], 0
+                ).astype(f32)
+                rows = pl.ds(pl.multiple_of(core * q_rows, 8), q_rows)
+                for i in range(parts):
+                    small_buf[b, i] = tall[i * q_rows : (i + 1) * q_rows]
+                    block = owner * parts + i
+
+                    @pl.when(block < cols // 128)
+                    def joint(b=b, i=i, rows=rows, block=block):
+                        at = pl.ds(pl.multiple_of(block * 128, 128), 128)
+                        pltpu.make_async_copy(
+                            small_buf.at[b, i], joint_out.at[rows, at], small_sems.at[b, i]
+                        ).start()
+
+                    @pl.when(block >= cols // 128)
+                    def proj(b=b, i=i, rows=rows, block=block):
+                        at = pl.ds(pl.multiple_of((block - cols // 128) * 128, 128), 128)
+                        pltpu.make_async_copy(
+                            small_buf.at[b, i], proj_out.at[rows, at], small_sems.at[b, i]
+                        ).start()
+
+        token_ref[...] = jnp.zeros(token_ref.shape, f32)
         for copy in copies:
             copy.wait()
-
-    count = len(slots)
-    return place_call(
+        for b in range(count):
+            for i in range(parts):
+                pltpu.make_async_copy(
+                    small_buf.at[b, i],
+                    proj_out.at[pl.ds(0, q_rows), pl.ds(0, 128)],
+                    small_sems.at[b, i],
+                ).wait()
+
+    anywhere = pl.BlockSpec(memory_space=pl.ANY)
+    result = pl.pallas_call(
         kernel,
-        [jax.ShapeDtypeStruct((D, ff_loc), f32)] * 2,
-        meta,
-        pairs,
-        [pltpu.VMEM((count, mlp_rows, ff_loc), f32)] * 2,
-        2 * count,
-        old,
-        through,
-    )
-
-
-def place_rest(meta, slots, pairs, down_rows, q_rows, ff_loc, cols, chips, old, through):
-    lanes_out = D // 128
-    piece = pairs[0][0].shape[0] - down_rows
-    width = (cols + D) // chips
-
-    def kernel(meta_ref, refs, outs, scratch):
-        down_buf, small_buf, sems = scratch
-        down_ref, joint_ref, out_ref = outs[:3]
-        copies = []
-        for k in range(2 * len(slots)):
-            ref = refs[k]
-            core = meta_ref[1] if k % 2 == 0 else 1 - meta_ref[1]
-            owner = meta_ref[12 + slots[k // 2]]
-            down_buf[k] = ref[piece:, :].astype(f32)
-            here = pl.ds(pl.multiple_of((core * chips + owner) * down_rows, 8), down_rows)
-            copy = pltpu.make_async_copy(down_buf.at[k], down_ref.at[here, :], sems.at[each * k])
-            copy.start()
-            copies.append(copy)
-            tall = jnp.concatenate(
-                [ref[:piece, i * 128 : (i + 1) * 128] for i in range(lanes_out)], 0
-            ).astype(f32)
-            rows = pl.ds(pl.multiple_of(core * q_rows, 8), q_rows)
-            for i in range(width // 128):
-                small_buf[k, i] = tall[i * q_rows : (i + 1) * q_rows]
-                block = owner * (width // 128) + i
-
-                @pl.when(block < cols // 128)
-                def joint(k=k, i=i, rows=rows, block=block):
-                    at = pl.ds(pl.multiple_of(block * 128, 128), 128)
-                    pltpu.make_async_copy(
-                        small_buf.at[k, i], joint_ref.at[rows, at], sems.at[each * k + 1 + i]
-                    ).start()
-
-                @pl.when(block >= cols // 128)
-                def out(k=k, i=i, rows=rows, block=block):
-                    at = pl.ds(pl.multiple_of((block - cols // 128) * 128, 128), 128)
-                    pltpu.make_async_copy(
-                        small_buf.at[k, i], out_ref.at[rows, at], sems.at[each * k + 1 + i]
-                    ).start()
-
-        for copy in copies:
-            copy.wait()
-        for k in range(2 * len(slots)):
-            for i in range(width // 128):
-                pltpu.make_async_copy(
-                    small_buf.at[k, i], out_ref.at[pl.ds(0, q_rows), pl.ds(0, 128)], sems.at[each * k + 1 + i]
-                ).wait()
-
-    count = 2 * len(slots)
-    each = 1 + width // 128
-    return place_call(
-        kernel,
-        [
+        out_shape=[
+            jax.ShapeDtypeStruct((D, ff_loc), f32),
+            jax.ShapeDtypeStruct((D, ff_loc), f32),
             jax.ShapeDtypeStruct((ff_loc, D), f32),
             jax.ShapeDtypeStruct((2 * q_rows, cols), f32),
             jax.ShapeDtypeStruct((2 * q_rows, D), f32),
+            jax.ShapeDtypeStruct((8, 128), f32),
         ],
-        meta,
-        pairs,
-        [
+        in_specs=[pl.BlockSpec(memory_space=pltpu.SMEM)]
+        + [pl.BlockSpec(memory_space=pltpu.VMEM)] * count
+        + [anywhere] * len(keep),
+        out_specs=[anywhere] * 5 + [pl.BlockSpec(memory_space=pltpu.VMEM)],
+        scratch_shapes=[
+            pltpu.VMEM((len(slots), mlp_rows, ff_loc), f32),
+            pltpu.VMEM((len(slots), mlp_rows, ff_loc), f32),
             pltpu.VMEM((count, down_rows, D), f32),
-            pltpu.VMEM((count, width // 128, q_rows, 128), f32),
+            pltpu.VMEM((count, parts, q_rows, 128), f32),
+            pltpu.SemaphoreType.DMA((4 * len(slots),)),
+            pltpu.SemaphoreType.DMA((count, parts)),
         ],
-        each * count,
-        old,
-        through,
-    )
+        input_output_aliases={1 + count + i: i for i in range(len(keep))},
+        compiler_params=pltpu.CompilerParams(vmem_limit_bytes=VMEM_BYTES),
+        cost_estimate=pl.CostEstimate(
+            flops=0, bytes_accessed=8 * sum(x.size for x in blocks), transcendentals=0
+        ),
+    )(meta, *blocks, *keep)
+    return list(result[:5]), result[5]
 
 
 def place_blocks(blocks, spots, out_shape, old=None):
@@ -909,7 +951,7 @@
     rest = ff_half - main
     width = main + 2 * rest
     first = core * main
-    tiled = 2 * rest == 128 and width % 256 == 0 and chips == 8 and (ff_half // chips) % 8 == 0
+    tiled = 2 * rest == 128 and width % 256 == 0 and chips == 8 and ff_half == chips * RING_ROWS
     ring = jnp.arange(chips, dtype=jnp.int32)
     owners_of = (net.pos - ring) % chips
     spots = jnp.concatenate(
@@ -934,7 +976,7 @@
         flops=2 * rows * D * 1152,
     )
 
-    slots = net.send_gather(pairs)
+    slots = net.ring_gather(pairs)
     mine = jnp.concatenate(slots, 0)
     other = net.swap(mine)
     order = jnp.array(net.order, jnp.int32)
@@ -977,7 +1019,7 @@
     down_rows = ff_half // chips
     mlp_rows = D // chips
     if tiled:
-        mid, gate_low, up_low, grad_mine, out_mine, sent = feed_forward(
+        x_turned, mid_turned, gate_low, up_low, grad_mine, out_mine, sent = feed_forward(
             spots, normed_two_group, grad_out_group, w_gate, w_up, w_down, width
         )
     else:
@@ -1009,11 +1051,67 @@
         piece = grad_chip[s * rows : (s + 1) * rows].astype(bf16)
         grad_two = grad_two + net.shift(piece, net.dp - s).astype(f32)
 
+    def attention_back(*after):
+        grad_hidden, grad_attn_low, grad_gain_two, grad_queries, terms_mine, terms_other = call(
+            lambda *refs: backward_kernel(ctx_count, *refs),
+            [
+                jax.ShapeDtypeStruct((rows, D), f32),
+                jax.ShapeDtypeStruct((rows, D), bf16),
+                jax.ShapeDtypeStruct((1, D), f32),
+                jax.ShapeDtypeStruct((rows, WIDTH_Q), f32),
+                jax.ShapeDtypeStruct((chips * rows, 2 * WIDTH_K), f32),
+                jax.ShapeDtypeStruct((chips * rows, 2 * WIDTH_K), bf16),
+            ],
+            [
+                meta, grad_two, hidden, cotangent[0], gain_two, w_out_full, spread, keys, values, lse,
+                attended,
+            ] + list(after),
+            smem=1,
+            loose=len(after),
+            scratch=[
+                pltpu.VMEM(padded, bf16),
+                pltpu.VMEM(padded, f32),
+                pltpu.VMEM((total_keys, WIDTH_K), f32),
+                pltpu.VMEM((total_keys, WIDTH_K), f32),
+            ],
+            flops=20 * KH * part_rows * total_keys * 128,
+        )
+        pair_sums = call(
+            pair_kernel,
+            [jax.ShapeDtypeStruct((rows, 2 * WIDTH_K), f32)]
+            + [jax.ShapeDtypeStruct((rows, 2 * WIDTH_K), bf16)] * (chips - 1),
+            [terms_mine, net.swap(terms_other)],
+        )
+        grad_pairs = net.ring_parts(pair_sums)
+        grad_joint_low, grad_input, grad_gain_one, grad_bias = call(
+            finish_kernel,
+            [
+                jax.ShapeDtypeStruct((rows, 1152), bf16),
+                jax.ShapeDtypeStruct((rows, D), f32),
+                jax.ShapeDtypeStruct((1, D), f32),
+                jax.ShapeDtypeStruct((1, 1152), f32),
+            ],
+            [grad_queries, x, gain_one, w_qkv_full, cosine, sine, grad_hidden] + grad_pairs,
+            flops=2 * rows * D * 1152,
+        )
+        return (
+            grad_hidden, grad_attn_low, grad_gain_two, grad_joint_low, grad_input, grad_gain_one,
+            grad_bias,
+        )
+
+    found = []
     if tiled:
+
+        def middle(*after):
+            found.extend(attention_back(*after))
+            return found[3]
+
         terms, head, tail = mlp_gradients(
-            spots, normed_two_group, grad_out_group, mid, gate_low, up_low, chips, down_rows, main
+            spots, x_turned, grad_out_group, mid_turned, gate_low, up_low, chips, down_rows, main
         )
-        sum_mlp, sum_down = net.ring_sum(head, tail, terms, terms.shape[1] - down_rows)
+        sum_mlp, sum_down = net.ring_sum(
+            head, tail, terms, terms.shape[1] - down_rows, middle
+        )
     else:
         part_down = jnp.einsum(
             "tf,td->fd", middle, grad_out_group, preferred_element_type=f32
@@ -1049,48 +1147,9 @@
 
         sum_mlp = net.ring_scatter([mlp_chunk(s) for s in range(chips)]).astype(bf16)
         sum_mlp = lax.optimization_barrier(sum_mlp)
-
-    grad_hidden, grad_attn_low, grad_gain_two, grad_queries, terms_mine, terms_other = call(
-        lambda *refs: backward_kernel(ctx_count, *refs),
-        [
-            jax.ShapeDtypeStruct((rows, D), f32),
-            jax.ShapeDtypeStruct((rows, D), bf16),
-            jax.ShapeDtypeStruct((1, D), f32),
-            jax.ShapeDtypeStruct((rows, WIDTH_Q), f32),
-            jax.ShapeDtypeStruct((chips * rows, 2 * WIDTH_K), f32),
-            jax.ShapeDtypeStruct((chips * rows, 2 * WIDTH_K), bf16),
-        ],
-        [
-            meta, grad_two, hidden, cotangent[0], gain_two, w_out_full, spread, keys, values, lse,
-            attended,
-        ],
-        smem=1,
-        scratch=[
-            pltpu.VMEM(padded, bf16),
-            pltpu.VMEM(padded, f32),
-            pltpu.VMEM((total_keys, WIDTH_K), f32),
-            pltpu.VMEM((total_keys, WIDTH_K), f32),
-        ],
-        flops=20 * KH * part_rows * total_keys * 128,
-    )
-    pair_sums = call(
-        pair_kernel,
-        [jax.ShapeDtypeStruct((rows, 2 * WIDTH_K), f32)]
-        + [jax.ShapeDtypeStruct((rows, 2 * WIDTH_K), bf16)] * (chips - 1),
-        [terms_mine, net.swap(terms_other)],
-    )
-    grad_pairs = [pair_sums[0]] + net.send_scatter(pair_sums)
-    grad_joint_low, grad_input, grad_gain_one, grad_bias = call(
-        finish_kernel,
-        [
-            jax.ShapeDtypeStruct((rows, 1152), bf16),
-            jax.ShapeDtypeStruct((rows, D), f32),
-            jax.ShapeDtypeStruct((1, D), f32),
-            jax.ShapeDtypeStruct((1, 1152), f32),
-        ],
-        [grad_queries, x, gain_one, w_qkv_full, cosine, sine, grad_hidden] + grad_pairs,
-        flops=2 * rows * D * 1152,
-    )
+        found.extend(attention_back())
+    grad_hidden, grad_attn_low, grad_gain_two, grad_joint_low, grad_input = found[:5]
+    grad_gain_one, grad_bias = found[5:]
 
     out_sum = mlp_chip[:rows]
     sent = jnp.concatenate([attended_low, grad_attn_low], 0)
@@ -1121,18 +1180,14 @@
             scratch=[pltpu.VMEM((D, qkv_cols + D), f32)],
             flops=4 * chip_rows * D * (qkv_cols + D),
         )
-        rest_block = call(
-            rest_kernel,
-            [jax.ShapeDtypeStruct((piece + down_rows, D), bf16)],
-            [terms_small[0]] + net.send_scatter(terms_small) + [sum_down],
+        block = call(
+            block_kernel,
+            [jax.ShapeDtypeStruct((sum_mlp.shape[0] + piece + down_rows, D), bf16)],
+            [sum_mlp, sum_down] + net.ring_parts(terms_small),
         )[0]
-        (grad_gate, grad_up), (grad_down, grad_joint, grad_out_proj) = net.gather_both(
-            sum_mlp,
-            rest_block,
-            lambda *args: place_pairs(spots, *args[:2], main, ff_loc, *args[2:]),
-            lambda *args: place_rest(
-                spots, *args[:2], down_rows, q_rows, ff_loc, qkv_cols, chips, *args[2:]
-            ),
+        sizes = (main, ff_loc, q_rows, qkv_cols, down_rows, chips)
+        grad_gate, grad_up, grad_down, grad_joint, grad_out_proj = net.gather_placed(
+            block, lambda slots, pairs, old: place_all(spots, slots, pairs, old, sizes)
         )
     else:
         q_first = net.d * (2 * q_rows) + core * q_rows

time: 378 us -> 388 us (1.026)
  waiting for transfers between devices: 119 us -> 150 us
  starting transfers between devices: 86.6 us -> 62.7 us
  local copies, waits for them, and re-layouts: 32.8 us -> 37.7 us
    ppermute x45 -> x40, waiting for transfers between devices: 78.1 us -> 115 us  [hop(): return lax.ppermute(x, 'ctx', perm)]
    ppermute x45 -> x40, starting transfers between devices: 67.5 us -> 41.6 us  [hop(): return lax.ppermute(x, 'ctx', perm)]
    pallas_call x18 -> x16, Pallas kernels: 92.1 us -> 84.4 us  [the longest x7 42.2 us: call(): pl.pallas_call(body, out_shape=list(outs), in_specs=specs, out_specs=[pl....]
    ppermute x7, waiting for transfers between devices: 25 us -> 18.8 us  [shift(): return lax.ppermute(x, 'dp', [(i, (i + step) % n) for i in range(n)])]
    pallas_call x6, Pallas kernels: 14.6 us -> 18.6 us  [ring_add(): pl.pallas_call(kernel, out_shape=jax.ShapeDtypeStruct((rows, columns), bf...]
    unnamed x144 -> x126, local copies, waits for them, and re-layouts: 17.3 us -> 18.8 us
  transfers between devices with their start and end apart: 82 -> 69, of which waited for: 28 -> 44; matrix products, arithmetic and copies ran while one was open for 7% -> 8% of each run, Pallas kernels for 25% -> 20%
where the time goes in v5:
time: 388 us; the launch traced here: 387 us
  waiting for transfers between devices  150 us (39%)
  Pallas kernels  118 us (30%)
  starting transfers between devices  62.7 us (16%)
  local copies, waits for them, and re-layouts  37.7 us (10%)
  other arithmetic  16.7 us (4%)
    ppermute x40, waiting for transfers between devices, hop(): return lax.ppermute(x, 'ctx', perm)  115 us
    pallas_call x7, Pallas kernels, call(): pl.pallas_call(body, out_shape=list(outs), in_specs=specs, out_specs=[pl....  42.2 us
    ppermute x40, starting transfers between devices, hop(): return lax.ppermute(x, 'ctx', perm)  41.6 us
    pallas_call x5, Pallas kernels, place_all(): pl.pallas_call(kernel, out_shape=[jax.ShapeDtypeStruct((D, ff_loc), f32),...  26 us
    unnamed x126, local copies, waits for them, and re-layouts  18.8 us
    ppermute x7, waiting for transfers between devices, shift(): return lax.ppermute(x, 'dp', [(i, (i + step) % n) for i in range(n)])  18.8 us
    pallas_call x6, Pallas kernels, ring_add(): pl.pallas_call(kernel, out_shape=jax.ShapeDtypeStruct((rows, columns), bf...  18.6 us
    pallas_call x1, Pallas kernels, feed_forward(): pl.pallas_call(lambda *refs: mlp_kernel(half, *refs), out_shape=[jax.Shap...  16.2 us
  transfers between devices with their start and end apart: 69, of which 44 were waited for; matrix products, arithmetic and copies ran while one was open for 8% of the time, Pallas kernels for 20%

profile of v5, /device:TPU:0, one launch (start us, length us, event | category | flops | bytes accessed | tf_op | source)
XLA Modules:
  0.0 386.9 jit_solution(9980325129139865014)
XLA Ops:
  12.1 4.5 %collective-permute-done = bf16[224,1152]{1,0:T(8,128)(2,1)S(1)} collective-permute-done((bf16[224,1152]{1,0:T(8,128)(2,1)S(1)}, bf16[224,1152]{1,0:T(8,128)(2,1)S(1)}, u32[]{:S(2)}, u32[]{:S(2)}) %collective-permute-start) | collective-permute-done | bytes 516128 | tf_op jit(solution)/shard_map/ppermute | solution.py:56
  51.7 10.4 %shard_map.196 = (bf16[128,896]{1,0:T(8,128)(2,1)}, f32[2,896,128]{2,1,0:T(8,128)}, f32[2,2,8,448]{3,2,1,0:T(8,128)}, bf16[2,896,128]{2,1,0:T(8,128)(2,1)}, bf16...) custom-call(s32[17]{0:T(128)} %pad_add_fusion.refs_0_, ...), custom_call_target="tpu_custom_call" | custom-call | flops 1879048192 | bytes 6516292 | tf_op jit(solution)/shard_map/pallas_call | solution.py:213
  65.1 4.8 %collective-permute-done.13 = bf16[128,896]{1,0:T(8,128)(2,1)S(1)} collective-permute-done((bf16[128,896]{1,0:T(8,128)(2,1)}, bf16[128,896]{1,0:T(8,128)(2,1)S(1)}, u32[]{:S(2)}, u32[]{:S(2)}) %collective-permute-start.13) | collective-permute-done | bytes 229408 | tf_op jit(solution)/shard_map/ppermute | solution.py:56
  73.8 16.2 %shard_map.197 = (bf16[896,512]{1,0:T(8,128)(2,1)}, bf16[1280,512]{1,0:T(8,128)(2,1)}, bf16[512,1280]{1,0:T(8,128)(2,1)}, bf16[512,1280]{1,0:T(8,128)(2,1)}, f32...) custom-call(s32[20]{0:T(128)} %concatenate.90.refs_0_.meta_ref, ...), custom_call_target="tpu_custom_call" | custom-call | flops 7046430720 | bytes 6881280 | tf_op jit(solution)/shard_map/pallas_call | solution.py:643
  90.3 12.2 %shard_map.198 = (bf16[8,456,896]{2,1,0:T(8,128)(2,1)}, bf16[304,896]{1,0:T(8,128)(2,1)}, bf16[152,896]{1,0:T(8,128)(2,1)}) custom-call(s32[20]{0:T(128)} %concatenate.90.refs_0_.meta_ref, bf16[896,512]{1,0:T(8,128)(2,1)} %get-tuple-element.113.refs_1_, bf16[512,896]{1,0:T(8,128)(2,1)} %get-tuple-element.189.refs_2_, ...), custom_call_target="tpu_custom_call" | custom-call | flops 3523215360 | bytes 13074432 | tf_op jit(solution)/shard_map/pallas_call | solution.py:728
  106.5 5.0 %collective-permute-done.20.refs_0_ = bf16[152,896]{1,0:T(8,128)(2,1)S(1)} collective-permute-done((bf16[152,896]{1,0:T(8,128)(2,1)}, bf16[152,896]{1,0:T(8,128)(2,1)S(1)}, u32[]{:S(2)}, u32[]{:S(2)}) %collective-permute-start.20) | collective-permute-done | bytes 272416 | tf_op jit(solution)/shard_map/ppermute | solution.py:64
  115.2 3.4 collective-permute-done.19.refs_0_
  123.2 15.0 %shard_map.201 = (f32[128,896]{1,0:T(8,128)}, bf16[128,896]{1,0:T(8,128)(2,1)}, f32[1,896]{1,0:T(1,128)}, f32[128,896]{1,0:T(8,128)}, f32[1024,256]{1,0:T(8,128)}, /*index=5*/bf16[1024,256]{1,0:T(8,128)(2,1)}) custom-call(s32[17]{0:T(128)} %pad_add_fusion.refs_0_, f32[128,896]{1,0:T(8,128)} %slice_add_fusion.refs_1_, f32[128,896]{1,0:T(8,128)} %get-tuple-element.100.refs_2_, ...), custom_call_target="tpu_custom_call" | custom-call | flops 4697620480 | bytes 9595972 | tf_op jit(solution)/shard_map/pallas_call | solution.py:213
  149.5 10.2 %collective-permute-done.27 = bf16[64,256]{1,0:T(8,128)(2,1)S(1)} collective-permute-done((bf16[64,256]{1,0:T(8,128)(2,1)S(1)}, bf16[64,256]{1,0:T(8,128)(2,1)S(1)}, u32[]{:S(2)}, u32[]{:S(2)}) %collective-permute-start.27) | collective-permute-done | bytes 32800 | tf_op jit(solution)/shard_map/ppermute | solution.py:64
  176.5 3.8 shard_map.203
  181.9 6.4 %collective-permute-done.37 = bf16[128,1152]{1,0:T(8,128)(2,1)S(1)} collective-permute-done((bf16[128,1152]{1,0:T(8,128)(2,1)}, bf16[128,1152]{1,0:T(8,128)(2,1)S(1)}, u32[]{:S(2)}, u32[]{:S(2)}) %collective-permute-start.37) | collective-permute-done | bytes 294944 | tf_op jit(solution)/shard_map/ppermute | solution.py:56
  203.9 5.4 %shard_map.209 = (bf16[64,896]{1,0:T(8,128)(2,1)}, bf16[64,896]{1,0:T(8,128)(2,1)}, bf16[64,896]{1,0:T(8,128)(2,1)}, bf16[64,896]{1,0:T(8,128)(2,1)}, bf16[64,89...) custom-call(s32[20]{0:T(128)} %concatenate.90.refs_0_.meta_ref, ...), custom_call_target="tpu_custom_call" | custom-call | flops 1879048192 | bytes 4849744 | tf_op jit(solution)/shard_map/pallas_call | solution.py:213
  211.9 3.5 collective-permute-done.35.refs_0_
  227.7 18.0 %collective-permute-done.40 = bf16[32,896]{1,0:T(8,128)(2,1)S(1)} collective-permute-done((bf16[32,896]{1,0:T(8,128)(2,1)S(1)}, bf16[32,896]{1,0:T(8,128)(2,1)S(1)}, u32[]{:S(2)}, u32[]{:S(2)}) %collective-permute-start.40) | collective-permute-done | bytes 57376 | tf_op jit(solution)/shard_map/ppermute | solution.py:64
  253.5 3.5 collective-permute-done.42
  268.6 4.1 %shard_map.211 = (f32[896,2432]{1,0:T(8,128)}, f32[896,2432]{1,0:T(8,128)}, f32[2432,896]{1,0:T(8,128)}, f32[448,1152]{1,0:T(8,128)}, f32[448,896]{1,0:T(8,128)}, /*index=5*/f32[8,128]{1,0:T(8,128)}) custom-call(s32[20]{0:T(128)} %concatenate.90.refs_0_.meta_ref, bf16[520,896]{1,0:T(8,128)(2,1)} %shard_map.210.refs_0_, bf16[520,896]{1,0:T(8,128)(2,1)} %copy-done.14), custom_call_target="tpu_custom_call" | custom-call | bytes 7454720 | tf_op jit(solution)/shard_map/pallas_call | solution.py:867
  272.7 15.5 %collective-permute-done.49.refs_1_ = bf16[520,896]{1,0:T(8,128)(2,1)S(1)} collective-permute-done((bf16[520,896]{1,0:T(8,128)(2,1)}, bf16[520,896]{1,0:T(8,128)(2,1)S(1)}, u32[]{:S(2)}, u32[]{:S(2)}) %collective-permute-start.49) | collective-permute-done | bytes 931872 | tf_op jit(solution)/shard_map/ppermute | solution.py:64
  294.5 5.9 %shard_map.213 = (f32[896,2432]{1,0:T(8,128)}, f32[896,2432]{1,0:T(8,128)}, f32[2432,896]{1,0:T(8,128)}, f32[448,1152]{1,0:T(8,128)}, f32[448,896]{1,0:T(8,128)}, /*index=5*/f32[8,128]{1,0:T(8,128)}) custom-call(s32[20]{0:T(128)} %concatenate.90.refs_0_.meta_ref, ...), custom_call_target="tpu_custom_call", output_to_operand_aliasing={{0}: (5, {}), {1}: (6, {}), {2}: (7, {}), {3}: (8, {}), {4}... | custom-call | bytes 14909440 | tf_op jit(solution)/shard_map/pallas_call | solution.py:867
  300.4 12.4 %collective-permute-done.53.refs_1_ = bf16[520,896]{1,0:T(8,128)(2,1)S(1)} collective-permute-done((bf16[520,896]{1,0:T(8,128)(2,1)}, bf16[520,896]{1,0:T(8,128)(2,1)S(1)}, u32[]{:S(2)}, u32[]{:S(2)}) %collective-permute-start.53) | collective-permute-done | bytes 931872 | tf_op jit(solution)/shard_map/ppermute | solution.py:64
  319.1 5.9 %shard_map.215 = (f32[896,2432]{1,0:T(8,128)}, f32[896,2432]{1,0:T(8,128)}, f32[2432,896]{1,0:T(8,128)}, f32[448,1152]{1,0:T(8,128)}, f32[448,896]{1,0:T(8,128)}, /*index=5*/f32[8,128]{1,0:T(8,128)}) custom-call(s32[20]{0:T(128)} %concatenate.90.refs_0_.meta_ref, ...), custom_call_target="tpu_custom_call", output_to_operand_aliasing={{0}: (5, {}), {1}: (6, {}), {2}: (7, {}), {3}: (8, {}), {4}... | custom-call | bytes 14909440 | tf_op jit(solution)/shard_map/pallas_call | solution.py:867
  325.0 12.4 %collective-permute-done.57.refs_1_ = bf16[520,896]{1,0:T(8,128)(2,1)S(1)} collective-permute-done((bf16[520,896]{1,0:T(8,128)(2,1)}, bf16[520,896]{1,0:T(8,128)(2,1)S(1)}, u32[]{:S(2)}, u32[]{:S(2)}) %collective-permute-start.57) | collective-permute-done | bytes 931872 | tf_op jit(solution)/shard_map/ppermute | solution.py:64
  344.4 7.9 %collective-permute-done.59 = bf16[264,896]{1,0:T(8,128)(2,1)S(1)} collective-permute-done((bf16[264,896]{1,0:T(8,128)(2,1)S(1)}, bf16[264,896]{1,0:T(8,128)(2,1)S(1)}, u32[]{:S(2)}, u32[]{:S(2)}) %collective-permute-start.59) | collective-permute-done | bytes 473120 | tf_op jit(solution)/shard_map/ppermute | solution.py:64
  375.7 5.9 %shard_map.217 = (f32[896,2432]{1,0:T(8,128)}, f32[896,2432]{1,0:T(8,128)}, f32[2432,896]{1,0:T(8,128)}, f32[448,1152]{1,0:T(8,128)}, f32[448,896]{1,0:T(8,128)}, /*index=5*/f32[8,128]{1,0:T(8,128)}) custom-call(s32[20]{0:T(128)} %concatenate.90.refs_0_.meta_ref, ...), custom_call_target="tpu_custom_call", output_to_operand_aliasing={{0}: (5, {}), {1}: (6, {}), {2}: (7, {}), {3}: (8, {}), {4}... | custom-call | bytes 14909440 | tf_op jit(solution)/shard_map/pallas_call | solution.py:867
  382.6 4.1 %shard_map.218 = (f32[896,2432]{1,0:T(8,128)}, f32[896,2432]{1,0:T(8,128)}, f32[2432,896]{1,0:T(8,128)}, f32[448,1152]{1,0:T(8,128)}, f32[448,896]{1,0:T(8,128)}, /*index=5*/f32[8,128]{1,0:T(8,128)}) custom-call(s32[20]{0:T(128)} %concatenate.90.refs_0_.meta_ref, ...), custom_call_target="tpu_custom_call", output_to_operand_aliasing={{0}: (3, {}), {1}: (4, {}), {2}: (5, {}), {3}: (6, {}), {4}... | custom-call | bytes 7454720 | tf_op jit(solution)/shard_map/pallas_call | solution.py:867
  (341 shorter events, 189.0 us)
Async XLA Ops:
  26.7 21.4 %collective-permute-start.15 = (bf16[128,1792]{1,0:T(8,128)(2,1)S(1)}, bf16[128,1792]{1,0:T(8,128)(2,1)S(1)}, u32[]{:S(2)}, u32[]{:S(2)}) collective-permute-start(bf16[128,1792]{1,0:T(8,128)(2,1)S(1)} %constant_dynamic-update-slice_fusion.9), channel_id=1, source_target_pairs={{0,16},{16,0},{1,17},{17,1},{2,18},{18,2},{3,19},{19,3},{4,20},{20... | collective-permute-start | bytes 1376264 | tf_op jit(solution)/shard_map/ppermute | solution.py:56
  28.6 18.9 %collective-permute-start.11 = (bf16[224,896]{1,0:T(8,128)(2,1)S(1)}, bf16[224,896]{1,0:T(8,128)(2,1)S(1)}, u32[]{:S(2)}, u32[]{:S(2)}) collective-permute-start(bf16[224,896]{1,0:T(8,128)(2,1)S(1)} %constant_dynamic-slice_fusion), channel_id=1, source_target_pairs={{0,16},{16,0},{1,17},{17,1},{2,18},{18,2},{3,19},{19,3},{4,20},{20... | collective-permute-start | bytes 1204232 | tf_op jit(solution)/shard_map/ppermute | solution.py:56
  48.2 22.8 %collective-permute-start.16 = (bf16[256,1792]{1,0:T(8,128)(2,1)S(1)}, bf16[256,1792]{1,0:T(8,128)(2,1)S(1)}, u32[]{:S(2)}, u32[]{:S(2)}) collective-permute-start(bf16[256,1792]{1,0:T(8,128)(2,1)S(1)} %pad_maximum_fusion.7), channel_id=1, source_target_pairs={{0,1},{1,0},{2,3},{3,2},{4,5},{5,4},{6,7},{7,6},{8,9},{9,8},{10,11... | collective-permute-start | bytes 2752520 | tf_op jit(solution)/shard_map/ppermute | solution.py:52
  104.7 17.7 %collective-permute-start.18 = (bf16[128,896]{1,0:T(8,128)(2,1)S(1)}, bf16[128,896]{1,0:T(8,128)(2,1)S(1)}, u32[]{:S(2)}, u32[]{:S(2)}) collective-permute-start(bf16[128,896]{1,0:T(8,128)(2,1)S(1)} %slice.177), channel_id=1, source_target_pairs={{0,16},{16,0},{1,17},{17,1},{2,18},{18,2},{3,19},{19,3},{4,20},{20... | collective-permute-start | bytes 688136 | tf_op jit(solution)/shard_map/ppermute | solution.py:56
  138.4 51.7 %collective-permute-start.34 = (bf16[456,896]{1,0:T(8,128)(2,1)S(1)}, bf16[456,896]{1,0:T(8,128)(2,1)S(1)}, u32[]{:S(2)}, u32[]{:S(2)}) collective-permute-start(bf16[456,896]{1,0:T(8,128)(2,1)S(1)} %copy-done.26), channel_id=1, source_target_pairs={{0,2},{1,3},{4,0},{5,1},{8,4},{9,5},{12,8},{13,9},{14,12},{15,13},... | collective-permute-start | bytes 2451464 | tf_op jit(solution)/shard_map/ppermute | solution.py:64
  140.0 55.8 %collective-permute-start.31 = (bf16[456,896]{1,0:T(8,128)(2,1)S(1)}, bf16[456,896]{1,0:T(8,128)(2,1)S(1)}, u32[]{:S(2)}, u32[]{:S(2)}) collective-permute-start(bf16[456,896]{1,0:T(8,128)(2,1)S(1)} %copy-done.25), channel_id=1, source_target_pairs={{0,4},{1,5},{4,8},{5,9},{8,12},{9,13},{12,14},{13,15},{14,10},{15,... | collective-permute-start | bytes 2451464 | tf_op jit(solution)/shard_map/ppermute | solution.py:64
  146.0 24.8 %collective-permute-start.21 = (bf16[384,896]{1,0:T(8,128)(2,1)S(1)}, bf16[384,896]{1,0:T(8,128)(2,1)S(1)}, u32[]{:S(2)}, u32[]{:S(2)}) collective-permute-start(bf16[384,896]{1,0:T(8,128)(2,1)S(1)} %pad_maximum_fusion.10), channel_id=1, source_target_pairs={{0,16},{16,0},{1,17},{17,1},{2,18},{18,2},{3,19},{19,3},{4,20},{20... | collective-permute-start | bytes 2064392 | tf_op jit(solution)/shard_map/ppermute | solution.py:56
  170.9 29.3 %collective-permute-start.39 = (bf16[512,896]{1,0:T(8,128)(2,1)S(1)}, bf16[512,896]{1,0:T(8,128)(2,1)S(1)}, u32[]{:S(2)}, u32[]{:S(2)}) collective-permute-start(bf16[512,896]{1,0:T(8,128)(2,1)S(1)} %pad_maximum_fusion.8), channel_id=1, source_target_pairs={{0,1},{1,0},{2,3},{3,2},{4,5},{5,4},{6,7},{7,6},{8,9},{9,8},{10,11... | collective-permute-start | bytes 2752520 | tf_op jit(solution)/shard_map/ppermute | solution.py:52
  194.1 21.2 %collective-permute-start.35 = (bf16[456,896]{1,0:T(8,128)(2,1)}, bf16[456,896]{1,0:T(8,128)(2,1)S(1)}, u32[]{:S(2)}, u32[]{:S(2)}) collective-permute-start(bf16[456,896]{1,0:T(8,128)(2,1)} %shard_map.206), channel_id=1, source_target_pairs={{0,2},{1,3},{4,0},{5,1},{8,4},{9,5},{12,8},{13,9},{14,12},{15,13},... | collective-permute-start | bytes 2451464 | tf_op jit(solution)/shard_map/ppermute | solution.py:64
  199.9 21.3 %collective-permute-start.32 = (bf16[456,896]{1,0:T(8,128)(2,1)}, bf16[456,896]{1,0:T(8,128)(2,1)S(1)}, u32[]{:S(2)}, u32[]{:S(2)}) collective-permute-start(bf16[456,896]{1,0:T(8,128)(2,1)} %shard_map.204), channel_id=1, source_target_pairs={{0,4},{1,5},{4,8},{5,9},{8,12},{9,13},{12,14},{13,15},{14,10},{15,... | collective-permute-start | bytes 2451464 | tf_op jit(solution)/shard_map/ppermute | solution.py:64
  210.1 15.9 %collective-permute-start.44 = (bf16[32,896]{1,0:T(8,128)(2,1)S(1)}, bf16[32,896]{1,0:T(8,128)(2,1)S(1)}, u32[]{:S(2)}, u32[]{:S(2)}) collective-permute-start(bf16[32,896]{1,0:T(8,128)(2,1)S(1)} %get-tuple-element.198), channel_id=1, source_target_pairs={{0,2},{1,3},{4,0},{5,1},{8,4},{9,5},{12,8},{13,9},{14,12},{15,13},... | collective-permute-start | bytes 172040 | tf_op jit(solution)/shard_map/ppermute | solution.py:64
  219.4 38.1 %collective-permute-start.36 = (bf16[456,896]{1,0:T(8,128)(2,1)}, bf16[456,896]{1,0:T(8,128)(2,1)S(1)}, u32[]{:S(2)}, u32[]{:S(2)}) collective-permute-start(bf16[456,896]{1,0:T(8,128)(2,1)} %shard_map.207), channel_id=1, source_target_pairs={{0,2},{1,3},{4,0},{5,1},{8,4},{9,5},{12,8},{13,9},{14,12},{15,13},... | collective-permute-start | bytes 2451464 | tf_op jit(solution)/shard_map/ppermute | solution.py:64
  225.2 32.4 %collective-permute-start.33 = (bf16[456,896]{1,0:T(8,128)(2,1)}, bf16[456,896]{1,0:T(8,128)(2,1)S(1)}, u32[]{:S(2)}, u32[]{:S(2)}) collective-permute-start(bf16[456,896]{1,0:T(8,128)(2,1)} %shard_map.205), channel_id=1, source_target_pairs={{0,4},{1,5},{4,8},{5,9},{8,12},{9,13},{12,14},{13,15},{14,10},{15,... | collective-permute-start | bytes 2451464 | tf_op jit(solution)/shard_map/ppermute | solution.py:64
  225.5 20.2 %collective-permute-start.40 = (bf16[32,896]{1,0:T(8,128)(2,1)S(1)}, bf16[32,896]{1,0:T(8,128)(2,1)S(1)}, u32[]{:S(2)}, u32[]{:S(2)}) collective-permute-start(bf16[32,896]{1,0:T(8,128)(2,1)S(1)} %get-tuple-element.199), channel_id=1, source_target_pairs={{0,4},{1,5},{4,8},{5,9},{8,12},{9,13},{12,14},{13,15},{14,10},{15,... | collective-permute-start | bytes 172040 | tf_op jit(solution)/shard_map/ppermute | solution.py:64
  226.1 20.2 %collective-permute-start.45 = (bf16[64,896]{1,0:T(8,128)(2,1)S(1)}, bf16[64,896]{1,0:T(8,128)(2,1)S(1)}, u32[]{:S(2)}, u32[]{:S(2)}) collective-permute-start(bf16[64,896]{1,0:T(8,128)(2,1)S(1)} %pad_maximum_fusion.14), channel_id=1, source_target_pairs={{0,2},{1,3},{4,0},{5,1},{8,4},{9,5},{12,8},{13,9},{14,12},{15,13},... | collective-permute-start | bytes 344072 | tf_op jit(solution)/shard_map/ppermute | solution.py:64
  265.0 23.3 %collective-permute-start.49 = (bf16[520,896]{1,0:T(8,128)(2,1)}, bf16[520,896]{1,0:T(8,128)(2,1)S(1)}, u32[]{:S(2)}, u32[]{:S(2)}) collective-permute-start(bf16[520,896]{1,0:T(8,128)(2,1)} %shard_map.210.refs_0_), channel_id=1, source_target_pairs={{0,4},{1,5},{4,8},{5,9},{8,12},{9,13},{12,14},{13,15},{14,10},{15,... | collective-permute-start | bytes 2795528 | tf_op jit(solution)/shard_map/ppermute | solution.py:64
  265.4 23.0 %collective-permute-start.50 = (bf16[520,896]{1,0:T(8,128)(2,1)}, bf16[520,896]{1,0:T(8,128)(2,1)S(1)}, u32[]{:S(2)}, u32[]{:S(2)}) collective-permute-start(bf16[520,896]{1,0:T(8,128)(2,1)} %shard_map.210.refs_0_), channel_id=1, source_target_pairs={{0,2},{1,3},{4,0},{5,1},{8,4},{9,5},{12,8},{13,9},{14,12},{15,13},... | collective-permute-start | bytes 2795528 | tf_op jit(solution)/shard_map/ppermute | solution.py:64
  290.0 22.8 %collective-permute-start.53 = (bf16[520,896]{1,0:T(8,128)(2,1)}, bf16[520,896]{1,0:T(8,128)(2,1)S(1)}, u32[]{:S(2)}, u32[]{:S(2)}) collective-permute-start(bf16[520,896]{1,0:T(8,128)(2,1)} %get-tuple-element.146.refs_0_), channel_id=1, source_target_pairs={{0,4},{1,5},{4,8},{5,9},{8,12},{9,13},{12,14},{13,15},{14,10},{15,... | collective-permute-start | bytes 2795528 | tf_op jit(solution)/shard_map/ppermute | solution.py:64
  290.6 22.5 %collective-permute-start.54 = (bf16[520,896]{1,0:T(8,128)(2,1)}, bf16[520,896]{1,0:T(8,128)(2,1)S(1)}, u32[]{:S(2)}, u32[]{:S(2)}) collective-permute-start(bf16[520,896]{1,0:T(8,128)(2,1)} %get-tuple-element.147.refs_2_), channel_id=1, source_target_pairs={{0,2},{1,3},{4,0},{5,1},{8,4},{9,5},{12,8},{13,9},{14,12},{15,13},... | collective-permute-start | bytes 2795528 | tf_op jit(solution)/shard_map/ppermute | solution.py:64
  314.6 22.8 %collective-permute-start.57 = (bf16[520,896]{1,0:T(8,128)(2,1)}, bf16[520,896]{1,0:T(8,128)(2,1)S(1)}, u32[]{:S(2)}, u32[]{:S(2)}) collective-permute-start(bf16[520,896]{1,0:T(8,128)(2,1)} %get-tuple-element.154.refs_0_), channel_id=1, source_target_pairs={{0,4},{1,5},{4,8},{5,9},{8,12},{9,13},{12,14},{13,15},{14,10},{15,... | collective-permute-start | bytes 2795528 | tf_op jit(solution)/shard_map/ppermute | solution.py:64
  316.1 22.5 %collective-permute-start.58 = (bf16[520,896]{1,0:T(8,128)(2,1)}, bf16[520,896]{1,0:T(8,128)(2,1)S(1)}, u32[]{:S(2)}, u32[]{:S(2)}) collective-permute-start(bf16[520,896]{1,0:T(8,128)(2,1)} %get-tuple-element.155.refs_2_), channel_id=1, source_target_pairs={{0,2},{1,3},{4,0},{5,1},{8,4},{9,5},{12,8},{13,9},{14,12},{15,13},... | collective-permute-start | bytes 2795528 | tf_op jit(solution)/shard_map/ppermute | solution.py:64
  343.9 30.5 %collective-permute-start.62 = (bf16[520,896]{1,0:T(8,128)(2,1)}, bf16[520,896]{1,0:T(8,128)(2,1)S(1)}, u32[]{:S(2)}, u32[]{:S(2)}) collective-permute-start(bf16[520,896]{1,0:T(8,128)(2,1)} %get-tuple-element.162.refs_0_), channel_id=1, source_target_pairs={{0,1},{1,0},{2,3},{3,2},{4,5},{5,4},{6,7},{7,6},{8,9},{9,8},{10,11... | collective-permute-start | bytes 2795528 | tf_op jit(solution)/shard_map/ppermute | solution.py:52
  343.9 30.5 %collective-permute-start.63 = (bf16[520,896]{1,0:T(8,128)(2,1)}, bf16[520,896]{1,0:T(8,128)(2,1)S(1)}, u32[]{:S(2)}, u32[]{:S(2)}) collective-permute-start(bf16[520,896]{1,0:T(8,128)(2,1)} %get-tuple-element.163.refs_2_), channel_id=1, source_target_pairs={{0,1},{1,0},{2,3},{3,2},{4,5},{5,4},{6,7},{7,6},{8,9},{9,8},{10,11... | collective-permute-start | bytes 2795528 | tf_op jit(solution)/shard_map/ppermute | solution.py:52
  354.6 27.0 %collective-permute-start.61 = (bf16[520,896]{1,0:T(8,128)(2,1)S(1)}, bf16[520,896]{1,0:T(8,128)(2,1)S(1)}, u32[]{:S(2)}, u32[]{:S(2)}) collective-permute-start(bf16[520,896]{1,0:T(8,128)(2,1)S(1)} %constant_dynamic-update-slice_fusion.11.refs_0_), channel_id=1, source_target_pairs={{0,1},{1,0},{2,3},{3,2},{4,5},{5,4},{6,7},{7,6},{8,9},{9,8},{10,11... | collective-permute-start | bytes 2795528 | tf_op jit(solution)/shard_map/ppermute | solution.py:52
  (102 other events, 815.5 us)

commit v6 on v5

--- a/solution.py
+++ b/solution.py
@@ -1,5 +1,3 @@
-import math
-
 import jax
 import jax.numpy as jnp
 from jax import lax
@@ -156,19 +154,24 @@
             fwd, back = self.hop(mine_f, 1), self.hop(mine_b, -1)
         return [local[0], fwd, back]
 
-    def ring_sum(self, head, tail, terms, split, middle):
+    def ring_sum(self, terms, stages):
         n = self.chips
         half = n // 2
-        fwd, back = self.hop(head, 1), self.hop(tail, -1)
-        token = None
+        fwd, back = self.hop(terms[half], 1), self.hop(terms[half - 1], -1)
+
+        def add(got, slot):
+            return (got.astype(f32) + terms[slot].astype(f32)).astype(bf16)
+
         for s in range(1, half):
-            after = token if s == half - 1 else None
-            fwd_sum = ring_add(fwd, terms, half + s, 0, after)
-            back_sum = ring_add(back, terms, half - s, 1, after)
-            if s == 1:
-                token = middle(fwd_sum, back_sum)
-            fwd, back = self.hop(fwd_sum, 1), self.hop(back_sum, -1)
-        return ring_end(fwd, back, terms, split)
+            fwd = add(fwd, half + s)
+            if s < half - 1:
+                back = add(back, half - 1 - s)
+                stages[s - 1](fwd, back)
+                fwd, back = self.hop(fwd, 1), self.hop(back, -1)
+            else:
+                stages[s - 1](fwd)
+                fwd = self.hop(fwd, 1)
+        return fwd, back
 
     def gather_placed(self, x, place):
         n = self.chips
@@ -186,8 +189,8 @@
             else:
                 cut = half_cut(fwd.shape[0])
                 fwd, back = self.hop(fwd[:cut], 1), self.hop(back[cut:], -1)
-        far = jnp.concatenate([fwd, back], 0)
         placed, token = place(*waiting, placed)
+        far = join(fwd, back, token)
         return place([half], [(far, self.swap(far))], placed)[0]
 
 
@@ -252,42 +255,17 @@
     )(token, *blocks)
 
 
-def ring_add(got, terms, slot, side, after=None):
-    rows, columns = terms.shape[1:]
-    some = got.shape[0]
-    step = math.gcd(rows, RING_ROWS)
-    steps, here = rows // step, some // step
-    first = 0 if side == 0 else steps - here
-
-    def kernel(*refs):
-        got_ref, term_ref, out_ref = refs[0], refs[1], refs[-1]
-        i = pl.program_id(0)
-        inside = (i >= first) & (i < first + here)
-
-        @pl.when(inside)
-        def add():
-            out_ref[...] = (got_ref[...].astype(f32) + term_ref[0].astype(f32)).astype(bf16)
-
-        @pl.when(jnp.logical_not(inside))
-        def keep():
-            out_ref[...] = term_ref[0]
-
-    extra = [] if after is None else [after]
-    return pl.pallas_call(
-        kernel,
-        out_shape=jax.ShapeDtypeStruct((rows, columns), bf16),
-        grid=(steps,),
-        in_specs=[
-            pl.BlockSpec((step, columns), lambda i: (jnp.clip(i - first, 0, here - 1), 0)),
-            pl.BlockSpec((1, step, columns), lambda i: (slot, i, 0)),
-        ]
-        + [pl.BlockSpec(memory_space=pl.ANY)] * len(extra),
-        out_specs=pl.BlockSpec((step, columns), lambda i: (i, 0)),
-        compiler_params=pltpu.CompilerParams(vmem_limit_bytes=VMEM_BYTES),
-        cost_estimate=pl.CostEstimate(
-            flops=0, bytes_accessed=6 * rows * columns, transcendentals=0
-        ),
-    )(got, terms, *extra)
+def join(first, second, token):
+    cut = first.shape[0]
+
+    def kernel(first_ref, second_ref, out_ref):
+        out_ref[:cut, :] = first_ref[...]
+        out_ref[cut:, :] = second_ref[...]
+
+    shape = (cut + second.shape[0], first.shape[1])
+    return call(
+        kernel, [jax.ShapeDtypeStruct(shape, first.dtype)], [first, second, token], loose=1
+    )[0]
 
 
 def ring_end(fwd, back, terms, split):
@@ -546,12 +524,14 @@
 
 
 def finish_kernel(
-    gq_ref, x_ref, gain_ref, w_ref, cos_ref, sin_ref, gh_ref, *refs
+    gq_ref, x_ref, gain_ref, w_ref, cos_ref, sin_ref, gh_ref, gain_two_ref, *refs
 ):
-    joint_ref, gx_ref, gain_grad_ref, bias_ref = refs[-4:]
+    sent_ref, gx_ref, gain_grad_ref, bias_ref = refs[-4:]
     pair = refs[0][...]
     for ref in refs[1:-4]:
         pair = pair + ref[...].astype(f32)
+    rows = pair.shape[0]
+    joint_ref = sent_ref.at[:rows, :]
     cosine = cos_ref[...]
     sine = sin_ref[...]
     early = lanes(cosine.shape) % HD < HD // 2
@@ -563,12 +543,21 @@
         joint_ref[:, at] = (grad * cosine + turned).astype(bf16)
     joint_ref[:, WIDTH_Q + WIDTH_K :] = pair[:, WIDTH_K:].astype(bf16)
     joint = joint_ref[...]
-    bias_ref[...] = jnp.sum(joint.astype(f32), 0, keepdims=True)
+    bias = jnp.sum(joint.astype(f32), 0, keepdims=True)
+    bias_ref[...] = bias
     grad = dot_nt(joint, w_ref[...])
     x = x_ref[...].astype(f32)
     inverse = lax.rsqrt(jnp.mean(x * x, -1, keepdims=True) + EPS)
     unit = x * inverse
-    gain_grad_ref[...] = jnp.sum(grad * unit, 0, keepdims=True)
+    gain = jnp.sum(grad * unit, 0, keepdims=True)
+    gain_grad_ref[...] = gain
+    wide = [jnp.zeros((1, bias.shape[1] - gain.shape[1]), f32)]
+    found = []
+    for row in (jnp.concatenate([gain] + wide, 1), jnp.concatenate([gain_two_ref[...]] + wide, 1), bias):
+        high = row.astype(bf16)
+        found += [high.astype(f32), row - high.astype(f32)]
+    found.append(jnp.zeros((sent_ref.shape[0] - rows - len(found), bias.shape[1]), f32))
+    sent_ref[rows:, :] = jnp.concatenate(found, 0).astype(bf16)
     scaled = grad * gain_ref[...]
     gx_ref[...] = gh_ref[...] + inverse * (
         scaled - unit * jnp.mean(scaled * unit, -1, keepdims=True)
@@ -677,7 +666,7 @@
 
 def mlp_grad_kernel(
     down_rows, main, meta_ref, xt_ref, gy_ref, midt_ref, gg_ref, gu_ref,
-    out_ref, head_ref, tail_ref, mlp_acc, down_acc,
+    out_ref, mlp_acc, down_acc,
 ):
     step = pl.program_id(0)
     core = meta_ref[1]
@@ -710,37 +699,23 @@
     first = pl.multiple_of(core * 64 + step * down_rows, 8)
     out_ref[0, columns * 16 :, :] = down_acc[pl.ds(first, down_rows), :].astype(bf16)
 
-    @pl.when(meta_ref[4 + step] == pl.num_programs(0) // 2)
-    def far():
-        head_ref[...] = out_ref[0, : head_ref.shape[0], :]
-        tail_ref[...] = out_ref[0, head_ref.shape[0] :, :]
-
 
 def mlp_gradients(meta, xt, gy, midt, gg, gu, chips, down_rows, main):
     tokens = gy.shape[0]
     columns = (2 * main + 128) // 128
-    cut = columns * 16
-    rows = cut + down_rows
+    rows = columns * 16 + down_rows
 
     def whole(x):
         return pl.BlockSpec(x.shape, lambda i, m: (0, 0))
 
     return pl.pallas_call(
         lambda *refs: mlp_grad_kernel(down_rows, main, *refs),
-        out_shape=[
-            jax.ShapeDtypeStruct((chips, rows, D), bf16),
-            jax.ShapeDtypeStruct((cut, D), bf16),
-            jax.ShapeDtypeStruct((rows - cut, D), bf16),
-        ],
+        out_shape=jax.ShapeDtypeStruct((chips, rows, D), bf16),
         grid_spec=pltpu.PrefetchScalarGridSpec(
             num_scalar_prefetch=1,
             grid=(chips,),
             in_specs=[whole(x) for x in (xt, gy, midt, gg, gu)],
-            out_specs=[
-                pl.BlockSpec((1, rows, D), lambda i, m: (m[4 + i], 0, 0)),
-                pl.BlockSpec((cut, D), lambda i, m: (0, 0)),
-                pl.BlockSpec((rows - cut, D), lambda i, m: (0, 0)),
-            ],
+            out_specs=pl.BlockSpec((1, rows, D), lambda i, m: (m[4 + i], 0, 0)),
             scratch_shapes=[
                 pltpu.VMEM((D, columns * 128), bf16),
                 pltpu.VMEM((midt.shape[0], D), f32),
@@ -754,22 +729,39 @@
     )(meta, xt, gy, midt, gg, gu)
 
 
-def small_grad_kernel(chips, q_rows, meta_ref, norm_ref, joint_ref, att_ref, ga_ref, *refs):
-    out_refs, acc = refs[:-1], refs[-1]
+def small_grad_kernel(
+    chips, q_rows, rows, meta_ref, norm_ref, joint_ref, att_ref, ga_ref, *refs
+):
+    out_refs, acc, sums_ref = refs[:-2], refs[-2], refs[-1]
     cols = joint_ref.shape[1]
-    acc[:, :cols] = dot_tn(norm_ref[...], joint_ref[...])
+    blocks = joint_ref.shape[0] // (rows + 16)
+    tokens = [joint_ref[b * (rows + 16) : b * (rows + 16) + rows, :] for b in range(blocks)]
+    sums = []
+    for b in range(blocks):
+        found = joint_ref[b * (rows + 16) + rows : (b + 1) * (rows + 16), :].astype(f32)
+        sums.append([found[2 * i : 2 * i + 1] + found[2 * i + 1 : 2 * i + 2] for i in range(3)])
+    sums = [(sums[0][i] + sums[1][i]) + (sums[2][i] + sums[3][i]) for i in range(3)]
+    sums_ref[...] = jnp.zeros_like(sums_ref)
+    sums_ref[:1, :D] = sums[0][:, :D]
+    sums_ref[:1, D : 2 * D] = sums[1][:, :D]
+    sums_ref[:1, 2 * D : 2 * D + cols] = sums[2]
+    acc[:, :cols] = dot_tn(norm_ref[...], jnp.concatenate(tokens, 0))
     acc[:, cols:] = dot_tn(att_ref[...], ga_ref[...])
     first = pl.multiple_of((2 * meta_ref[0] + meta_ref[1]) * q_rows, 16)
     width = acc.shape[1] // chips
+    share = sums_ref.shape[1] // chips
     for out_ref, slot in zip(out_refs, range(chips)):
-        column = pl.multiple_of(meta_ref[12 + slot] * width, 128)
-        block = acc[pl.ds(first, q_rows), pl.ds(column, width)]
+        owner = meta_ref[12 + slot]
+        block = acc[pl.ds(first, q_rows), pl.ds(pl.multiple_of(owner * width, 128), width)]
         tall = jnp.concatenate(
             [block[:, i * 128 : (i + 1) * 128] for i in range(width // 128)], 0
         ).astype(bf16)
-        piece = out_ref.shape[0]
+        piece = out_ref.shape[0] - 16
         for i in range(D // 128):
-            out_ref[:, i * 128 : (i + 1) * 128] = tall[i * piece : (i + 1) * piece]
+            out_ref[:piece, i * 128 : (i + 1) * 128] = tall[i * piece : (i + 1) * piece]
+        vector = sums_ref[:, pl.ds(pl.multiple_of(owner * share, 128), share)]
+        out_ref[piece:, :] = jnp.zeros((16, D), bf16)
+        out_ref[piece:, :share] = jnp.concatenate([vector, vector], 0).astype(bf16)
 
 
 def place_all(meta, slots, pairs, old, sizes):
@@ -781,16 +773,19 @@
     top = columns * 16
     blocks = [x for pair in pairs for x in pair]
     count = len(blocks)
-    piece = blocks[0].shape[0] - top - down_rows
+    piece = blocks[0].shape[0] - top - down_rows - 16
+    share = 3 * 128
     parts = (cols + D) // chips // 128
     keep = [] if old is None else list(old)
 
     def kernel(meta_ref, *refs):
         ins = refs[:count]
-        gate_out, up_out, down_out, joint_out, proj_out, token_ref = refs[
-            count + len(keep) : count + len(keep) + 6
+        gate_out, up_out, down_out, joint_out, proj_out, sums_out, token_ref = refs[
+            count + len(keep) : count + len(keep) + 7
         ]
-        gate_buf, up_buf, down_buf, small_buf, sems, small_sems = refs[count + len(keep) + 6 :]
+        gate_buf, up_buf, down_buf, small_buf, sums_buf, sems, small_sems = refs[
+            count + len(keep) + 7 :
+        ]
         core_zero = meta_ref[1] == 0
         copies = []
 
@@ -822,14 +817,17 @@
                     up_buf[k, :, main : main + 128] = pltpu.roll(jnp.where(left, one, zero), 64, 1)
             owner = meta_ref[12 + slot]
             here = pl.ds(pl.multiple_of(owner * mlp_rows, 8), mlp_rows)
-            send(gate_buf.at[k], gate_out.at[here, :], sems.at[4 * k])
-            send(up_buf.at[k], up_out.at[here, :], sems.at[4 * k + 1])
+            send(gate_buf.at[k], gate_out.at[here, :], sems.at[5 * k])
+            send(up_buf.at[k], up_out.at[here, :], sems.at[5 * k + 1])
+            sums_buf[k] = ins[2 * k][top + piece : top + piece + 16, :share].astype(f32)[:8]
+            here = pl.ds(pl.multiple_of(owner * 8, 8), 8)
+            send(sums_buf.at[k], sums_out.at[here, :], sems.at[5 * k + 4])
             for side in range(2):
                 b = 2 * k + side
                 core = meta_ref[1] if side == 0 else 1 - meta_ref[1]
-                down_buf[b] = ins[b][top + piece :, :].astype(f32)
+                down_buf[b] = ins[b][top + piece + 16 :, :].astype(f32)
                 here = pl.ds(pl.multiple_of((core * chips + owner) * down_rows, 8), down_rows)
-                send(down_buf.at[b], down_out.at[here, :], sems.at[4 * k + 2 + side])
+                send(down_buf.at[b], down_out.at[here, :], sems.at[5 * k + 2 + side])
                 tall = jnp.concatenate(
                     [ins[b][top : top + piece, i * 128 : (i + 1) * 128] for i in range(lanes_out)], 0
                 ).astype(f32)
@@ -872,18 +870,20 @@
             jax.ShapeDtypeStruct((ff_loc, D), f32),
             jax.ShapeDtypeStruct((2 * q_rows, cols), f32),
             jax.ShapeDtypeStruct((2 * q_rows, D), f32),
+            jax.ShapeDtypeStruct((8 * chips, share), f32),
             jax.ShapeDtypeStruct((8, 128), f32),
         ],
         in_specs=[pl.BlockSpec(memory_space=pltpu.SMEM)]
         + [pl.BlockSpec(memory_space=pltpu.VMEM)] * count
         + [anywhere] * len(keep),
-        out_specs=[anywhere] * 5 + [pl.BlockSpec(memory_space=pltpu.VMEM)],
+        out_specs=[anywhere] * 6 + [pl.BlockSpec(memory_space=pltpu.VMEM)],
         scratch_shapes=[
             pltpu.VMEM((len(slots), mlp_rows, ff_loc), f32),
             pltpu.VMEM((len(slots), mlp_rows, ff_loc), f32),
             pltpu.VMEM((count, down_rows, D), f32),
             pltpu.VMEM((count, parts, q_rows, 128), f32),
-            pltpu.SemaphoreType.DMA((4 * len(slots),)),
+            pltpu.VMEM((len(slots), 8, share), f32),
+            pltpu.SemaphoreType.DMA((5 * len(slots),)),
             pltpu.SemaphoreType.DMA((count, parts)),
         ],
         input_output_aliases={1 + count + i: i for i in range(len(keep))},
@@ -892,7 +892,7 @@
             flops=0, bytes_accessed=8 * sum(x.size for x in blocks), transcendentals=0
         ),
     )(meta, *blocks, *keep)
-    return list(result[:5]), result[5]
+    return list(result[:6]), result[6]
 
 
 def place_blocks(blocks, spots, out_shape, old=None):
@@ -951,7 +951,7 @@
     rest = ff_half - main
     width = main + 2 * rest
     first = core * main
-    tiled = 2 * rest == 128 and width % 256 == 0 and chips == 8 and ff_half == chips * RING_ROWS
+    tiled = net.dp == 2 and 2 * rest == 128 and width % 256 == 0 and chips == 8 and ff_half == chips * RING_ROWS
     ring = jnp.arange(chips, dtype=jnp.int32)
     owners_of = (net.pos - ring) % chips
     spots = jnp.concatenate(
@@ -1051,7 +1051,7 @@
         piece = grad_chip[s * rows : (s + 1) * rows].astype(bf16)
         grad_two = grad_two + net.shift(piece, net.dp - s).astype(f32)
 
-    def attention_back(*after):
+    def attention_back():
         grad_hidden, grad_attn_low, grad_gain_two, grad_queries, terms_mine, terms_other = call(
             lambda *refs: backward_kernel(ctx_count, *refs),
             [
@@ -1065,9 +1065,8 @@
             [
                 meta, grad_two, hidden, cotangent[0], gain_two, w_out_full, spread, keys, values, lse,
                 attended,
-            ] + list(after),
+            ],
             smem=1,
-            loose=len(after),
             scratch=[
                 pltpu.VMEM(padded, bf16),
                 pltpu.VMEM(padded, f32),
@@ -1076,42 +1075,58 @@
             ],
             flops=20 * KH * part_rows * total_keys * 128,
         )
-        pair_sums = call(
-            pair_kernel,
-            [jax.ShapeDtypeStruct((rows, 2 * WIDTH_K), f32)]
-            + [jax.ShapeDtypeStruct((rows, 2 * WIDTH_K), bf16)] * (chips - 1),
-            [terms_mine, net.swap(terms_other)],
-        )
-        grad_pairs = net.ring_parts(pair_sums)
-        grad_joint_low, grad_input, grad_gain_one, grad_bias = call(
-            finish_kernel,
-            [
-                jax.ShapeDtypeStruct((rows, 1152), bf16),
-                jax.ShapeDtypeStruct((rows, D), f32),
-                jax.ShapeDtypeStruct((1, D), f32),
-                jax.ShapeDtypeStruct((1, 1152), f32),
-            ],
-            [grad_queries, x, gain_one, w_qkv_full, cosine, sine, grad_hidden] + grad_pairs,
-            flops=2 * rows * D * 1152,
-        )
-        return (
-            grad_hidden, grad_attn_low, grad_gain_two, grad_joint_low, grad_input, grad_gain_one,
-            grad_bias,
-        )
+        swapped_terms = net.swap(terms_other)
+
+        def finish(wait_pairs=()):
+            pair_sums = call(
+                pair_kernel,
+                [jax.ShapeDtypeStruct((rows, 2 * WIDTH_K), f32)]
+                + [jax.ShapeDtypeStruct((rows, 2 * WIDTH_K), bf16)] * (chips - 1),
+                [terms_mine, swapped_terms] + list(wait_pairs),
+                loose=len(wait_pairs),
+            )
+            grad_pairs = net.ring_parts(pair_sums)
+
+            def last(wait_finish=()):
+                joint, grad_input, grad_gain_one, grad_bias = call(
+                    finish_kernel,
+                    [
+                        jax.ShapeDtypeStruct((rows + 16, 1152), bf16),
+                        jax.ShapeDtypeStruct((rows, D), f32),
+                        jax.ShapeDtypeStruct((1, D), f32),
+                        jax.ShapeDtypeStruct((1, 1152), f32),
+                    ],
+                    [grad_queries, x, gain_one, w_qkv_full, cosine, sine, grad_hidden, grad_gain_two]
+                    + grad_pairs
+                    + list(wait_finish),
+                    flops=2 * rows * D * 1152,
+                    loose=len(wait_finish),
+                )
+                return (grad_attn_low, grad_gain_two, joint, grad_input, grad_gain_one, grad_bias)
+
+            return last
+
+        return finish
 
     found = []
+    steps = [attention_back()]
     if tiled:
 
-        def middle(*after):
-            found.extend(attention_back(*after))
-            return found[3]
-
-        terms, head, tail = mlp_gradients(
+        def pairs_stage(*blocks):
+            steps.append(steps[0](blocks))
+
+        def finish_stage(*blocks):
+            found.extend(steps[1](blocks))
+
+        def small_stage(*blocks):
+            found.append(blocks)
+
+        terms = mlp_gradients(
             spots, x_turned, grad_out_group, mid_turned, gate_low, up_low, chips, down_rows, main
         )
-        sum_mlp, sum_down = net.ring_sum(
-            head, tail, terms, terms.shape[1] - down_rows, middle
-        )
+        fwd, back = net.ring_sum(terms, [pairs_stage, finish_stage, small_stage])
+        wait_small = found.pop()
+        sum_mlp, sum_down = ring_end(fwd, back, terms, terms.shape[1] - down_rows)
     else:
         part_down = jnp.einsum(
             "tf,td->fd", middle, grad_out_group, preferred_element_type=f32
@@ -1147,9 +1162,8 @@
 
         sum_mlp = net.ring_scatter([mlp_chunk(s) for s in range(chips)]).astype(bf16)
         sum_mlp = lax.optimization_barrier(sum_mlp)
-        found.extend(attention_back())
-    grad_hidden, grad_attn_low, grad_gain_two, grad_joint_low, grad_input = found[:5]
-    grad_gain_one, grad_bias = found[5:]
+        found.extend(steps[0]()())
+    grad_attn_low, grad_gain_two, grad_joint_low, grad_input, grad_gain_one, grad_bias = found
 
     out_sum = mlp_chip[:rows]
     sent = jnp.concatenate([attended_low, grad_attn_low], 0)
@@ -1169,26 +1183,30 @@
 
     q_rows = w_qkv.shape[0] // 2
     qkv_cols = w_qkv.shape[1]
+    if not tiled:
+        grad_joint_low = grad_joint_low[:rows]
     joint_group = net.group_gather(grad_joint_low)
     if tiled:
         piece = q_rows * (qkv_cols + D) // chips // D
         terms_small = call(
-            lambda *refs: small_grad_kernel(chips, q_rows, *refs),
-            [jax.ShapeDtypeStruct((piece, D), bf16)] * chips,
-            [spots, normed_one_group, joint_group, attended_group, grad_attn_group],
+            lambda *refs: small_grad_kernel(chips, q_rows, rows, *refs),
+            [jax.ShapeDtypeStruct((piece + 16, D), bf16)] * chips,
+            [spots, normed_one_group, joint_group, attended_group, grad_attn_group, *wait_small],
             smem=1,
-            scratch=[pltpu.VMEM((D, qkv_cols + D), f32)],
+            loose=len(wait_small),
+            scratch=[pltpu.VMEM((D, qkv_cols + D), f32), pltpu.VMEM((8, 3 * 128 * chips), f32)],
             flops=4 * chip_rows * D * (qkv_cols + D),
         )
         block = call(
             block_kernel,
-            [jax.ShapeDtypeStruct((sum_mlp.shape[0] + piece + down_rows, D), bf16)],
+            [jax.ShapeDtypeStruct((sum_mlp.shape[0] + piece + 16 + down_rows, D), bf16)],
             [sum_mlp, sum_down] + net.ring_parts(terms_small),
         )[0]
         sizes = (main, ff_loc, q_rows, qkv_cols, down_rows, chips)
-        grad_gate, grad_up, grad_down, grad_joint, grad_out_proj = net.gather_placed(
+        grad_gate, grad_up, grad_down, grad_joint, grad_out_proj, sums = net.gather_placed(
             block, lambda slots, pairs, old: place_all(spots, slots, pairs, old, sizes)
         )
+        small = sums.reshape(chips, 8, 384)[:, 0].reshape(-1)[: 2 * D + qkv_cols]
     else:
         q_first = net.d * (2 * q_rows) + core * q_rows
         group_rows = 2 * net.dp * rows
@@ -1260,8 +1278,7 @@
             )
 
         grad_joint, grad_out_proj = grad_small[:, :qkv_cols], grad_small[:, qkv_cols:]
-
-    small = net.total(jnp.concatenate([grad_gain_one, grad_gain_two, grad_bias], 1))[0]
+        small = net.total(jnp.concatenate([grad_gain_one, grad_gain_two, grad_bias], 1))[0]
     return (
         output[None],
         grad_input[None],

time: 388 us -> 365 us (0.941)
  Pallas kernels: 118 us -> 102 us
  waiting for transfers between devices: 150 us -> 139 us
  other arithmetic: 16.7 us -> 26.2 us
  starting transfers between devices: 62.7 us -> 54.7 us
    pallas_call x6 -> x0, Pallas kernels: 18.6 us -> none  [ring_add(): pl.pallas_call(kernel, out_shape=jax.ShapeDtypeStruct((rows, columns), bf...]
    ppermute x4 -> x0, waiting for transfers between devices: 9.07 us -> none  [the longest x3 7.66 us: total(): x = x + lax.ppermute(x, 'ctx', [(i, i ^ 2 * bit) for i in range(self.ctx)])]
    ppermute x4 -> x0, starting transfers between devices: 6.1 us -> none  [the longest x3 4.5 us: total(): x = x + lax.ppermute(x, 'ctx', [(i, i ^ 2 * bit) for i in range(self.ctx)])]
    convert_element_type x0 -> x3, other arithmetic: none -> 4.78 us  [add(): return (got.astype(f32) + terms[slot].astype(f32)).astype(bf16)]
    unnamed x126 -> x107, local copies, waits for them, and re-layouts: 18.8 us -> 15.7 us
    pallas_call x7 -> x8, Pallas kernels: 42.2 us -> 44.7 us  [call(): pl.pallas_call(body, out_shape=list(outs), in_specs=specs, out_specs=[pl....]
    ppermute x40 -> x39, waiting for transfers between devices: 115 us -> 113 us  [hop(): return lax.ppermute(x, 'ctx', perm)]
    ppermute x40 -> x39, starting transfers between devices: 41.6 us -> 41.2 us  [hop(): return lax.ppermute(x, 'ctx', perm)]
  transfers between devices with their start and end apart: 69 -> 63, of which waited for: 44 -> 37; matrix products, arithmetic and copies ran while one was open for 8% -> 12% of each run, Pallas kernels for 20% -> 18%
where the time goes in v6:
time: 365 us; the launch traced here: 363 us
  waiting for transfers between devices  139 us (38%)
  Pallas kernels  102 us (28%)
  starting transfers between devices  54.7 us (15%)
  local copies, waits for them, and re-layouts  40.5 us (11%)
  other arithmetic  26.2 us (7%)
    ppermute x39, waiting for transfers between devices, hop(): return lax.ppermute(x, 'ctx', perm)  113 us
    pallas_call x8, Pallas kernels, call(): pl.pallas_call(body, out_shape=list(outs), in_specs=specs, out_specs=[pl....  44.7 us
    ppermute x39, starting transfers between devices, hop(): return lax.ppermute(x, 'ctx', perm)  41.2 us
    pallas_call x5, Pallas kernels, place_all(): pl.pallas_call(kernel, out_shape=[jax.ShapeDtypeStruct((D, ff_loc), f32),...  26.2 us
    ppermute x7, waiting for transfers between devices, shift(): return lax.ppermute(x, 'dp', [(i, (i + step) % n) for i in range(n)])  20.5 us
    pallas_call x1, Pallas kernels, feed_forward(): pl.pallas_call(lambda *refs: mlp_kernel(half, *refs), out_shape=[jax.Shap...  16.3 us
    unnamed x107, local copies, waits for them, and re-layouts  15.7 us
    pallas_call x1, Pallas kernels, mlp_gradients(): pl.pallas_call(lambda *refs: mlp_grad_kernel(down_rows, main, *refs), out...  11.7 us
  transfers between devices with their start and end apart: 63, of which 37 were waited for; matrix products, arithmetic and copies ran while one was open for 12% of the time, Pallas kernels for 18%

profile of v6, /device:TPU:0, one launch (start us, length us, event | category | flops | bytes accessed | tf_op | source)
XLA Modules:
  0.0 363.4 jit_solution(9423529905567057206)
XLA Ops:
  1.8 3.0 collective-permute-start
  12.1 4.6 %collective-permute-done = bf16[224,1152]{1,0:T(8,128)(2,1)S(1)} collective-permute-done((bf16[224,1152]{1,0:T(8,128)(2,1)S(1)}, bf16[224,1152]{1,0:T(8,128)(2,1)S(1)}, u32[]{:S(2)}, u32[]{:S(2)}) %collective-permute-start) | collective-permute-done | bytes 516128 | tf_op jit(solution)/shard_map/ppermute | solution.py:54
  20.5 3.2 shard_map.195
  49.2 10.3 %shard_map.196 = (bf16[128,896]{1,0:T(8,128)(2,1)}, f32[2,896,128]{2,1,0:T(8,128)}, f32[2,2,8,448]{3,2,1,0:T(8,128)}, bf16[2,896,128]{2,1,0:T(8,128)(2,1)}, bf16...) custom-call(s32[17]{0:T(128)} %pad_add_fusion.refs_0_, ...), custom_call_target="tpu_custom_call" | custom-call | flops 1879048192 | bytes 6516292 | tf_op jit(solution)/shard_map/pallas_call | solution.py:216
  62.5 5.2 %collective-permute-done.13 = bf16[128,896]{1,0:T(8,128)(2,1)S(1)} collective-permute-done((bf16[128,896]{1,0:T(8,128)(2,1)}, bf16[128,896]{1,0:T(8,128)(2,1)S(1)}, u32[]{:S(2)}, u32[]{:S(2)}) %collective-permute-start.13) | collective-permute-done | bytes 229408 | tf_op jit(solution)/shard_map/ppermute | solution.py:54
  71.5 16.3 %shard_map.197 = (bf16[896,512]{1,0:T(8,128)(2,1)}, bf16[1280,512]{1,0:T(8,128)(2,1)}, bf16[512,1280]{1,0:T(8,128)(2,1)}, bf16[512,1280]{1,0:T(8,128)(2,1)}, f32...) custom-call(s32[20]{0:T(128)} %concatenate.84.refs_0_.meta_ref, ...), custom_call_target="tpu_custom_call" | custom-call | flops 7046430720 | bytes 6881280 | tf_op jit(solution)/shard_map/pallas_call | solution.py:632
  88.1 11.7 %shard_map.199.term_ref = bf16[8,456,896]{2,1,0:T(8,128)(2,1)} custom-call(s32[20]{0:T(128)} %concatenate.84.refs_0_.meta_ref, bf16[896,512]{1,0:T(8,128)(2,1)} %get-tuple-element.120.refs_1_, bf16[512,896]{1,0:T(8,128)(2,1)} %get-tuple-element.195.refs_2_, bf16[1280,512]{1,0:T(8,128)(2,1)} %get-tuple-element.121.refs_3_, ...), custom_call_target="tpu_custom_call" | custom-call | flops 3523215360 | bytes 13074432 | tf_op jit(solution)/shard_map/pallas_call | solution.py:711
  109.0 13.8 %collective-permute-done.21 = bf16[456,896]{1,0:T(8,128)(2,1)S(1)} collective-permute-done((bf16[456,896]{1,0:T(8,128)(2,1)S(1)}, bf16[456,896]{1,0:T(8,128)(2,1)S(1)}, u32[]{:S(2)}, u32[]{:S(2)}) %collective-permute-start.21) | collective-permute-done | bytes 817184 | tf_op jit(solution)/shard_map/ppermute | solution.py:62
  125.7 14.9 %shard_map.198 = (f32[128,896]{1,0:T(8,128)}, bf16[128,896]{1,0:T(8,128)(2,1)}, f32[1,896]{1,0:T(1,128)}, f32[128,896]{1,0:T(8,128)}, f32[1024,256]{1,0:T(8,128)}, /*index=5*/bf16[1024,256]{1,0:T(8,128)(2,1)}) custom-call(s32[17]{0:T(128)} %pad_add_fusion.refs_0_, f32[128,896]{1,0:T(8,128)} %slice_add_fusion.refs_1_, f32[128,896]{1,0:T(8,128)} %get-tuple-element.101.refs_2_, ...), custom_call_target="tpu_custom_call" | custom-call | flops 4697620480 | bytes 7961668 | tf_op jit(solution)/shard_map/pallas_call | solution.py:216
  142.9 2.9 fusion.2
  159.7 12.8 %collective-permute-done.27 = bf16[64,256]{1,0:T(8,128)(2,1)S(1)} collective-permute-done((bf16[64,256]{1,0:T(8,128)(2,1)S(1)}, bf16[64,256]{1,0:T(8,128)(2,1)S(1)}, u32[]{:S(2)}, u32[]{:S(2)}) %collective-permute-start.27) | collective-permute-done | bytes 32800 | tf_op jit(solution)/shard_map/ppermute | solution.py:62
  186.2 3.8 %shard_map.201 = (bf16[144,1152]{1,0:T(8,128)(2,1)}, f32[128,896]{1,0:T(8,128)}, f32[1,896]{1,0:T(1,128)}, f32[1,1152]{1,0:T(1,128)}) custom-call(f32[128,896]{1,0:T(8,128)} %get-tuple-element.115.refs_0_, bf16[128,896]{1,0:T(8,128)(2,1)} %bitcast.56, f32[1,896]{1,0:T(1,128)} %broadcast_in_dim.22.refs_1_.refs_2_, ...), custom_call_target="tpu_custom_call" | custom-call | flops 264241152 | bytes 6044672 | tf_op jit(solution)/shard_map/pallas_call | solution.py:216
  190.6 9.3 %collective-permute-done.36 = bf16[144,1152]{1,0:T(8,128)(2,1)S(1)} collective-permute-done((bf16[144,1152]{1,0:T(8,128)(2,1)}, bf16[144,1152]{1,0:T(8,128)(2,1)S(1)}, u32[]{:S(2)}, u32[]{:S(2)}) %collective-permute-start.36) | collective-permute-done | bytes 331808 | tf_op jit(solution)/shard_map/ppermute | solution.py:54
  205.0 5.6 %shard_map.203 = (bf16[80,896]{1,0:T(8,128)(2,1)}, bf16[80,896]{1,0:T(8,128)(2,1)}, bf16[80,896]{1,0:T(8,128)(2,1)}, bf16[80,896]{1,0:T(8,128)(2,1)}, bf16[80,89...) custom-call(s32[20]{0:T(128)} %concatenate.84.refs_0_.meta_ref, ...), custom_call_target="tpu_custom_call" | custom-call | flops 1879048192 | bytes 6043728 | tf_op jit(solution)/shard_map/pallas_call | solution.py:216
  220.2 16.3 %collective-permute-done.43 = bf16[40,896]{1,0:T(8,128)(2,1)S(1)} collective-permute-done((bf16[40,896]{1,0:T(8,128)(2,1)S(1)}, bf16[40,896]{1,0:T(8,128)(2,1)S(1)}, u32[]{:S(2)}, u32[]{:S(2)}) %collective-permute-start.43) | collective-permute-done | bytes 71712 | tf_op jit(solution)/shard_map/ppermute | solution.py:62
  260.2 4.1 %shard_map.205 = (f32[896,2432]{1,0:T(8,128)}, f32[896,2432]{1,0:T(8,128)}, f32[2432,896]{1,0:T(8,128)}, f32[448,1152]{1,0:T(8,128)}, f32[448,896]{1,0:T(8,128)}, /*index=5*/f32[64,384]{1,0:T(8,128)}, f32[8,128]{1,0:T(8,128)}) custom-call(s32[20]{0:T(128)} %concatenate.84.refs_0_.meta_ref, bf16[536,896]{1,0:T(8,128)(2,1)} %shard_map.204.refs_0_, ...), custom_call_target="tpu_custom_call" | custom-call | bytes 7684096 | tf_op jit(solution)/shard_map/pallas_call | solution.py:865
  264.4 16.1 %collective-permute-done.48.refs_1_ = bf16[536,896]{1,0:T(8,128)(2,1)S(1)} collective-permute-done((bf16[536,896]{1,0:T(8,128)(2,1)}, bf16[536,896]{1,0:T(8,128)(2,1)S(1)}, u32[]{:S(2)}, u32[]{:S(2)}) %collective-permute-start.48) | collective-permute-done | bytes 960544 | tf_op jit(solution)/shard_map/ppermute | solution.py:62
  287.7 6.0 %shard_map.207 = (f32[896,2432]{1,0:T(8,128)}, f32[896,2432]{1,0:T(8,128)}, f32[2432,896]{1,0:T(8,128)}, f32[448,1152]{1,0:T(8,128)}, f32[448,896]{1,0:T(8,128)}, /*index=5*/f32[64,384]{1,0:T(8,128)}, f32[8,128]{1,0:T(8,128)}) custom-call(s32[20]{0:T(128)} %concatenate.84.refs_0_.meta_ref, ...), custom_call_target="tpu_custom_call", output_to_operand_aliasing={{0}: (5, {}), {1}: (6, {}), {2}: (7, {}), {3}: (8, {}), {4}... | custom-call | bytes 15368192 | tf_op jit(solution)/shard_map/pallas_call | solution.py:865
  293.7 12.8 %collective-permute-done.52.refs_1_ = bf16[536,896]{1,0:T(8,128)(2,1)S(1)} collective-permute-done((bf16[536,896]{1,0:T(8,128)(2,1)}, bf16[536,896]{1,0:T(8,128)(2,1)S(1)}, u32[]{:S(2)}, u32[]{:S(2)}) %collective-permute-start.52) | collective-permute-done | bytes 960544 | tf_op jit(solution)/shard_map/ppermute | solution.py:62
  313.6 6.0 %shard_map.209 = (f32[896,2432]{1,0:T(8,128)}, f32[896,2432]{1,0:T(8,128)}, f32[2432,896]{1,0:T(8,128)}, f32[448,1152]{1,0:T(8,128)}, f32[448,896]{1,0:T(8,128)}, /*index=5*/f32[64,384]{1,0:T(8,128)}, f32[8,128]{1,0:T(8,128)}) custom-call(s32[20]{0:T(128)} %concatenate.84.refs_0_.meta_ref, ...), custom_call_target="tpu_custom_call", output_to_operand_aliasing={{0}: (5, {}), {1}: (6, {}), {2}: (7, {}), {3}: (8, {}), {4}... | custom-call | bytes 15368192 | tf_op jit(solution)/shard_map/pallas_call | solution.py:865
  319.6 12.8 %collective-permute-done.56.refs_1_ = bf16[536,896]{1,0:T(8,128)(2,1)S(1)} collective-permute-done((bf16[536,896]{1,0:T(8,128)(2,1)}, bf16[536,896]{1,0:T(8,128)(2,1)S(1)}, u32[]{:S(2)}, u32[]{:S(2)}) %collective-permute-start.56) | collective-permute-done | bytes 960544 | tf_op jit(solution)/shard_map/ppermute | solution.py:62
  340.5 6.0 %shard_map.211 = (f32[896,2432]{1,0:T(8,128)}, f32[896,2432]{1,0:T(8,128)}, f32[2432,896]{1,0:T(8,128)}, f32[448,1152]{1,0:T(8,128)}, f32[448,896]{1,0:T(8,128)}, /*index=5*/f32[64,384]{1,0:T(8,128)}, f32[8,128]{1,0:T(8,128)}) custom-call(s32[20]{0:T(128)} %concatenate.84.refs_0_.meta_ref, ...), custom_call_target="tpu_custom_call", output_to_operand_aliasing={{0}: (5, {}), {1}: (6, {}), {2}: (7, {}), {3}: (8, {}), {4}... | custom-call | bytes 15368192 | tf_op jit(solution)/shard_map/pallas_call | solution.py:865
  346.5 3.8 %collective-permute-done.59.refs_1_ = bf16[264,896]{1,0:T(8,128)(2,1)S(1)} collective-permute-done((bf16[264,896]{1,0:T(8,128)(2,1)S(1)}, bf16[264,896]{1,0:T(8,128)(2,1)S(1)}, u32[]{:S(2)}, u32[]{:S(2)}) %collective-permute-start.59) | collective-permute-done | bytes 473120 | tf_op jit(solution)/shard_map/ppermute | solution.py:62
  357.2 4.1 %shard_map.213 = (f32[896,2432]{1,0:T(8,128)}, f32[896,2432]{1,0:T(8,128)}, f32[2432,896]{1,0:T(8,128)}, f32[448,1152]{1,0:T(8,128)}, f32[448,896]{1,0:T(8,128)}, /*index=5*/f32[64,384]{1,0:T(8,128)}, f32[8,128]{1,0:T(8,128)}) custom-call(s32[20]{0:T(128)} %concatenate.84.refs_0_.meta_ref, ...), custom_call_target="tpu_custom_call", output_to_operand_aliasing={{0}: (3, {}), {1}: (4, {}), {2}: (5, {}), {3}: (6, {}), {4}... | custom-call | bytes 7684096 | tf_op jit(solution)/shard_map/pallas_call | solution.py:865
  (303 shorter events, 156.6 us)
Async XLA Ops:
  25.8 18.6 %collective-permute-start.11 = (bf16[224,896]{1,0:T(8,128)(2,1)S(1)}, bf16[224,896]{1,0:T(8,128)(2,1)S(1)}, u32[]{:S(2)}, u32[]{:S(2)}) collective-permute-start(bf16[224,896]{1,0:T(8,128)(2,1)S(1)} %constant_dynamic-slice_fusion), channel_id=1, source_target_pairs={{0,16},{16,0},{1,17},{17,1},{2,18},{18,2},{3,19},{19,3},{4,20},{20... | collective-permute-start | bytes 1204232 | tf_op jit(solution)/shard_map/ppermute | solution.py:54
  28.6 18.0 %collective-permute-start.15 = (bf16[128,1792]{1,0:T(8,128)(2,1)S(1)}, bf16[128,1792]{1,0:T(8,128)(2,1)S(1)}, u32[]{:S(2)}, u32[]{:S(2)}) collective-permute-start(bf16[128,1792]{1,0:T(8,128)(2,1)S(1)} %constant_dynamic-update-slice_fusion.9), channel_id=1, source_target_pairs={{0,16},{16,0},{1,17},{17,1},{2,18},{18,2},{3,19},{19,3},{4,20},{20... | collective-permute-start | bytes 1376264 | tf_op jit(solution)/shard_map/ppermute | solution.py:54
  46.6 22.1 %collective-permute-start.16 = (bf16[256,1792]{1,0:T(8,128)(2,1)S(1)}, bf16[256,1792]{1,0:T(8,128)(2,1)S(1)}, u32[]{:S(2)}, u32[]{:S(2)}) collective-permute-start(bf16[256,1792]{1,0:T(8,128)(2,1)S(1)} %pad_maximum_fusion.7), channel_id=1, source_target_pairs={{0,1},{1,0},{2,3},{3,2},{4,5},{5,4},{6,7},{7,6},{8,9},{9,8},{10,11... | collective-permute-start | bytes 2752520 | tf_op jit(solution)/shard_map/ppermute | solution.py:50
  87.8 16.6 %collective-permute-start.17 = (bf16[512,896]{1,0:T(8,128)(2,1)}, bf16[512,896]{1,0:T(8,128)(2,1)S(1)}, u32[]{:S(2)}, u32[]{:S(2)}) collective-permute-start(bf16[512,896]{1,0:T(8,128)(2,1)} %get-tuple-element.106), channel_id=1, source_target_pairs={{0,1},{1,0},{2,3},{3,2},{4,5},{5,4},{6,7},{7,6},{8,9},{9,8},{10,11... | collective-permute-start | bytes 2752520 | tf_op jit(solution)/shard_map/ppermute | solution.py:50
  102.4 20.4 %collective-permute-start.21 = (bf16[456,896]{1,0:T(8,128)(2,1)S(1)}, bf16[456,896]{1,0:T(8,128)(2,1)S(1)}, u32[]{:S(2)}, u32[]{:S(2)}) collective-permute-start(bf16[456,896]{1,0:T(8,128)(2,1)S(1)} %get-tuple-element.189), channel_id=1, source_target_pairs={{0,4},{1,5},{4,8},{5,9},{8,12},{9,13},{12,14},{13,15},{14,10},{15,... | collective-permute-start | bytes 2451464 | tf_op jit(solution)/shard_map/ppermute | solution.py:62
  104.2 37.3 %collective-permute-start.22 = (bf16[456,896]{1,0:T(8,128)(2,1)}, bf16[456,896]{1,0:T(8,128)(2,1)}, u32[]{:S(2)}, u32[]{:S(2)}) collective-permute-start(bf16[456,896]{1,0:T(8,128)(2,1)} %get-tuple-element.188), channel_id=1, source_target_pairs={{0,2},{1,3},{4,0},{5,1},{8,4},{9,5},{12,8},{13,9},{14,12},{15,13},... | collective-permute-start | bytes 2451464 | tf_op jit(solution)/shard_map/ppermute | solution.py:62
  107.3 17.6 %collective-permute-start.18 = (bf16[128,896]{1,0:T(8,128)(2,1)S(1)}, bf16[128,896]{1,0:T(8,128)(2,1)S(1)}, u32[]{:S(2)}, u32[]{:S(2)}) collective-permute-start(bf16[128,896]{1,0:T(8,128)(2,1)S(1)} %slice.223), channel_id=1, source_target_pairs={{0,16},{16,0},{1,17},{17,1},{2,18},{18,2},{3,19},{19,3},{4,20},{20... | collective-permute-start | bytes 688136 | tf_op jit(solution)/shard_map/ppermute | solution.py:54
  123.0 19.9 %collective-permute-start.31 = (bf16[456,896]{1,0:T(8,128)(2,1)S(1)}, bf16[456,896]{1,0:T(8,128)(2,1)}, u32[]{:S(2)}, u32[]{:S(2)}) collective-permute-start(bf16[456,896]{1,0:T(8,128)(2,1)S(1)} %fusion.4.refs_2_), channel_id=1, source_target_pairs={{0,4},{1,5},{4,8},{5,9},{8,12},{9,13},{12,14},{13,15},{14,10},{15,... | collective-permute-start | bytes 2451464 | tf_op jit(solution)/shard_map/ppermute | solution.py:62
  151.7 30.5 %collective-permute-start.19 = (bf16[384,896]{1,0:T(8,128)(2,1)S(1)}, bf16[384,896]{1,0:T(8,128)(2,1)S(1)}, u32[]{:S(2)}, u32[]{:S(2)}) collective-permute-start(bf16[384,896]{1,0:T(8,128)(2,1)S(1)} %pad_maximum_fusion.10), channel_id=1, source_target_pairs={{0,16},{16,0},{1,17},{17,1},{2,18},{18,2},{3,19},{19,3},{4,20},{20... | collective-permute-start | bytes 2064392 | tf_op jit(solution)/shard_map/ppermute | solution.py:54
  153.2 30.8 %collective-permute-start.32 = (bf16[456,896]{1,0:T(8,128)(2,1)S(1)}, bf16[456,896]{1,0:T(8,128)(2,1)S(1)}, u32[]{:S(2)}, u32[]{:S(2)}) collective-permute-start(bf16[456,896]{1,0:T(8,128)(2,1)S(1)} %copy-done.7), channel_id=1, source_target_pairs={{0,2},{1,3},{4,0},{5,1},{8,4},{9,5},{12,8},{13,9},{14,12},{15,13},... | collective-permute-start | bytes 2451464 | tf_op jit(solution)/shard_map/ppermute | solution.py:62
  153.7 30.4 %collective-permute-start.33 = (bf16[456,896]{1,0:T(8,128)(2,1)}, bf16[456,896]{1,0:T(8,128)(2,1)S(1)}, u32[]{:S(2)}, u32[]{:S(2)}) collective-permute-start(bf16[456,896]{1,0:T(8,128)(2,1)} %get-tuple-element.186.refs_11_), channel_id=1, source_target_pairs={{0,4},{1,5},{4,8},{5,9},{8,12},{9,13},{12,14},{13,15},{14,10},{15,... | collective-permute-start | bytes 2451464 | tf_op jit(solution)/shard_map/ppermute | solution.py:62
  156.0 16.4 %collective-permute-start.27 = (bf16[64,256]{1,0:T(8,128)(2,1)S(1)}, bf16[64,256]{1,0:T(8,128)(2,1)S(1)}, u32[]{:S(2)}, u32[]{:S(2)}) collective-permute-start(bf16[64,256]{1,0:T(8,128)(2,1)S(1)} %get-tuple-element.206), channel_id=1, source_target_pairs={{0,2},{1,3},{4,0},{5,1},{8,4},{9,5},{12,8},{13,9},{14,12},{15,13},... | collective-permute-start | bytes 98312 | tf_op jit(solution)/shard_map/ppermute | solution.py:62
  158.0 15.6 %collective-permute-start.24 = (bf16[128,256]{1,0:T(8,128)(2,1)S(1)}, bf16[128,256]{1,0:T(8,128)(2,1)S(1)}, u32[]{:S(2)}, u32[]{:S(2)}) collective-permute-start(bf16[128,256]{1,0:T(8,128)(2,1)S(1)} %pad_maximum_fusion.15), channel_id=1, source_target_pairs={{0,4},{1,5},{4,8},{5,9},{8,12},{9,13},{12,14},{13,15},{14,10},{15,... | collective-permute-start | bytes 196616 | tf_op jit(solution)/shard_map/ppermute | solution.py:62
  184.0 17.0 %collective-permute-start.38 = (bf16[512,896]{1,0:T(8,128)(2,1)}, bf16[512,896]{1,0:T(8,128)(2,1)}, u32[]{:S(2)}, u32[]{:S(2)}) collective-permute-start(bf16[512,896]{1,0:T(8,128)(2,1)} %pad_maximum_fusion.8), channel_id=1, source_target_pairs={{0,1},{1,0},{2,3},{3,2},{4,5},{5,4},{6,7},{7,6},{8,9},{9,8},{10,11... | collective-permute-start | bytes 2752520 | tf_op jit(solution)/shard_map/ppermute | solution.py:50
  213.4 35.5 %collective-permute-start.34 = (bf16[456,896]{1,0:T(8,128)(2,1)S(1)}, bf16[456,896]{1,0:T(8,128)(2,1)S(1)}, u32[]{:S(2)}, u32[]{:S(2)}) collective-permute-start(bf16[456,896]{1,0:T(8,128)(2,1)S(1)} %copy-done.30), channel_id=1, source_target_pairs={{0,4},{1,5},{4,8},{5,9},{8,12},{9,13},{12,14},{13,15},{14,10},{15,... | collective-permute-start | bytes 2451464 | tf_op jit(solution)/shard_map/ppermute | solution.py:62
  215.0 33.9 %collective-permute-start.35 = (bf16[456,896]{1,0:T(8,128)(2,1)S(1)}, bf16[456,896]{1,0:T(8,128)(2,1)S(1)}, u32[]{:S(2)}, u32[]{:S(2)}) collective-permute-start(bf16[456,896]{1,0:T(8,128)(2,1)S(1)} %copy-done.9), channel_id=1, source_target_pairs={{0,2},{1,3},{4,0},{5,1},{8,4},{9,5},{12,8},{13,9},{14,12},{15,13},... | collective-permute-start | bytes 2451464 | tf_op jit(solution)/shard_map/ppermute | solution.py:62
  216.3 20.2 %collective-permute-start.43 = (bf16[40,896]{1,0:T(8,128)(2,1)S(1)}, bf16[40,896]{1,0:T(8,128)(2,1)S(1)}, u32[]{:S(2)}, u32[]{:S(2)}) collective-permute-start(bf16[40,896]{1,0:T(8,128)(2,1)S(1)} %get-tuple-element.204), channel_id=1, source_target_pairs={{0,2},{1,3},{4,0},{5,1},{8,4},{9,5},{12,8},{13,9},{14,12},{15,13},... | collective-permute-start | bytes 215048 | tf_op jit(solution)/shard_map/ppermute | solution.py:62
  218.4 19.5 %collective-permute-start.40 = (bf16[80,896]{1,0:T(8,128)(2,1)S(1)}, bf16[80,896]{1,0:T(8,128)(2,1)S(1)}, u32[]{:S(2)}, u32[]{:S(2)}) collective-permute-start(bf16[80,896]{1,0:T(8,128)(2,1)S(1)} %pad_maximum_fusion.13), channel_id=1, source_target_pairs={{0,4},{1,5},{4,8},{5,9},{8,12},{9,13},{12,14},{13,15},{14,10},{15,... | collective-permute-start | bytes 430088 | tf_op jit(solution)/shard_map/ppermute | solution.py:62
  256.5 23.9 %collective-permute-start.48 = (bf16[536,896]{1,0:T(8,128)(2,1)}, bf16[536,896]{1,0:T(8,128)(2,1)S(1)}, u32[]{:S(2)}, u32[]{:S(2)}) collective-permute-start(bf16[536,896]{1,0:T(8,128)(2,1)} %shard_map.204.refs_0_), channel_id=1, source_target_pairs={{0,4},{1,5},{4,8},{5,9},{8,12},{9,13},{12,14},{13,15},{14,10},{15,... | collective-permute-start | bytes 2881544 | tf_op jit(solution)/shard_map/ppermute | solution.py:62
  258.0 23.6 %collective-permute-start.49 = (bf16[536,896]{1,0:T(8,128)(2,1)}, bf16[536,896]{1,0:T(8,128)(2,1)S(1)}, u32[]{:S(2)}, u32[]{:S(2)}) collective-permute-start(bf16[536,896]{1,0:T(8,128)(2,1)} %shard_map.204.refs_0_), channel_id=1, source_target_pairs={{0,2},{1,3},{4,0},{5,1},{8,4},{9,5},{12,8},{13,9},{14,12},{15,13},... | collective-permute-start | bytes 2881544 | tf_op jit(solution)/shard_map/ppermute | solution.py:62
  283.1 23.4 %collective-permute-start.52 = (bf16[536,896]{1,0:T(8,128)(2,1)}, bf16[536,896]{1,0:T(8,128)(2,1)S(1)}, u32[]{:S(2)}, u32[]{:S(2)}) collective-permute-start(bf16[536,896]{1,0:T(8,128)(2,1)} %get-tuple-element.145.refs_0_), channel_id=1, source_target_pairs={{0,4},{1,5},{4,8},{5,9},{8,12},{9,13},{12,14},{13,15},{14,10},{15,... | collective-permute-start | bytes 2881544 | tf_op jit(solution)/shard_map/ppermute | solution.py:62
  284.5 23.1 %collective-permute-start.53 = (bf16[536,896]{1,0:T(8,128)(2,1)}, bf16[536,896]{1,0:T(8,128)(2,1)S(1)}, u32[]{:S(2)}, u32[]{:S(2)}) collective-permute-start(bf16[536,896]{1,0:T(8,128)(2,1)} %get-tuple-element.146.refs_2_), channel_id=1, source_target_pairs={{0,2},{1,3},{4,0},{5,1},{8,4},{9,5},{12,8},{13,9},{14,12},{15,13},... | collective-permute-start | bytes 2881544 | tf_op jit(solution)/shard_map/ppermute | solution.py:62
  309.0 23.4 %collective-permute-start.56 = (bf16[536,896]{1,0:T(8,128)(2,1)}, bf16[536,896]{1,0:T(8,128)(2,1)S(1)}, u32[]{:S(2)}, u32[]{:S(2)}) collective-permute-start(bf16[536,896]{1,0:T(8,128)(2,1)} %get-tuple-element.154.refs_0_), channel_id=1, source_target_pairs={{0,4},{1,5},{4,8},{5,9},{8,12},{9,13},{12,14},{13,15},{14,10},{15,... | collective-permute-start | bytes 2881544 | tf_op jit(solution)/shard_map/ppermute | solution.py:62
  310.4 23.1 %collective-permute-start.57 = (bf16[536,896]{1,0:T(8,128)(2,1)}, bf16[536,896]{1,0:T(8,128)(2,1)S(1)}, u32[]{:S(2)}, u32[]{:S(2)}) collective-permute-start(bf16[536,896]{1,0:T(8,128)(2,1)} %get-tuple-element.155.refs_2_), channel_id=1, source_target_pairs={{0,2},{1,3},{4,0},{5,1},{8,4},{9,5},{12,8},{13,9},{14,12},{15,13},... | collective-permute-start | bytes 2881544 | tf_op jit(solution)/shard_map/ppermute | solution.py:62
  (88 other events, 644.3 us)

commit v7 on v6

--- a/solution.py
+++ b/solution.py
@@ -64,9 +64,12 @@
     def owner(self, slot):
         return (self.pos - slot) % self.chips
 
+    def group_parts(self, x):
+        chip = jnp.concatenate([x] + [self.shift(x, s) for s in range(1, self.dp)], 0)
+        return chip, self.swap(chip)
+
     def group_gather(self, x):
-        chip = jnp.concatenate([x] + [self.shift(x, s) for s in range(1, self.dp)], 0)
-        return jnp.concatenate([chip, self.swap(chip)], 0)
+        return jnp.concatenate(self.group_parts(x), 0)
 
     def ring_gather(self, x):
         n = self.chips
@@ -268,32 +271,19 @@
     )[0]
 
 
-def ring_end(fwd, back, terms, split):
-    rows, columns = terms.shape[1:]
+def ring_end(fwd, back, term, split):
+    rows, columns = term.shape
 
     def kernel(fwd_ref, back_ref, term_ref, first_ref, rest_ref):
         for ref, here in ((first_ref, slice(0, split)), (rest_ref, slice(split, rows))):
             total = fwd_ref[here, :].astype(f32) + back_ref[here, :].astype(f32)
-            ref[...] = (total + term_ref[0, here, :].astype(f32)).astype(bf16)
-
-    whole = pl.BlockSpec((rows, columns), lambda i: (0, 0))
-    return pl.pallas_call(
-        kernel,
-        out_shape=[
-            jax.ShapeDtypeStruct((split, columns), bf16),
-            jax.ShapeDtypeStruct((rows - split, columns), bf16),
-        ],
-        grid=(1,),
-        in_specs=[whole, whole, pl.BlockSpec((1, rows, columns), lambda i: (0, 0, 0))],
-        out_specs=[
-            pl.BlockSpec((split, columns), lambda i: (0, 0)),
-            pl.BlockSpec((rows - split, columns), lambda i: (0, 0)),
-        ],
-        compiler_params=pltpu.CompilerParams(vmem_limit_bytes=VMEM_BYTES),
-        cost_estimate=pl.CostEstimate(
-            flops=0, bytes_accessed=8 * rows * columns, transcendentals=0
-        ),
-    )(fwd, back, terms)
+            ref[...] = (total + term_ref[here, :].astype(f32)).astype(bf16)
+
+    outs = [
+        jax.ShapeDtypeStruct((split, columns), bf16),
+        jax.ShapeDtypeStruct((rows - split, columns), bf16),
+    ]
+    return call(kernel, outs, [fwd, back, term])
 
 
 def pair_kernel(mine_ref, got_ref, *out_refs):
@@ -565,11 +555,20 @@
 
 
 def mlp_kernel(
-    half_rows, spots_ref, x_ref, gy_ref, gate_a, gate_b, up_a, up_b, down_a, down_b,
+    half_rows, spots_ref, x_a, x_b, gy_a, gy_b, gate_a, gate_b, up_a, up_b, down_a, down_b,
     xt_ref, midt_ref, gg_ref, gu_ref, gx_ref, out_ref, send_ref,
-    wg_all, wu_all, wd_all, mid_all, gg_all, gu_all,
+    x_all, gy_all, wg_all, wu_all, wd_all, mid_all, gg_all, gu_all,
 ):
     step = pl.program_id(0)
+
+    @pl.when(step == 0)
+    def start():
+        x_all[:half_rows] = x_a[...]
+        x_all[half_rows:] = x_b[...]
+        gy_all[:half_rows] = gy_a[...]
+        gy_all[half_rows:] = gy_b[...]
+        xt_ref[...] = x_all[...].T
+
     here = pl.ds(pl.multiple_of(step * 256, 256), 256)
     wg = jnp.concatenate([gate_a[...], gate_b[...]], 1)
     wu = jnp.concatenate([up_a[...], up_b[...]], 1)
@@ -580,28 +579,21 @@
     core = spots_ref[1]
     column = lanes((1, 256)) + (step * 256 + spots_ref[2])
     own = (column < spots_ref[3]) == (core == 0)
-    tokens = x_ref.shape[0]
-    for r in range(0, tokens, 256):
-        rows = slice(r, r + 256)
-        x = x_ref[rows, :]
-        gate = jnp.dot(x, wg, preferred_element_type=f32)
-        up = jnp.dot(x, wu, preferred_element_type=f32)
-        grad = jnp.where(own, dot_nt(gy_ref[rows, :], wd), 0.0)
-        sigma = jax.nn.sigmoid(gate)
-        active = gate * sigma
-        middle = jnp.where(own, active * up, 0.0).astype(bf16)
-        grad_gate = (grad * up * (sigma + active * (1.0 - sigma))).astype(bf16)
-        grad_up = (grad * active).astype(bf16)
-        midt_ref[:, rows] = middle.T
-        gg_ref[rows, :] = grad_gate
-        gu_ref[rows, :] = grad_up
-        mid_all[rows, here] = middle
-        gg_all[rows, here] = grad_gate
-        gu_all[rows, here] = grad_up
-
-    @pl.when(step == 0)
-    def transpose():
-        xt_ref[...] = x_ref[...].T
+    x = x_all[...]
+    gate = jnp.dot(x, wg, preferred_element_type=f32)
+    up = jnp.dot(x, wu, preferred_element_type=f32)
+    grad = jnp.where(own, dot_nt(gy_all[...], wd), 0.0)
+    sigma = jax.nn.sigmoid(gate)
+    active = gate * sigma
+    middle = jnp.where(own, active * up, 0.0).astype(bf16)
+    grad_gate = (grad * up * (sigma + active * (1.0 - sigma))).astype(bf16)
+    grad_up = (grad * active).astype(bf16)
+    midt_ref[...] = middle.T
+    gg_ref[...] = grad_gate
+    gu_ref[...] = grad_up
+    mid_all[:, here] = middle
+    gg_all[:, here] = grad_gate
+    gu_all[:, here] = grad_up
 
     @pl.when(step == pl.num_programs(0) - 1)
     def end():
@@ -613,9 +605,9 @@
         send_ref[half_rows:] = out[half_rows:].astype(bf16)
 
 
-def feed_forward(meta, x, gy, w_gate, w_up, w_down, width):
-    tokens = x.shape[0]
-    half = tokens // 2
+def feed_forward(meta, x, early, w_gate, w_up, w_down, width):
+    half = x[0].shape[0]
+    tokens = 2 * half
     steps = width // 256
     tiles = width // 128 - 1
 
@@ -643,7 +635,8 @@
         grid_spec=pltpu.PrefetchScalarGridSpec(
             num_scalar_prefetch=1,
             grid=(steps,),
-            in_specs=[whole, whole, columns(0), columns(1), columns(0), columns(1), rows(0), rows(1)],
+            in_specs=[halves] * 4
+            + [columns(0), columns(1), columns(0), columns(1), rows(0), rows(1)],
             out_specs=[
                 pl.BlockSpec((D, tokens), lambda i, m: (0, 0)),
                 pl.BlockSpec((256, tokens), lambda i, m: (i, 0)),
@@ -653,7 +646,8 @@
                 halves,
                 whole,
             ],
-            scratch_shapes=[pltpu.VMEM((D, width), bf16)] * 2
+            scratch_shapes=[pltpu.VMEM((tokens, D), bf16)] * 2
+            + [pltpu.VMEM((D, width), bf16)] * 2
             + [pltpu.VMEM((width, D), bf16)]
             + [pltpu.VMEM((tokens, width), bf16)] * 3,
         ),
@@ -661,92 +655,101 @@
         cost_estimate=pl.CostEstimate(
             flops=12 * tokens * width * D, bytes_accessed=6 * width * D, transcendentals=0
         ),
-    )(meta, x, gy, w_gate, w_gate, w_up, w_up, w_down, w_down)
-
-
-def mlp_grad_kernel(
-    down_rows, main, meta_ref, xt_ref, gy_ref, midt_ref, gg_ref, gu_ref,
-    out_ref, mlp_acc, down_acc,
-):
-    step = pl.program_id(0)
+    )(meta, *x, *early, w_gate, w_gate, w_up, w_up, w_down, w_down)
+
+
+def mlp_grad_kernel(chips, down_rows, main, meta_ref, xt_ref, gy_a, gy_b, midt_ref, gg_ref, gu_ref, *refs):
+    out_refs = refs[:chips]
+    mlp_acc, down_acc, blocks, sems = refs[chips:]
     core = meta_ref[1]
     at_main = pl.ds(pl.multiple_of(core * 128, 128), main)
     at_tile = pl.ds(pl.multiple_of((1 - core) * main, 128), 128)
-
-    @pl.when(step == 0)
-    def products():
-        xt = xt_ref[...]
-        mlp_acc[:, :main] = jnp.dot(
-            xt, gg_ref[:, at_main], preferred_element_type=f32
-        ).astype(bf16)
-        mlp_acc[:, main : 2 * main] = jnp.dot(
-            xt, gu_ref[:, at_main], preferred_element_type=f32
-        ).astype(bf16)
-        mixed = gg_ref[:, at_tile].astype(f32) + pltpu.roll(gu_ref[:, at_tile].astype(f32), 64, 1)
-        mlp_acc[:, 2 * main :] = jnp.dot(
-            xt, mixed.astype(bf16), preferred_element_type=f32
-        ).astype(bf16)
-        down_acc[...] = jnp.dot(midt_ref[...], gy_ref[...], preferred_element_type=f32)
-
-    mlp_rows = mlp_acc.shape[0] // pl.num_programs(0)
+    xt = xt_ref[...]
+    mlp_acc[:, :main] = jnp.dot(xt, gg_ref[:, at_main], preferred_element_type=f32).astype(bf16)
+    mlp_acc[:, main : 2 * main] = jnp.dot(
+        xt, gu_ref[:, at_main], preferred_element_type=f32
+    ).astype(bf16)
+    mixed = gg_ref[:, at_tile].astype(f32) + pltpu.roll(gu_ref[:, at_tile].astype(f32), 64, 1)
+    mlp_acc[:, 2 * main :] = jnp.dot(
+        xt, mixed.astype(bf16), preferred_element_type=f32
+    ).astype(bf16)
+    gy = jnp.concatenate([gy_a[:, :D], gy_b[:, :D]], 0)
+    down_acc[...] = jnp.dot(midt_ref[...], gy, preferred_element_type=f32)
+
+    mlp_rows = mlp_acc.shape[0] // chips
     columns = mlp_acc.shape[1] // 128
-    block = mlp_acc[pl.ds(pl.multiple_of(step * mlp_rows, 16), mlp_rows), :]
-    for j in range(columns):
-        for i in range(mlp_rows // 16):
-            out_ref[0, j * 16 : (j + 1) * 16, i * 128 : (i + 1) * 128] = block[
-                i * 16 : (i + 1) * 16, j * 128 : (j + 1) * 128
-            ]
-    first = pl.multiple_of(core * 64 + step * down_rows, 8)
-    out_ref[0, columns * 16 :, :] = down_acc[pl.ds(first, down_rows), :].astype(bf16)
-
-
-def mlp_gradients(meta, xt, gy, midt, gg, gu, chips, down_rows, main):
-    tokens = gy.shape[0]
+    half = chips // 2
+    copies = []
+    for slot in sorted(range(chips), key=lambda s: abs(s - half) if s else chips):
+        owner = meta_ref[12 + slot]
+        block = mlp_acc[pl.ds(pl.multiple_of(owner * mlp_rows, 16), mlp_rows), :]
+        for j in range(columns):
+            for i in range(mlp_rows // 16):
+                blocks[slot, j * 16 : (j + 1) * 16, i * 128 : (i + 1) * 128] = block[
+                    i * 16 : (i + 1) * 16, j * 128 : (j + 1) * 128
+                ]
+        first = pl.multiple_of(core * 64 + owner * down_rows, 8)
+        blocks[slot, columns * 16 :, :] = down_acc[pl.ds(first, down_rows), :].astype(bf16)
+        copy = pltpu.make_async_copy(blocks.at[slot], out_refs[slot], sems.at[slot])
+        copy.start()
+        copies.append(copy)
+    for copy in copies:
+        copy.wait()
+
+
+def mlp_gradients(meta, xt, early, midt, gg, gu, after, chips, down_rows, main):
+    tokens = gg.shape[0]
     columns = (2 * main + 128) // 128
     rows = columns * 16 + down_rows
-
-    def whole(x):
-        return pl.BlockSpec(x.shape, lambda i, m: (0, 0))
+    args = [meta, xt, *early, midt, gg, gu]
+    anywhere = pl.BlockSpec(memory_space=pl.ANY)
+
+    def kernel(*refs):
+        mlp_grad_kernel(chips, down_rows, main, *refs[: len(args)], *refs[len(args) + 1 :])
 
     return pl.pallas_call(
-        lambda *refs: mlp_grad_kernel(down_rows, main, *refs),
-        out_shape=jax.ShapeDtypeStruct((chips, rows, D), bf16),
-        grid_spec=pltpu.PrefetchScalarGridSpec(
-            num_scalar_prefetch=1,
-            grid=(chips,),
-            in_specs=[whole(x) for x in (xt, gy, midt, gg, gu)],
-            out_specs=pl.BlockSpec((1, rows, D), lambda i, m: (m[4 + i], 0, 0)),
-            scratch_shapes=[
-                pltpu.VMEM((D, columns * 128), bf16),
-                pltpu.VMEM((midt.shape[0], D), f32),
-            ],
-        ),
+        kernel,
+        out_shape=[jax.ShapeDtypeStruct((rows, D), bf16)] * chips,
+        in_specs=[pl.BlockSpec(memory_space=pltpu.SMEM)]
+        + [pl.BlockSpec(memory_space=pltpu.VMEM)] * (len(args) - 1)
+        + [anywhere],
+        out_specs=[anywhere] * chips,
+        scratch_shapes=[
+            pltpu.VMEM((D, columns * 128), bf16),
+            pltpu.VMEM((midt.shape[0], D), f32),
+            pltpu.VMEM((chips, rows, D), bf16),
+            pltpu.SemaphoreType.DMA((chips,)),
+        ],
         compiler_params=pltpu.CompilerParams(vmem_limit_bytes=VMEM_BYTES),
         cost_estimate=pl.CostEstimate(
             flops=6 * tokens * midt.shape[0] * D, bytes_accessed=4 * chips * rows * D,
             transcendentals=0,
         ),
-    )(meta, xt, gy, midt, gg, gu)
+    )(*args, after)
 
 
 def small_grad_kernel(
-    chips, q_rows, rows, meta_ref, norm_ref, joint_ref, att_ref, ga_ref, *refs
+    chips, q_rows, rows, meta_ref, norm_a, norm_b, joint_a, joint_b, near_a, near_b, *refs
 ):
     out_refs, acc, sums_ref = refs[:-2], refs[-2], refs[-1]
-    cols = joint_ref.shape[1]
-    blocks = joint_ref.shape[0] // (rows + 16)
-    tokens = [joint_ref[b * (rows + 16) : b * (rows + 16) + rows, :] for b in range(blocks)]
-    sums = []
-    for b in range(blocks):
-        found = joint_ref[b * (rows + 16) + rows : (b + 1) * (rows + 16), :].astype(f32)
-        sums.append([found[2 * i : 2 * i + 1] + found[2 * i + 1 : 2 * i + 2] for i in range(3)])
+    cols = joint_a.shape[1]
+    tokens, sums, attended, grads = [], [], [], []
+    for joint_ref, near_ref in ((joint_a, near_a), (joint_b, near_b)):
+        for b in range(2):
+            at = b * (rows + 16)
+            tokens.append(joint_ref[at : at + rows, :])
+            found = joint_ref[at + rows : at + rows + 16, :].astype(f32)
+            sums.append([found[2 * i : 2 * i + 1] + found[2 * i + 1 : 2 * i + 2] for i in range(3)])
+            attended.append(near_ref[2 * b * rows : (2 * b + 1) * rows, :])
+            grads.append(near_ref[(2 * b + 1) * rows : (2 * b + 2) * rows, :])
+    norm = jnp.concatenate([norm_a[:, D:], norm_b[:, D:]], 0)
     sums = [(sums[0][i] + sums[1][i]) + (sums[2][i] + sums[3][i]) for i in range(3)]
     sums_ref[...] = jnp.zeros_like(sums_ref)
     sums_ref[:1, :D] = sums[0][:, :D]
     sums_ref[:1, D : 2 * D] = sums[1][:, :D]
     sums_ref[:1, 2 * D : 2 * D + cols] = sums[2]
-    acc[:, :cols] = dot_tn(norm_ref[...], jnp.concatenate(tokens, 0))
-    acc[:, cols:] = dot_tn(att_ref[...], ga_ref[...])
+    acc[:, :cols] = dot_tn(norm, jnp.concatenate(tokens, 0))
+    acc[:, cols:] = dot_tn(jnp.concatenate(attended, 0), jnp.concatenate(grads, 0))
     first = pl.multiple_of((2 * meta_ref[0] + meta_ref[1]) * q_rows, 16)
     width = acc.shape[1] // chips
     share = sums_ref.shape[1] // chips
@@ -986,9 +989,7 @@
 
     late_w, late_g, late_n, unused = lax.optimization_barrier((w_out, cotangent[0], normed_one, pairs))
     w_out_full = net.full_rows(late_w)
-    early_group = net.group_gather(jnp.concatenate([late_g, late_n], 1))
-    grad_out_group = early_group[:, :D]
-    normed_one_group = early_group[:, D:]
+    early = net.group_parts(jnp.concatenate([late_g, late_n], 1))
 
     total_keys = rows * ctx_count
     padded = (KH, 2 * part_rows, 128)
@@ -1014,15 +1015,17 @@
         flops=8 * KH * part_rows * total_keys * 128,
     )
 
-    normed_two_group = net.group_gather(normed_two)
+    normed_two_parts = net.group_parts(normed_two)
     chip_rows = net.dp * rows
     down_rows = ff_half // chips
     mlp_rows = D // chips
     if tiled:
         x_turned, mid_turned, gate_low, up_low, grad_mine, out_mine, sent = feed_forward(
-            spots, normed_two_group, grad_out_group, w_gate, w_up, w_down, width
+            spots, normed_two_parts, early, w_gate, w_up, w_down, width
         )
     else:
+        normed_two_group = jnp.concatenate(normed_two_parts, 0)
+        grad_out_group = jnp.concatenate(early, 0)[:, :D]
         own_cols = (jnp.arange(width) + first < ff_half) == (core == 0)
         wg = lax.dynamic_slice(w_gate, (0, first), (D, width))
         wu = lax.dynamic_slice(w_up, (0, first), (D, width))
@@ -1048,8 +1051,8 @@
     mlp_chip = out_mine + swapped[chip_rows:].astype(f32)
     grad_two = grad_chip[:rows]
     for s in range(1, net.dp):
-        piece = grad_chip[s * rows : (s + 1) * rows].astype(bf16)
-        grad_two = grad_two + net.shift(piece, net.dp - s).astype(f32)
+        sent_two = grad_chip[s * rows : (s + 1) * rows].astype(bf16)
+        grad_two = grad_two + net.shift(sent_two, net.dp - s).astype(f32)
 
     def attention_back():
         grad_hidden, grad_attn_low, grad_gain_two, grad_queries, terms_mine, terms_other = call(
@@ -1122,11 +1125,11 @@
             found.append(blocks)
 
         terms = mlp_gradients(
-            spots, x_turned, grad_out_group, mid_turned, gate_low, up_low, chips, down_rows, main
+            spots, x_turned, early, mid_turned, gate_low, up_low, sent_two, chips, down_rows, main
         )
         fwd, back = net.ring_sum(terms, [pairs_stage, finish_stage, small_stage])
         wait_small = found.pop()
-        sum_mlp, sum_down = ring_end(fwd, back, terms, terms.shape[1] - down_rows)
+        sum_mlp, sum_down = ring_end(fwd, back, terms[0], terms[0].shape[0] - down_rows)
     else:
         part_down = jnp.einsum(
             "tf,td->fd", middle, grad_out_group, preferred_element_type=f32
@@ -1177,21 +1180,16 @@
         gathered.append(got[rows:])
     output = (hidden + out_sum).astype(bf16)
     gathered = jnp.concatenate(gathered, 0)
-    gathered = jnp.concatenate([gathered, net.swap(gathered)], 0).reshape(2 * net.dp, 2, rows, D)
-    attended_group = gathered[:, 0].reshape(2 * net.dp * rows, D)
-    grad_attn_group = gathered[:, 1].reshape(2 * net.dp * rows, D)
+    near = (gathered, net.swap(gathered))
 
     q_rows = w_qkv.shape[0] // 2
     qkv_cols = w_qkv.shape[1]
-    if not tiled:
-        grad_joint_low = grad_joint_low[:rows]
-    joint_group = net.group_gather(grad_joint_low)
     if tiled:
         piece = q_rows * (qkv_cols + D) // chips // D
         terms_small = call(
             lambda *refs: small_grad_kernel(chips, q_rows, rows, *refs),
             [jax.ShapeDtypeStruct((piece + 16, D), bf16)] * chips,
-            [spots, normed_one_group, joint_group, attended_group, grad_attn_group, *wait_small],
+            [spots, *early, *net.group_parts(grad_joint_low), *near, *wait_small],
             smem=1,
             loose=len(wait_small),
             scratch=[pltpu.VMEM((D, qkv_cols + D), f32), pltpu.VMEM((8, 3 * 128 * chips), f32)],
@@ -1208,6 +1206,11 @@
         )
         small = sums.reshape(chips, 8, 384)[:, 0].reshape(-1)[: 2 * D + qkv_cols]
     else:
+        gathered = jnp.concatenate(near, 0).reshape(2 * net.dp, 2, rows, D)
+        attended_group = gathered[:, 0].reshape(2 * net.dp * rows, D)
+        grad_attn_group = gathered[:, 1].reshape(2 * net.dp * rows, D)
+        normed_one_group = jnp.concatenate(early, 0)[:, D:]
+        joint_group = net.group_gather(grad_joint_low[:rows])
         q_first = net.d * (2 * q_rows) + core * q_rows
         group_rows = 2 * net.dp * rows
         part_out = jnp.einsum(

time: 365 us -> 353 us (0.967)
  other arithmetic: 26.2 us -> 19.2 us
    ppermute x7, waiting for transfers between devices: 20.5 us -> 14.8 us  [shift(): return lax.ppermute(x, 'dp', [(i, (i + step) % n) for i in range(n)])]
    concatenate x7 -> x1, other arithmetic: 5.68 us -> 0.06 us  [group_parts(): jnp.concatenate([x] + [self.shift(x, s) for s in range(1, self.dp)], 0)]
    pallas_call x2 -> x1, Pallas kernels: 14.4 us -> 10 us  [mlp_gradients(): pl.pallas_call(kernel, out_shape=[jax.ShapeDtypeStruct((rows, D), bf16)]...]
    unnamed x107 -> x135, local copies, waits for them, and re-layouts: 15.7 us -> 19.9 us
    pallas_call x8 -> x9, Pallas kernels: 44.7 us -> 47.7 us  [call(): pl.pallas_call(body, out_shape=list(outs), in_specs=specs, out_specs=[pl....]
  transfers between devices with their start and end apart: 63 -> 63, of which waited for: 37 -> 38; matrix products, arithmetic and copies ran while one was open for 12% -> 9% of each run, Pallas kernels for 18% -> 17%
where the time goes in v7:
time: 353 us; the launch traced here: 352 us
  waiting for transfers between devices  138 us (39%)
  Pallas kernels  100 us (28%)
  starting transfers between devices  54.4 us (15%)
  local copies, waits for them, and re-layouts  38.6 us (11%)
  other arithmetic  19.2 us (5%)
    ppermute x39, waiting for transfers between devices, hop(): return lax.ppermute(x, 'ctx', perm)  114 us
    pallas_call x9, Pallas kernels, call(): pl.pallas_call(body, out_shape=list(outs), in_specs=specs, out_specs=[pl....  47.7 us
    ppermute x39, starting transfers between devices, hop(): return lax.ppermute(x, 'ctx', perm)  41.2 us
    pallas_call x5, Pallas kernels, place_all(): pl.pallas_call(kernel, out_shape=[jax.ShapeDtypeStruct((D, ff_loc), f32),...  26.3 us
    unnamed x135, local copies, waits for them, and re-layouts  19.9 us
    pallas_call x1, Pallas kernels, feed_forward(): pl.pallas_call(lambda *refs: mlp_kernel(half, *refs), out_shape=[jax.Shap...  16.2 us
    ppermute x7, waiting for transfers between devices, shift(): return lax.ppermute(x, 'dp', [(i, (i + step) % n) for i in range(n)])  14.8 us
    ppermute x7, starting transfers between devices, shift(): return lax.ppermute(x, 'dp', [(i, (i + step) % n) for i in range(n)])  10.2 us
  transfers between devices with their start and end apart: 63, of which 38 were waited for; matrix products, arithmetic and copies ran while one was open for 9% of the time, Pallas kernels for 17%

profile of v7, /device:TPU:0, one launch (start us, length us, event | category | flops | bytes accessed | tf_op | source)
XLA Modules:
  0.0 351.8 jit_solution(15481562987141729036)
XLA Ops:
  1.8 3.0 collective-permute-start
  12.0 4.6 %collective-permute-done = bf16[224,1152]{1,0:T(8,128)(2,1)S(1)} collective-permute-done((bf16[224,1152]{1,0:T(8,128)(2,1)S(1)}, bf16[224,1152]{1,0:T(8,128)(2,1)S(1)}, u32[]{:S(2)}, u32[]{:S(2)}) %collective-permute-start) | collective-permute-done | bytes 516128 | tf_op jit(solution)/shard_map/ppermute | solution.py:54
  20.5 3.2 shard_map.195
  49.6 10.3 %shard_map.196 = (bf16[128,896]{1,0:T(8,128)(2,1)}, f32[2,896,128]{2,1,0:T(8,128)}, f32[2,2,8,448]{3,2,1,0:T(8,128)}, bf16[2,896,128]{2,1,0:T(8,128)(2,1)}, bf16...) custom-call(s32[17]{0:T(128)} %pad_add_fusion.refs_0_, ...), custom_call_target="tpu_custom_call" | custom-call | flops 1879048192 | bytes 6516292 | tf_op jit(solution)/shard_map/pallas_call | solution.py:219
  62.6 5.1 %collective-permute-done.13 = bf16[128,896]{1,0:T(8,128)(2,1)S(1)} collective-permute-done((bf16[128,896]{1,0:T(8,128)(2,1)}, bf16[128,896]{1,0:T(8,128)(2,1)S(1)}, u32[]{:S(2)}, u32[]{:S(2)}) %collective-permute-start.13) | collective-permute-done | bytes 229408 | tf_op jit(solution)/shard_map/ppermute | solution.py:54
  70.9 16.2 %shard_map.197 = (bf16[896,512]{1,0:T(8,128)(2,1)}, bf16[1280,512]{1,0:T(8,128)(2,1)}, bf16[512,1280]{1,0:T(8,128)(2,1)}, bf16[512,1280]{1,0:T(8,128)(2,1)}, f32...) custom-call(s32[20]{0:T(128)} %concatenate.68.refs_0_.meta_ref, bf16[256,896]{1,0:T(8,128)(2,1)} %copy-done.17, ...), custom_call_target="tpu_custom_call" | custom-call | flops 7046430720 | bytes 6881280 | tf_op jit(solution)/shard_map/pallas_call | solution.py:624
  93.5 10.0 %shard_map.199 = (bf16[456,896]{1,0:T(8,128)(2,1)}, bf16[456,896]{1,0:T(8,128)(2,1)}, bf16[456,896]{1,0:T(8,128)(2,1)}, bf16[456,896]{1,0:T(8,128)(2,1)}, bf16[4...) custom-call(s32[20]{0:T(128)} %concatenate.68.refs_0_.meta_ref, ...), custom_call_target="tpu_custom_call" | custom-call | flops 3523215360 | bytes 13074432 | tf_op jit(solution)/shard_map/pallas_call | solution.py:710
  106.5 15.0 %shard_map.198 = (f32[128,896]{1,0:T(8,128)}, bf16[128,896]{1,0:T(8,128)(2,1)}, f32[1,896]{1,0:T(1,128)}, f32[128,896]{1,0:T(8,128)}, f32[1024,256]{1,0:T(8,128)}, /*index=5*/bf16[1024,256]{1,0:T(8,128)(2,1)}) custom-call(s32[17]{0:T(128)} %pad_add_fusion.refs_0_, f32[128,896]{1,0:T(8,128)} %slice_add_fusion.refs_1_, f32[128,896]{1,0:T(8,128)} %get-tuple-element.109.refs_2_, ...), custom_call_target="tpu_custom_call" | custom-call | flops 4697620480 | bytes 7961668 | tf_op jit(solution)/shard_map/pallas_call | solution.py:219
  139.6 14.5 %collective-permute-done.27 = bf16[64,256]{1,0:T(8,128)(2,1)S(1)} collective-permute-done((bf16[64,256]{1,0:T(8,128)(2,1)S(1)}, bf16[64,256]{1,0:T(8,128)(2,1)S(1)}, u32[]{:S(2)}, u32[]{:S(2)}) %collective-permute-start.27) | collective-permute-done | bytes 32800 | tf_op jit(solution)/shard_map/ppermute | solution.py:62
  168.2 3.8 %shard_map.201 = (bf16[144,1152]{1,0:T(8,128)(2,1)}, f32[128,896]{1,0:T(8,128)}, f32[1,896]{1,0:T(1,128)}, f32[1,1152]{1,0:T(1,128)}) custom-call(f32[128,896]{1,0:T(8,128)} %get-tuple-element.123.refs_0_, bf16[128,896]{1,0:T(8,128)(2,1)} %bitcast.17, f32[1,896]{1,0:T(1,128)} %broadcast_in_dim.22.refs_1_.refs_2_, ...), custom_call_target="tpu_custom_call" | custom-call | flops 264241152 | bytes 6044672 | tf_op jit(solution)/shard_map/pallas_call | solution.py:219
  175.9 3.6 %collective-permute-done.36 = bf16[144,1152]{1,0:T(8,128)(2,1)S(1)} collective-permute-done((bf16[144,1152]{1,0:T(8,128)(2,1)}, bf16[144,1152]{1,0:T(8,128)(2,1)S(1)}, u32[]{:S(2)}, u32[]{:S(2)}) %collective-permute-start.36) | collective-permute-done | bytes 331808 | tf_op jit(solution)/shard_map/ppermute | solution.py:54
  179.6 13.7 %collective-permute-done.33 = bf16[456,896]{1,0:T(8,128)(2,1)S(1)} collective-permute-done((bf16[456,896]{1,0:T(8,128)(2,1)S(1)}, bf16[456,896]{1,0:T(8,128)(2,1)S(1)}, u32[]{:S(2)}, u32[]{:S(2)}) %collective-permute-start.33) | collective-permute-done | bytes 817184 | tf_op jit(solution)/shard_map/ppermute | solution.py:62
  196.2 5.8 %shard_map.203 = (bf16[80,896]{1,0:T(8,128)(2,1)}, bf16[80,896]{1,0:T(8,128)(2,1)}, bf16[80,896]{1,0:T(8,128)(2,1)}, bf16[80,896]{1,0:T(8,128)(2,1)}, bf16[80,89...) custom-call(s32[20]{0:T(128)} %concatenate.68.refs_0_.meta_ref, ...), custom_call_target="tpu_custom_call" | custom-call | flops 1879048192 | bytes 6961232 | tf_op jit(solution)/shard_map/pallas_call | solution.py:219
  211.4 13.8 %collective-permute-done.43 = bf16[40,896]{1,0:T(8,128)(2,1)S(1)} collective-permute-done((bf16[40,896]{1,0:T(8,128)(2,1)S(1)}, bf16[40,896]{1,0:T(8,128)(2,1)S(1)}, u32[]{:S(2)}, u32[]{:S(2)}) %collective-permute-start.43) | collective-permute-done | bytes 71712 | tf_op jit(solution)/shard_map/ppermute | solution.py:62
  239.1 2.7 shard_map.202
  249.2 4.1 %shard_map.205 = (f32[896,2432]{1,0:T(8,128)}, f32[896,2432]{1,0:T(8,128)}, f32[2432,896]{1,0:T(8,128)}, f32[448,1152]{1,0:T(8,128)}, f32[448,896]{1,0:T(8,128)}, /*index=5*/f32[64,384]{1,0:T(8,128)}, f32[8,128]{1,0:T(8,128)}) custom-call(s32[20]{0:T(128)} %concatenate.68.refs_0_.meta_ref, bf16[536,896]{1,0:T(8,128)(2,1)} %shard_map.204.refs_0_, ...), custom_call_target="tpu_custom_call" | custom-call | bytes 7684096 | tf_op jit(solution)/shard_map/pallas_call | solution.py:868
  253.4 16.0 %collective-permute-done.48.refs_1_ = bf16[536,896]{1,0:T(8,128)(2,1)S(1)} collective-permute-done((bf16[536,896]{1,0:T(8,128)(2,1)}, bf16[536,896]{1,0:T(8,128)(2,1)S(1)}, u32[]{:S(2)}, u32[]{:S(2)}) %collective-permute-start.48) | collective-permute-done | bytes 960544 | tf_op jit(solution)/shard_map/ppermute | solution.py:62
  276.9 6.0 %shard_map.207 = (f32[896,2432]{1,0:T(8,128)}, f32[896,2432]{1,0:T(8,128)}, f32[2432,896]{1,0:T(8,128)}, f32[448,1152]{1,0:T(8,128)}, f32[448,896]{1,0:T(8,128)}, /*index=5*/f32[64,384]{1,0:T(8,128)}, f32[8,128]{1,0:T(8,128)}) custom-call(s32[20]{0:T(128)} %concatenate.68.refs_0_.meta_ref, ...), custom_call_target="tpu_custom_call", output_to_operand_aliasing={{0}: (5, {}), {1}: (6, {}), {2}: (7, {}), {3}: (8, {}), {4}... | custom-call | bytes 15368192 | tf_op jit(solution)/shard_map/pallas_call | solution.py:868
  282.9 12.8 %collective-permute-done.52.refs_1_ = bf16[536,896]{1,0:T(8,128)(2,1)S(1)} collective-permute-done((bf16[536,896]{1,0:T(8,128)(2,1)}, bf16[536,896]{1,0:T(8,128)(2,1)S(1)}, u32[]{:S(2)}, u32[]{:S(2)}) %collective-permute-start.52) | collective-permute-done | bytes 960544 | tf_op jit(solution)/shard_map/ppermute | solution.py:62
  302.4 6.0 %shard_map.209 = (f32[896,2432]{1,0:T(8,128)}, f32[896,2432]{1,0:T(8,128)}, f32[2432,896]{1,0:T(8,128)}, f32[448,1152]{1,0:T(8,128)}, f32[448,896]{1,0:T(8,128)}, /*index=5*/f32[64,384]{1,0:T(8,128)}, f32[8,128]{1,0:T(8,128)}) custom-call(s32[20]{0:T(128)} %concatenate.68.refs_0_.meta_ref, ...), custom_call_target="tpu_custom_call", output_to_operand_aliasing={{0}: (5, {}), {1}: (6, {}), {2}: (7, {}), {3}: (8, {}), {4}... | custom-call | bytes 15368192 | tf_op jit(solution)/shard_map/pallas_call | solution.py:868
  308.4 12.8 %collective-permute-done.56.refs_1_ = bf16[536,896]{1,0:T(8,128)(2,1)S(1)} collective-permute-done((bf16[536,896]{1,0:T(8,128)(2,1)}, bf16[536,896]{1,0:T(8,128)(2,1)S(1)}, u32[]{:S(2)}, u32[]{:S(2)}) %collective-permute-start.56) | collective-permute-done | bytes 960544 | tf_op jit(solution)/shard_map/ppermute | solution.py:62
  328.8 6.0 %shard_map.211 = (f32[896,2432]{1,0:T(8,128)}, f32[896,2432]{1,0:T(8,128)}, f32[2432,896]{1,0:T(8,128)}, f32[448,1152]{1,0:T(8,128)}, f32[448,896]{1,0:T(8,128)}, /*index=5*/f32[64,384]{1,0:T(8,128)}, f32[8,128]{1,0:T(8,128)}) custom-call(s32[20]{0:T(128)} %concatenate.68.refs_0_.meta_ref, ...), custom_call_target="tpu_custom_call", output_to_operand_aliasing={{0}: (5, {}), {1}: (6, {}), {2}: (7, {}), {3}: (8, {}), {4}... | custom-call | bytes 15368192 | tf_op jit(solution)/shard_map/pallas_call | solution.py:868
  334.9 3.8 %collective-permute-done.59.refs_1_ = bf16[264,896]{1,0:T(8,128)(2,1)S(1)} collective-permute-done((bf16[264,896]{1,0:T(8,128)(2,1)S(1)}, bf16[264,896]{1,0:T(8,128)(2,1)S(1)}, u32[]{:S(2)}, u32[]{:S(2)}) %collective-permute-start.59) | collective-permute-done | bytes 473120 | tf_op jit(solution)/shard_map/ppermute | solution.py:62
  345.5 4.1 %shard_map.213 = (f32[896,2432]{1,0:T(8,128)}, f32[896,2432]{1,0:T(8,128)}, f32[2432,896]{1,0:T(8,128)}, f32[448,1152]{1,0:T(8,128)}, f32[448,896]{1,0:T(8,128)}, /*index=5*/f32[64,384]{1,0:T(8,128)}, f32[8,128]{1,0:T(8,128)}) custom-call(s32[20]{0:T(128)} %concatenate.68.refs_0_.meta_ref, ...), custom_call_target="tpu_custom_call", output_to_operand_aliasing={{0}: (3, {}), {1}: (4, {}), {2}: (5, {}), {3}: (6, {}), {4}... | custom-call | bytes 7684096 | tf_op jit(solution)/shard_map/pallas_call | solution.py:868
  (327 shorter events, 153.4 us)
Async XLA Ops:
  1.8 14.8 %collective-permute-start = (bf16[224,1152]{1,0:T(8,128)(2,1)S(1)}, bf16[224,1152]{1,0:T(8,128)(2,1)S(1)}, u32[]{:S(2)}, u32[]{:S(2)}) collective-permute-start(bf16[224,1152]{1,0:T(8,128)(2,1)S(1)} %constant_dynamic-slice_fusion.1), channel_id=1, source_target_pairs={{0,16},{16,0},{1,17},{17,1},{2,18},{18,2},{3,19},{19,3},{4,20},{20... | collective-permute-start | bytes 1548296 | tf_op jit(solution)/shard_map/ppermute | solution.py:54
  25.8 18.6 %collective-permute-start.11 = (bf16[224,896]{1,0:T(8,128)(2,1)S(1)}, bf16[224,896]{1,0:T(8,128)(2,1)S(1)}, u32[]{:S(2)}, u32[]{:S(2)}) collective-permute-start(bf16[224,896]{1,0:T(8,128)(2,1)S(1)} %constant_dynamic-slice_fusion), channel_id=1, source_target_pairs={{0,16},{16,0},{1,17},{17,1},{2,18},{18,2},{3,19},{19,3},{4,20},{20... | collective-permute-start | bytes 1204232 | tf_op jit(solution)/shard_map/ppermute | solution.py:54
  28.6 18.0 %collective-permute-start.15 = (bf16[128,1792]{1,0:T(8,128)(2,1)S(1)}, bf16[128,1792]{1,0:T(8,128)(2,1)S(1)}, u32[]{:S(2)}, u32[]{:S(2)}) collective-permute-start(bf16[128,1792]{1,0:T(8,128)(2,1)S(1)} %constant_dynamic-update-slice_fusion.11), channel_id=1, source_target_pairs={{0,16},{16,0},{1,17},{17,1},{2,18},{18,2},{3,19},{19,3},{4,20},{20... | collective-permute-start | bytes 1376264 | tf_op jit(solution)/shard_map/ppermute | solution.py:54
  46.6 22.5 %collective-permute-start.16 = (bf16[256,1792]{1,0:T(8,128)(2,1)S(1)}, bf16[256,1792]{1,0:T(8,128)(2,1)S(1)}, u32[]{:S(2)}, u32[]{:S(2)}) collective-permute-start(bf16[256,1792]{1,0:T(8,128)(2,1)S(1)} %pad_maximum_fusion.3.refs_3_.refs_2_.refs_1_), channel_id=1, source_target_pairs={{0,1},{1,0},{2,3},{3,2},{4,5},{5,4},{6,7},{7,6},{8,9},{9,8},{10,11... | collective-permute-start | bytes 2752520 | tf_op jit(solution)/shard_map/ppermute | solution.py:50
  103.5 20.5 %collective-permute-start.21 = (bf16[456,896]{1,0:T(8,128)(2,1)}, bf16[456,896]{1,0:T(8,128)(2,1)S(1)}, u32[]{:S(2)}, u32[]{:S(2)}) collective-permute-start(bf16[456,896]{1,0:T(8,128)(2,1)} %get-tuple-element.132), channel_id=1, source_target_pairs={{0,4},{1,5},{4,8},{5,9},{8,12},{9,13},{12,14},{13,15},{14,10},{15,... | collective-permute-start | bytes 2451464 | tf_op jit(solution)/shard_map/ppermute | solution.py:62
  105.2 20.2 %collective-permute-start.22 = (bf16[456,896]{1,0:T(8,128)(2,1)}, bf16[456,896]{1,0:T(8,128)(2,1)S(1)}, u32[]{:S(2)}, u32[]{:S(2)}) collective-permute-start(bf16[456,896]{1,0:T(8,128)(2,1)} %get-tuple-element.134), channel_id=1, source_target_pairs={{0,2},{1,3},{4,0},{5,1},{8,4},{9,5},{12,8},{13,9},{14,12},{15,13},... | collective-permute-start | bytes 2451464 | tf_op jit(solution)/shard_map/ppermute | solution.py:62
  132.1 27.4 %collective-permute-start.19 = (bf16[384,896]{1,0:T(8,128)(2,1)S(1)}, bf16[384,896]{1,0:T(8,128)(2,1)S(1)}, u32[]{:S(2)}, u32[]{:S(2)}) collective-permute-start(bf16[384,896]{1,0:T(8,128)(2,1)S(1)} %pad_maximum_fusion.6), channel_id=1, source_target_pairs={{0,16},{16,0},{1,17},{17,1},{2,18},{18,2},{3,19},{19,3},{4,20},{20... | collective-permute-start | bytes 2064392 | tf_op jit(solution)/shard_map/ppermute | solution.py:54
  133.1 30.6 %collective-permute-start.31 = (bf16[456,896]{1,0:T(8,128)(2,1)S(1)}, bf16[456,896]{1,0:T(8,128)(2,1)S(1)}, u32[]{:S(2)}, u32[]{:S(2)}) collective-permute-start(bf16[456,896]{1,0:T(8,128)(2,1)S(1)} %copy-done.7), channel_id=1, source_target_pairs={{0,4},{1,5},{4,8},{5,9},{8,12},{9,13},{12,14},{13,15},{14,10},{15,... | collective-permute-start | bytes 2451464 | tf_op jit(solution)/shard_map/ppermute | solution.py:62
  134.7 30.2 %collective-permute-start.32 = (bf16[456,896]{1,0:T(8,128)(2,1)S(1)}, bf16[456,896]{1,0:T(8,128)(2,1)S(1)}, u32[]{:S(2)}, u32[]{:S(2)}) collective-permute-start(bf16[456,896]{1,0:T(8,128)(2,1)S(1)} %copy-done.8), channel_id=1, source_target_pairs={{0,2},{1,3},{4,0},{5,1},{8,4},{9,5},{12,8},{13,9},{14,12},{15,13},... | collective-permute-start | bytes 2451464 | tf_op jit(solution)/shard_map/ppermute | solution.py:62
  135.9 18.1 %collective-permute-start.27 = (bf16[64,256]{1,0:T(8,128)(2,1)S(1)}, bf16[64,256]{1,0:T(8,128)(2,1)S(1)}, u32[]{:S(2)}, u32[]{:S(2)}) collective-permute-start(bf16[64,256]{1,0:T(8,128)(2,1)S(1)} %get-tuple-element.212), channel_id=1, source_target_pairs={{0,2},{1,3},{4,0},{5,1},{8,4},{9,5},{12,8},{13,9},{14,12},{15,13},... | collective-permute-start | bytes 98312 | tf_op jit(solution)/shard_map/ppermute | solution.py:62
  137.9 16.6 %collective-permute-start.24 = (bf16[128,256]{1,0:T(8,128)(2,1)S(1)}, bf16[128,256]{1,0:T(8,128)(2,1)S(1)}, u32[]{:S(2)}, u32[]{:S(2)}) collective-permute-start(bf16[128,256]{1,0:T(8,128)(2,1)S(1)} %pad_maximum_fusion.9), channel_id=1, source_target_pairs={{0,4},{1,5},{4,8},{5,9},{8,12},{9,13},{12,14},{13,15},{14,10},{15,... | collective-permute-start | bytes 196616 | tf_op jit(solution)/shard_map/ppermute | solution.py:62
  172.7 21.8 %collective-permute-start.38 = (bf16[512,896]{1,0:T(8,128)(2,1)S(1)}, bf16[512,896]{1,0:T(8,128)(2,1)S(1)}, u32[]{:S(2)}, u32[]{:S(2)}) collective-permute-start(bf16[512,896]{1,0:T(8,128)(2,1)S(1)} %pad_maximum_fusion.4.refs_5_), channel_id=1, source_target_pairs={{0,1},{1,0},{2,3},{3,2},{4,5},{5,4},{6,7},{7,6},{8,9},{9,8},{10,11... | collective-permute-start | bytes 2752520 | tf_op jit(solution)/shard_map/ppermute | solution.py:50
  173.2 20.1 %collective-permute-start.33 = (bf16[456,896]{1,0:T(8,128)(2,1)S(1)}, bf16[456,896]{1,0:T(8,128)(2,1)S(1)}, u32[]{:S(2)}, u32[]{:S(2)}) collective-permute-start(bf16[456,896]{1,0:T(8,128)(2,1)S(1)} %copy-done.10), channel_id=1, source_target_pairs={{0,4},{1,5},{4,8},{5,9},{8,12},{9,13},{12,14},{13,15},{14,10},{15,... | collective-permute-start | bytes 2451464 | tf_op jit(solution)/shard_map/ppermute | solution.py:62
  179.5 14.9 %collective-permute-start.37 = (bf16[288,1152]{1,0:T(8,128)(2,1)S(1)}, bf16[288,1152]{1,0:T(8,128)(2,1)S(1)}, u32[]{:S(2)}, u32[]{:S(2)}) collective-permute-start(bf16[288,1152]{1,0:T(8,128)(2,1)S(1)} %constant_dynamic-update-slice_fusion.13.refs_3_), channel_id=1, source_target_pairs={{0,1},{1,0},{2,3},{3,2},{4,5},{5,4},{6,7},{7,6},{8,9},{9,8},{10,11... | collective-permute-start | bytes 1990664 | tf_op jit(solution)/shard_map/ppermute | solution.py:50
  204.6 33.3 %collective-permute-start.35 = (bf16[456,896]{1,0:T(8,128)(2,1)S(1)}, bf16[456,896]{1,0:T(8,128)(2,1)S(1)}, u32[]{:S(2)}, u32[]{:S(2)}) collective-permute-start(bf16[456,896]{1,0:T(8,128)(2,1)S(1)} %copy-done.9), channel_id=1, source_target_pairs={{0,2},{1,3},{4,0},{5,1},{8,4},{9,5},{12,8},{13,9},{14,12},{15,13},... | collective-permute-start | bytes 2451464 | tf_op jit(solution)/shard_map/ppermute | solution.py:62
  205.0 32.9 %collective-permute-start.34 = (bf16[456,896]{1,0:T(8,128)(2,1)S(1)}, bf16[456,896]{1,0:T(8,128)(2,1)S(1)}, u32[]{:S(2)}, u32[]{:S(2)}) collective-permute-start(bf16[456,896]{1,0:T(8,128)(2,1)S(1)} %copy-done.33), channel_id=1, source_target_pairs={{0,4},{1,5},{4,8},{5,9},{8,12},{9,13},{12,14},{13,15},{14,10},{15,... | collective-permute-start | bytes 2451464 | tf_op jit(solution)/shard_map/ppermute | solution.py:62
  207.5 17.7 %collective-permute-start.43 = (bf16[40,896]{1,0:T(8,128)(2,1)S(1)}, bf16[40,896]{1,0:T(8,128)(2,1)S(1)}, u32[]{:S(2)}, u32[]{:S(2)}) collective-permute-start(bf16[40,896]{1,0:T(8,128)(2,1)S(1)} %get-tuple-element.210), channel_id=1, source_target_pairs={{0,2},{1,3},{4,0},{5,1},{8,4},{9,5},{12,8},{13,9},{14,12},{15,13},... | collective-permute-start | bytes 215048 | tf_op jit(solution)/shard_map/ppermute | solution.py:62
  209.8 17.8 %collective-permute-start.40 = (bf16[80,896]{1,0:T(8,128)(2,1)S(1)}, bf16[80,896]{1,0:T(8,128)(2,1)S(1)}, u32[]{:S(2)}, u32[]{:S(2)}) collective-permute-start(bf16[80,896]{1,0:T(8,128)(2,1)S(1)} %pad_maximum_fusion.7), channel_id=1, source_target_pairs={{0,4},{1,5},{4,8},{5,9},{8,12},{9,13},{12,14},{13,15},{14,10},{15,... | collective-permute-start | bytes 430088 | tf_op jit(solution)/shard_map/ppermute | solution.py:62
  245.5 23.9 %collective-permute-start.48 = (bf16[536,896]{1,0:T(8,128)(2,1)}, bf16[536,896]{1,0:T(8,128)(2,1)S(1)}, u32[]{:S(2)}, u32[]{:S(2)}) collective-permute-start(bf16[536,896]{1,0:T(8,128)(2,1)} %shard_map.204.refs_0_), channel_id=1, source_target_pairs={{0,4},{1,5},{4,8},{5,9},{8,12},{9,13},{12,14},{13,15},{14,10},{15,... | collective-permute-start | bytes 2881544 | tf_op jit(solution)/shard_map/ppermute | solution.py:62
  247.3 23.6 %collective-permute-start.49 = (bf16[536,896]{1,0:T(8,128)(2,1)}, bf16[536,896]{1,0:T(8,128)(2,1)S(1)}, u32[]{:S(2)}, u32[]{:S(2)}) collective-permute-start(bf16[536,896]{1,0:T(8,128)(2,1)} %shard_map.204.refs_0_), channel_id=1, source_target_pairs={{0,2},{1,3},{4,0},{5,1},{8,4},{9,5},{12,8},{13,9},{14,12},{15,13},... | collective-permute-start | bytes 2881544 | tf_op jit(solution)/shard_map/ppermute | solution.py:62
  272.3 23.4 %collective-permute-start.52 = (bf16[536,896]{1,0:T(8,128)(2,1)}, bf16[536,896]{1,0:T(8,128)(2,1)S(1)}, u32[]{:S(2)}, u32[]{:S(2)}) collective-permute-start(bf16[536,896]{1,0:T(8,128)(2,1)} %get-tuple-element.161.refs_0_), channel_id=1, source_target_pairs={{0,4},{1,5},{4,8},{5,9},{8,12},{9,13},{12,14},{13,15},{14,10},{15,... | collective-permute-start | bytes 2881544 | tf_op jit(solution)/shard_map/ppermute | solution.py:62
  273.2 23.1 %collective-permute-start.53 = (bf16[536,896]{1,0:T(8,128)(2,1)}, bf16[536,896]{1,0:T(8,128)(2,1)S(1)}, u32[]{:S(2)}, u32[]{:S(2)}) collective-permute-start(bf16[536,896]{1,0:T(8,128)(2,1)} %get-tuple-element.162.refs_2_), channel_id=1, source_target_pairs={{0,2},{1,3},{4,0},{5,1},{8,4},{9,5},{12,8},{13,9},{14,12},{15,13},... | collective-permute-start | bytes 2881544 | tf_op jit(solution)/shard_map/ppermute | solution.py:62
  297.8 23.4 %collective-permute-start.56 = (bf16[536,896]{1,0:T(8,128)(2,1)}, bf16[536,896]{1,0:T(8,128)(2,1)S(1)}, u32[]{:S(2)}, u32[]{:S(2)}) collective-permute-start(bf16[536,896]{1,0:T(8,128)(2,1)} %get-tuple-element.170.refs_0_), channel_id=1, source_target_pairs={{0,4},{1,5},{4,8},{5,9},{8,12},{9,13},{12,14},{13,15},{14,10},{15,... | collective-permute-start | bytes 2881544 | tf_op jit(solution)/shard_map/ppermute | solution.py:62
  298.7 23.1 %collective-permute-start.57 = (bf16[536,896]{1,0:T(8,128)(2,1)}, bf16[536,896]{1,0:T(8,128)(2,1)S(1)}, u32[]{:S(2)}, u32[]{:S(2)}) collective-permute-start(bf16[536,896]{1,0:T(8,128)(2,1)} %get-tuple-element.171.refs_2_), channel_id=1, source_target_pairs={{0,2},{1,3},{4,0},{5,1},{8,4},{9,5},{12,8},{13,9},{14,12},{15,13},... | collective-permute-start | bytes 2881544 | tf_op jit(solution)/shard_map/ppermute | solution.py:62
  (102 other events, 725.0 us)

commit v8 on v7

--- a/solution.py
+++ b/solution.py
@@ -200,6 +200,7 @@
 VMEM_BYTES = 56 * 1024 * 1024
 KEYS = 256
 RING_ROWS = 152
+LIGHT = pl.CostEstimate(flops=0, bytes_accessed=1024, transcendentals=0)
 
 
 def full_spec(shape):
@@ -223,7 +224,7 @@
         out_specs=[pl.BlockSpec(memory_space=pltpu.VMEM)] * len(outs),
         scratch_shapes=list(scratch),
         compiler_params=pltpu.CompilerParams(vmem_limit_bytes=VMEM_BYTES),
-        cost_estimate=pl.CostEstimate(flops=flops, bytes_accessed=moved, transcendentals=0),
+        cost_estimate=LIGHT,
     )(*args)
 
 
@@ -254,7 +255,7 @@
         in_specs=[anywhere] * (count + 1),
         out_specs=[anywhere] * count,
         input_output_aliases={i + 1: i for i in range(count)},
-        cost_estimate=pl.CostEstimate(flops=0, bytes_accessed=1024, transcendentals=0),
+        cost_estimate=LIGHT,
     )(token, *blocks)
 
 
@@ -652,9 +653,7 @@
             + [pltpu.VMEM((tokens, width), bf16)] * 3,
         ),
         compiler_params=pltpu.CompilerParams(vmem_limit_bytes=VMEM_BYTES),
-        cost_estimate=pl.CostEstimate(
-            flops=12 * tokens * width * D, bytes_accessed=6 * width * D, transcendentals=0
-        ),
+        cost_estimate=LIGHT,
     )(meta, *x, *early, w_gate, w_gate, w_up, w_up, w_down, w_down)
 
 
@@ -721,10 +720,7 @@
             pltpu.SemaphoreType.DMA((chips,)),
         ],
         compiler_params=pltpu.CompilerParams(vmem_limit_bytes=VMEM_BYTES),
-        cost_estimate=pl.CostEstimate(
-            flops=6 * tokens * midt.shape[0] * D, bytes_accessed=4 * chips * rows * D,
-            transcendentals=0,
-        ),
+        cost_estimate=LIGHT,
     )(*args, after)
 
 
@@ -891,9 +887,7 @@
         ],
         input_output_aliases={1 + count + i: i for i in range(len(keep))},
         compiler_params=pltpu.CompilerParams(vmem_limit_bytes=VMEM_BYTES),
-        cost_estimate=pl.CostEstimate(
-            flops=0, bytes_accessed=8 * sum(x.size for x in blocks), transcendentals=0
-        ),
+        cost_estimate=LIGHT,
     )(meta, *blocks, *keep)
     return list(result[:6]), result[6]
 

time: 353 us -> 358 us (1.014)
  waiting for transfers between devices: 138 us -> 142 us
    ppermute x7, waiting for transfers between devices: 14.8 us -> 20.4 us  [shift(): return lax.ppermute(x, 'dp', [(i, (i + step) % n) for i in range(n)])]
  transfers between devices with their start and end apart: 63 -> 63, of which waited for: 38 -> 37; matrix products, arithmetic and copies ran while one was open for 9% -> 9% of each run, Pallas kernels for 17% -> 14%
where the time goes in v8:
time: 358 us; the launch traced here: 357 us
  waiting for transfers between devices  142 us (40%)
  Pallas kernels  100 us (28%)
  starting transfers between devices  54.9 us (15%)
  local copies, waits for them, and re-layouts  39.3 us (11%)
  other arithmetic  19.3 us (5%)
    ppermute x39, waiting for transfers between devices, hop(): return lax.ppermute(x, 'ctx', perm)  113 us
    pallas_call x9, Pallas kernels, call(): pl.pallas_call(body, out_shape=list(outs), in_specs=specs, out_specs=[pl....  47.7 us
    ppermute x39, starting transfers between devices, hop(): return lax.ppermute(x, 'ctx', perm)  41.1 us
    pallas_call x5, Pallas kernels, place_all(): pl.pallas_call(kernel, out_shape=[jax.ShapeDtypeStruct((D, ff_loc), f32),...  26.3 us
    ppermute x7, waiting for transfers between devices, shift(): return lax.ppermute(x, 'dp', [(i, (i + step) % n) for i in range(n)])  20.4 us
    unnamed x135, local copies, waits for them, and re-layouts  19.8 us
    pallas_call x1, Pallas kernels, feed_forward(): pl.pallas_call(lambda *refs: mlp_kernel(half, *refs), out_shape=[jax.Shap...  16.2 us
    ppermute x7, starting transfers between devices, shift(): return lax.ppermute(x, 'dp', [(i, (i + step) % n) for i in range(n)])  10.7 us
  transfers between devices with their start and end apart: 63, of which 37 were waited for; matrix products, arithmetic and copies ran while one was open for 9% of the time, Pallas kernels for 14%

profile of v8, /device:TPU:0, one launch (start us, length us, event | category | flops | bytes accessed | tf_op | source)
XLA Modules:
  0.0 357.0 jit_solution(5971653193537923583)
XLA Ops:
  1.8 3.0 collective-permute-start
  12.1 4.5 %collective-permute-done = bf16[224,1152]{1,0:T(8,128)(2,1)S(1)} collective-permute-done((bf16[224,1152]{1,0:T(8,128)(2,1)S(1)}, bf16[224,1152]{1,0:T(8,128)(2,1)S(1)}, u32[]{:S(2)}, u32[]{:S(2)}) %collective-permute-start) | collective-permute-done | bytes 516128 | tf_op jit(solution)/shard_map/ppermute | solution.py:54
  20.5 3.2 shard_map.195
  49.6 10.3 %shard_map.196 = (bf16[128,896]{1,0:T(8,128)(2,1)}, f32[2,896,128]{2,1,0:T(8,128)}, f32[2,2,8,448]{3,2,1,0:T(8,128)}, bf16[2,896,128]{2,1,0:T(8,128)(2,1)}, bf16...) custom-call(s32[17]{0:T(128)} %pad_add_fusion.refs_0_, ...), custom_call_target="tpu_custom_call" | custom-call | bytes 1024 | tf_op jit(solution)/shard_map/pallas_call | solution.py:220
  62.6 5.1 %collective-permute-done.13 = bf16[128,896]{1,0:T(8,128)(2,1)S(1)} collective-permute-done((bf16[128,896]{1,0:T(8,128)(2,1)}, bf16[128,896]{1,0:T(8,128)(2,1)S(1)}, u32[]{:S(2)}, u32[]{:S(2)}) %collective-permute-start.13) | collective-permute-done | bytes 229408 | tf_op jit(solution)/shard_map/ppermute | solution.py:54
  70.9 16.2 %shard_map.197 = (bf16[896,512]{1,0:T(8,128)(2,1)}, bf16[1280,512]{1,0:T(8,128)(2,1)}, bf16[512,1280]{1,0:T(8,128)(2,1)}, bf16[512,1280]{1,0:T(8,128)(2,1)}, f32...) custom-call(s32[20]{0:T(128)} %concatenate.68.refs_0_.meta_ref, bf16[256,896]{1,0:T(8,128)(2,1)} %copy-done.22, ...), custom_call_target="tpu_custom_call" | custom-call | bytes 1024 | tf_op jit(solution)/shard_map/pallas_call | solution.py:625
  92.5 10.0 %shard_map.199 = (bf16[456,896]{1,0:T(8,128)(2,1)}, bf16[456,896]{1,0:T(8,128)(2,1)}, bf16[456,896]{1,0:T(8,128)(2,1)}, bf16[456,896]{1,0:T(8,128)(2,1)}, bf16[4...) custom-call(s32[20]{0:T(128)} %concatenate.68.refs_0_.meta_ref, ...), custom_call_target="tpu_custom_call" | custom-call | bytes 1024 | tf_op jit(solution)/shard_map/pallas_call | solution.py:709
  106.4 5.7 %collective-permute-done.18 = bf16[128,896]{1,0:T(8,128)(2,1)S(1)} collective-permute-done((bf16[128,896]{1,0:T(8,128)(2,1)S(1)}, bf16[128,896]{1,0:T(8,128)(2,1)S(1)}, u32[]{:S(2)}, u32[]{:S(2)}) %collective-permute-start.18) | collective-permute-done | bytes 229408 | tf_op jit(solution)/shard_map/ppermute | solution.py:54
  112.9 15.0 %shard_map.198 = (f32[128,896]{1,0:T(8,128)}, bf16[128,896]{1,0:T(8,128)(2,1)}, f32[1,896]{1,0:T(1,128)}, f32[128,896]{1,0:T(8,128)}, f32[1024,256]{1,0:T(8,128)}, /*index=5*/bf16[1024,256]{1,0:T(8,128)(2,1)}) custom-call(s32[17]{0:T(128)} %pad_add_fusion.refs_0_, f32[128,896]{1,0:T(8,128)} %slice_add_fusion.refs_1_, f32[128,896]{1,0:T(8,128)} %get-tuple-element.109.refs_2_, ...), custom_call_target="tpu_custom_call" | custom-call | bytes 1024 | tf_op jit(solution)/shard_map/pallas_call | solution.py:220
  143.9 15.6 %collective-permute-done.27 = bf16[64,256]{1,0:T(8,128)(2,1)S(1)} collective-permute-done((bf16[64,256]{1,0:T(8,128)(2,1)S(1)}, bf16[64,256]{1,0:T(8,128)(2,1)S(1)}, u32[]{:S(2)}, u32[]{:S(2)}) %collective-permute-start.27) | collective-permute-done | bytes 32800 | tf_op jit(solution)/shard_map/ppermute | solution.py:62
  173.7 3.8 %shard_map.201 = (bf16[144,1152]{1,0:T(8,128)(2,1)}, f32[128,896]{1,0:T(8,128)}, f32[1,896]{1,0:T(1,128)}, f32[1,1152]{1,0:T(1,128)}) custom-call(f32[128,896]{1,0:T(8,128)} %get-tuple-element.123.refs_0_, bf16[128,896]{1,0:T(8,128)(2,1)} %bitcast.16, f32[1,896]{1,0:T(1,128)} %broadcast_in_dim.22.refs_1_.refs_2_, ...), custom_call_target="tpu_custom_call" | custom-call | bytes 1024 | tf_op jit(solution)/shard_map/pallas_call | solution.py:220
  181.3 3.7 %collective-permute-done.36 = bf16[144,1152]{1,0:T(8,128)(2,1)S(1)} collective-permute-done((bf16[144,1152]{1,0:T(8,128)(2,1)}, bf16[144,1152]{1,0:T(8,128)(2,1)S(1)}, u32[]{:S(2)}, u32[]{:S(2)}) %collective-permute-start.36) | collective-permute-done | bytes 331808 | tf_op jit(solution)/shard_map/ppermute | solution.py:54
  185.1 13.8 %collective-permute-done.33 = bf16[456,896]{1,0:T(8,128)(2,1)S(1)} collective-permute-done((bf16[456,896]{1,0:T(8,128)(2,1)S(1)}, bf16[456,896]{1,0:T(8,128)(2,1)S(1)}, u32[]{:S(2)}, u32[]{:S(2)}) %collective-permute-start.33) | collective-permute-done | bytes 817184 | tf_op jit(solution)/shard_map/ppermute | solution.py:62
  201.8 5.8 %shard_map.203 = (bf16[80,896]{1,0:T(8,128)(2,1)}, bf16[80,896]{1,0:T(8,128)(2,1)}, bf16[80,896]{1,0:T(8,128)(2,1)}, bf16[80,896]{1,0:T(8,128)(2,1)}, bf16[80,89...) custom-call(s32[20]{0:T(128)} %concatenate.68.refs_0_.meta_ref, ...), custom_call_target="tpu_custom_call" | custom-call | bytes 1024 | tf_op jit(solution)/shard_map/pallas_call | solution.py:220
  217.0 13.8 %collective-permute-done.43 = bf16[40,896]{1,0:T(8,128)(2,1)S(1)} collective-permute-done((bf16[40,896]{1,0:T(8,128)(2,1)S(1)}, bf16[40,896]{1,0:T(8,128)(2,1)S(1)}, u32[]{:S(2)}, u32[]{:S(2)}) %collective-permute-start.43) | collective-permute-done | bytes 71712 | tf_op jit(solution)/shard_map/ppermute | solution.py:62
  254.9 4.1 %shard_map.205 = (f32[896,2432]{1,0:T(8,128)}, f32[896,2432]{1,0:T(8,128)}, f32[2432,896]{1,0:T(8,128)}, f32[448,1152]{1,0:T(8,128)}, f32[448,896]{1,0:T(8,128)}, /*index=5*/f32[64,384]{1,0:T(8,128)}, f32[8,128]{1,0:T(8,128)}) custom-call(s32[20]{0:T(128)} %concatenate.68.refs_0_.meta_ref, bf16[536,896]{1,0:T(8,128)(2,1)} %shard_map.204.refs_0_, ...), custom_call_target="tpu_custom_call" | custom-call | bytes 1024 | tf_op jit(solution)/shard_map/pallas_call | solution.py:864
  259.0 16.0 %collective-permute-done.48.refs_1_ = bf16[536,896]{1,0:T(8,128)(2,1)S(1)} collective-permute-done((bf16[536,896]{1,0:T(8,128)(2,1)}, bf16[536,896]{1,0:T(8,128)(2,1)S(1)}, u32[]{:S(2)}, u32[]{:S(2)}) %collective-permute-start.48) | collective-permute-done | bytes 960544 | tf_op jit(solution)/shard_map/ppermute | solution.py:62
  282.4 6.0 %shard_map.207 = (f32[896,2432]{1,0:T(8,128)}, f32[896,2432]{1,0:T(8,128)}, f32[2432,896]{1,0:T(8,128)}, f32[448,1152]{1,0:T(8,128)}, f32[448,896]{1,0:T(8,128)}, /*index=5*/f32[64,384]{1,0:T(8,128)}, f32[8,128]{1,0:T(8,128)}) custom-call(s32[20]{0:T(128)} %concatenate.68.refs_0_.meta_ref, ...), custom_call_target="tpu_custom_call", output_to_operand_aliasing={{0}: (5, {}), {1}: (6, {}), {2}: (7, {}), {3}: (8, {}), {4}... | custom-call | bytes 1024 | tf_op jit(solution)/shard_map/pallas_call | solution.py:864
  288.4 12.8 %collective-permute-done.52.refs_1_ = bf16[536,896]{1,0:T(8,128)(2,1)S(1)} collective-permute-done((bf16[536,896]{1,0:T(8,128)(2,1)}, bf16[536,896]{1,0:T(8,128)(2,1)S(1)}, u32[]{:S(2)}, u32[]{:S(2)}) %collective-permute-start.52) | collective-permute-done | bytes 960544 | tf_op jit(solution)/shard_map/ppermute | solution.py:62
  307.8 6.0 %shard_map.209 = (f32[896,2432]{1,0:T(8,128)}, f32[896,2432]{1,0:T(8,128)}, f32[2432,896]{1,0:T(8,128)}, f32[448,1152]{1,0:T(8,128)}, f32[448,896]{1,0:T(8,128)}, /*index=5*/f32[64,384]{1,0:T(8,128)}, f32[8,128]{1,0:T(8,128)}) custom-call(s32[20]{0:T(128)} %concatenate.68.refs_0_.meta_ref, ...), custom_call_target="tpu_custom_call", output_to_operand_aliasing={{0}: (5, {}), {1}: (6, {}), {2}: (7, {}), {3}: (8, {}), {4}... | custom-call | bytes 1024 | tf_op jit(solution)/shard_map/pallas_call | solution.py:864
  313.8 12.8 %collective-permute-done.56.refs_1_ = bf16[536,896]{1,0:T(8,128)(2,1)S(1)} collective-permute-done((bf16[536,896]{1,0:T(8,128)(2,1)}, bf16[536,896]{1,0:T(8,128)(2,1)S(1)}, u32[]{:S(2)}, u32[]{:S(2)}) %collective-permute-start.56) | collective-permute-done | bytes 960544 | tf_op jit(solution)/shard_map/ppermute | solution.py:62
  334.1 6.1 %shard_map.211 = (f32[896,2432]{1,0:T(8,128)}, f32[896,2432]{1,0:T(8,128)}, f32[2432,896]{1,0:T(8,128)}, f32[448,1152]{1,0:T(8,128)}, f32[448,896]{1,0:T(8,128)}, /*index=5*/f32[64,384]{1,0:T(8,128)}, f32[8,128]{1,0:T(8,128)}) custom-call(s32[20]{0:T(128)} %concatenate.68.refs_0_.meta_ref, ...), custom_call_target="tpu_custom_call", output_to_operand_aliasing={{0}: (5, {}), {1}: (6, {}), {2}: (7, {}), {3}: (8, {}), {4}... | custom-call | bytes 1024 | tf_op jit(solution)/shard_map/pallas_call | solution.py:864
  340.2 3.7 %collective-permute-done.59.refs_1_ = bf16[264,896]{1,0:T(8,128)(2,1)S(1)} collective-permute-done((bf16[264,896]{1,0:T(8,128)(2,1)S(1)}, bf16[264,896]{1,0:T(8,128)(2,1)S(1)}, u32[]{:S(2)}, u32[]{:S(2)}) %collective-permute-start.59) | collective-permute-done | bytes 473120 | tf_op jit(solution)/shard_map/ppermute | solution.py:62
  350.8 4.1 %shard_map.213 = (f32[896,2432]{1,0:T(8,128)}, f32[896,2432]{1,0:T(8,128)}, f32[2432,896]{1,0:T(8,128)}, f32[448,1152]{1,0:T(8,128)}, f32[448,896]{1,0:T(8,128)}, /*index=5*/f32[64,384]{1,0:T(8,128)}, f32[8,128]{1,0:T(8,128)}) custom-call(s32[20]{0:T(128)} %concatenate.68.refs_0_.meta_ref, ...), custom_call_target="tpu_custom_call", output_to_operand_aliasing={{0}: (3, {}), {1}: (4, {}), {2}: (5, {}), {3}: (6, {}), {4}... | custom-call | bytes 1024 | tf_op jit(solution)/shard_map/pallas_call | solution.py:864
  (327 shorter events, 154.5 us)
Async XLA Ops:
  1.8 14.8 %collective-permute-start = (bf16[224,1152]{1,0:T(8,128)(2,1)S(1)}, bf16[224,1152]{1,0:T(8,128)(2,1)S(1)}, u32[]{:S(2)}, u32[]{:S(2)}) collective-permute-start(bf16[224,1152]{1,0:T(8,128)(2,1)S(1)} %constant_dynamic-slice_fusion.1), channel_id=1, source_target_pairs={{0,16},{16,0},{1,17},{17,1},{2,18},{18,2},{3,19},{19,3},{4,20},{20... | collective-permute-start | bytes 1548296 | tf_op jit(solution)/shard_map/ppermute | solution.py:54
  25.8 18.6 %collective-permute-start.11 = (bf16[224,896]{1,0:T(8,128)(2,1)S(1)}, bf16[224,896]{1,0:T(8,128)(2,1)S(1)}, u32[]{:S(2)}, u32[]{:S(2)}) collective-permute-start(bf16[224,896]{1,0:T(8,128)(2,1)S(1)} %constant_dynamic-slice_fusion), channel_id=1, source_target_pairs={{0,16},{16,0},{1,17},{17,1},{2,18},{18,2},{3,19},{19,3},{4,20},{20... | collective-permute-start | bytes 1204232 | tf_op jit(solution)/shard_map/ppermute | solution.py:54
  28.6 18.0 %collective-permute-start.15 = (bf16[128,1792]{1,0:T(8,128)(2,1)S(1)}, bf16[128,1792]{1,0:T(8,128)(2,1)S(1)}, u32[]{:S(2)}, u32[]{:S(2)}) collective-permute-start(bf16[128,1792]{1,0:T(8,128)(2,1)S(1)} %constant_dynamic-update-slice_fusion.11), channel_id=1, source_target_pairs={{0,16},{16,0},{1,17},{17,1},{2,18},{18,2},{3,19},{19,3},{4,20},{20... | collective-permute-start | bytes 1376264 | tf_op jit(solution)/shard_map/ppermute | solution.py:54
  46.6 22.6 %collective-permute-start.16 = (bf16[256,1792]{1,0:T(8,128)(2,1)S(1)}, bf16[256,1792]{1,0:T(8,128)(2,1)S(1)}, u32[]{:S(2)}, u32[]{:S(2)}) collective-permute-start(bf16[256,1792]{1,0:T(8,128)(2,1)S(1)} %pad_maximum_fusion.3.refs_3_.refs_2_.refs_1_), channel_id=1, source_target_pairs={{0,1},{1,0},{2,3},{3,2},{4,5},{5,4},{6,7},{7,6},{8,9},{9,8},{10,11... | collective-permute-start | bytes 2752520 | tf_op jit(solution)/shard_map/ppermute | solution.py:50
  102.6 25.4 %collective-permute-start.21 = (bf16[456,896]{1,0:T(8,128)(2,1)}, bf16[456,896]{1,0:T(8,128)(2,1)S(1)}, u32[]{:S(2)}, u32[]{:S(2)}) collective-permute-start(bf16[456,896]{1,0:T(8,128)(2,1)} %get-tuple-element.132), channel_id=1, source_target_pairs={{0,4},{1,5},{4,8},{5,9},{8,12},{9,13},{12,14},{13,15},{14,10},{15,... | collective-permute-start | bytes 2451464 | tf_op jit(solution)/shard_map/ppermute | solution.py:62
  104.4 24.7 %collective-permute-start.22 = (bf16[456,896]{1,0:T(8,128)(2,1)}, bf16[456,896]{1,0:T(8,128)(2,1)S(1)}, u32[]{:S(2)}, u32[]{:S(2)}) collective-permute-start(bf16[456,896]{1,0:T(8,128)(2,1)} %get-tuple-element.134), channel_id=1, source_target_pairs={{0,2},{1,3},{4,0},{5,1},{8,4},{9,5},{12,8},{13,9},{14,12},{15,13},... | collective-permute-start | bytes 2451464 | tf_op jit(solution)/shard_map/ppermute | solution.py:62
  135.9 28.5 %collective-permute-start.19 = (bf16[384,896]{1,0:T(8,128)(2,1)S(1)}, bf16[384,896]{1,0:T(8,128)(2,1)S(1)}, u32[]{:S(2)}, u32[]{:S(2)}) collective-permute-start(bf16[384,896]{1,0:T(8,128)(2,1)S(1)} %pad_maximum_fusion.6), channel_id=1, source_target_pairs={{0,16},{16,0},{1,17},{17,1},{2,18},{18,2},{3,19},{19,3},{4,20},{20... | collective-permute-start | bytes 2064392 | tf_op jit(solution)/shard_map/ppermute | solution.py:54
  137.5 31.8 %collective-permute-start.31 = (bf16[456,896]{1,0:T(8,128)(2,1)S(1)}, bf16[456,896]{1,0:T(8,128)(2,1)S(1)}, u32[]{:S(2)}, u32[]{:S(2)}) collective-permute-start(bf16[456,896]{1,0:T(8,128)(2,1)S(1)} %copy-done.9), channel_id=1, source_target_pairs={{0,4},{1,5},{4,8},{5,9},{8,12},{9,13},{12,14},{13,15},{14,10},{15,... | collective-permute-start | bytes 2451464 | tf_op jit(solution)/shard_map/ppermute | solution.py:62
  139.1 31.3 %collective-permute-start.32 = (bf16[456,896]{1,0:T(8,128)(2,1)S(1)}, bf16[456,896]{1,0:T(8,128)(2,1)S(1)}, u32[]{:S(2)}, u32[]{:S(2)}) collective-permute-start(bf16[456,896]{1,0:T(8,128)(2,1)S(1)} %copy-done.10), channel_id=1, source_target_pairs={{0,2},{1,3},{4,0},{5,1},{8,4},{9,5},{12,8},{13,9},{14,12},{15,13},... | collective-permute-start | bytes 2451464 | tf_op jit(solution)/shard_map/ppermute | solution.py:62
  140.3 19.2 %collective-permute-start.27 = (bf16[64,256]{1,0:T(8,128)(2,1)S(1)}, bf16[64,256]{1,0:T(8,128)(2,1)S(1)}, u32[]{:S(2)}, u32[]{:S(2)}) collective-permute-start(bf16[64,256]{1,0:T(8,128)(2,1)S(1)} %get-tuple-element.212), channel_id=1, source_target_pairs={{0,2},{1,3},{4,0},{5,1},{8,4},{9,5},{12,8},{13,9},{14,12},{15,13},... | collective-permute-start | bytes 98312 | tf_op jit(solution)/shard_map/ppermute | solution.py:62
  142.3 17.8 %collective-permute-start.24 = (bf16[128,256]{1,0:T(8,128)(2,1)S(1)}, bf16[128,256]{1,0:T(8,128)(2,1)S(1)}, u32[]{:S(2)}, u32[]{:S(2)}) collective-permute-start(bf16[128,256]{1,0:T(8,128)(2,1)S(1)} %pad_maximum_fusion.9), channel_id=1, source_target_pairs={{0,4},{1,5},{4,8},{5,9},{8,12},{9,13},{12,14},{13,15},{14,10},{15,... | collective-permute-start | bytes 196616 | tf_op jit(solution)/shard_map/ppermute | solution.py:62
  178.2 21.8 %collective-permute-start.38 = (bf16[512,896]{1,0:T(8,128)(2,1)S(1)}, bf16[512,896]{1,0:T(8,128)(2,1)S(1)}, u32[]{:S(2)}, u32[]{:S(2)}) collective-permute-start(bf16[512,896]{1,0:T(8,128)(2,1)S(1)} %pad_maximum_fusion.4.refs_5_), channel_id=1, source_target_pairs={{0,1},{1,0},{2,3},{3,2},{4,5},{5,4},{6,7},{7,6},{8,9},{9,8},{10,11... | collective-permute-start | bytes 2752520 | tf_op jit(solution)/shard_map/ppermute | solution.py:50
  178.7 20.2 %collective-permute-start.33 = (bf16[456,896]{1,0:T(8,128)(2,1)S(1)}, bf16[456,896]{1,0:T(8,128)(2,1)S(1)}, u32[]{:S(2)}, u32[]{:S(2)}) collective-permute-start(bf16[456,896]{1,0:T(8,128)(2,1)S(1)} %copy-done.13), channel_id=1, source_target_pairs={{0,4},{1,5},{4,8},{5,9},{8,12},{9,13},{12,14},{13,15},{14,10},{15,... | collective-permute-start | bytes 2451464 | tf_op jit(solution)/shard_map/ppermute | solution.py:62
  185.0 15.0 %collective-permute-start.37 = (bf16[288,1152]{1,0:T(8,128)(2,1)S(1)}, bf16[288,1152]{1,0:T(8,128)(2,1)S(1)}, u32[]{:S(2)}, u32[]{:S(2)}) collective-permute-start(bf16[288,1152]{1,0:T(8,128)(2,1)S(1)} %constant_dynamic-update-slice_fusion.13.refs_3_), channel_id=1, source_target_pairs={{0,1},{1,0},{2,3},{3,2},{4,5},{5,4},{6,7},{7,6},{8,9},{9,8},{10,11... | collective-permute-start | bytes 1990664 | tf_op jit(solution)/shard_map/ppermute | solution.py:50
  210.2 33.3 %collective-permute-start.35 = (bf16[456,896]{1,0:T(8,128)(2,1)S(1)}, bf16[456,896]{1,0:T(8,128)(2,1)S(1)}, u32[]{:S(2)}, u32[]{:S(2)}) collective-permute-start(bf16[456,896]{1,0:T(8,128)(2,1)S(1)} %copy-done.11), channel_id=1, source_target_pairs={{0,2},{1,3},{4,0},{5,1},{8,4},{9,5},{12,8},{13,9},{14,12},{15,13},... | collective-permute-start | bytes 2451464 | tf_op jit(solution)/shard_map/ppermute | solution.py:62
  210.6 32.9 %collective-permute-start.34 = (bf16[456,896]{1,0:T(8,128)(2,1)S(1)}, bf16[456,896]{1,0:T(8,128)(2,1)S(1)}, u32[]{:S(2)}, u32[]{:S(2)}) collective-permute-start(bf16[456,896]{1,0:T(8,128)(2,1)S(1)} %copy-done.12), channel_id=1, source_target_pairs={{0,4},{1,5},{4,8},{5,9},{8,12},{9,13},{12,14},{13,15},{14,10},{15,... | collective-permute-start | bytes 2451464 | tf_op jit(solution)/shard_map/ppermute | solution.py:62
  213.1 17.7 %collective-permute-start.43 = (bf16[40,896]{1,0:T(8,128)(2,1)S(1)}, bf16[40,896]{1,0:T(8,128)(2,1)S(1)}, u32[]{:S(2)}, u32[]{:S(2)}) collective-permute-start(bf16[40,896]{1,0:T(8,128)(2,1)S(1)} %get-tuple-element.210), channel_id=1, source_target_pairs={{0,2},{1,3},{4,0},{5,1},{8,4},{9,5},{12,8},{13,9},{14,12},{15,13},... | collective-permute-start | bytes 215048 | tf_op jit(solution)/shard_map/ppermute | solution.py:62
  215.4 17.9 %collective-permute-start.40 = (bf16[80,896]{1,0:T(8,128)(2,1)S(1)}, bf16[80,896]{1,0:T(8,128)(2,1)S(1)}, u32[]{:S(2)}, u32[]{:S(2)}) collective-permute-start(bf16[80,896]{1,0:T(8,128)(2,1)S(1)} %pad_maximum_fusion.7), channel_id=1, source_target_pairs={{0,4},{1,5},{4,8},{5,9},{8,12},{9,13},{12,14},{13,15},{14,10},{15,... | collective-permute-start | bytes 430088 | tf_op jit(solution)/shard_map/ppermute | solution.py:62
  251.2 23.9 %collective-permute-start.48 = (bf16[536,896]{1,0:T(8,128)(2,1)}, bf16[536,896]{1,0:T(8,128)(2,1)S(1)}, u32[]{:S(2)}, u32[]{:S(2)}) collective-permute-start(bf16[536,896]{1,0:T(8,128)(2,1)} %shard_map.204.refs_0_), channel_id=1, source_target_pairs={{0,4},{1,5},{4,8},{5,9},{8,12},{9,13},{12,14},{13,15},{14,10},{15,... | collective-permute-start | bytes 2881544 | tf_op jit(solution)/shard_map/ppermute | solution.py:62
  252.7 23.6 %collective-permute-start.49 = (bf16[536,896]{1,0:T(8,128)(2,1)}, bf16[536,896]{1,0:T(8,128)(2,1)S(1)}, u32[]{:S(2)}, u32[]{:S(2)}) collective-permute-start(bf16[536,896]{1,0:T(8,128)(2,1)} %shard_map.204.refs_0_), channel_id=1, source_target_pairs={{0,2},{1,3},{4,0},{5,1},{8,4},{9,5},{12,8},{13,9},{14,12},{15,13},... | collective-permute-start | bytes 2881544 | tf_op jit(solution)/shard_map/ppermute | solution.py:62
  277.8 23.4 %collective-permute-start.52 = (bf16[536,896]{1,0:T(8,128)(2,1)}, bf16[536,896]{1,0:T(8,128)(2,1)S(1)}, u32[]{:S(2)}, u32[]{:S(2)}) collective-permute-start(bf16[536,896]{1,0:T(8,128)(2,1)} %get-tuple-element.161.refs_0_), channel_id=1, source_target_pairs={{0,4},{1,5},{4,8},{5,9},{8,12},{9,13},{12,14},{13,15},{14,10},{15,... | collective-permute-start | bytes 2881544 | tf_op jit(solution)/shard_map/ppermute | solution.py:62
  278.6 23.1 %collective-permute-start.53 = (bf16[536,896]{1,0:T(8,128)(2,1)}, bf16[536,896]{1,0:T(8,128)(2,1)S(1)}, u32[]{:S(2)}, u32[]{:S(2)}) collective-permute-start(bf16[536,896]{1,0:T(8,128)(2,1)} %get-tuple-element.162.refs_2_), channel_id=1, source_target_pairs={{0,2},{1,3},{4,0},{5,1},{8,4},{9,5},{12,8},{13,9},{14,12},{15,13},... | collective-permute-start | bytes 2881544 | tf_op jit(solution)/shard_map/ppermute | solution.py:62
  303.2 23.4 %collective-permute-start.56 = (bf16[536,896]{1,0:T(8,128)(2,1)}, bf16[536,896]{1,0:T(8,128)(2,1)S(1)}, u32[]{:S(2)}, u32[]{:S(2)}) collective-permute-start(bf16[536,896]{1,0:T(8,128)(2,1)} %get-tuple-element.170.refs_0_), channel_id=1, source_target_pairs={{0,4},{1,5},{4,8},{5,9},{8,12},{9,13},{12,14},{13,15},{14,10},{15,... | collective-permute-start | bytes 2881544 | tf_op jit(solution)/shard_map/ppermute | solution.py:62
  304.0 23.1 %collective-permute-start.57 = (bf16[536,896]{1,0:T(8,128)(2,1)}, bf16[536,896]{1,0:T(8,128)(2,1)S(1)}, u32[]{:S(2)}, u32[]{:S(2)}) collective-permute-start(bf16[536,896]{1,0:T(8,128)(2,1)} %get-tuple-element.171.refs_2_), channel_id=1, source_target_pairs={{0,2},{1,3},{4,0},{5,1},{8,4},{9,5},{12,8},{13,9},{14,12},{15,13},... | collective-permute-start | bytes 2881544 | tf_op jit(solution)/shard_map/ppermute | solution.py:62
  (102 other events, 735.3 us)

commit v9 on v7

--- a/solution.py
+++ b/solution.py
@@ -157,26 +157,20 @@
             fwd, back = self.hop(mine_f, 1), self.hop(mine_b, -1)
         return [local[0], fwd, back]
 
-    def ring_sum(self, terms, stages):
-        n = self.chips
-        half = n // 2
+    def ring_sum(self, terms):
+        half = self.chips // 2
         fwd, back = self.hop(terms[half], 1), self.hop(terms[half - 1], -1)
 
         def add(got, slot):
             return (got.astype(f32) + terms[slot].astype(f32)).astype(bf16)
 
         for s in range(1, half):
-            fwd = add(fwd, half + s)
+            fwd = self.hop(add(fwd, half + s), 1)
             if s < half - 1:
-                back = add(back, half - 1 - s)
-                stages[s - 1](fwd, back)
-                fwd, back = self.hop(fwd, 1), self.hop(back, -1)
-            else:
-                stages[s - 1](fwd)
-                fwd = self.hop(fwd, 1)
+                back = self.hop(add(back, half - 1 - s), -1)
         return fwd, back
 
-    def gather_placed(self, x, place):
+    def gather_placed(self, x, place, rest):
         n = self.chips
         half = n // 2
         fwd = back = x
@@ -194,7 +188,7 @@
                 fwd, back = self.hop(fwd[:cut], 1), self.hop(back[cut:], -1)
         placed, token = place(*waiting, placed)
         far = join(fwd, back, token)
-        return place([half], [(far, self.swap(far))], placed)[0]
+        return place([half], [(far, self.swap(far))], placed, rest)[0]
 
 
 VMEM_BYTES = 56 * 1024 * 1024
@@ -433,9 +427,16 @@
     normed_ref[...] = (hidden * inverse * gain_ref[...]).astype(bf16)
 
 
+def turn_back(grad, cos_ref, sin_ref):
+    scaled = grad * sin_ref[...]
+    early = lanes(grad.shape) % HD < HD // 2
+    turned = jnp.where(early, pltpu.roll(scaled, 96, 1), -pltpu.roll(scaled, 32, 1))
+    return grad * cos_ref[...] + turned
+
+
 def backward_kernel(
     ctx, meta_ref, gn_ref, hidden_ref, gout_ref, gain_ref, w_ref, spread_ref, k_ref, v_ref, lse_ref,
-    o_ref,
+    o_ref, cos_ref, sin_ref,
     gh_ref, ga_ref, gain_grad_ref, gq_ref, mine_ref, other_ref,
     go_ref, gqs_ref, gk_ref, gv_ref,
 ):
@@ -500,7 +501,8 @@
         lax.fori_loop(0, last, body, 0)
         step(last, True)
     for tile in range(WIDTH_Q // 128):
-        gq_ref[:, tile * 128 : (tile + 1) * 128] = join_heads(gqs_ref, half, tile) * HD ** (-0.5)
+        grad = join_heads(gqs_ref, half, tile) * HD ** (-0.5)
+        gq_ref[:, tile * 128 : (tile + 1) * 128] = turn_back(grad, cos_ref, sin_ref).astype(bf16)
     for j in range(ctx):
         dst = mine_ref if j < chips else other_ref
         at = (j % chips) * rows
@@ -513,6 +515,9 @@
             dst[to, WIDTH_K:] = gv_ref[frm, :].astype(dst.dtype)
 
 
+SUM_ROWS = 16
+
+
 def finish_kernel(
     gq_ref, x_ref, gain_ref, w_ref, cos_ref, sin_ref, gh_ref, gain_two_ref, *refs
 ):
@@ -521,18 +526,10 @@
     for ref in refs[1:-4]:
         pair = pair + ref[...].astype(f32)
     rows = pair.shape[0]
-    joint_ref = sent_ref.at[:rows, :]
-    cosine = cos_ref[...]
-    sine = sin_ref[...]
-    early = lanes(cosine.shape) % HD < HD // 2
-    for i in range((WIDTH_Q + WIDTH_K) // 128):
-        at = slice(i * 128, (i + 1) * 128)
-        grad = gq_ref[:, at] if i * 128 < WIDTH_Q else pair[:, :WIDTH_K]
-        scaled = grad * sine
-        turned = jnp.where(early, pltpu.roll(scaled, 96, 1), -pltpu.roll(scaled, 32, 1))
-        joint_ref[:, at] = (grad * cosine + turned).astype(bf16)
-    joint_ref[:, WIDTH_Q + WIDTH_K :] = pair[:, WIDTH_K:].astype(bf16)
-    joint = joint_ref[...]
+    keys = turn_back(pair[:, :WIDTH_K], cos_ref, sin_ref)
+    pair = jnp.concatenate([keys, pair[:, WIDTH_K:]], 1).astype(bf16)
+    sent_ref[:rows, :] = pair
+    joint = jnp.concatenate([gq_ref[...], pair], 1)
     bias = jnp.sum(joint.astype(f32), 0, keepdims=True)
     bias_ref[...] = bias
     grad = dot_nt(joint, w_ref[...])
@@ -541,17 +538,33 @@
     unit = x * inverse
     gain = jnp.sum(grad * unit, 0, keepdims=True)
     gain_grad_ref[...] = gain
-    wide = [jnp.zeros((1, bias.shape[1] - gain.shape[1]), f32)]
-    found = []
-    for row in (jnp.concatenate([gain] + wide, 1), jnp.concatenate([gain_two_ref[...]] + wide, 1), bias):
-        high = row.astype(bf16)
-        found += [high.astype(f32), row - high.astype(f32)]
-    found.append(jnp.zeros((sent_ref.shape[0] - rows - len(found), bias.shape[1]), f32))
-    sent_ref[rows:, :] = jnp.concatenate(found, 0).astype(bf16)
     scaled = grad * gain_ref[...]
     gx_ref[...] = gh_ref[...] + inverse * (
         scaled - unit * jnp.mean(scaled * unit, -1, keepdims=True)
     )
+    sums = jnp.concatenate([gain, gain_two_ref[...], bias], 1)
+    width = pair.shape[1]
+    sums = jnp.concatenate([sums, jnp.zeros((1, -sums.shape[1] % width), f32)], 1)
+    found = [sums[:, i : i + width] for i in range(0, sums.shape[1], width)]
+    found += [jnp.zeros((1, width), f32)] * (SUM_ROWS - len(found))
+    sums = jnp.concatenate(found, 0)
+    high = sums.astype(bf16)
+    sent_ref[rows : rows + SUM_ROWS, :] = high
+    sent_ref[rows + SUM_ROWS :, :] = (sums - high.astype(f32)).astype(bf16)
+
+
+def pair_grad_kernel(rows, half_width, meta_ref, norm_ref, own_ref, peer_ref, out_ref, turned_ref):
+    turned_ref[...] = norm_ref[:, D:].T
+    first = pl.multiple_of(meta_ref[0] * half_width, 16)
+    both = jnp.concatenate([own_ref[:rows, :], peer_ref[:rows, :]], 0)
+    part = jnp.dot(turned_ref[pl.ds(first, half_width), :], both, preferred_element_type=f32)
+    out_ref[:half_width, :] = part.astype(bf16)
+
+    def sums(ref):
+        high = ref[rows : rows + SUM_ROWS, :].astype(f32)
+        return high + ref[rows + SUM_ROWS :, :].astype(f32)
+
+    out_ref[half_width:, :] = (sums(own_ref) + sums(peer_ref)).astype(bf16)
 
 
 def mlp_kernel(
@@ -729,45 +742,37 @@
 
 
 def small_grad_kernel(
-    chips, q_rows, rows, meta_ref, norm_a, norm_b, joint_a, joint_b, near_a, near_b, *refs
+    chips, q_rows, rows, cols, meta_ref, norm_a, norm_b, att_a, att_b, near_a, near_b, *refs
 ):
-    out_refs, acc, sums_ref = refs[:-2], refs[-2], refs[-1]
-    cols = joint_a.shape[1]
-    tokens, sums, attended, grads = [], [], [], []
-    for joint_ref, near_ref in ((joint_a, near_a), (joint_b, near_b)):
+    out_refs, acc, turned_ref = refs[:-2], refs[-2], refs[-1]
+    first = pl.multiple_of((2 * meta_ref[0] + meta_ref[1]) * q_rows, 16)
+    grads, queries = [], []
+    for near_ref in (near_a, near_b):
         for b in range(2):
-            at = b * (rows + 16)
-            tokens.append(joint_ref[at : at + rows, :])
-            found = joint_ref[at + rows : at + rows + 16, :].astype(f32)
-            sums.append([found[2 * i : 2 * i + 1] + found[2 * i + 1 : 2 * i + 2] for i in range(3)])
-            attended.append(near_ref[2 * b * rows : (2 * b + 1) * rows, :])
-            grads.append(near_ref[(2 * b + 1) * rows : (2 * b + 2) * rows, :])
-    norm = jnp.concatenate([norm_a[:, D:], norm_b[:, D:]], 0)
-    sums = [(sums[0][i] + sums[1][i]) + (sums[2][i] + sums[3][i]) for i in range(3)]
-    sums_ref[...] = jnp.zeros_like(sums_ref)
-    sums_ref[:1, :D] = sums[0][:, :D]
-    sums_ref[:1, D : 2 * D] = sums[1][:, :D]
-    sums_ref[:1, 2 * D : 2 * D + cols] = sums[2]
-    acc[:, :cols] = dot_tn(norm, jnp.concatenate(tokens, 0))
-    acc[:, cols:] = dot_tn(jnp.concatenate(attended, 0), jnp.concatenate(grads, 0))
-    first = pl.multiple_of((2 * meta_ref[0] + meta_ref[1]) * q_rows, 16)
+            grads.append(near_ref[2 * b * rows : (2 * b + 1) * rows, :])
+            queries.append(near_ref[(2 * b + 1) * rows : (2 * b + 2) * rows, :])
+    turned_ref[...] = jnp.concatenate([norm_a[:, D:], norm_b[:, D:]], 0).T
+    acc[:, :WIDTH_Q] = jnp.dot(
+        turned_ref[pl.ds(first, q_rows), :],
+        jnp.concatenate(queries, 0),
+        preferred_element_type=f32,
+    ).astype(bf16)
+    acc[:, WIDTH_Q:cols] = jnp.zeros((q_rows, cols - WIDTH_Q), bf16)
+    turned_ref[...] = jnp.concatenate([att_a[...], att_b[...]], 0).T
+    acc[:, cols:] = jnp.dot(
+        turned_ref[pl.ds(first, q_rows), :], jnp.concatenate(grads, 0), preferred_element_type=f32
+    ).astype(bf16)
     width = acc.shape[1] // chips
-    share = sums_ref.shape[1] // chips
     for out_ref, slot in zip(out_refs, range(chips)):
         owner = meta_ref[12 + slot]
-        block = acc[pl.ds(first, q_rows), pl.ds(pl.multiple_of(owner * width, 128), width)]
-        tall = jnp.concatenate(
-            [block[:, i * 128 : (i + 1) * 128] for i in range(width // 128)], 0
-        ).astype(bf16)
-        piece = out_ref.shape[0] - 16
+        block = acc[:, pl.ds(pl.multiple_of(owner * width, 128), width)]
+        tall = jnp.concatenate([block[:, i * 128 : (i + 1) * 128] for i in range(width // 128)], 0)
+        piece = out_ref.shape[0]
         for i in range(D // 128):
-            out_ref[:piece, i * 128 : (i + 1) * 128] = tall[i * piece : (i + 1) * piece]
-        vector = sums_ref[:, pl.ds(pl.multiple_of(owner * share, 128), share)]
-        out_ref[piece:, :] = jnp.zeros((16, D), bf16)
-        out_ref[piece:, :share] = jnp.concatenate([vector, vector], 0).astype(bf16)
-
-
-def place_all(meta, slots, pairs, old, sizes):
+            out_ref[:, i * 128 : (i + 1) * 128] = tall[i * piece : (i + 1) * piece]
+
+
+def place_all(meta, slots, pairs, old, sizes, rest=None):
     main, ff_loc, q_rows, cols, down_rows, chips = sizes
     mlp_rows = D // chips
     columns = (2 * main + 128) // 128
@@ -776,18 +781,18 @@
     top = columns * 16
     blocks = [x for pair in pairs for x in pair]
     count = len(blocks)
-    piece = blocks[0].shape[0] - top - down_rows - 16
-    share = 3 * 128
+    piece = blocks[0].shape[0] - top - down_rows
     parts = (cols + D) // chips // 128
     keep = [] if old is None else list(old)
+    last = [] if rest is None else [rest]
+    known = WIDTH_Q // 128
 
     def kernel(meta_ref, *refs):
         ins = refs[:count]
-        gate_out, up_out, down_out, joint_out, proj_out, sums_out, token_ref = refs[
-            count + len(keep) : count + len(keep) + 7
-        ]
-        gate_buf, up_buf, down_buf, small_buf, sums_buf, sems, small_sems = refs[
-            count + len(keep) + 7 :
+        outs_at = count + len(last) + len(keep)
+        gate_out, up_out, down_out, joint_out, proj_out, token_ref = refs[outs_at : outs_at + 6]
+        gate_buf, up_buf, down_buf, small_buf, rest_buf, sems, small_sems, rest_sem = refs[
+            outs_at + 6 :
         ]
         core_zero = meta_ref[1] == 0
         copies = []
@@ -820,17 +825,14 @@
                     up_buf[k, :, main : main + 128] = pltpu.roll(jnp.where(left, one, zero), 64, 1)
             owner = meta_ref[12 + slot]
             here = pl.ds(pl.multiple_of(owner * mlp_rows, 8), mlp_rows)
-            send(gate_buf.at[k], gate_out.at[here, :], sems.at[5 * k])
-            send(up_buf.at[k], up_out.at[here, :], sems.at[5 * k + 1])
-            sums_buf[k] = ins[2 * k][top + piece : top + piece + 16, :share].astype(f32)[:8]
-            here = pl.ds(pl.multiple_of(owner * 8, 8), 8)
-            send(sums_buf.at[k], sums_out.at[here, :], sems.at[5 * k + 4])
+            send(gate_buf.at[k], gate_out.at[here, :], sems.at[4 * k])
+            send(up_buf.at[k], up_out.at[here, :], sems.at[4 * k + 1])
             for side in range(2):
                 b = 2 * k + side
                 core = meta_ref[1] if side == 0 else 1 - meta_ref[1]
-                down_buf[b] = ins[b][top + piece + 16 :, :].astype(f32)
+                down_buf[b] = ins[b][top + piece :, :].astype(f32)
                 here = pl.ds(pl.multiple_of((core * chips + owner) * down_rows, 8), down_rows)
-                send(down_buf.at[b], down_out.at[here, :], sems.at[5 * k + 2 + side])
+                send(down_buf.at[b], down_out.at[here, :], sems.at[4 * k + 2 + side])
                 tall = jnp.concatenate(
                     [ins[b][top : top + piece, i * 128 : (i + 1) * 128] for i in range(lanes_out)], 0
                 ).astype(f32)
@@ -839,7 +841,7 @@
                     small_buf[b, i] = tall[i * q_rows : (i + 1) * q_rows]
                     block = owner * parts + i
 
-                    @pl.when(block < cols // 128)
+                    @pl.when(block < known)
                     def joint(b=b, i=i, rows=rows, block=block):
                         at = pl.ds(pl.multiple_of(block * 128, 128), 128)
                         pltpu.make_async_copy(
@@ -854,15 +856,22 @@
                         ).start()
 
         token_ref[...] = jnp.zeros(token_ref.shape, f32)
+        if last:
+            rest_buf[...] = refs[count][: 2 * q_rows, :].astype(f32)
+            send(rest_buf, joint_out.at[:, WIDTH_Q:cols], rest_sem)
         for copy in copies:
             copy.wait()
         for b in range(count):
             for i in range(parts):
-                pltpu.make_async_copy(
-                    small_buf.at[b, i],
-                    proj_out.at[pl.ds(0, q_rows), pl.ds(0, 128)],
-                    small_sems.at[b, i],
-                ).wait()
+                block = meta_ref[12 + slots[b // 2]] * parts + i
+
+                @pl.when((block < known) | (block >= cols // 128))
+                def done(b=b, i=i):
+                    pltpu.make_async_copy(
+                        small_buf.at[b, i],
+                        proj_out.at[pl.ds(0, q_rows), pl.ds(0, 128)],
+                        small_sems.at[b, i],
+                    ).wait()
 
     anywhere = pl.BlockSpec(memory_space=pl.ANY)
     result = pl.pallas_call(
@@ -873,29 +882,29 @@
             jax.ShapeDtypeStruct((ff_loc, D), f32),
             jax.ShapeDtypeStruct((2 * q_rows, cols), f32),
             jax.ShapeDtypeStruct((2 * q_rows, D), f32),
-            jax.ShapeDtypeStruct((8 * chips, share), f32),
             jax.ShapeDtypeStruct((8, 128), f32),
         ],
         in_specs=[pl.BlockSpec(memory_space=pltpu.SMEM)]
-        + [pl.BlockSpec(memory_space=pltpu.VMEM)] * count
+        + [pl.BlockSpec(memory_space=pltpu.VMEM)] * (count + len(last))
         + [anywhere] * len(keep),
-        out_specs=[anywhere] * 6 + [pl.BlockSpec(memory_space=pltpu.VMEM)],
+        out_specs=[anywhere] * 5 + [pl.BlockSpec(memory_space=pltpu.VMEM)],
         scratch_shapes=[
             pltpu.VMEM((len(slots), mlp_rows, ff_loc), f32),
             pltpu.VMEM((len(slots), mlp_rows, ff_loc), f32),
             pltpu.VMEM((count, down_rows, D), f32),
             pltpu.VMEM((count, parts, q_rows, 128), f32),
-            pltpu.VMEM((len(slots), 8, share), f32),
-            pltpu.SemaphoreType.DMA((5 * len(slots),)),
+            pltpu.VMEM((2 * q_rows, cols - WIDTH_Q), f32),
+            pltpu.SemaphoreType.DMA((4 * len(slots),)),
             pltpu.SemaphoreType.DMA((count, parts)),
+            pltpu.SemaphoreType.DMA,
         ],
-        input_output_aliases={1 + count + i: i for i in range(len(keep))},
+        input_output_aliases={1 + count + len(last) + i: i for i in range(len(keep))},
         compiler_params=pltpu.CompilerParams(vmem_limit_bytes=VMEM_BYTES),
         cost_estimate=pl.CostEstimate(
             flops=0, bytes_accessed=8 * sum(x.size for x in blocks), transcendentals=0
         ),
-    )(meta, *blocks, *keep)
-    return list(result[:6]), result[6]
+    )(meta, *blocks, *last, *keep)
+    return list(result[:5]), result[5]
 
 
 def place_blocks(blocks, spots, out_shape, old=None):
@@ -1061,13 +1070,13 @@
                 jax.ShapeDtypeStruct((rows, D), f32),
                 jax.ShapeDtypeStruct((rows, D), bf16),
                 jax.ShapeDtypeStruct((1, D), f32),
-                jax.ShapeDtypeStruct((rows, WIDTH_Q), f32),
+                jax.ShapeDtypeStruct((rows, WIDTH_Q), bf16),
                 jax.ShapeDtypeStruct((chips * rows, 2 * WIDTH_K), f32),
                 jax.ShapeDtypeStruct((chips * rows, 2 * WIDTH_K), bf16),
             ],
             [
                 meta, grad_two, hidden, cotangent[0], gain_two, w_out_full, spread, keys, values, lse,
-                attended,
+                attended, cosine, sine,
             ],
             smem=1,
             scratch=[
@@ -1078,58 +1087,39 @@
             ],
             flops=20 * KH * part_rows * total_keys * 128,
         )
-        swapped_terms = net.swap(terms_other)
-
-        def finish(wait_pairs=()):
-            pair_sums = call(
-                pair_kernel,
-                [jax.ShapeDtypeStruct((rows, 2 * WIDTH_K), f32)]
-                + [jax.ShapeDtypeStruct((rows, 2 * WIDTH_K), bf16)] * (chips - 1),
-                [terms_mine, swapped_terms] + list(wait_pairs),
-                loose=len(wait_pairs),
+        pair_sums = call(
+            pair_kernel,
+            [jax.ShapeDtypeStruct((rows, 2 * WIDTH_K), f32)]
+            + [jax.ShapeDtypeStruct((rows, 2 * WIDTH_K), bf16)] * (chips - 1),
+            [terms_mine, net.swap(terms_other)],
+        )
+        grad_pairs = net.ring_parts(pair_sums)
+
+        def finish(*after):
+            return call(
+                finish_kernel,
+                [
+                    jax.ShapeDtypeStruct((rows + 2 * SUM_ROWS, 2 * WIDTH_K), bf16),
+                    jax.ShapeDtypeStruct((rows, D), f32),
+                    jax.ShapeDtypeStruct((1, D), f32),
+                    jax.ShapeDtypeStruct((1, w_qkv.shape[1]), f32),
+                ],
+                [grad_queries, x, gain_one, w_qkv_full, cosine, sine, grad_hidden, grad_gain_two]
+                + grad_pairs
+                + list(after),
+                loose=len(after),
             )
-            grad_pairs = net.ring_parts(pair_sums)
-
-            def last(wait_finish=()):
-                joint, grad_input, grad_gain_one, grad_bias = call(
-                    finish_kernel,
-                    [
-                        jax.ShapeDtypeStruct((rows + 16, 1152), bf16),
-                        jax.ShapeDtypeStruct((rows, D), f32),
-                        jax.ShapeDtypeStruct((1, D), f32),
-                        jax.ShapeDtypeStruct((1, 1152), f32),
-                    ],
-                    [grad_queries, x, gain_one, w_qkv_full, cosine, sine, grad_hidden, grad_gain_two]
-                    + grad_pairs
-                    + list(wait_finish),
-                    flops=2 * rows * D * 1152,
-                    loose=len(wait_finish),
-                )
-                return (grad_attn_low, grad_gain_two, joint, grad_input, grad_gain_one, grad_bias)
-
-            return last
-
-        return finish
-
-    found = []
-    steps = [attention_back()]
+
+        return grad_attn_low, grad_gain_two, grad_queries, finish
+
+    grad_attn_low, grad_gain_two, grad_queries, finish = attention_back()
     if tiled:
-
-        def pairs_stage(*blocks):
-            steps.append(steps[0](blocks))
-
-        def finish_stage(*blocks):
-            found.extend(steps[1](blocks))
-
-        def small_stage(*blocks):
-            found.append(blocks)
-
         terms = mlp_gradients(
             spots, x_turned, early, mid_turned, gate_low, up_low, sent_two, chips, down_rows, main
         )
-        fwd, back = net.ring_sum(terms, [pairs_stage, finish_stage, small_stage])
-        wait_small = found.pop()
+        fwd, back = net.ring_sum(terms)
         sum_mlp, sum_down = ring_end(fwd, back, terms[0], terms[0].shape[0] - down_rows)
+        pair_sent, grad_input, grad_gain_one, grad_bias = finish(sum_down)
     else:
         part_down = jnp.einsum(
             "tf,td->fd", middle, grad_out_group, preferred_element_type=f32
@@ -1165,52 +1155,57 @@
 
         sum_mlp = net.ring_scatter([mlp_chunk(s) for s in range(chips)]).astype(bf16)
         sum_mlp = lax.optimization_barrier(sum_mlp)
-        found.extend(steps[0]()())
-    grad_attn_low, grad_gain_two, grad_joint_low, grad_input, grad_gain_one, grad_bias = found
+        pair_sent, grad_input, grad_gain_one, grad_bias = finish()
 
     out_sum = mlp_chip[:rows]
-    sent = jnp.concatenate([attended_low, grad_attn_low], 0)
-    gathered = [sent]
     for s in range(1, net.dp):
-        got = net.shift(
-            jnp.concatenate([mlp_chip[s * rows : (s + 1) * rows].astype(bf16), sent], 0),
-            net.dp - s,
-        )
-        out_sum = out_sum + got[:rows].astype(f32)
-        gathered.append(got[rows:])
+        got = net.shift(mlp_chip[s * rows : (s + 1) * rows].astype(bf16), net.dp - s)
+        out_sum = out_sum + got.astype(f32)
     output = (hidden + out_sum).astype(bf16)
-    gathered = jnp.concatenate(gathered, 0)
-    near = (gathered, net.swap(gathered))
+    near = net.group_parts(jnp.concatenate([grad_attn_low, grad_queries], 0))
+    attended_parts = net.group_parts(attended_low)
 
     q_rows = w_qkv.shape[0] // 2
     qkv_cols = w_qkv.shape[1]
     if tiled:
         piece = q_rows * (qkv_cols + D) // chips // D
         terms_small = call(
-            lambda *refs: small_grad_kernel(chips, q_rows, rows, *refs),
-            [jax.ShapeDtypeStruct((piece + 16, D), bf16)] * chips,
-            [spots, *early, *net.group_parts(grad_joint_low), *near, *wait_small],
+            lambda *refs: small_grad_kernel(chips, q_rows, rows, qkv_cols, *refs),
+            [jax.ShapeDtypeStruct((piece, D), bf16)] * chips,
+            [spots, *early, *attended_parts, *near],
             smem=1,
-            loose=len(wait_small),
-            scratch=[pltpu.VMEM((D, qkv_cols + D), f32), pltpu.VMEM((8, 3 * 128 * chips), f32)],
+            scratch=[
+                pltpu.VMEM((q_rows, qkv_cols + D), bf16),
+                pltpu.VMEM((D, 2 * chip_rows), bf16),
+            ],
             flops=4 * chip_rows * D * (qkv_cols + D),
         )
         block = call(
             block_kernel,
-            [jax.ShapeDtypeStruct((sum_mlp.shape[0] + piece + 16 + down_rows, D), bf16)],
+            [jax.ShapeDtypeStruct((sum_mlp.shape[0] + piece + down_rows, D), bf16)],
             [sum_mlp, sum_down] + net.ring_parts(terms_small),
         )[0]
+        part_pair = call(
+            lambda *refs: pair_grad_kernel(rows, 2 * q_rows, *refs),
+            [jax.ShapeDtypeStruct((2 * q_rows + SUM_ROWS, 2 * WIDTH_K), bf16)],
+            [spots, early[0], pair_sent, net.shift(pair_sent, 1)],
+            smem=1,
+            scratch=[pltpu.VMEM((D, chip_rows), bf16)],
+        )[0]
+        grad_pair = lax.psum(part_pair, "ctx")
+        small = grad_pair[2 * q_rows :].reshape(-1)[: 2 * D + qkv_cols].astype(f32)
         sizes = (main, ff_loc, q_rows, qkv_cols, down_rows, chips)
-        grad_gate, grad_up, grad_down, grad_joint, grad_out_proj, sums = net.gather_placed(
-            block, lambda slots, pairs, old: place_all(spots, slots, pairs, old, sizes)
+        grad_gate, grad_up, grad_down, grad_joint, grad_out_proj = net.gather_placed(
+            block,
+            lambda slots, pairs, old, rest=None: place_all(spots, slots, pairs, old, sizes, rest),
+            grad_pair,
         )
-        small = sums.reshape(chips, 8, 384)[:, 0].reshape(-1)[: 2 * D + qkv_cols]
     else:
         gathered = jnp.concatenate(near, 0).reshape(2 * net.dp, 2, rows, D)
-        attended_group = gathered[:, 0].reshape(2 * net.dp * rows, D)
-        grad_attn_group = gathered[:, 1].reshape(2 * net.dp * rows, D)
+        grad_attn_group = gathered[:, 0].reshape(2 * net.dp * rows, D)
+        attended_group = jnp.concatenate(attended_parts, 0)
         normed_one_group = jnp.concatenate(early, 0)[:, D:]
-        joint_group = net.group_gather(grad_joint_low[:rows])
+        joint_group = net.group_gather(jnp.concatenate([grad_queries, pair_sent[:rows]], 1))
         q_first = net.d * (2 * q_rows) + core * q_rows
         group_rows = 2 * net.dp * rows
         part_out = jnp.einsum(

time: 353 us -> 451 us (1.28)
  waiting for transfers between devices: 138 us -> 228 us
  between operations: 1.34 us -> 14.9 us
  other arithmetic: 19.2 us -> 14 us
    psum x0 -> x1, waiting for transfers between devices: none -> 74.3 us  [local(): grad_pair = lax.psum(part_pair, 'ctx')]
    ppermute x7 -> x9, waiting for transfers between devices: 14.8 us -> 27.3 us  [shift(): return lax.ppermute(x, 'dp', [(i, (i + step) % n) for i in range(n)])]
    ppermute x39, waiting for transfers between devices: 114 us -> 120 us  [hop(): return lax.ppermute(x, 'ctx', perm)]
    ppermute x7 -> x9, starting transfers between devices: 10.2 us -> 11.8 us  [shift(): return lax.ppermute(x, 'dp', [(i, (i + step) % n) for i in range(n)])]
    pallas_call x9 -> x10, Pallas kernels: 47.7 us -> 47.9 us  [call(): pl.pallas_call(body, out_shape=list(outs), in_specs=specs, out_specs=[pl....]
  transfers between devices with their start and end apart: 63 -> 66, of which waited for: 38 -> 30; matrix products, arithmetic and copies ran while one was open for 9% -> 6% of each run, Pallas kernels for 17% -> 13%
where the time goes in v9:
time: 451 us; the launch traced here: 450 us
  waiting for transfers between devices  228 us (51%)
  Pallas kernels  100 us (22%)
  starting transfers between devices  55.4 us (12%)
  local copies, waits for them, and re-layouts  37 us (8%)
  between operations  14.9 us (3%)
  other arithmetic  14 us (3%)
    ppermute x39, waiting for transfers between devices, hop(): return lax.ppermute(x, 'ctx', perm)  120 us
    psum x1, waiting for transfers between devices, local(): grad_pair = lax.psum(part_pair, 'ctx')  74.3 us
    pallas_call x10, Pallas kernels, call(): pl.pallas_call(body, out_shape=list(outs), in_specs=specs, out_specs=[pl....  47.9 us
    ppermute x39, starting transfers between devices, hop(): return lax.ppermute(x, 'ctx', perm)  40.6 us
    ppermute x9, waiting for transfers between devices, shift(): return lax.ppermute(x, 'dp', [(i, (i + step) % n) for i in range(n)])  27.3 us
    pallas_call x5, Pallas kernels, place_all(): pl.pallas_call(kernel, out_shape=[jax.ShapeDtypeStruct((D, ff_loc), f32),...  26.1 us
    unnamed x135, local copies, waits for them, and re-layouts  19.5 us
    pallas_call x1, Pallas kernels, feed_forward(): pl.pallas_call(lambda *refs: mlp_kernel(half, *refs), out_shape=[jax.Shap...  16.2 us
  transfers between devices with their start and end apart: 66, of which 30 were waited for; matrix products, arithmetic and copies ran while one was open for 6% of the time, Pallas kernels for 13%

profile of v9, /device:TPU:0, one launch (start us, length us, event | category | flops | bytes accessed | tf_op | source)
XLA Modules:
  0.0 449.7 jit_solution(6902828535830803976)
XLA Ops:
  18.5 4.7 %collective-permute-done = bf16[224,1152]{1,0:T(8,128)(2,1)S(1)} collective-permute-done((bf16[224,1152]{1,0:T(8,128)(2,1)S(1)}, bf16[224,1152]{1,0:T(8,128)(2,1)S(1)}, u32[]{:S(2)}, u32[]{:S(2)}) %collective-permute-start) | collective-permute-done | bytes 516128 | tf_op jit(solution)/shard_map/ppermute | solution.py:54
  56.2 10.3 %shard_map.196 = (bf16[128,896]{1,0:T(8,128)(2,1)}, f32[2,896,128]{2,1,0:T(8,128)}, f32[2,2,8,448]{3,2,1,0:T(8,128)}, bf16[2,896,128]{2,1,0:T(8,128)(2,1)}, bf16...) custom-call(s32[17]{0:T(128)} %pad_add_fusion.refs_0_, ...), custom_call_target="tpu_custom_call" | custom-call | flops 1879048192 | bytes 6516292 | tf_op jit(solution)/shard_map/pallas_call | solution.py:213
  69.2 5.1 %collective-permute-done.13 = bf16[128,896]{1,0:T(8,128)(2,1)S(1)} collective-permute-done((bf16[128,896]{1,0:T(8,128)(2,1)}, bf16[128,896]{1,0:T(8,128)(2,1)S(1)}, u32[]{:S(2)}, u32[]{:S(2)}) %collective-permute-start.13) | collective-permute-done | bytes 229408 | tf_op jit(solution)/shard_map/ppermute | solution.py:54
  77.3 16.2 %shard_map.197 = (bf16[896,512]{1,0:T(8,128)(2,1)}, bf16[1280,512]{1,0:T(8,128)(2,1)}, bf16[512,1280]{1,0:T(8,128)(2,1)}, bf16[512,1280]{1,0:T(8,128)(2,1)}, f32...) custom-call(s32[20]{0:T(128)} %concatenate.66.refs_0_.meta_ref, bf16[256,896]{1,0:T(8,128)(2,1)} %copy-done.11, ...), custom_call_target="tpu_custom_call" | custom-call | flops 7046430720 | bytes 6881280 | tf_op jit(solution)/shard_map/pallas_call | solution.py:637
  100.7 6.2 %collective-permute-done.19 = bf16[128,896]{1,0:T(8,128)(2,1)S(1)} collective-permute-done((bf16[128,896]{1,0:T(8,128)(2,1)S(1)}, bf16[128,896]{1,0:T(8,128)(2,1)S(1)}, u32[]{:S(2)}, u32[]{:S(2)}) %collective-permute-start.19) | collective-permute-done | bytes 229408 | tf_op jit(solution)/shard_map/ppermute | solution.py:54
  107.8 15.0 %shard_map.198 = (f32[128,896]{1,0:T(8,128)}, bf16[128,896]{1,0:T(8,128)(2,1)}, f32[1,896]{1,0:T(1,128)}, bf16[128,896]{1,0:T(8,128)(2,1)}, f32[1024,256]{1,0:T(8,128)}, /*index=5*/bf16[1024,256]{1,0:T(8,128)(2,1)}) custom-call(s32[17]{0:T(128)} %pad_add_fusion.refs_0_, f32[128,896]{1,0:T(8,128)} %slice_add_fusion.refs_1_, ...), custom_call_target="tpu_custom_call" | custom-call | flops 4697620480 | bytes 7863364 | tf_op jit(solution)/shard_map/pallas_call | solution.py:213
  125.6 10.1 %shard_map.200 = (bf16[456,896]{1,0:T(8,128)(2,1)}, bf16[456,896]{1,0:T(8,128)(2,1)}, bf16[456,896]{1,0:T(8,128)(2,1)}, bf16[456,896]{1,0:T(8,128)(2,1)}, bf16[4...) custom-call(s32[20]{0:T(128)} %concatenate.66.refs_0_.meta_ref, ...), custom_call_target="tpu_custom_call" | custom-call | flops 3523215360 | bytes 13074432 | tf_op jit(solution)/shard_map/pallas_call | solution.py:723
  138.4 5.5 %collective-permute-done.36 = bf16[128,896]{1,0:T(8,128)(2,1)S(1)} collective-permute-done((bf16[128,896]{1,0:T(8,128)(2,1)S(1)}, bf16[128,896]{1,0:T(8,128)(2,1)S(1)}, u32[]{:S(2)}, u32[]{:S(2)}) %collective-permute-start.36) | collective-permute-done | bytes 229408 | tf_op jit(solution)/shard_map/ppermute | solution.py:54
  144.0 11.4 %collective-permute-done.29 = bf16[456,896]{1,0:T(8,128)(2,1)S(1)} collective-permute-done((bf16[456,896]{1,0:T(8,128)(2,1)}, bf16[456,896]{1,0:T(8,128)(2,1)S(1)}, u32[]{:S(2)}, u32[]{:S(2)}) %collective-permute-start.29) | collective-permute-done | bytes 817184 | tf_op jit(solution)/shard_map/ppermute | solution.py:62
  159.7 4.2 shard_map.203
  168.5 6.5 %collective-permute-done.30 = bf16[456,896]{1,0:T(8,128)(2,1)S(1)} collective-permute-done((bf16[456,896]{1,0:T(8,128)(2,1)S(1)}, bf16[456,896]{1,0:T(8,128)(2,1)S(1)}, u32[]{:S(2)}, u32[]{:S(2)}) %collective-permute-start.30) | collective-permute-done | bytes 817184 | tf_op jit(solution)/shard_map/ppermute | solution.py:62
  179.8 16.0 %collective-permute-done.31 = bf16[456,896]{1,0:T(8,128)(2,1)S(1)} collective-permute-done((bf16[456,896]{1,0:T(8,128)(2,1)S(1)}, bf16[456,896]{1,0:T(8,128)(2,1)S(1)}, u32[]{:S(2)}, u32[]{:S(2)}) %collective-permute-start.31) | collective-permute-done | bytes 817184 | tf_op jit(solution)/shard_map/ppermute | solution.py:62
  200.4 16.1 %collective-permute-done.42 = bf16[64,896]{1,0:T(8,128)(2,1)S(1)} collective-permute-done((bf16[64,896]{1,0:T(8,128)(2,1)S(1)}, bf16[64,896]{1,0:T(8,128)(2,1)S(1)}, u32[]{:S(2)}, u32[]{:S(2)}) %collective-permute-start.42) | collective-permute-done | bytes 114720 | tf_op jit(solution)/shard_map/ppermute | solution.py:62
  229.7 4.1 shard_map.205
  233.8 15.5 %collective-permute-done.49.refs_1_ = bf16[520,896]{1,0:T(8,128)(2,1)S(1)} collective-permute-done((bf16[520,896]{1,0:T(8,128)(2,1)}, bf16[520,896]{1,0:T(8,128)(2,1)S(1)}, u32[]{:S(2)}, u32[]{:S(2)}) %collective-permute-start.49) | collective-permute-done | bytes 931872 | tf_op jit(solution)/shard_map/ppermute | solution.py:62
  262.7 6.0 %shard_map.207 = (f32[896,2432]{1,0:T(8,128)}, f32[896,2432]{1,0:T(8,128)}, f32[2432,896]{1,0:T(8,128)}, f32[448,1152]{1,0:T(8,128)}, f32[448,896]{1,0:T(8,128)}, /*index=5*/f32[8,128]{1,0:T(8,128)}) custom-call(s32[20]{0:T(128)} %concatenate.66.refs_0_.meta_ref, ...), custom_call_target="tpu_custom_call", output_to_operand_aliasing={{0}: (5, {}), {1}: (6, {}), {2}: (7, {}), {3}: (8, {}), {4}... | custom-call | bytes 14909440 | tf_op jit(solution)/shard_map/pallas_call | solution.py:877
  268.7 6.5 %collective-permute-done.53.refs_1_ = bf16[520,896]{1,0:T(8,128)(2,1)S(1)} collective-permute-done((bf16[520,896]{1,0:T(8,128)(2,1)}, bf16[520,896]{1,0:T(8,128)(2,1)S(1)}, u32[]{:S(2)}, u32[]{:S(2)}) %collective-permute-start.53) | collective-permute-done | bytes 931872 | tf_op jit(solution)/shard_map/ppermute | solution.py:62
  280.2 22.1 %collective-permute-done.25 = bf16[64,256]{1,0:T(8,128)(2,1)S(1)} collective-permute-done((bf16[64,256]{1,0:T(8,128)(2,1)S(1)}, bf16[64,256]{1,0:T(8,128)(2,1)S(1)}, u32[]{:S(2)}, u32[]{:S(2)}) %collective-permute-start.25) | collective-permute-done | bytes 32800 | tf_op jit(solution)/shard_map/ppermute | solution.py:62
  309.6 6.0 %shard_map.209 = (f32[896,2432]{1,0:T(8,128)}, f32[896,2432]{1,0:T(8,128)}, f32[2432,896]{1,0:T(8,128)}, f32[448,1152]{1,0:T(8,128)}, f32[448,896]{1,0:T(8,128)}, /*index=5*/f32[8,128]{1,0:T(8,128)}) custom-call(s32[20]{0:T(128)} %concatenate.66.refs_0_.meta_ref, ...), custom_call_target="tpu_custom_call", output_to_operand_aliasing={{0}: (5, {}), {1}: (6, {}), {2}: (7, {}), {3}: (8, {}), {4}... | custom-call | bytes 14909440 | tf_op jit(solution)/shard_map/pallas_call | solution.py:877
  325.9 11.6 %collective-permute-done.28.refs_10_ = bf16[128,256]{1,0:T(8,128)(2,1)S(1)} collective-permute-done((bf16[128,256]{1,0:T(8,128)(2,1)S(1)}, bf16[128,256]{1,0:T(8,128)(2,1)S(1)}, u32[]{:S(2)}, u32[]{:S(2)}) %collective-permute-start.28) | collective-permute-done | bytes 65568 | tf_op jit(solution)/shard_map/ppermute | solution.py:62
  342.3 4.4 collective-permute-done.64.refs_3_
  350.9 5.9 %shard_map.211 = (f32[896,2432]{1,0:T(8,128)}, f32[896,2432]{1,0:T(8,128)}, f32[2432,896]{1,0:T(8,128)}, f32[448,1152]{1,0:T(8,128)}, f32[448,896]{1,0:T(8,128)}, /*index=5*/f32[8,128]{1,0:T(8,128)}) custom-call(s32[20]{0:T(128)} %concatenate.66.refs_0_.meta_ref, ...), custom_call_target="tpu_custom_call", output_to_operand_aliasing={{0}: (5, {}), {1}: (6, {}), {2}: (7, {}), {3}: (8, {}), {4}... | custom-call | bytes 14909440 | tf_op jit(solution)/shard_map/pallas_call | solution.py:877
  361.4 74.3 %all-reduce.2.cloned.1.call-done.refs_2_ = bf16[464,256]{1,0:T(8,128)(2,1)} async-done(((bf16[464,256]{1,0:T(8,128)(2,1)}), bf16[464,256]{1,0:T(8,128)(2,1)}) %all-reduce.2.cloned.1.call-update) | async-done | bytes 237584 | tf_op jit(solution)/shard_map/psum | solution.py:1195
  438.6 4.3 shard_map.214
  (333 shorter events, 147.2 us)
Async XLA Ops:
  7.2 428.5 %all-reduce.2.cloned.1.call-start = ((), (), s32[]{:S(2)}) async-start(), calls=%async_computation | async-start | bytes 475136 | tf_op jit(solution)/shard_map/psum | solution.py:1195
  53.1 22.5 %collective-permute-start.16 = (bf16[256,1792]{1,0:T(8,128)(2,1)S(1)}, bf16[256,1792]{1,0:T(8,128)(2,1)S(1)}, u32[]{:S(2)}, u32[]{:S(2)}) collective-permute-start(bf16[256,1792]{1,0:T(8,128)(2,1)S(1)} %pad_maximum_fusion.3.refs_3_.refs_2_.refs_1_), channel_id=1, source_target_pairs={{0,1},{1,0},{2,3},{3,2},{4,5},{5,4},{6,7},{7,6},{8,9},{9,8},{10,11... | collective-permute-start | bytes 2752520 | tf_op jit(solution)/shard_map/ppermute | solution.py:50
  135.7 19.7 %collective-permute-start.29 = (bf16[456,896]{1,0:T(8,128)(2,1)}, bf16[456,896]{1,0:T(8,128)(2,1)S(1)}, u32[]{:S(2)}, u32[]{:S(2)}) collective-permute-start(bf16[456,896]{1,0:T(8,128)(2,1)} %get-tuple-element.133), channel_id=1, source_target_pairs={{0,4},{1,5},{4,8},{5,9},{8,12},{9,13},{12,14},{13,15},{14,10},{15,... | collective-permute-start | bytes 2451464 | tf_op jit(solution)/shard_map/ppermute | solution.py:62
  138.3 19.6 %collective-permute-start.39 = (bf16[512,896]{1,0:T(8,128)(2,1)S(1)}, bf16[512,896]{1,0:T(8,128)(2,1)S(1)}, u32[]{:S(2)}, u32[]{:S(2)}) collective-permute-start(bf16[512,896]{1,0:T(8,128)(2,1)S(1)} %constant_dynamic-update-slice_fusion.15.refs_5_), channel_id=1, source_target_pairs={{0,1},{1,0},{2,3},{3,2},{4,5},{5,4},{6,7},{7,6},{8,9},{9,8},{10,11... | collective-permute-start | bytes 2752520 | tf_op jit(solution)/shard_map/ppermute | solution.py:50
  175.2 20.6 %collective-permute-start.31 = (bf16[456,896]{1,0:T(8,128)(2,1)S(1)}, bf16[456,896]{1,0:T(8,128)(2,1)S(1)}, u32[]{:S(2)}, u32[]{:S(2)}) collective-permute-start(bf16[456,896]{1,0:T(8,128)(2,1)S(1)} %add_convert_fusion.3), channel_id=1, source_target_pairs={{0,4},{1,5},{4,8},{5,9},{8,12},{9,13},{12,14},{13,15},{14,10},{15,... | collective-permute-start | bytes 2451464 | tf_op jit(solution)/shard_map/ppermute | solution.py:62
  177.1 41.6 %collective-permute-start.35 = (bf16[456,896]{1,0:T(8,128)(2,1)S(1)}, bf16[456,896]{1,0:T(8,128)(2,1)S(1)}, u32[]{:S(2)}, u32[]{:S(2)}) collective-permute-start(bf16[456,896]{1,0:T(8,128)(2,1)S(1)} %add_convert_fusion), channel_id=1, source_target_pairs={{0,2},{1,3},{4,0},{5,1},{8,4},{9,5},{12,8},{13,9},{14,12},{15,13},... | collective-permute-start | bytes 2451464 | tf_op jit(solution)/shard_map/ppermute | solution.py:62
  177.6 20.6 %collective-permute-start.41 = (bf16[64,896]{1,0:T(8,128)(2,1)S(1)}, bf16[64,896]{1,0:T(8,128)(2,1)S(1)}, u32[]{:S(2)}, u32[]{:S(2)}) collective-permute-start(bf16[64,896]{1,0:T(8,128)(2,1)S(1)} %pad_maximum_fusion.6), channel_id=1, source_target_pairs={{0,4},{1,5},{4,8},{5,9},{8,12},{9,13},{12,14},{13,15},{14,10},{15,... | collective-permute-start | bytes 344072 | tf_op jit(solution)/shard_map/ppermute | solution.py:62
  179.3 20.6 %collective-permute-start.45 = (bf16[64,896]{1,0:T(8,128)(2,1)S(1)}, bf16[64,896]{1,0:T(8,128)(2,1)S(1)}, u32[]{:S(2)}, u32[]{:S(2)}) collective-permute-start(bf16[64,896]{1,0:T(8,128)(2,1)S(1)} %pad_maximum_fusion.7), channel_id=1, source_target_pairs={{0,2},{1,3},{4,0},{5,1},{8,4},{9,5},{12,8},{13,9},{14,12},{15,13},... | collective-permute-start | bytes 344072 | tf_op jit(solution)/shard_map/ppermute | solution.py:62
  196.0 22.7 %collective-permute-start.32 = (bf16[456,896]{1,0:T(8,128)(2,1)S(1)}, bf16[456,896]{1,0:T(8,128)(2,1)S(1)}, u32[]{:S(2)}, u32[]{:S(2)}) collective-permute-start(bf16[456,896]{1,0:T(8,128)(2,1)S(1)} %add_convert_fusion.2), channel_id=1, source_target_pairs={{0,4},{1,5},{4,8},{5,9},{8,12},{9,13},{12,14},{13,15},{14,10},{15,... | collective-permute-start | bytes 2451464 | tf_op jit(solution)/shard_map/ppermute | solution.py:62
  226.0 23.3 %collective-permute-start.49 = (bf16[520,896]{1,0:T(8,128)(2,1)}, bf16[520,896]{1,0:T(8,128)(2,1)S(1)}, u32[]{:S(2)}, u32[]{:S(2)}) collective-permute-start(bf16[520,896]{1,0:T(8,128)(2,1)} %shard_map.204.refs_0_), channel_id=1, source_target_pairs={{0,4},{1,5},{4,8},{5,9},{8,12},{9,13},{12,14},{13,15},{14,10},{15,... | collective-permute-start | bytes 2795528 | tf_op jit(solution)/shard_map/ppermute | solution.py:62
  227.6 23.0 %collective-permute-start.50 = (bf16[520,896]{1,0:T(8,128)(2,1)}, bf16[520,896]{1,0:T(8,128)(2,1)S(1)}, u32[]{:S(2)}, u32[]{:S(2)}) collective-permute-start(bf16[520,896]{1,0:T(8,128)(2,1)} %shard_map.204.refs_0_), channel_id=1, source_target_pairs={{0,2},{1,3},{4,0},{5,1},{8,4},{9,5},{12,8},{13,9},{14,12},{15,13},... | collective-permute-start | bytes 2795528 | tf_op jit(solution)/shard_map/ppermute | solution.py:62
  252.0 23.1 %collective-permute-start.53 = (bf16[520,896]{1,0:T(8,128)(2,1)}, bf16[520,896]{1,0:T(8,128)(2,1)S(1)}, u32[]{:S(2)}, u32[]{:S(2)}) collective-permute-start(bf16[520,896]{1,0:T(8,128)(2,1)} %get-tuple-element.155.refs_0_), channel_id=1, source_target_pairs={{0,4},{1,5},{4,8},{5,9},{8,12},{9,13},{12,14},{13,15},{14,10},{15,... | collective-permute-start | bytes 2795528 | tf_op jit(solution)/shard_map/ppermute | solution.py:62
  253.6 22.5 %collective-permute-start.54 = (bf16[520,896]{1,0:T(8,128)(2,1)}, bf16[520,896]{1,0:T(8,128)(2,1)S(1)}, u32[]{:S(2)}, u32[]{:S(2)}) collective-permute-start(bf16[520,896]{1,0:T(8,128)(2,1)} %get-tuple-element.156.refs_2_), channel_id=1, source_target_pairs={{0,2},{1,3},{4,0},{5,1},{8,4},{9,5},{12,8},{13,9},{14,12},{15,13},... | collective-permute-start | bytes 2795528 | tf_op jit(solution)/shard_map/ppermute | solution.py:62
  259.9 19.8 %collective-permute-start.21 = (bf16[64,256]{1,0:T(8,128)(2,1)S(1)}, bf16[64,256]{1,0:T(8,128)(2,1)S(1)}, u32[]{:S(2)}, u32[]{:S(2)}) collective-permute-start(bf16[64,256]{1,0:T(8,128)(2,1)S(1)} %get-tuple-element.203), channel_id=1, source_target_pairs={{0,4},{1,5},{4,8},{5,9},{8,12},{9,13},{12,14},{13,15},{14,10},{15,... | collective-permute-start | bytes 98312 | tf_op jit(solution)/shard_map/ppermute | solution.py:62
  277.1 30.0 %collective-permute-start.55 = (bf16[520,896]{1,0:T(8,128)(2,1)}, bf16[520,896]{1,0:T(8,128)(2,1)S(1)}, u32[]{:S(2)}, u32[]{:S(2)}) collective-permute-start(bf16[520,896]{1,0:T(8,128)(2,1)} %get-tuple-element.163.refs_0_), channel_id=1, source_target_pairs={{0,1},{1,0},{2,3},{3,2},{4,5},{5,4},{6,7},{7,6},{8,9},{9,8},{10,11... | collective-permute-start | bytes 2795528 | tf_op jit(solution)/shard_map/ppermute | solution.py:50
  277.1 31.6 %collective-permute-start.56 = (bf16[520,896]{1,0:T(8,128)(2,1)}, bf16[520,896]{1,0:T(8,128)(2,1)S(1)}, u32[]{:S(2)}, u32[]{:S(2)}) collective-permute-start(bf16[520,896]{1,0:T(8,128)(2,1)} %get-tuple-element.164.refs_2_), channel_id=1, source_target_pairs={{0,1},{1,0},{2,3},{3,2},{4,5},{5,4},{6,7},{7,6},{8,9},{9,8},{10,11... | collective-permute-start | bytes 2795528 | tf_op jit(solution)/shard_map/ppermute | solution.py:50
  277.6 38.0 %collective-permute-start.57 = (bf16[520,896]{1,0:T(8,128)(2,1)}, bf16[520,896]{1,0:T(8,128)(2,1)S(1)}, u32[]{:S(2)}, u32[]{:S(2)}) collective-permute-start(bf16[520,896]{1,0:T(8,128)(2,1)} %get-tuple-element.163.refs_0_), channel_id=1, source_target_pairs={{0,4},{1,5},{4,8},{5,9},{8,12},{9,13},{12,14},{13,15},{14,10},{15,... | collective-permute-start | bytes 2795528 | tf_op jit(solution)/shard_map/ppermute | solution.py:62
  279.1 36.5 %collective-permute-start.58 = (bf16[520,896]{1,0:T(8,128)(2,1)}, bf16[520,896]{1,0:T(8,128)(2,1)S(1)}, u32[]{:S(2)}, u32[]{:S(2)}) collective-permute-start(bf16[520,896]{1,0:T(8,128)(2,1)} %get-tuple-element.164.refs_2_), channel_id=1, source_target_pairs={{0,2},{1,3},{4,0},{5,1},{8,4},{9,5},{12,8},{13,9},{14,12},{15,13},... | collective-permute-start | bytes 2795528 | tf_op jit(solution)/shard_map/ppermute | solution.py:62
  279.6 22.6 %collective-permute-start.25 = (bf16[64,256]{1,0:T(8,128)(2,1)S(1)}, bf16[64,256]{1,0:T(8,128)(2,1)S(1)}, u32[]{:S(2)}, u32[]{:S(2)}) collective-permute-start(bf16[64,256]{1,0:T(8,128)(2,1)S(1)} %get-tuple-element.202), channel_id=1, source_target_pairs={{0,2},{1,3},{4,0},{5,1},{8,4},{9,5},{12,8},{13,9},{14,12},{15,13},... | collective-permute-start | bytes 98312 | tf_op jit(solution)/shard_map/ppermute | solution.py:62
  316.8 32.8 %collective-permute-start.61 = (bf16[520,896]{1,0:T(8,128)(2,1)}, bf16[520,896]{1,0:T(8,128)(2,1)S(1)}, u32[]{:S(2)}, u32[]{:S(2)}) collective-permute-start(bf16[520,896]{1,0:T(8,128)(2,1)} %get-tuple-element.171.refs_0_), channel_id=1, source_target_pairs={{0,1},{1,0},{2,3},{3,2},{4,5},{5,4},{6,7},{7,6},{8,9},{9,8},{10,11... | collective-permute-start | bytes 2795528 | tf_op jit(solution)/shard_map/ppermute | solution.py:50
  316.9 32.8 %collective-permute-start.62 = (bf16[520,896]{1,0:T(8,128)(2,1)}, bf16[520,896]{1,0:T(8,128)(2,1)S(1)}, u32[]{:S(2)}, u32[]{:S(2)}) collective-permute-start(bf16[520,896]{1,0:T(8,128)(2,1)} %get-tuple-element.172.refs_2_), channel_id=1, source_target_pairs={{0,1},{1,0},{2,3},{3,2},{4,5},{5,4},{6,7},{7,6},{8,9},{9,8},{10,11... | collective-permute-start | bytes 2795528 | tf_op jit(solution)/shard_map/ppermute | solution.py:50
  323.2 33.5 %collective-permute-start.59 = (bf16[264,896]{1,0:T(8,128)(2,1)}, bf16[264,896]{1,0:T(8,128)(2,1)S(1)}, u32[]{:S(2)}, u32[]{:S(2)}) collective-permute-start(bf16[264,896]{1,0:T(8,128)(2,1)} %slice.103), channel_id=1, source_target_pairs={{0,4},{1,5},{4,8},{5,9},{8,12},{9,13},{12,14},{13,15},{14,10},{15,... | collective-permute-start | bytes 1419272 | tf_op jit(solution)/shard_map/ppermute | solution.py:62
  324.3 32.4 %collective-permute-start.60 = (bf16[256,896]{1,0:T(8,128)(2,1)}, bf16[256,896]{1,0:T(8,128)(2,1)}, u32[]{:S(2)}, u32[]{:S(2)}) collective-permute-start(bf16[256,896]{1,0:T(8,128)(2,1)} %slice.104), channel_id=1, source_target_pairs={{0,2},{1,3},{4,0},{5,1},{8,4},{9,5},{12,8},{13,9},{14,12},{15,13},... | collective-permute-start | bytes 1376264 | tf_op jit(solution)/shard_map/ppermute | solution.py:62
  359.7 77.9 %collective-permute-start.63 = (bf16[520,896]{1,0:T(8,128)(2,1)}, bf16[520,896]{1,0:T(8,128)(2,1)S(1)}, u32[]{:S(2)}, u32[]{:S(2)}) collective-permute-start(bf16[520,896]{1,0:T(8,128)(2,1)} %shard_map.212.refs_0_), channel_id=1, source_target_pairs={{0,1},{1,0},{2,3},{3,2},{4,5},{5,4},{6,7},{7,6},{8,9},{9,8},{10,11... | collective-permute-start | bytes 2795528 | tf_op jit(solution)/shard_map/ppermute | solution.py:50
  (102 other events, 905.7 us)
Sparse Core Ops, SparseCore 0:
  349.7 85.9 all-reduce.1

commit v10 on v9

--- a/solution.py
+++ b/solution.py
@@ -147,6 +147,7 @@
             return (got.astype(f32) + mine.astype(f32)).astype(bf16)
 
         fwd, back = self.hop(local[half][:cut], 1), self.hop(local[half][cut:], -1)
+        marks = [(fwd, back)]
         for s in range(1, half):
             mine_f, mine_b = local[half + s], local[half - s]
             if s == 1:
@@ -155,9 +156,26 @@
             else:
                 mine_f, mine_b = add(fwd, mine_f), add(back, mine_b)
             fwd, back = self.hop(mine_f, 1), self.hop(mine_b, -1)
-        return [local[0], fwd, back]
-
-    def ring_sum(self, terms):
+            marks.append((fwd, back))
+        return [local[0], fwd, back], marks
+
+    def exchange_sum(self, x):
+        half = x.shape[0] // 2
+
+        def add(a, b):
+            return (a.astype(f32) + b.astype(f32)).astype(bf16)
+
+        x = add(x, self.swap(x))
+        x = lax.dynamic_slice(x, (self.core * half, 0), (half, x.shape[1]))
+        marks = [x]
+        bit = 1
+        while bit < self.chips:
+            x = add(x, lax.ppermute(x, "ctx", [(i, i ^ (2 * bit)) for i in range(self.ctx)]))
+            marks.append(x)
+            bit *= 2
+        return x, marks
+
+    def ring_sum(self, terms, marks):
         half = self.chips // 2
         fwd, back = self.hop(terms[half], 1), self.hop(terms[half - 1], -1)
 
@@ -165,12 +183,17 @@
             return (got.astype(f32) + terms[slot].astype(f32)).astype(bf16)
 
         for s in range(1, half):
-            fwd = self.hop(add(fwd, half + s), 1)
+            blocks = [add(fwd, half + s)]
             if s < half - 1:
-                back = self.hop(add(back, half - 1 - s), -1)
+                blocks.append(add(back, half - 1 - s))
+            if s > 1:
+                blocks = gate(marks[s - 2], blocks)
+            fwd = self.hop(blocks[0], 1)
+            if s < half - 1:
+                back = self.hop(blocks[1], -1)
         return fwd, back
 
-    def gather_placed(self, x, place, rest):
+    def gather_placed(self, x, place, rest, marks):
         n = self.chips
         half = n // 2
         fwd = back = x
@@ -179,7 +202,7 @@
         for s in range(1, half + 1):
             if s > 1:
                 placed, token = place(*waiting, placed)
-                fwd, back = gate(token, fwd, back)
+                fwd, back = gate([token] + marks[s - 2], [fwd, back])
                 waiting = ([s - 1, n - s + 1], [(fwd, self.swap(fwd)), (back, self.swap(back))])
             if s < half:
                 fwd, back = self.hop(fwd, 1), self.hop(back, -1)
@@ -235,8 +258,8 @@
     return lax.dot_general(a, b, (((0,), (0,)), ((), ())), preferred_element_type=f32)
 
 
-def gate(token, *blocks):
-    count = len(blocks)
+def gate(tokens, blocks):
+    count, before = len(blocks), len(tokens)
     anywhere = pl.BlockSpec(memory_space=pl.ANY)
 
     def kernel(*refs):
@@ -245,11 +268,11 @@
     return pl.pallas_call(
         kernel,
         out_shape=[jax.ShapeDtypeStruct(x.shape, x.dtype) for x in blocks],
-        in_specs=[anywhere] * (count + 1),
+        in_specs=[anywhere] * (before + count),
         out_specs=[anywhere] * count,
-        input_output_aliases={i + 1: i for i in range(count)},
+        input_output_aliases={before + i: i for i in range(count)},
         cost_estimate=pl.CostEstimate(flops=0, bytes_accessed=1024, transcendentals=0),
-    )(token, *blocks)
+    )(*tokens, *blocks)
 
 
 def join(first, second, token):
@@ -784,7 +807,7 @@
     piece = blocks[0].shape[0] - top - down_rows
     parts = (cols + D) // chips // 128
     keep = [] if old is None else list(old)
-    last = [] if rest is None else [rest]
+    last = [] if rest is None else list(rest)
     known = WIDTH_Q // 128
 
     def kernel(meta_ref, *refs):
@@ -857,8 +880,10 @@
 
         token_ref[...] = jnp.zeros(token_ref.shape, f32)
         if last:
-            rest_buf[...] = refs[count][: 2 * q_rows, :].astype(f32)
-            send(rest_buf, joint_out.at[:, WIDTH_Q:cols], rest_sem)
+            rows = last[0].shape[0]
+            for core, ref in ((meta_ref[1], refs[count]), (1 - meta_ref[1], refs[count + 1])):
+                rest_buf[pl.ds(pl.multiple_of(core * rows, 8), rows), :] = ref[...].astype(f32)
+            send(rest_buf.at[: 2 * q_rows, :], joint_out.at[:, WIDTH_Q:cols], rest_sem)
         for copy in copies:
             copy.wait()
         for b in range(count):
@@ -893,7 +918,7 @@
             pltpu.VMEM((len(slots), mlp_rows, ff_loc), f32),
             pltpu.VMEM((count, down_rows, D), f32),
             pltpu.VMEM((count, parts, q_rows, 128), f32),
-            pltpu.VMEM((2 * q_rows, cols - WIDTH_Q), f32),
+            pltpu.VMEM((2 * q_rows + SUM_ROWS, cols - WIDTH_Q), f32),
             pltpu.SemaphoreType.DMA((4 * len(slots),)),
             pltpu.SemaphoreType.DMA((count, parts)),
             pltpu.SemaphoreType.DMA,
@@ -1063,7 +1088,7 @@
         sent_two = grad_chip[s * rows : (s + 1) * rows].astype(bf16)
         grad_two = grad_two + net.shift(sent_two, net.dp - s).astype(f32)
 
-    def attention_back():
+    def attention_back(*after):
         grad_hidden, grad_attn_low, grad_gain_two, grad_queries, terms_mine, terms_other = call(
             lambda *refs: backward_kernel(ctx_count, *refs),
             [
@@ -1076,9 +1101,10 @@
             ],
             [
                 meta, grad_two, hidden, cotangent[0], gain_two, w_out_full, spread, keys, values, lse,
-                attended, cosine, sine,
+                attended, cosine, sine, *after,
             ],
             smem=1,
+            loose=len(after),
             scratch=[
                 pltpu.VMEM(padded, bf16),
                 pltpu.VMEM(padded, f32),
@@ -1093,9 +1119,9 @@
             + [jax.ShapeDtypeStruct((rows, 2 * WIDTH_K), bf16)] * (chips - 1),
             [terms_mine, net.swap(terms_other)],
         )
-        grad_pairs = net.ring_parts(pair_sums)
-
-        def finish(*after):
+        grad_pairs, marks = net.ring_parts(pair_sums)
+
+        def finish():
             return call(
                 finish_kernel,
                 [
@@ -1105,21 +1131,18 @@
                     jax.ShapeDtypeStruct((1, w_qkv.shape[1]), f32),
                 ],
                 [grad_queries, x, gain_one, w_qkv_full, cosine, sine, grad_hidden, grad_gain_two]
-                + grad_pairs
-                + list(after),
-                loose=len(after),
+                + grad_pairs,
             )
 
-        return grad_attn_low, grad_gain_two, grad_queries, finish
-
-    grad_attn_low, grad_gain_two, grad_queries, finish = attention_back()
+        return grad_attn_low, grad_gain_two, grad_queries, finish, marks
+
     if tiled:
         terms = mlp_gradients(
             spots, x_turned, early, mid_turned, gate_low, up_low, sent_two, chips, down_rows, main
         )
-        fwd, back = net.ring_sum(terms)
+        grad_attn_low, grad_gain_two, grad_queries, finish, marks = attention_back(terms[0])
+        fwd, back = net.ring_sum(terms, marks)
         sum_mlp, sum_down = ring_end(fwd, back, terms[0], terms[0].shape[0] - down_rows)
-        pair_sent, grad_input, grad_gain_one, grad_bias = finish(sum_down)
     else:
         part_down = jnp.einsum(
             "tf,td->fd", middle, grad_out_group, preferred_element_type=f32
@@ -1155,7 +1178,8 @@
 
         sum_mlp = net.ring_scatter([mlp_chunk(s) for s in range(chips)]).astype(bf16)
         sum_mlp = lax.optimization_barrier(sum_mlp)
-        pair_sent, grad_input, grad_gain_one, grad_bias = finish()
+        grad_attn_low, grad_gain_two, grad_queries, finish, marks = attention_back()
+    pair_sent, grad_input, grad_gain_one, grad_bias = finish()
 
     out_sum = mlp_chip[:rows]
     for s in range(1, net.dp):
@@ -1183,7 +1207,8 @@
         block = call(
             block_kernel,
             [jax.ShapeDtypeStruct((sum_mlp.shape[0] + piece + down_rows, D), bf16)],
-            [sum_mlp, sum_down] + net.ring_parts(terms_small),
+            [sum_mlp, sum_down] + net.ring_parts(terms_small)[0] + list(marks[2]),
+            loose=2,
         )[0]
         part_pair = call(
             lambda *refs: pair_grad_kernel(rows, 2 * q_rows, *refs),
@@ -1192,13 +1217,16 @@
             smem=1,
             scratch=[pltpu.VMEM((D, chip_rows), bf16)],
         )[0]
-        grad_pair = lax.psum(part_pair, "ctx")
-        small = grad_pair[2 * q_rows :].reshape(-1)[: 2 * D + qkv_cols].astype(f32)
+        grad_pair, steps = net.exchange_sum(part_pair)
+        pair_halves = (grad_pair, net.swap(grad_pair))
+        sums = jnp.where(core == 1, *pair_halves)[-SUM_ROWS:]
+        small = sums.reshape(-1)[: 2 * D + qkv_cols].astype(f32)
         sizes = (main, ff_loc, q_rows, qkv_cols, down_rows, chips)
         grad_gate, grad_up, grad_down, grad_joint, grad_out_proj = net.gather_placed(
             block,
             lambda slots, pairs, old, rest=None: place_all(spots, slots, pairs, old, sizes, rest),
-            grad_pair,
+            pair_halves,
+            [[part_pair], [steps[1]], [steps[2]]],
         )
     else:
         gathered = jnp.concatenate(near, 0).reshape(2 * net.dp, 2, rows, D)

time: 451 us -> 377 us (0.84)
  waiting for transfers between devices: 228 us -> 148 us
  between operations: 14.9 us -> 1.8 us
  starting transfers between devices: 55.4 us -> 66.3 us
  other arithmetic: 14 us -> 21.6 us
    psum x1 -> x0, waiting for transfers between devices: 74.3 us -> none  [local(): grad_pair = lax.psum(part_pair, 'ctx')]
    ppermute x0 -> x3, waiting for transfers between devices: none -> 59.8 us  [exchange_sum(): lax.ppermute(x, 'ctx', [(i, i ^ 2 * bit) for i in range(self.ctx)])]
    ppermute x39, waiting for transfers between devices: 120 us -> 65.7 us  [hop(): return lax.ppermute(x, 'ctx', perm)]
    ppermute x9, waiting for transfers between devices: 27.3 us -> 18.7 us  [shift(): return lax.ppermute(x, 'dp', [(i, (i + step) % n) for i in range(n)])]
    convert_element_type x12, other arithmetic: 0.25 us -> 4.9 us  [add(): return (got.astype(f32) + mine.astype(f32)).astype(bf16)]
    unnamed x135 -> x142, local copies, waits for them, and re-layouts: 19.5 us -> 18.6 us
  transfers between devices with their start and end apart: 66 -> 70, of which waited for: 30 -> 27; matrix products, arithmetic and copies ran while one was open for 6% -> 11% of each run, Pallas kernels for 13% -> 20%
where the time goes in v10:
time: 377 us; the launch traced here: 375 us
  waiting for transfers between devices  148 us (39%)
  Pallas kernels  100 us (27%)
  starting transfers between devices  66.3 us (18%)
  local copies, waits for them, and re-layouts  37.9 us (10%)
  other arithmetic  21.6 us (6%)
    ppermute x39, waiting for transfers between devices, hop(): return lax.ppermute(x, 'ctx', perm)  65.7 us
    ppermute x3, waiting for transfers between devices, exchange_sum(): lax.ppermute(x, 'ctx', [(i, i ^ 2 * bit) for i in range(self.ctx)])  59.8 us
    pallas_call x10, Pallas kernels, call(): pl.pallas_call(body, out_shape=list(outs), in_specs=specs, out_specs=[pl....  47.8 us
    ppermute x39, starting transfers between devices, hop(): return lax.ppermute(x, 'ctx', perm)  43.7 us
    pallas_call x5, Pallas kernels, place_all(): pl.pallas_call(kernel, out_shape=[jax.ShapeDtypeStruct((D, ff_loc), f32),...  26.1 us
    ppermute x9, waiting for transfers between devices, shift(): return lax.ppermute(x, 'dp', [(i, (i + step) % n) for i in range(n)])  18.7 us
    unnamed x142, local copies, waits for them, and re-layouts  18.6 us
    pallas_call x1, Pallas kernels, feed_forward(): pl.pallas_call(lambda *refs: mlp_kernel(half, *refs), out_shape=[jax.Shap...  16.3 us
  transfers between devices with their start and end apart: 70, of which 27 were waited for; matrix products, arithmetic and copies ran while one was open for 11% of the time, Pallas kernels for 20%

profile of v10, /device:TPU:0, one launch (start us, length us, event | category | flops | bytes accessed | tf_op | source)
XLA Modules:
  0.0 375.4 jit_solution(11380250414616900684)
XLA Ops:
  12.1 4.5 %collective-permute-done = bf16[224,1152]{1,0:T(8,128)(2,1)S(1)} collective-permute-done((bf16[224,1152]{1,0:T(8,128)(2,1)S(1)}, bf16[224,1152]{1,0:T(8,128)(2,1)S(1)}, u32[]{:S(2)}, u32[]{:S(2)}) %collective-permute-start) | collective-permute-done | bytes 516128 | tf_op jit(solution)/shard_map/ppermute | solution.py:54
  20.5 3.2 shard_map.195
  49.6 10.3 %shard_map.196 = (bf16[128,896]{1,0:T(8,128)(2,1)}, f32[2,896,128]{2,1,0:T(8,128)}, f32[2,2,8,448]{3,2,1,0:T(8,128)}, bf16[2,896,128]{2,1,0:T(8,128)(2,1)}, bf16...) custom-call(s32[17]{0:T(128)} %pad_add_fusion.refs_0_, ...), custom_call_target="tpu_custom_call" | custom-call | flops 1879048192 | bytes 6516292 | tf_op jit(solution)/shard_map/pallas_call | solution.py:236
  62.6 5.1 %collective-permute-done.13 = bf16[128,896]{1,0:T(8,128)(2,1)S(1)} collective-permute-done((bf16[128,896]{1,0:T(8,128)(2,1)}, bf16[128,896]{1,0:T(8,128)(2,1)S(1)}, u32[]{:S(2)}, u32[]{:S(2)}) %collective-permute-start.13) | collective-permute-done | bytes 229408 | tf_op jit(solution)/shard_map/ppermute | solution.py:54
  71.0 16.3 %shard_map.197 = (bf16[896,512]{1,0:T(8,128)(2,1)}, bf16[1280,512]{1,0:T(8,128)(2,1)}, bf16[512,1280]{1,0:T(8,128)(2,1)}, bf16[512,1280]{1,0:T(8,128)(2,1)}, f32...) custom-call(s32[20]{0:T(128)} %concatenate.66.refs_0_.meta_ref, bf16[256,896]{1,0:T(8,128)(2,1)} %copy-done.13, ...), custom_call_target="tpu_custom_call" | custom-call | flops 7046430720 | bytes 6881280 | tf_op jit(solution)/shard_map/pallas_call | solution.py:660
  93.5 10.0 %shard_map.198 = (bf16[456,896]{1,0:T(8,128)(2,1)}, bf16[456,896]{1,0:T(8,128)(2,1)}, bf16[456,896]{1,0:T(8,128)(2,1)}, bf16[456,896]{1,0:T(8,128)(2,1)}, bf16[4...) custom-call(s32[20]{0:T(128)} %concatenate.66.refs_0_.meta_ref, ...), custom_call_target="tpu_custom_call" | custom-call | flops 3523215360 | bytes 13074432 | tf_op jit(solution)/shard_map/pallas_call | solution.py:746
  104.4 14.9 %shard_map.199 = (f32[128,896]{1,0:T(8,128)}, bf16[128,896]{1,0:T(8,128)(2,1)}, f32[1,896]{1,0:T(1,128)}, bf16[128,896]{1,0:T(8,128)(2,1)}, f32[1024,256]{1,0:T(8,128)}, /*index=5*/bf16[1024,256]{1,0:T(8,128)(2,1)}) custom-call(s32[17]{0:T(128)} %pad_add_fusion.refs_0_, f32[128,896]{1,0:T(8,128)} %slice_add_fusion.refs_1_, ...), custom_call_target="tpu_custom_call" | custom-call | flops 4697620480 | bytes 8680516 | tf_op jit(solution)/shard_map/pallas_call | solution.py:236
  130.2 5.0 %collective-permute-done.38 = bf16[256,896]{1,0:T(8,128)(2,1)S(1)} collective-permute-done((bf16[256,896]{1,0:T(8,128)(2,1)S(1)}, bf16[256,896]{1,0:T(8,128)(2,1)S(1)}, u32[]{:S(2)}, u32[]{:S(2)}) %collective-permute-start.38) | collective-permute-done | bytes 458784 | tf_op jit(solution)/shard_map/ppermute | solution.py:54
  136.9 4.2 %collective-permute-done.21.refs_0_ = bf16[64,256]{1,0:T(8,128)(2,1)S(1)} collective-permute-done((bf16[64,256]{1,0:T(8,128)(2,1)S(1)}, bf16[64,256]{1,0:T(8,128)(2,1)S(1)}, u32[]{:S(2)}, u32[]{:S(2)}) %collective-permute-start.21) | collective-permute-done | bytes 32800 | tf_op jit(solution)/shard_map/ppermute | solution.py:62
  153.3 4.2 %shard_map.205 = (bf16[64,896]{1,0:T(8,128)(2,1)}, bf16[64,896]{1,0:T(8,128)(2,1)}, bf16[64,896]{1,0:T(8,128)(2,1)}, bf16[64,896]{1,0:T(8,128)(2,1)}, bf16[64,89...) custom-call(s32[20]{0:T(128)} %concatenate.66.refs_0_.meta_ref, ...), custom_call_target="tpu_custom_call" | custom-call | flops 1879048192 | bytes 5505104 | tf_op jit(solution)/shard_map/pallas_call | solution.py:236
  161.7 6.4 %collective-permute-done.30 = bf16[456,896]{1,0:T(8,128)(2,1)S(1)} collective-permute-done((bf16[456,896]{1,0:T(8,128)(2,1)S(1)}, bf16[456,896]{1,0:T(8,128)(2,1)S(1)}, u32[]{:S(2)}, u32[]{:S(2)}) %collective-permute-start.30) | collective-permute-done | bytes 817184 | tf_op jit(solution)/shard_map/ppermute | solution.py:62
  174.6 17.0 %collective-permute-done.41 = bf16[64,896]{1,0:T(8,128)(2,1)S(1)} collective-permute-done((bf16[64,896]{1,0:T(8,128)(2,1)S(1)}, bf16[64,896]{1,0:T(8,128)(2,1)S(1)}, u32[]{:S(2)}, u32[]{:S(2)}) %collective-permute-start.41) | collective-permute-done | bytes 114720 | tf_op jit(solution)/shard_map/ppermute | solution.py:62
  205.5 5.8 %collective-permute-done.34.refs_0_ = bf16[456,896]{1,0:T(8,128)(2,1)S(1)} collective-permute-done((bf16[456,896]{1,0:T(8,128)(2,1)}, bf16[456,896]{1,0:T(8,128)(2,1)S(1)}, u32[]{:S(2)}, u32[]{:S(2)}) %collective-permute-start.34) | collective-permute-done | bytes 817184 | tf_op jit(solution)/shard_map/ppermute | solution.py:62
  224.1 18.5 %collective-permute-done.24.refs_9_ = bf16[128,256]{1,0:T(8,128)(2,1)S(1)} collective-permute-done((bf16[128,256]{1,0:T(8,128)(2,1)S(1)}, bf16[128,256]{1,0:T(8,128)(2,1)S(1)}, u32[]{:S(2)}, u32[]{:S(2)}) %collective-permute-start.24) | collective-permute-done | bytes 65568 | tf_op jit(solution)/shard_map/ppermute | solution.py:62
  244.2 3.6 shard_map.201
  256.6 4.1 %shard_map.207 = (f32[896,2432]{1,0:T(8,128)}, f32[896,2432]{1,0:T(8,128)}, f32[2432,896]{1,0:T(8,128)}, f32[448,1152]{1,0:T(8,128)}, f32[448,896]{1,0:T(8,128)}, /*index=5*/f32[8,128]{1,0:T(8,128)}) custom-call(s32[20]{0:T(128)} %concatenate.66.refs_0_.meta_ref, bf16[520,896]{1,0:T(8,128)(2,1)} %shard_map.206.refs_0_, bf16[520,896]{1,0:T(8,128)(2,1)} %copy-done.14), custom_call_target="tpu_custom_call" | custom-call | bytes 7454720 | tf_op jit(solution)/shard_map/pallas_call | solution.py:902
  266.7 21.1 %collective-permute-done.55 = bf16[232,256]{1,0:T(8,128)(2,1)S(1)} collective-permute-done((bf16[232,256]{1,0:T(8,128)(2,1)S(1)}, bf16[232,256]{1,0:T(8,128)(2,1)S(1)}, u32[]{:S(2)}, u32[]{:S(2)}) %collective-permute-start.55) | collective-permute-done | bytes 118816 | tf_op jit(solution)/shard_map/ppermute | solution.py:173
  288.5 6.0 %shard_map.210 = (f32[896,2432]{1,0:T(8,128)}, f32[896,2432]{1,0:T(8,128)}, f32[2432,896]{1,0:T(8,128)}, f32[448,1152]{1,0:T(8,128)}, f32[448,896]{1,0:T(8,128)}, /*index=5*/f32[8,128]{1,0:T(8,128)}) custom-call(s32[20]{0:T(128)} %concatenate.66.refs_0_.meta_ref, ...), custom_call_target="tpu_custom_call", output_to_operand_aliasing={{0}: (5, {}), {1}: (6, {}), {2}: (7, {}), {3}: (8, {}), {4}... | custom-call | bytes 14909440 | tf_op jit(solution)/shard_map/pallas_call | solution.py:902
  298.3 23.3 %collective-permute-done.60 = bf16[232,256]{1,0:T(8,128)(2,1)S(1)} collective-permute-done((bf16[232,256]{1,0:T(8,128)(2,1)S(1)}, bf16[232,256]{1,0:T(8,128)(2,1)S(1)}, u32[]{:S(2)}, u32[]{:S(2)}) %collective-permute-start.60) | collective-permute-done | bytes 118816 | tf_op jit(solution)/shard_map/ppermute | solution.py:173
  323.5 5.9 %shard_map.212 = (f32[896,2432]{1,0:T(8,128)}, f32[896,2432]{1,0:T(8,128)}, f32[2432,896]{1,0:T(8,128)}, f32[448,1152]{1,0:T(8,128)}, f32[448,896]{1,0:T(8,128)}, /*index=5*/f32[8,128]{1,0:T(8,128)}) custom-call(s32[20]{0:T(128)} %concatenate.66.refs_0_.meta_ref, ...), custom_call_target="tpu_custom_call", output_to_operand_aliasing={{0}: (5, {}), {1}: (6, {}), {2}: (7, {}), {3}: (8, {}), {4}... | custom-call | bytes 14909440 | tf_op jit(solution)/shard_map/pallas_call | solution.py:902
  336.9 3.9 %collective-permute-start.68 = (bf16[232,256]{1,0:T(8,128)(2,1)S(1)}, bf16[232,256]{1,0:T(8,128)(2,1)S(1)}, u32[]{:S(2)}, u32[]{:S(2)}) collective-permute-start(bf16[232,256]{1,0:T(8,128)(2,1)S(1)} %copy-done.11), channel_id=1, source_target_pairs={{0,8},{1,9},{2,10},{3,11},{4,12},{5,13},{6,14},{7,15},{8,0},{9,1},... | collective-permute-start | bytes 356360 | tf_op jit(solution)/shard_map/ppermute | solution.py:173
  340.8 15.4 %collective-permute-done.68 = bf16[232,256]{1,0:T(8,128)(2,1)S(1)} collective-permute-done((bf16[232,256]{1,0:T(8,128)(2,1)S(1)}, bf16[232,256]{1,0:T(8,128)(2,1)S(1)}, u32[]{:S(2)}, u32[]{:S(2)}) %collective-permute-start.68) | collective-permute-done | bytes 118816 | tf_op jit(solution)/shard_map/ppermute | solution.py:173
  358.4 5.8 %shard_map.214 = (f32[896,2432]{1,0:T(8,128)}, f32[896,2432]{1,0:T(8,128)}, f32[2432,896]{1,0:T(8,128)}, f32[448,1152]{1,0:T(8,128)}, f32[448,896]{1,0:T(8,128)}, /*index=5*/f32[8,128]{1,0:T(8,128)}) custom-call(s32[20]{0:T(128)} %concatenate.66.refs_0_.meta_ref, ...), custom_call_target="tpu_custom_call", output_to_operand_aliasing={{0}: (5, {}), {1}: (6, {}), {2}: (7, {}), {3}: (8, {}), {4}... | custom-call | bytes 14909440 | tf_op jit(solution)/shard_map/pallas_call | solution.py:902
  370.9 4.3 %shard_map.216 = (f32[896,2432]{1,0:T(8,128)}, f32[896,2432]{1,0:T(8,128)}, f32[2432,896]{1,0:T(8,128)}, f32[448,1152]{1,0:T(8,128)}, f32[448,896]{1,0:T(8,128)}, /*index=5*/f32[8,128]{1,0:T(8,128)}) custom-call(s32[20]{0:T(128)} %concatenate.66.refs_0_.meta_ref, ...), custom_call_target="tpu_custom_call", output_to_operand_aliasing={{0}: (5, {}), {1}: (6, {}), {2}: (7, {}), {3}: (8, {}), {4}... | custom-call | bytes 7454720 | tf_op jit(solution)/shard_map/pallas_call | solution.py:902
  (354 shorter events, 154.8 us)
Async XLA Ops:
  46.6 22.7 %collective-permute-start.16 = (bf16[256,1792]{1,0:T(8,128)(2,1)S(1)}, bf16[256,1792]{1,0:T(8,128)(2,1)S(1)}, u32[]{:S(2)}, u32[]{:S(2)}) collective-permute-start(bf16[256,1792]{1,0:T(8,128)(2,1)S(1)} %pad_maximum_fusion.3.refs_3_.refs_2_.refs_1_), channel_id=1, source_target_pairs={{0,1},{1,0},{2,3},{3,2},{4,5},{5,4},{6,7},{7,6},{8,9},{9,8},{10,11... | collective-permute-start | bytes 2752520 | tf_op jit(solution)/shard_map/ppermute | solution.py:50
  87.8 31.7 %collective-permute-start.36 = (bf16[128,896]{1,0:T(8,128)(2,1)S(1)}, bf16[128,896]{1,0:T(8,128)(2,1)S(1)}, u32[]{:S(2)}, u32[]{:S(2)}) collective-permute-start(bf16[128,896]{1,0:T(8,128)(2,1)S(1)} %copy-done.38), channel_id=1, source_target_pairs={{0,16},{16,0},{1,17},{17,1},{2,18},{18,2},{3,19},{19,3},{4,20},{20... | collective-permute-start | bytes 688136 | tf_op jit(solution)/shard_map/ppermute | solution.py:54
  119.5 32.3 %collective-permute-start.37 = (bf16[256,896]{1,0:T(8,128)(2,1)S(1)}, bf16[256,896]{1,0:T(8,128)(2,1)S(1)}, u32[]{:S(2)}, u32[]{:S(2)}) collective-permute-start(bf16[256,896]{1,0:T(8,128)(2,1)S(1)} %constant_dynamic-update-slice_fusion.13.refs_3_), channel_id=1, source_target_pairs={{0,1},{1,0},{2,3},{3,2},{4,5},{5,4},{6,7},{7,6},{8,9},{9,8},{10,11... | collective-permute-start | bytes 1376264 | tf_op jit(solution)/shard_map/ppermute | solution.py:50
  120.0 28.0 %collective-permute-start.29 = (bf16[456,896]{1,0:T(8,128)(2,1)}, bf16[456,896]{1,0:T(8,128)(2,1)S(1)}, u32[]{:S(2)}, u32[]{:S(2)}) collective-permute-start(bf16[456,896]{1,0:T(8,128)(2,1)} %get-tuple-element.137), channel_id=1, source_target_pairs={{0,4},{1,5},{4,8},{5,9},{8,12},{9,13},{12,14},{13,15},{14,10},{15,... | collective-permute-start | bytes 2451464 | tf_op jit(solution)/shard_map/ppermute | solution.py:62
  121.6 27.1 %collective-permute-start.31 = (bf16[456,896]{1,0:T(8,128)(2,1)S(1)}, bf16[456,896]{1,0:T(8,128)(2,1)S(1)}, u32[]{:S(2)}, u32[]{:S(2)}) collective-permute-start(bf16[456,896]{1,0:T(8,128)(2,1)S(1)} %copy-done.61), channel_id=1, source_target_pairs={{0,2},{1,3},{4,0},{5,1},{8,4},{9,5},{12,8},{13,9},{14,12},{15,13},... | collective-permute-start | bytes 2451464 | tf_op jit(solution)/shard_map/ppermute | solution.py:62
  148.0 46.7 %collective-permute-start.26 = (bf16[128,256]{1,0:T(8,128)(2,1)}, bf16[128,256]{1,0:T(8,128)(2,1)S(1)}, u32[]{:S(2)}, u32[]{:S(2)}) collective-permute-start(bf16[128,256]{1,0:T(8,128)(2,1)} %pad_maximum_fusion.9), channel_id=1, source_target_pairs={{0,2},{1,3},{4,0},{5,1},{8,4},{9,5},{12,8},{13,9},{14,12},{15,13},... | collective-permute-start | bytes 196616 | tf_op jit(solution)/shard_map/ppermute | solution.py:62
  151.9 63.0 %collective-permute-start.23 = (bf16[128,256]{1,0:T(8,128)(2,1)}, bf16[128,256]{1,0:T(8,128)(2,1)S(1)}, u32[]{:S(2)}, u32[]{:S(2)}) collective-permute-start(bf16[128,256]{1,0:T(8,128)(2,1)} %add_convert_fusion.16), channel_id=1, source_target_pairs={{0,4},{1,5},{4,8},{5,9},{8,12},{9,13},{12,14},{13,15},{14,10},{15,... | collective-permute-start | bytes 196616 | tf_op jit(solution)/shard_map/ppermute | solution.py:62
  172.4 31.4 %collective-permute-start.35 = (bf16[456,896]{1,0:T(8,128)(2,1)}, bf16[456,896]{1,0:T(8,128)(2,1)S(1)}, u32[]{:S(2)}, u32[]{:S(2)}) collective-permute-start(bf16[456,896]{1,0:T(8,128)(2,1)} %get-tuple-element.145), channel_id=1, source_target_pairs={{0,2},{1,3},{4,0},{5,1},{8,4},{9,5},{12,8},{13,9},{14,12},{15,13},... | collective-permute-start | bytes 2451464 | tf_op jit(solution)/shard_map/ppermute | solution.py:62
  217.9 37.7 %collective-permute-start.48 = (bf16[520,896]{1,0:T(8,128)(2,1)}, bf16[520,896]{1,0:T(8,128)(2,1)S(1)}, u32[]{:S(2)}, u32[]{:S(2)}) collective-permute-start(bf16[520,896]{1,0:T(8,128)(2,1)} %shard_map.206.refs_0_), channel_id=1, source_target_pairs={{0,1},{1,0},{2,3},{3,2},{4,5},{5,4},{6,7},{7,6},{8,9},{9,8},{10,11... | collective-permute-start | bytes 2795528 | tf_op jit(solution)/shard_map/ppermute | solution.py:50
  217.9 42.8 %collective-permute-start.50 = (bf16[520,896]{1,0:T(8,128)(2,1)}, bf16[520,896]{1,0:T(8,128)(2,1)S(1)}, u32[]{:S(2)}, u32[]{:S(2)}) collective-permute-start(bf16[520,896]{1,0:T(8,128)(2,1)} %shard_map.206.refs_0_), channel_id=1, source_target_pairs={{0,4},{1,5},{4,8},{5,9},{8,12},{9,13},{12,14},{13,15},{14,10},{15,... | collective-permute-start | bytes 2795528 | tf_op jit(solution)/shard_map/ppermute | solution.py:62
  219.2 41.6 %collective-permute-start.51 = (bf16[520,896]{1,0:T(8,128)(2,1)}, bf16[520,896]{1,0:T(8,128)(2,1)S(1)}, u32[]{:S(2)}, u32[]{:S(2)}) collective-permute-start(bf16[520,896]{1,0:T(8,128)(2,1)} %shard_map.206.refs_0_), channel_id=1, source_target_pairs={{0,2},{1,3},{4,0},{5,1},{8,4},{9,5},{12,8},{13,9},{14,12},{15,13},... | collective-permute-start | bytes 2795528 | tf_op jit(solution)/shard_map/ppermute | solution.py:62
  262.0 26.5 %collective-permute-start.52 = (bf16[520,896]{1,0:T(8,128)(2,1)}, bf16[520,896]{1,0:T(8,128)(2,1)}, u32[]{:S(2)}, u32[]{:S(2)}) collective-permute-start(bf16[520,896]{1,0:T(8,128)(2,1)} %get-tuple-element.160.refs_0_), channel_id=1, source_target_pairs={{0,1},{1,0},{2,3},{3,2},{4,5},{5,4},{6,7},{7,6},{8,9},{9,8},{10,11... | collective-permute-start | bytes 2795528 | tf_op jit(solution)/shard_map/ppermute | solution.py:50
  262.0 26.5 %collective-permute-start.53 = (bf16[520,896]{1,0:T(8,128)(2,1)}, bf16[520,896]{1,0:T(8,128)(2,1)}, u32[]{:S(2)}, u32[]{:S(2)}) collective-permute-start(bf16[520,896]{1,0:T(8,128)(2,1)} %get-tuple-element.161.refs_2_), channel_id=1, source_target_pairs={{0,1},{1,0},{2,3},{3,2},{4,5},{5,4},{6,7},{7,6},{8,9},{9,8},{10,11... | collective-permute-start | bytes 2795528 | tf_op jit(solution)/shard_map/ppermute | solution.py:50
  262.5 32.0 %collective-permute-start.56 = (bf16[520,896]{1,0:T(8,128)(2,1)}, bf16[520,896]{1,0:T(8,128)(2,1)S(1)}, u32[]{:S(2)}, u32[]{:S(2)}) collective-permute-start(bf16[520,896]{1,0:T(8,128)(2,1)} %get-tuple-element.160.refs_0_), channel_id=1, source_target_pairs={{0,4},{1,5},{4,8},{5,9},{8,12},{9,13},{12,14},{13,15},{14,10},{15,... | collective-permute-start | bytes 2795528 | tf_op jit(solution)/shard_map/ppermute | solution.py:62
  264.1 30.4 %collective-permute-start.57 = (bf16[520,896]{1,0:T(8,128)(2,1)}, bf16[520,896]{1,0:T(8,128)(2,1)S(1)}, u32[]{:S(2)}, u32[]{:S(2)}) collective-permute-start(bf16[520,896]{1,0:T(8,128)(2,1)} %get-tuple-element.161.refs_2_), channel_id=1, source_target_pairs={{0,2},{1,3},{4,0},{5,1},{8,4},{9,5},{12,8},{13,9},{14,12},{15,13},... | collective-permute-start | bytes 2795528 | tf_op jit(solution)/shard_map/ppermute | solution.py:62
  295.7 26.5 %collective-permute-start.58 = (bf16[520,896]{1,0:T(8,128)(2,1)}, bf16[520,896]{1,0:T(8,128)(2,1)S(1)}, u32[]{:S(2)}, u32[]{:S(2)}) collective-permute-start(bf16[520,896]{1,0:T(8,128)(2,1)} %get-tuple-element.168.refs_0_), channel_id=1, source_target_pairs={{0,1},{1,0},{2,3},{3,2},{4,5},{5,4},{6,7},{7,6},{8,9},{9,8},{10,11... | collective-permute-start | bytes 2795528 | tf_op jit(solution)/shard_map/ppermute | solution.py:50
  295.7 26.5 %collective-permute-start.59 = (bf16[520,896]{1,0:T(8,128)(2,1)}, bf16[520,896]{1,0:T(8,128)(2,1)S(1)}, u32[]{:S(2)}, u32[]{:S(2)}) collective-permute-start(bf16[520,896]{1,0:T(8,128)(2,1)} %get-tuple-element.169.refs_2_), channel_id=1, source_target_pairs={{0,1},{1,0},{2,3},{3,2},{4,5},{5,4},{6,7},{7,6},{8,9},{9,8},{10,11... | collective-permute-start | bytes 2795528 | tf_op jit(solution)/shard_map/ppermute | solution.py:50
  296.2 33.2 %collective-permute-start.61 = (bf16[520,896]{1,0:T(8,128)(2,1)}, bf16[520,896]{1,0:T(8,128)(2,1)S(1)}, u32[]{:S(2)}, u32[]{:S(2)}) collective-permute-start(bf16[520,896]{1,0:T(8,128)(2,1)} %get-tuple-element.168.refs_0_), channel_id=1, source_target_pairs={{0,4},{1,5},{4,8},{5,9},{8,12},{9,13},{12,14},{13,15},{14,10},{15,... | collective-permute-start | bytes 2795528 | tf_op jit(solution)/shard_map/ppermute | solution.py:62
  296.3 33.2 %collective-permute-start.62 = (bf16[520,896]{1,0:T(8,128)(2,1)}, bf16[520,896]{1,0:T(8,128)(2,1)S(1)}, u32[]{:S(2)}, u32[]{:S(2)}) collective-permute-start(bf16[520,896]{1,0:T(8,128)(2,1)} %get-tuple-element.169.refs_2_), channel_id=1, source_target_pairs={{0,2},{1,3},{4,0},{5,1},{8,4},{9,5},{12,8},{13,9},{14,12},{15,13},... | collective-permute-start | bytes 2795528 | tf_op jit(solution)/shard_map/ppermute | solution.py:62
  298.3 23.3 %collective-permute-start.60 = (bf16[232,256]{1,0:T(8,128)(2,1)S(1)}, bf16[232,256]{1,0:T(8,128)(2,1)S(1)}, u32[]{:S(2)}, u32[]{:S(2)}) collective-permute-start(bf16[232,256]{1,0:T(8,128)(2,1)S(1)} %copy-done.12), channel_id=1, source_target_pairs={{0,4},{1,5},{2,6},{3,7},{4,0},{5,1},{6,2},{7,3},{8,12},{9,13},{10,... | collective-permute-start | bytes 356360 | tf_op jit(solution)/shard_map/ppermute | solution.py:173
  330.7 26.5 %collective-permute-start.65 = (bf16[520,896]{1,0:T(8,128)(2,1)}, bf16[520,896]{1,0:T(8,128)(2,1)S(1)}, u32[]{:S(2)}, u32[]{:S(2)}) collective-permute-start(bf16[520,896]{1,0:T(8,128)(2,1)} %get-tuple-element.176.refs_0_), channel_id=1, source_target_pairs={{0,1},{1,0},{2,3},{3,2},{4,5},{5,4},{6,7},{7,6},{8,9},{9,8},{10,11... | collective-permute-start | bytes 2795528 | tf_op jit(solution)/shard_map/ppermute | solution.py:50
  330.7 26.6 %collective-permute-start.66 = (bf16[520,896]{1,0:T(8,128)(2,1)}, bf16[520,896]{1,0:T(8,128)(2,1)S(1)}, u32[]{:S(2)}, u32[]{:S(2)}) collective-permute-start(bf16[520,896]{1,0:T(8,128)(2,1)} %get-tuple-element.177.refs_2_), channel_id=1, source_target_pairs={{0,1},{1,0},{2,3},{3,2},{4,5},{5,4},{6,7},{7,6},{8,9},{9,8},{10,11... | collective-permute-start | bytes 2795528 | tf_op jit(solution)/shard_map/ppermute | solution.py:50
  333.1 31.3 %collective-permute-start.63 = (bf16[264,896]{1,0:T(8,128)(2,1)}, bf16[264,896]{1,0:T(8,128)(2,1)S(1)}, u32[]{:S(2)}, u32[]{:S(2)}) collective-permute-start(bf16[264,896]{1,0:T(8,128)(2,1)} %slice.103), channel_id=1, source_target_pairs={{0,4},{1,5},{4,8},{5,9},{8,12},{9,13},{12,14},{13,15},{14,10},{15,... | collective-permute-start | bytes 1419272 | tf_op jit(solution)/shard_map/ppermute | solution.py:62
  335.1 29.2 %collective-permute-start.64 = (bf16[256,896]{1,0:T(8,128)(2,1)}, bf16[256,896]{1,0:T(8,128)(2,1)}, u32[]{:S(2)}, u32[]{:S(2)}) collective-permute-start(bf16[256,896]{1,0:T(8,128)(2,1)} %slice.104), channel_id=1, source_target_pairs={{0,2},{1,3},{4,0},{5,1},{8,4},{9,5},{12,8},{13,9},{14,12},{15,13},... | collective-permute-start | bytes 1376264 | tf_op jit(solution)/shard_map/ppermute | solution.py:62
  (110 other events, 862.2 us)

commit v11 on v10

--- a/solution.py
+++ b/solution.py
@@ -175,7 +175,7 @@
             bit *= 2
         return x, marks
 
-    def ring_sum(self, terms, marks):
+    def ring_sum(self, terms, between):
         half = self.chips // 2
         fwd, back = self.hop(terms[half], 1), self.hop(terms[half - 1], -1)
 
@@ -186,7 +186,9 @@
             blocks = [add(fwd, half + s)]
             if s < half - 1:
                 blocks.append(add(back, half - 1 - s))
-            if s > 1:
+            if s == 1:
+                marks = between(*blocks)
+            else:
                 blocks = gate(marks[s - 2], blocks)
             fwd = self.hop(blocks[0], 1)
             if s < half - 1:
@@ -1113,15 +1115,19 @@
             ],
             flops=20 * KH * part_rows * total_keys * 128,
         )
-        pair_sums = call(
-            pair_kernel,
-            [jax.ShapeDtypeStruct((rows, 2 * WIDTH_K), f32)]
-            + [jax.ShapeDtypeStruct((rows, 2 * WIDTH_K), bf16)] * (chips - 1),
-            [terms_mine, net.swap(terms_other)],
-        )
-        grad_pairs, marks = net.ring_parts(pair_sums)
-
-        def finish():
+        other_terms = net.swap(terms_other)
+
+        def row_sums(*after):
+            pair_sums = call(
+                pair_kernel,
+                [jax.ShapeDtypeStruct((rows, 2 * WIDTH_K), f32)]
+                + [jax.ShapeDtypeStruct((rows, 2 * WIDTH_K), bf16)] * (chips - 1),
+                [terms_mine, other_terms, *after],
+                loose=len(after),
+            )
+            return net.ring_parts(pair_sums)
+
+        def finish(grad_pairs):
             return call(
                 finish_kernel,
                 [
@@ -1134,14 +1140,21 @@
                 + grad_pairs,
             )
 
-        return grad_attn_low, grad_gain_two, grad_queries, finish, marks
+        return grad_attn_low, grad_gain_two, grad_queries, row_sums, finish
 
     if tiled:
         terms = mlp_gradients(
             spots, x_turned, early, mid_turned, gate_low, up_low, sent_two, chips, down_rows, main
         )
-        grad_attn_low, grad_gain_two, grad_queries, finish, marks = attention_back(terms[0])
-        fwd, back = net.ring_sum(terms, marks)
+        grad_attn_low, grad_gain_two, grad_queries, row_sums, finish = attention_back(terms[0])
+        found = []
+
+        def between(*blocks):
+            found.extend(row_sums(*blocks))
+            return found[1]
+
+        fwd, back = net.ring_sum(terms, between)
+        grad_pairs, marks = found
         sum_mlp, sum_down = ring_end(fwd, back, terms[0], terms[0].shape[0] - down_rows)
     else:
         part_down = jnp.einsum(
@@ -1178,8 +1191,9 @@
 
         sum_mlp = net.ring_scatter([mlp_chunk(s) for s in range(chips)]).astype(bf16)
         sum_mlp = lax.optimization_barrier(sum_mlp)
-        grad_attn_low, grad_gain_two, grad_queries, finish, marks = attention_back()
-    pair_sent, grad_input, grad_gain_one, grad_bias = finish()
+        grad_attn_low, grad_gain_two, grad_queries, row_sums, finish = attention_back()
+        grad_pairs, marks = row_sums()
+    pair_sent, grad_input, grad_gain_one, grad_bias = finish(grad_pairs)
 
     out_sum = mlp_chip[:rows]
     for s in range(1, net.dp):

time: 377 us -> 396 us (1.050)
  waiting for transfers between devices: 148 us -> 170 us
  starting transfers between devices: 66.3 us -> 59.4 us
    ppermute x39, waiting for transfers between devices: 65.7 us -> 81.8 us  [hop(): return lax.ppermute(x, 'ctx', perm)]
    ppermute x9, waiting for transfers between devices: 18.7 us -> 23.5 us  [shift(): return lax.ppermute(x, 'dp', [(i, (i + step) % n) for i in range(n)])]
  transfers between devices with their start and end apart: 70 -> 70, of which waited for: 27 -> 27; matrix products, arithmetic and copies ran while one was open for 11% -> 11% of each run, Pallas kernels for 20% -> 19%
where the time goes in v11:
time: 396 us; the launch traced here: 394 us
  waiting for transfers between devices  170 us (43%)
  Pallas kernels  100 us (25%)
  starting transfers between devices  59.4 us (15%)
  local copies, waits for them, and re-layouts  38.6 us (10%)
  other arithmetic  24.2 us (6%)
    ppermute x39, waiting for transfers between devices, hop(): return lax.ppermute(x, 'ctx', perm)  81.8 us
    ppermute x3, waiting for transfers between devices, exchange_sum(): lax.ppermute(x, 'ctx', [(i, i ^ 2 * bit) for i in range(self.ctx)])  59.7 us
    pallas_call x10, Pallas kernels, call(): pl.pallas_call(body, out_shape=list(outs), in_specs=specs, out_specs=[pl....  47.9 us
    ppermute x39, starting transfers between devices, hop(): return lax.ppermute(x, 'ctx', perm)  41.1 us
    pallas_call x5, Pallas kernels, place_all(): pl.pallas_call(kernel, out_shape=[jax.ShapeDtypeStruct((D, ff_loc), f32),...  26.1 us
    ppermute x9, waiting for transfers between devices, shift(): return lax.ppermute(x, 'dp', [(i, (i + step) % n) for i in range(n)])  23.5 us
    unnamed x142, local copies, waits for them, and re-layouts  19.5 us
    pallas_call x1, Pallas kernels, feed_forward(): pl.pallas_call(lambda *refs: mlp_kernel(half, *refs), out_shape=[jax.Shap...  16.3 us
  transfers between devices with their start and end apart: 70, of which 27 were waited for; matrix products, arithmetic and copies ran while one was open for 11% of the time, Pallas kernels for 19%

profile of v11, /device:TPU:0, one launch (start us, length us, event | category | flops | bytes accessed | tf_op | source)
XLA Modules:
  0.0 394.4 jit_solution(16383507183841260526)
XLA Ops:
  12.0 4.6 %collective-permute-done = bf16[224,1152]{1,0:T(8,128)(2,1)S(1)} collective-permute-done((bf16[224,1152]{1,0:T(8,128)(2,1)S(1)}, bf16[224,1152]{1,0:T(8,128)(2,1)S(1)}, u32[]{:S(2)}, u32[]{:S(2)}) %collective-permute-start) | collective-permute-done | bytes 516128 | tf_op jit(solution)/shard_map/ppermute | solution.py:54
  20.5 3.2 shard_map.195
  49.6 10.3 %shard_map.196 = (bf16[128,896]{1,0:T(8,128)(2,1)}, f32[2,896,128]{2,1,0:T(8,128)}, f32[2,2,8,448]{3,2,1,0:T(8,128)}, bf16[2,896,128]{2,1,0:T(8,128)(2,1)}, bf16...) custom-call(s32[17]{0:T(128)} %pad_add_fusion.refs_0_, ...), custom_call_target="tpu_custom_call" | custom-call | flops 1879048192 | bytes 6516292 | tf_op jit(solution)/shard_map/pallas_call | solution.py:238
  62.7 5.1 %collective-permute-done.13 = bf16[128,896]{1,0:T(8,128)(2,1)S(1)} collective-permute-done((bf16[128,896]{1,0:T(8,128)(2,1)}, bf16[128,896]{1,0:T(8,128)(2,1)S(1)}, u32[]{:S(2)}, u32[]{:S(2)}) %collective-permute-start.13) | collective-permute-done | bytes 229408 | tf_op jit(solution)/shard_map/ppermute | solution.py:54
  70.9 16.3 %shard_map.197 = (bf16[896,512]{1,0:T(8,128)(2,1)}, bf16[1280,512]{1,0:T(8,128)(2,1)}, bf16[512,1280]{1,0:T(8,128)(2,1)}, bf16[512,1280]{1,0:T(8,128)(2,1)}, f32...) custom-call(s32[20]{0:T(128)} %concatenate.66.refs_0_.meta_ref, bf16[256,896]{1,0:T(8,128)(2,1)} %copy-done.14, ...), custom_call_target="tpu_custom_call" | custom-call | flops 7046430720 | bytes 6881280 | tf_op jit(solution)/shard_map/pallas_call | solution.py:662
  93.4 10.0 %shard_map.198 = (bf16[456,896]{1,0:T(8,128)(2,1)}, bf16[456,896]{1,0:T(8,128)(2,1)}, bf16[456,896]{1,0:T(8,128)(2,1)}, bf16[456,896]{1,0:T(8,128)(2,1)}, bf16[4...) custom-call(s32[20]{0:T(128)} %concatenate.66.refs_0_.meta_ref, ...), custom_call_target="tpu_custom_call" | custom-call | flops 3523215360 | bytes 13074432 | tf_op jit(solution)/shard_map/pallas_call | solution.py:748
  106.0 14.9 %shard_map.199 = (f32[128,896]{1,0:T(8,128)}, bf16[128,896]{1,0:T(8,128)(2,1)}, f32[1,896]{1,0:T(1,128)}, bf16[128,896]{1,0:T(8,128)(2,1)}, f32[1024,256]{1,0:T(8,128)}, /*index=5*/bf16[1024,256]{1,0:T(8,128)(2,1)}) custom-call(s32[17]{0:T(128)} %pad_add_fusion.refs_0_, f32[128,896]{1,0:T(8,128)} %slice_add_fusion.refs_1_, ...), custom_call_target="tpu_custom_call" | custom-call | flops 4697620480 | bytes 8680516 | tf_op jit(solution)/shard_map/pallas_call | solution.py:238
  126.6 8.9 %collective-permute-done.38 = bf16[256,896]{1,0:T(8,128)(2,1)S(1)} collective-permute-done((bf16[256,896]{1,0:T(8,128)(2,1)S(1)}, bf16[256,896]{1,0:T(8,128)(2,1)S(1)}, u32[]{:S(2)}, u32[]{:S(2)}) %collective-permute-start.38) | collective-permute-done | bytes 458784 | tf_op jit(solution)/shard_map/ppermute | solution.py:54
  136.8 5.9 %collective-permute-done.22 = bf16[456,896]{1,0:T(8,128)(2,1)S(1)} collective-permute-done((bf16[456,896]{1,0:T(8,128)(2,1)S(1)}, bf16[456,896]{1,0:T(8,128)(2,1)S(1)}, u32[]{:S(2)}, u32[]{:S(2)}) %collective-permute-start.22) | collective-permute-done | bytes 817184 | tf_op jit(solution)/shard_map/ppermute | solution.py:62
  154.1 17.7 %collective-permute-done.27.refs_1_ = bf16[64,256]{1,0:T(8,128)(2,1)S(1)} collective-permute-done((bf16[64,256]{1,0:T(8,128)(2,1)S(1)}, bf16[64,256]{1,0:T(8,128)(2,1)S(1)}, u32[]{:S(2)}, u32[]{:S(2)}) %collective-permute-start.27) | collective-permute-done | bytes 32800 | tf_op jit(solution)/shard_map/ppermute | solution.py:62
  179.7 4.2 %shard_map.205 = (bf16[64,896]{1,0:T(8,128)(2,1)}, bf16[64,896]{1,0:T(8,128)(2,1)}, bf16[64,896]{1,0:T(8,128)(2,1)}, bf16[64,896]{1,0:T(8,128)(2,1)}, bf16[64,89...) custom-call(s32[20]{0:T(128)} %concatenate.66.refs_0_.meta_ref, ...), custom_call_target="tpu_custom_call" | custom-call | flops 1879048192 | bytes 5505104 | tf_op jit(solution)/shard_map/pallas_call | solution.py:238
  194.5 17.1 %collective-permute-done.41 = bf16[64,896]{1,0:T(8,128)(2,1)S(1)} collective-permute-done((bf16[64,896]{1,0:T(8,128)(2,1)S(1)}, bf16[64,896]{1,0:T(8,128)(2,1)S(1)}, u32[]{:S(2)}, u32[]{:S(2)}) %collective-permute-start.41) | collective-permute-done | bytes 114720 | tf_op jit(solution)/shard_map/ppermute | solution.py:62
  223.9 9.0 %collective-permute-done.34.refs_0_ = bf16[456,896]{1,0:T(8,128)(2,1)S(1)} collective-permute-done((bf16[456,896]{1,0:T(8,128)(2,1)}, bf16[456,896]{1,0:T(8,128)(2,1)S(1)}, u32[]{:S(2)}, u32[]{:S(2)}) %collective-permute-start.34) | collective-permute-done | bytes 817184 | tf_op jit(solution)/shard_map/ppermute | solution.py:62
  245.6 18.5 %collective-permute-done.26.refs_9_ = bf16[128,256]{1,0:T(8,128)(2,1)S(1)} collective-permute-done((bf16[128,256]{1,0:T(8,128)(2,1)S(1)}, bf16[128,256]{1,0:T(8,128)(2,1)S(1)}, u32[]{:S(2)}, u32[]{:S(2)}) %collective-permute-start.26) | collective-permute-done | bytes 65568 | tf_op jit(solution)/shard_map/ppermute | solution.py:62
  266.0 3.6 shard_map.201
  270.7 3.5 collective-permute-done.49.refs_3_
  278.1 4.1 %shard_map.207 = (f32[896,2432]{1,0:T(8,128)}, f32[896,2432]{1,0:T(8,128)}, f32[2432,896]{1,0:T(8,128)}, f32[448,1152]{1,0:T(8,128)}, f32[448,896]{1,0:T(8,128)}, /*index=5*/f32[8,128]{1,0:T(8,128)}) custom-call(s32[20]{0:T(128)} %concatenate.66.refs_0_.meta_ref, bf16[520,896]{1,0:T(8,128)(2,1)} %shard_map.206.refs_0_, bf16[520,896]{1,0:T(8,128)(2,1)} %copy-done.15), custom_call_target="tpu_custom_call" | custom-call | bytes 7454720 | tf_op jit(solution)/shard_map/pallas_call | solution.py:904
  288.3 21.0 %collective-permute-done.55 = bf16[232,256]{1,0:T(8,128)(2,1)S(1)} collective-permute-done((bf16[232,256]{1,0:T(8,128)(2,1)S(1)}, bf16[232,256]{1,0:T(8,128)(2,1)S(1)}, u32[]{:S(2)}, u32[]{:S(2)}) %collective-permute-start.55) | collective-permute-done | bytes 118816 | tf_op jit(solution)/shard_map/ppermute | solution.py:173
  310.0 6.0 %shard_map.210 = (f32[896,2432]{1,0:T(8,128)}, f32[896,2432]{1,0:T(8,128)}, f32[2432,896]{1,0:T(8,128)}, f32[448,1152]{1,0:T(8,128)}, f32[448,896]{1,0:T(8,128)}, /*index=5*/f32[8,128]{1,0:T(8,128)}) custom-call(s32[20]{0:T(128)} %concatenate.66.refs_0_.meta_ref, ...), custom_call_target="tpu_custom_call", output_to_operand_aliasing={{0}: (5, {}), {1}: (6, {}), {2}: (7, {}), {3}: (8, {}), {4}... | custom-call | bytes 14909440 | tf_op jit(solution)/shard_map/pallas_call | solution.py:904
  319.8 23.3 %collective-permute-done.60 = bf16[232,256]{1,0:T(8,128)(2,1)S(1)} collective-permute-done((bf16[232,256]{1,0:T(8,128)(2,1)S(1)}, bf16[232,256]{1,0:T(8,128)(2,1)S(1)}, u32[]{:S(2)}, u32[]{:S(2)}) %collective-permute-start.60) | collective-permute-done | bytes 118816 | tf_op jit(solution)/shard_map/ppermute | solution.py:173
  345.0 5.9 %shard_map.212 = (f32[896,2432]{1,0:T(8,128)}, f32[896,2432]{1,0:T(8,128)}, f32[2432,896]{1,0:T(8,128)}, f32[448,1152]{1,0:T(8,128)}, f32[448,896]{1,0:T(8,128)}, /*index=5*/f32[8,128]{1,0:T(8,128)}) custom-call(s32[20]{0:T(128)} %concatenate.66.refs_0_.meta_ref, ...), custom_call_target="tpu_custom_call", output_to_operand_aliasing={{0}: (5, {}), {1}: (6, {}), {2}: (7, {}), {3}: (8, {}), {4}... | custom-call | bytes 14909440 | tf_op jit(solution)/shard_map/pallas_call | solution.py:904
  359.7 15.4 %collective-permute-done.68 = bf16[232,256]{1,0:T(8,128)(2,1)S(1)} collective-permute-done((bf16[232,256]{1,0:T(8,128)(2,1)S(1)}, bf16[232,256]{1,0:T(8,128)(2,1)S(1)}, u32[]{:S(2)}, u32[]{:S(2)}) %collective-permute-start.68) | collective-permute-done | bytes 118816 | tf_op jit(solution)/shard_map/ppermute | solution.py:173
  377.5 5.8 %shard_map.214 = (f32[896,2432]{1,0:T(8,128)}, f32[896,2432]{1,0:T(8,128)}, f32[2432,896]{1,0:T(8,128)}, f32[448,1152]{1,0:T(8,128)}, f32[448,896]{1,0:T(8,128)}, /*index=5*/f32[8,128]{1,0:T(8,128)}) custom-call(s32[20]{0:T(128)} %concatenate.66.refs_0_.meta_ref, ...), custom_call_target="tpu_custom_call", output_to_operand_aliasing={{0}: (5, {}), {1}: (6, {}), {2}: (7, {}), {3}: (8, {}), {4}... | custom-call | bytes 14909440 | tf_op jit(solution)/shard_map/pallas_call | solution.py:904
  390.0 4.3 %shard_map.216 = (f32[896,2432]{1,0:T(8,128)}, f32[896,2432]{1,0:T(8,128)}, f32[2432,896]{1,0:T(8,128)}, f32[448,1152]{1,0:T(8,128)}, f32[448,896]{1,0:T(8,128)}, /*index=5*/f32[8,128]{1,0:T(8,128)}) custom-call(s32[20]{0:T(128)} %concatenate.66.refs_0_.meta_ref, ...), custom_call_target="tpu_custom_call", output_to_operand_aliasing={{0}: (5, {}), {1}: (6, {}), {2}: (7, {}), {3}: (8, {}), {4}... | custom-call | bytes 7454720 | tf_op jit(solution)/shard_map/pallas_call | solution.py:904
  (354 shorter events, 154.1 us)
Async XLA Ops:
  103.5 32.2 %collective-permute-start.21 = (bf16[456,896]{1,0:T(8,128)(2,1)}, bf16[456,896]{1,0:T(8,128)(2,1)S(1)}, u32[]{:S(2)}, u32[]{:S(2)}) collective-permute-start(bf16[456,896]{1,0:T(8,128)(2,1)} %get-tuple-element.128), channel_id=1, source_target_pairs={{0,4},{1,5},{4,8},{5,9},{8,12},{9,13},{12,14},{13,15},{14,10},{15,... | collective-permute-start | bytes 2451464 | tf_op jit(solution)/shard_map/ppermute | solution.py:62
  123.1 26.0 %collective-permute-start.36 = (bf16[128,896]{1,0:T(8,128)(2,1)S(1)}, bf16[128,896]{1,0:T(8,128)(2,1)S(1)}, u32[]{:S(2)}, u32[]{:S(2)}) collective-permute-start(bf16[128,896]{1,0:T(8,128)(2,1)S(1)} %copy-done.39), channel_id=1, source_target_pairs={{0,16},{16,0},{1,17},{17,1},{2,18},{18,2},{3,19},{19,3},{4,20},{20... | collective-permute-start | bytes 688136 | tf_op jit(solution)/shard_map/ppermute | solution.py:54
  135.6 44.1 %collective-permute-start.39 = (bf16[512,896]{1,0:T(8,128)(2,1)S(1)}, bf16[512,896]{1,0:T(8,128)(2,1)}, u32[]{:S(2)}, u32[]{:S(2)}) collective-permute-start(bf16[512,896]{1,0:T(8,128)(2,1)S(1)} %constant_dynamic-update-slice_fusion.15.refs_5_), channel_id=1, source_target_pairs={{0,1},{1,0},{2,3},{3,2},{4,5},{5,4},{6,7},{7,6},{8,9},{9,8},{10,11... | collective-permute-start | bytes 2752520 | tf_op jit(solution)/shard_map/ppermute | solution.py:50
  149.2 28.9 %collective-permute-start.37 = (bf16[256,896]{1,0:T(8,128)(2,1)S(1)}, bf16[256,896]{1,0:T(8,128)(2,1)S(1)}, u32[]{:S(2)}, u32[]{:S(2)}) collective-permute-start(bf16[256,896]{1,0:T(8,128)(2,1)S(1)} %constant_dynamic-update-slice_fusion.13.refs_3_), channel_id=1, source_target_pairs={{0,1},{1,0},{2,3},{3,2},{4,5},{5,4},{6,7},{7,6},{8,9},{9,8},{10,11... | collective-permute-start | bytes 1376264 | tf_op jit(solution)/shard_map/ppermute | solution.py:50
  149.3 38.7 %collective-permute-start.31 = (bf16[456,896]{1,0:T(8,128)(2,1)S(1)}, bf16[456,896]{1,0:T(8,128)(2,1)S(1)}, u32[]{:S(2)}, u32[]{:S(2)}) collective-permute-start(bf16[456,896]{1,0:T(8,128)(2,1)S(1)} %copy-done.8), channel_id=1, source_target_pairs={{0,4},{1,5},{4,8},{5,9},{8,12},{9,13},{12,14},{13,15},{14,10},{15,... | collective-permute-start | bytes 2451464 | tf_op jit(solution)/shard_map/ppermute | solution.py:62
  150.9 38.8 %collective-permute-start.32 = (bf16[456,896]{1,0:T(8,128)(2,1)S(1)}, bf16[456,896]{1,0:T(8,128)(2,1)S(1)}, u32[]{:S(2)}, u32[]{:S(2)}) collective-permute-start(bf16[456,896]{1,0:T(8,128)(2,1)S(1)} %copy-done.7), channel_id=1, source_target_pairs={{0,2},{1,3},{4,0},{5,1},{8,4},{9,5},{12,8},{13,9},{14,12},{15,13},... | collective-permute-start | bytes 2451464 | tf_op jit(solution)/shard_map/ppermute | solution.py:62
  176.1 38.7 %collective-permute-start.28 = (bf16[128,256]{1,0:T(8,128)(2,1)}, bf16[128,256]{1,0:T(8,128)(2,1)S(1)}, u32[]{:S(2)}, u32[]{:S(2)}) collective-permute-start(bf16[128,256]{1,0:T(8,128)(2,1)} %pad_maximum_fusion.9), channel_id=1, source_target_pairs={{0,2},{1,3},{4,0},{5,1},{8,4},{9,5},{12,8},{13,9},{14,12},{15,13},... | collective-permute-start | bytes 196616 | tf_op jit(solution)/shard_map/ppermute | solution.py:62
  178.1 58.4 %collective-permute-start.25 = (bf16[128,256]{1,0:T(8,128)(2,1)}, bf16[128,256]{1,0:T(8,128)(2,1)S(1)}, u32[]{:S(2)}, u32[]{:S(2)}) collective-permute-start(bf16[128,256]{1,0:T(8,128)(2,1)} %add_convert_fusion.16), channel_id=1, source_target_pairs={{0,4},{1,5},{4,8},{5,9},{8,12},{9,13},{12,14},{13,15},{14,10},{15,... | collective-permute-start | bytes 196616 | tf_op jit(solution)/shard_map/ppermute | solution.py:62
  192.3 31.0 %collective-permute-start.35 = (bf16[456,896]{1,0:T(8,128)(2,1)}, bf16[456,896]{1,0:T(8,128)(2,1)S(1)}, u32[]{:S(2)}, u32[]{:S(2)}) collective-permute-start(bf16[456,896]{1,0:T(8,128)(2,1)} %get-tuple-element.145), channel_id=1, source_target_pairs={{0,2},{1,3},{4,0},{5,1},{8,4},{9,5},{12,8},{13,9},{14,12},{15,13},... | collective-permute-start | bytes 2451464 | tf_op jit(solution)/shard_map/ppermute | solution.py:62
  239.5 37.7 %collective-permute-start.48 = (bf16[520,896]{1,0:T(8,128)(2,1)}, bf16[520,896]{1,0:T(8,128)(2,1)S(1)}, u32[]{:S(2)}, u32[]{:S(2)}) collective-permute-start(bf16[520,896]{1,0:T(8,128)(2,1)} %shard_map.206.refs_0_), channel_id=1, source_target_pairs={{0,1},{1,0},{2,3},{3,2},{4,5},{5,4},{6,7},{7,6},{8,9},{9,8},{10,11... | collective-permute-start | bytes 2795528 | tf_op jit(solution)/shard_map/ppermute | solution.py:50
  239.5 42.7 %collective-permute-start.50 = (bf16[520,896]{1,0:T(8,128)(2,1)}, bf16[520,896]{1,0:T(8,128)(2,1)S(1)}, u32[]{:S(2)}, u32[]{:S(2)}) collective-permute-start(bf16[520,896]{1,0:T(8,128)(2,1)} %shard_map.206.refs_0_), channel_id=1, source_target_pairs={{0,4},{1,5},{4,8},{5,9},{8,12},{9,13},{12,14},{13,15},{14,10},{15,... | collective-permute-start | bytes 2795528 | tf_op jit(solution)/shard_map/ppermute | solution.py:62
  241.0 41.3 %collective-permute-start.51 = (bf16[520,896]{1,0:T(8,128)(2,1)}, bf16[520,896]{1,0:T(8,128)(2,1)S(1)}, u32[]{:S(2)}, u32[]{:S(2)}) collective-permute-start(bf16[520,896]{1,0:T(8,128)(2,1)} %shard_map.206.refs_0_), channel_id=1, source_target_pairs={{0,2},{1,3},{4,0},{5,1},{8,4},{9,5},{12,8},{13,9},{14,12},{15,13},... | collective-permute-start | bytes 2795528 | tf_op jit(solution)/shard_map/ppermute | solution.py:62
  283.5 26.5 %collective-permute-start.52 = (bf16[520,896]{1,0:T(8,128)(2,1)}, bf16[520,896]{1,0:T(8,128)(2,1)}, u32[]{:S(2)}, u32[]{:S(2)}) collective-permute-start(bf16[520,896]{1,0:T(8,128)(2,1)} %get-tuple-element.160.refs_0_), channel_id=1, source_target_pairs={{0,1},{1,0},{2,3},{3,2},{4,5},{5,4},{6,7},{7,6},{8,9},{9,8},{10,11... | collective-permute-start | bytes 2795528 | tf_op jit(solution)/shard_map/ppermute | solution.py:50
  283.5 26.5 %collective-permute-start.53 = (bf16[520,896]{1,0:T(8,128)(2,1)}, bf16[520,896]{1,0:T(8,128)(2,1)}, u32[]{:S(2)}, u32[]{:S(2)}) collective-permute-start(bf16[520,896]{1,0:T(8,128)(2,1)} %get-tuple-element.161.refs_2_), channel_id=1, source_target_pairs={{0,1},{1,0},{2,3},{3,2},{4,5},{5,4},{6,7},{7,6},{8,9},{9,8},{10,11... | collective-permute-start | bytes 2795528 | tf_op jit(solution)/shard_map/ppermute | solution.py:50
  284.0 32.0 %collective-permute-start.56 = (bf16[520,896]{1,0:T(8,128)(2,1)}, bf16[520,896]{1,0:T(8,128)(2,1)S(1)}, u32[]{:S(2)}, u32[]{:S(2)}) collective-permute-start(bf16[520,896]{1,0:T(8,128)(2,1)} %get-tuple-element.160.refs_0_), channel_id=1, source_target_pairs={{0,4},{1,5},{4,8},{5,9},{8,12},{9,13},{12,14},{13,15},{14,10},{15,... | collective-permute-start | bytes 2795528 | tf_op jit(solution)/shard_map/ppermute | solution.py:62
  285.2 30.8 %collective-permute-start.57 = (bf16[520,896]{1,0:T(8,128)(2,1)}, bf16[520,896]{1,0:T(8,128)(2,1)S(1)}, u32[]{:S(2)}, u32[]{:S(2)}) collective-permute-start(bf16[520,896]{1,0:T(8,128)(2,1)} %get-tuple-element.161.refs_2_), channel_id=1, source_target_pairs={{0,2},{1,3},{4,0},{5,1},{8,4},{9,5},{12,8},{13,9},{14,12},{15,13},... | collective-permute-start | bytes 2795528 | tf_op jit(solution)/shard_map/ppermute | solution.py:62
  317.2 26.5 %collective-permute-start.58 = (bf16[520,896]{1,0:T(8,128)(2,1)}, bf16[520,896]{1,0:T(8,128)(2,1)S(1)}, u32[]{:S(2)}, u32[]{:S(2)}) collective-permute-start(bf16[520,896]{1,0:T(8,128)(2,1)} %get-tuple-element.168.refs_0_), channel_id=1, source_target_pairs={{0,1},{1,0},{2,3},{3,2},{4,5},{5,4},{6,7},{7,6},{8,9},{9,8},{10,11... | collective-permute-start | bytes 2795528 | tf_op jit(solution)/shard_map/ppermute | solution.py:50
  317.2 26.5 %collective-permute-start.59 = (bf16[520,896]{1,0:T(8,128)(2,1)}, bf16[520,896]{1,0:T(8,128)(2,1)S(1)}, u32[]{:S(2)}, u32[]{:S(2)}) collective-permute-start(bf16[520,896]{1,0:T(8,128)(2,1)} %get-tuple-element.169.refs_2_), channel_id=1, source_target_pairs={{0,1},{1,0},{2,3},{3,2},{4,5},{5,4},{6,7},{7,6},{8,9},{9,8},{10,11... | collective-permute-start | bytes 2795528 | tf_op jit(solution)/shard_map/ppermute | solution.py:50
  317.7 33.2 %collective-permute-start.61 = (bf16[520,896]{1,0:T(8,128)(2,1)}, bf16[520,896]{1,0:T(8,128)(2,1)S(1)}, u32[]{:S(2)}, u32[]{:S(2)}) collective-permute-start(bf16[520,896]{1,0:T(8,128)(2,1)} %get-tuple-element.168.refs_0_), channel_id=1, source_target_pairs={{0,4},{1,5},{4,8},{5,9},{8,12},{9,13},{12,14},{13,15},{14,10},{15,... | collective-permute-start | bytes 2795528 | tf_op jit(solution)/shard_map/ppermute | solution.py:62
  317.7 33.2 %collective-permute-start.62 = (bf16[520,896]{1,0:T(8,128)(2,1)}, bf16[520,896]{1,0:T(8,128)(2,1)S(1)}, u32[]{:S(2)}, u32[]{:S(2)}) collective-permute-start(bf16[520,896]{1,0:T(8,128)(2,1)} %get-tuple-element.169.refs_2_), channel_id=1, source_target_pairs={{0,2},{1,3},{4,0},{5,1},{8,4},{9,5},{12,8},{13,9},{14,12},{15,13},... | collective-permute-start | bytes 2795528 | tf_op jit(solution)/shard_map/ppermute | solution.py:62
  352.2 24.0 %collective-permute-start.65 = (bf16[520,896]{1,0:T(8,128)(2,1)}, bf16[520,896]{1,0:T(8,128)(2,1)S(1)}, u32[]{:S(2)}, u32[]{:S(2)}) collective-permute-start(bf16[520,896]{1,0:T(8,128)(2,1)} %get-tuple-element.176.refs_0_), channel_id=1, source_target_pairs={{0,1},{1,0},{2,3},{3,2},{4,5},{5,4},{6,7},{7,6},{8,9},{9,8},{10,11... | collective-permute-start | bytes 2795528 | tf_op jit(solution)/shard_map/ppermute | solution.py:50
  352.2 24.1 %collective-permute-start.66 = (bf16[520,896]{1,0:T(8,128)(2,1)}, bf16[520,896]{1,0:T(8,128)(2,1)S(1)}, u32[]{:S(2)}, u32[]{:S(2)}) collective-permute-start(bf16[520,896]{1,0:T(8,128)(2,1)} %get-tuple-element.177.refs_2_), channel_id=1, source_target_pairs={{0,1},{1,0},{2,3},{3,2},{4,5},{5,4},{6,7},{7,6},{8,9},{9,8},{10,11... | collective-permute-start | bytes 2795528 | tf_op jit(solution)/shard_map/ppermute | solution.py:50
  354.5 28.8 %collective-permute-start.63 = (bf16[264,896]{1,0:T(8,128)(2,1)}, bf16[264,896]{1,0:T(8,128)(2,1)S(1)}, u32[]{:S(2)}, u32[]{:S(2)}) collective-permute-start(bf16[264,896]{1,0:T(8,128)(2,1)} %slice.103), channel_id=1, source_target_pairs={{0,4},{1,5},{4,8},{5,9},{8,12},{9,13},{12,14},{13,15},{14,10},{15,... | collective-permute-start | bytes 1419272 | tf_op jit(solution)/shard_map/ppermute | solution.py:62
  356.6 26.8 %collective-permute-start.64 = (bf16[256,896]{1,0:T(8,128)(2,1)}, bf16[256,896]{1,0:T(8,128)(2,1)}, u32[]{:S(2)}, u32[]{:S(2)}) collective-permute-start(bf16[256,896]{1,0:T(8,128)(2,1)} %slice.104), channel_id=1, source_target_pairs={{0,2},{1,3},{4,0},{5,1},{8,4},{9,5},{12,8},{13,9},{14,12},{15,13},... | collective-permute-start | bytes 1376264 | tf_op jit(solution)/shard_map/ppermute | solution.py:62
  (110 other events, 909.8 us)

commit v12 on v11

--- a/solution.py
+++ b/solution.py
@@ -767,15 +767,15 @@
 
 
 def small_grad_kernel(
-    chips, q_rows, rows, cols, meta_ref, norm_a, norm_b, att_a, att_b, near_a, near_b, *refs
+    chips, q_rows, rows, cols, meta_ref, norm_a, norm_b, near_a, near_b, *refs
 ):
     out_refs, acc, turned_ref = refs[:-2], refs[-2], refs[-1]
     first = pl.multiple_of((2 * meta_ref[0] + meta_ref[1]) * q_rows, 16)
-    grads, queries = [], []
+    grads, queries, attended = [], [], []
     for near_ref in (near_a, near_b):
         for b in range(2):
-            grads.append(near_ref[2 * b * rows : (2 * b + 1) * rows, :])
-            queries.append(near_ref[(2 * b + 1) * rows : (2 * b + 2) * rows, :])
+            for i, found in enumerate((grads, queries, attended)):
+                found.append(near_ref[(3 * b + i) * rows : (3 * b + i + 1) * rows, :])
     turned_ref[...] = jnp.concatenate([norm_a[:, D:], norm_b[:, D:]], 0).T
     acc[:, :WIDTH_Q] = jnp.dot(
         turned_ref[pl.ds(first, q_rows), :],
@@ -783,7 +783,7 @@
         preferred_element_type=f32,
     ).astype(bf16)
     acc[:, WIDTH_Q:cols] = jnp.zeros((q_rows, cols - WIDTH_Q), bf16)
-    turned_ref[...] = jnp.concatenate([att_a[...], att_b[...]], 0).T
+    turned_ref[...] = jnp.concatenate(attended, 0).T
     acc[:, cols:] = jnp.dot(
         turned_ref[pl.ds(first, q_rows), :], jnp.concatenate(grads, 0), preferred_element_type=f32
     ).astype(bf16)
@@ -1200,8 +1200,7 @@
         got = net.shift(mlp_chip[s * rows : (s + 1) * rows].astype(bf16), net.dp - s)
         out_sum = out_sum + got.astype(f32)
     output = (hidden + out_sum).astype(bf16)
-    near = net.group_parts(jnp.concatenate([grad_attn_low, grad_queries], 0))
-    attended_parts = net.group_parts(attended_low)
+    near = net.group_parts(jnp.concatenate([grad_attn_low, grad_queries, attended_low], 0))
 
     q_rows = w_qkv.shape[0] // 2
     qkv_cols = w_qkv.shape[1]
@@ -1210,7 +1209,7 @@
         terms_small = call(
             lambda *refs: small_grad_kernel(chips, q_rows, rows, qkv_cols, *refs),
             [jax.ShapeDtypeStruct((piece, D), bf16)] * chips,
-            [spots, *early, *attended_parts, *near],
+            [spots, *early, *near],
             smem=1,
             scratch=[
                 pltpu.VMEM((q_rows, qkv_cols + D), bf16),
@@ -1221,7 +1220,7 @@
         block = call(
             block_kernel,
             [jax.ShapeDtypeStruct((sum_mlp.shape[0] + piece + down_rows, D), bf16)],
-            [sum_mlp, sum_down] + net.ring_parts(terms_small)[0] + list(marks[2]),
+            [sum_mlp, sum_down] + net.ring_parts(terms_small)[0] + list(marks[3]),
             loose=2,
         )[0]
         part_pair = call(
@@ -1243,9 +1242,9 @@
             [[part_pair], [steps[1]], [steps[2]]],
         )
     else:
-        gathered = jnp.concatenate(near, 0).reshape(2 * net.dp, 2, rows, D)
+        gathered = jnp.concatenate(near, 0).reshape(2 * net.dp, 3, rows, D)
         grad_attn_group = gathered[:, 0].reshape(2 * net.dp * rows, D)
-        attended_group = jnp.concatenate(attended_parts, 0)
+        attended_group = gathered[:, 2].reshape(2 * net.dp * rows, D)
         normed_one_group = jnp.concatenate(early, 0)[:, D:]
         joint_group = net.group_gather(jnp.concatenate([grad_queries, pair_sent[:rows]], 1))
         q_first = net.d * (2 * q_rows) + core * q_rows

time: 396 us -> 369 us (0.932)
  waiting for transfers between devices: 170 us -> 149 us
  starting transfers between devices: 59.4 us -> 55.2 us
    ppermute x39, waiting for transfers between devices: 81.8 us -> 67.3 us  [hop(): return lax.ppermute(x, 'ctx', perm)]
    ppermute x9 -> x8, waiting for transfers between devices: 23.5 us -> 16.8 us  [shift(): return lax.ppermute(x, 'dp', [(i, (i + step) % n) for i in range(n)])]
    ppermute x9 -> x8, starting transfers between devices: 12.9 us -> 12.2 us  [shift(): return lax.ppermute(x, 'dp', [(i, (i + step) % n) for i in range(n)])]
    unnamed x142 -> x140, local copies, waits for them, and re-layouts: 19.5 us -> 19.8 us
  transfers between devices with their start and end apart: 70 -> 68, of which waited for: 27 -> 27; matrix products, arithmetic and copies ran while one was open for 11% -> 11% of each run, Pallas kernels for 19% -> 20%
where the time goes in v12:
time: 369 us; the launch traced here: 367 us
  waiting for transfers between devices  149 us (40%)
  Pallas kernels  100 us (27%)
  starting transfers between devices  55.2 us (15%)
  local copies, waits for them, and re-layouts  39.8 us (11%)
  other arithmetic  21.4 us (6%)
    ppermute x39, waiting for transfers between devices, hop(): return lax.ppermute(x, 'ctx', perm)  67.3 us
    ppermute x3, waiting for transfers between devices, exchange_sum(): lax.ppermute(x, 'ctx', [(i, i ^ 2 * bit) for i in range(self.ctx)])  59.5 us
    pallas_call x10, Pallas kernels, call(): pl.pallas_call(body, out_shape=list(outs), in_specs=specs, out_specs=[pl....  47.9 us
    ppermute x39, starting transfers between devices, hop(): return lax.ppermute(x, 'ctx', perm)  37.9 us
    pallas_call x5, Pallas kernels, place_all(): pl.pallas_call(kernel, out_shape=[jax.ShapeDtypeStruct((D, ff_loc), f32),...  26 us
    unnamed x140, local copies, waits for them, and re-layouts  19.8 us
    ppermute x8, waiting for transfers between devices, shift(): return lax.ppermute(x, 'dp', [(i, (i + step) % n) for i in range(n)])  16.8 us
    pallas_call x1, Pallas kernels, feed_forward(): pl.pallas_call(lambda *refs: mlp_kernel(half, *refs), out_shape=[jax.Shap...  16.2 us
  transfers between devices with their start and end apart: 68, of which 27 were waited for; matrix products, arithmetic and copies ran while one was open for 11% of the time, Pallas kernels for 20%

profile of v12, /device:TPU:0, one launch (start us, length us, event | category | flops | bytes accessed | tf_op | source)
XLA Modules:
  0.0 367.3 jit_solution(4036684166620698960)
XLA Ops:
  11.9 4.7 %collective-permute-done = bf16[224,1152]{1,0:T(8,128)(2,1)S(1)} collective-permute-done((bf16[224,1152]{1,0:T(8,128)(2,1)S(1)}, bf16[224,1152]{1,0:T(8,128)(2,1)S(1)}, u32[]{:S(2)}, u32[]{:S(2)}) %collective-permute-start) | collective-permute-done | bytes 516128 | tf_op jit(solution)/shard_map/ppermute | solution.py:54
  20.4 3.2 shard_map.195
  49.5 10.3 %shard_map.196 = (bf16[128,896]{1,0:T(8,128)(2,1)}, f32[2,896,128]{2,1,0:T(8,128)}, f32[2,2,8,448]{3,2,1,0:T(8,128)}, bf16[2,896,128]{2,1,0:T(8,128)(2,1)}, bf16...) custom-call(s32[17]{0:T(128)} %pad_add_fusion.refs_0_, ...), custom_call_target="tpu_custom_call" | custom-call | flops 1879048192 | bytes 6516292 | tf_op jit(solution)/shard_map/pallas_call | solution.py:238
  62.6 5.1 %collective-permute-done.13 = bf16[128,896]{1,0:T(8,128)(2,1)S(1)} collective-permute-done((bf16[128,896]{1,0:T(8,128)(2,1)}, bf16[128,896]{1,0:T(8,128)(2,1)S(1)}, u32[]{:S(2)}, u32[]{:S(2)}) %collective-permute-start.13) | collective-permute-done | bytes 229408 | tf_op jit(solution)/shard_map/ppermute | solution.py:54
  70.8 16.2 %shard_map.197 = (bf16[896,512]{1,0:T(8,128)(2,1)}, bf16[1280,512]{1,0:T(8,128)(2,1)}, bf16[512,1280]{1,0:T(8,128)(2,1)}, bf16[512,1280]{1,0:T(8,128)(2,1)}, f32...) custom-call(s32[20]{0:T(128)} %concatenate.63.refs_0_.meta_ref, bf16[256,896]{1,0:T(8,128)(2,1)} %copy-done.17, ...), custom_call_target="tpu_custom_call" | custom-call | flops 7046430720 | bytes 6881280 | tf_op jit(solution)/shard_map/pallas_call | solution.py:662
  94.2 10.1 %shard_map.198 = (bf16[456,896]{1,0:T(8,128)(2,1)}, bf16[456,896]{1,0:T(8,128)(2,1)}, bf16[456,896]{1,0:T(8,128)(2,1)}, bf16[456,896]{1,0:T(8,128)(2,1)}, bf16[4...) custom-call(s32[20]{0:T(128)} %concatenate.63.refs_0_.meta_ref, ...), custom_call_target="tpu_custom_call" | custom-call | flops 3523215360 | bytes 13074432 | tf_op jit(solution)/shard_map/pallas_call | solution.py:748
  107.2 14.9 %shard_map.199 = (f32[128,896]{1,0:T(8,128)}, bf16[128,896]{1,0:T(8,128)(2,1)}, f32[1,896]{1,0:T(1,128)}, bf16[128,896]{1,0:T(8,128)(2,1)}, f32[1024,256]{1,0:T(8,128)}, /*index=5*/bf16[1024,256]{1,0:T(8,128)(2,1)}) custom-call(s32[17]{0:T(128)} %pad_add_fusion.refs_0_, f32[128,896]{1,0:T(8,128)} %slice_add_fusion.refs_1_, ...), custom_call_target="tpu_custom_call" | custom-call | flops 4697620480 | bytes 8680516 | tf_op jit(solution)/shard_map/pallas_call | solution.py:238
  143.7 13.1 %collective-permute-done.27.refs_1_ = bf16[64,256]{1,0:T(8,128)(2,1)S(1)} collective-permute-done((bf16[64,256]{1,0:T(8,128)(2,1)S(1)}, bf16[64,256]{1,0:T(8,128)(2,1)S(1)}, u32[]{:S(2)}, u32[]{:S(2)}) %collective-permute-start.27) | collective-permute-done | bytes 32800 | tf_op jit(solution)/shard_map/ppermute | solution.py:62
  165.6 4.2 %shard_map.205 = (bf16[64,896]{1,0:T(8,128)(2,1)}, bf16[64,896]{1,0:T(8,128)(2,1)}, bf16[64,896]{1,0:T(8,128)(2,1)}, bf16[64,896]{1,0:T(8,128)(2,1)}, bf16[64,89...) custom-call(s32[20]{0:T(128)} %concatenate.63.refs_0_.meta_ref, ...), custom_call_target="tpu_custom_call" | custom-call | flops 1879048192 | bytes 5505104 | tf_op jit(solution)/shard_map/pallas_call | solution.py:238
  176.1 7.4 %collective-permute-done.38 = bf16[32,896]{1,0:T(8,128)(2,1)S(1)} collective-permute-done((bf16[32,896]{1,0:T(8,128)(2,1)S(1)}, bf16[32,896]{1,0:T(8,128)(2,1)S(1)}, u32[]{:S(2)}, u32[]{:S(2)}) %collective-permute-start.38) | collective-permute-done | bytes 57376 | tf_op jit(solution)/shard_map/ppermute | solution.py:62
  184.8 7.6 %collective-permute-done.42 = bf16[32,896]{1,0:T(8,128)(2,1)S(1)} collective-permute-done((bf16[32,896]{1,0:T(8,128)(2,1)S(1)}, bf16[32,896]{1,0:T(8,128)(2,1)S(1)}, u32[]{:S(2)}, u32[]{:S(2)}) %collective-permute-start.42) | collective-permute-done | bytes 57376 | tf_op jit(solution)/shard_map/ppermute | solution.py:62
  199.5 16.0 %collective-permute-done.40 = bf16[64,896]{1,0:T(8,128)(2,1)S(1)} collective-permute-done((bf16[64,896]{1,0:T(8,128)(2,1)S(1)}, bf16[64,896]{1,0:T(8,128)(2,1)S(1)}, u32[]{:S(2)}, u32[]{:S(2)}) %collective-permute-start.40) | collective-permute-done | bytes 114720 | tf_op jit(solution)/shard_map/ppermute | solution.py:62
  215.6 4.7 %collective-permute-done.44 = bf16[64,896]{1,0:T(8,128)(2,1)S(1)} collective-permute-done((bf16[64,896]{1,0:T(8,128)(2,1)S(1)}, bf16[64,896]{1,0:T(8,128)(2,1)S(1)}, u32[]{:S(2)}, u32[]{:S(2)}) %collective-permute-start.44) | collective-permute-done | bytes 114720 | tf_op jit(solution)/shard_map/ppermute | solution.py:62
  232.0 3.6 shard_map.201
  237.0 3.2 collective-permute-done.47.refs_3_
  244.1 4.1 %shard_map.207 = (f32[896,2432]{1,0:T(8,128)}, f32[896,2432]{1,0:T(8,128)}, f32[2432,896]{1,0:T(8,128)}, f32[448,1152]{1,0:T(8,128)}, f32[448,896]{1,0:T(8,128)}, /*index=5*/f32[8,128]{1,0:T(8,128)}) custom-call(s32[20]{0:T(128)} %concatenate.63.refs_0_.meta_ref, bf16[520,896]{1,0:T(8,128)(2,1)} %shard_map.206.refs_0_, bf16[520,896]{1,0:T(8,128)(2,1)} %copy-done.18), custom_call_target="tpu_custom_call" | custom-call | bytes 7454720 | tf_op jit(solution)/shard_map/pallas_call | solution.py:904
  248.2 5.0 %collective-permute-done.48.refs_2_ = bf16[520,896]{1,0:T(8,128)(2,1)S(1)} collective-permute-done((bf16[520,896]{1,0:T(8,128)(2,1)}, bf16[520,896]{1,0:T(8,128)(2,1)S(1)}, u32[]{:S(2)}, u32[]{:S(2)}) %collective-permute-start.48) | collective-permute-done | bytes 931872 | tf_op jit(solution)/shard_map/ppermute | solution.py:62
  260.2 20.7 %collective-permute-done.53 = bf16[232,256]{1,0:T(8,128)(2,1)S(1)} collective-permute-done((bf16[232,256]{1,0:T(8,128)(2,1)S(1)}, bf16[232,256]{1,0:T(8,128)(2,1)S(1)}, u32[]{:S(2)}, u32[]{:S(2)}) %collective-permute-start.53) | collective-permute-done | bytes 118816 | tf_op jit(solution)/shard_map/ppermute | solution.py:173
  282.6 5.9 %shard_map.210 = (f32[896,2432]{1,0:T(8,128)}, f32[896,2432]{1,0:T(8,128)}, f32[2432,896]{1,0:T(8,128)}, f32[448,1152]{1,0:T(8,128)}, f32[448,896]{1,0:T(8,128)}, /*index=5*/f32[8,128]{1,0:T(8,128)}) custom-call(s32[20]{0:T(128)} %concatenate.63.refs_0_.meta_ref, ...), custom_call_target="tpu_custom_call", output_to_operand_aliasing={{0}: (5, {}), {1}: (6, {}), {2}: (7, {}), {3}: (8, {}), {4}... | custom-call | bytes 14909440 | tf_op jit(solution)/shard_map/pallas_call | solution.py:904
  292.3 23.3 %collective-permute-done.58 = bf16[232,256]{1,0:T(8,128)(2,1)S(1)} collective-permute-done((bf16[232,256]{1,0:T(8,128)(2,1)S(1)}, bf16[232,256]{1,0:T(8,128)(2,1)S(1)}, u32[]{:S(2)}, u32[]{:S(2)}) %collective-permute-start.58) | collective-permute-done | bytes 118816 | tf_op jit(solution)/shard_map/ppermute | solution.py:173
  317.6 5.9 %shard_map.212 = (f32[896,2432]{1,0:T(8,128)}, f32[896,2432]{1,0:T(8,128)}, f32[2432,896]{1,0:T(8,128)}, f32[448,1152]{1,0:T(8,128)}, f32[448,896]{1,0:T(8,128)}, /*index=5*/f32[8,128]{1,0:T(8,128)}) custom-call(s32[20]{0:T(128)} %concatenate.63.refs_0_.meta_ref, ...), custom_call_target="tpu_custom_call", output_to_operand_aliasing={{0}: (5, {}), {1}: (6, {}), {2}: (7, {}), {3}: (8, {}), {4}... | custom-call | bytes 14909440 | tf_op jit(solution)/shard_map/pallas_call | solution.py:904
  332.1 15.5 %collective-permute-done.66 = bf16[232,256]{1,0:T(8,128)(2,1)S(1)} collective-permute-done((bf16[232,256]{1,0:T(8,128)(2,1)S(1)}, bf16[232,256]{1,0:T(8,128)(2,1)S(1)}, u32[]{:S(2)}, u32[]{:S(2)}) %collective-permute-start.66) | collective-permute-done | bytes 118816 | tf_op jit(solution)/shard_map/ppermute | solution.py:173
  350.4 5.8 %shard_map.214 = (f32[896,2432]{1,0:T(8,128)}, f32[896,2432]{1,0:T(8,128)}, f32[2432,896]{1,0:T(8,128)}, f32[448,1152]{1,0:T(8,128)}, f32[448,896]{1,0:T(8,128)}, /*index=5*/f32[8,128]{1,0:T(8,128)}) custom-call(s32[20]{0:T(128)} %concatenate.63.refs_0_.meta_ref, ...), custom_call_target="tpu_custom_call", output_to_operand_aliasing={{0}: (5, {}), {1}: (6, {}), {2}: (7, {}), {3}: (8, {}), {4}... | custom-call | bytes 14909440 | tf_op jit(solution)/shard_map/pallas_call | solution.py:904
  362.9 4.2 %shard_map.216 = (f32[896,2432]{1,0:T(8,128)}, f32[896,2432]{1,0:T(8,128)}, f32[2432,896]{1,0:T(8,128)}, f32[448,1152]{1,0:T(8,128)}, f32[448,896]{1,0:T(8,128)}, /*index=5*/f32[8,128]{1,0:T(8,128)}) custom-call(s32[20]{0:T(128)} %concatenate.63.refs_0_.meta_ref, ...), custom_call_target="tpu_custom_call", output_to_operand_aliasing={{0}: (5, {}), {1}: (6, {}), {2}: (7, {}), {3}: (8, {}), {4}... | custom-call | bytes 7454720 | tf_op jit(solution)/shard_map/pallas_call | solution.py:904
  (347 shorter events, 150.8 us)
Async XLA Ops:
  46.5 22.5 %collective-permute-start.16 = (bf16[256,1792]{1,0:T(8,128)(2,1)S(1)}, bf16[256,1792]{1,0:T(8,128)(2,1)S(1)}, u32[]{:S(2)}, u32[]{:S(2)}) collective-permute-start(bf16[256,1792]{1,0:T(8,128)(2,1)S(1)} %pad_maximum_fusion.3.refs_3_.refs_2_.refs_1_), channel_id=1, source_target_pairs={{0,1},{1,0},{2,3},{3,2},{4,5},{5,4},{6,7},{7,6},{8,9},{9,8},{10,11... | collective-permute-start | bytes 2752520 | tf_op jit(solution)/shard_map/ppermute | solution.py:50
  134.8 26.9 %collective-permute-start.31 = (bf16[456,896]{1,0:T(8,128)(2,1)S(1)}, bf16[456,896]{1,0:T(8,128)(2,1)S(1)}, u32[]{:S(2)}, u32[]{:S(2)}) collective-permute-start(bf16[456,896]{1,0:T(8,128)(2,1)S(1)} %copy-done.7), channel_id=1, source_target_pairs={{0,4},{1,5},{4,8},{5,9},{8,12},{9,13},{12,14},{13,15},{14,10},{15,... | collective-permute-start | bytes 2451464 | tf_op jit(solution)/shard_map/ppermute | solution.py:62
  136.4 26.3 %collective-permute-start.32 = (bf16[456,896]{1,0:T(8,128)(2,1)S(1)}, bf16[456,896]{1,0:T(8,128)(2,1)S(1)}, u32[]{:S(2)}, u32[]{:S(2)}) collective-permute-start(bf16[456,896]{1,0:T(8,128)(2,1)S(1)} %copy-done.8), channel_id=1, source_target_pairs={{0,2},{1,3},{4,0},{5,1},{8,4},{9,5},{12,8},{13,9},{14,12},{15,13},... | collective-permute-start | bytes 2451464 | tf_op jit(solution)/shard_map/ppermute | solution.py:62
  142.1 23.5 %collective-permute-start.37 = (bf16[768,896]{1,0:T(8,128)(2,1)}, bf16[768,896]{1,0:T(8,128)(2,1)}, u32[]{:S(2)}, u32[]{:S(2)}) collective-permute-start(bf16[768,896]{1,0:T(8,128)(2,1)} %constant_dynamic-update-slice_fusion.13.refs_3_), channel_id=1, source_target_pairs={{0,1},{1,0},{2,3},{3,2},{4,5},{5,4},{6,7},{7,6},{8,9},{9,8},{10,11... | collective-permute-start | bytes 4128776 | tf_op jit(solution)/shard_map/ppermute | solution.py:50
  161.2 59.7 %collective-permute-start.29 = (bf16[128,256]{1,0:T(8,128)(2,1)S(1)}, bf16[128,256]{1,0:T(8,128)(2,1)S(1)}, u32[]{:S(2)}, u32[]{:S(2)}) collective-permute-start(bf16[128,256]{1,0:T(8,128)(2,1)S(1)} %add_convert_fusion.14), channel_id=1, source_target_pairs={{0,2},{1,3},{4,0},{5,1},{8,4},{9,5},{12,8},{13,9},{14,12},{15,13},... | collective-permute-start | bytes 196616 | tf_op jit(solution)/shard_map/ppermute | solution.py:62
  163.9 29.8 %collective-permute-start.33 = (bf16[456,896]{1,0:T(8,128)(2,1)}, bf16[456,896]{1,0:T(8,128)(2,1)S(1)}, u32[]{:S(2)}, u32[]{:S(2)}) collective-permute-start(bf16[456,896]{1,0:T(8,128)(2,1)} %get-tuple-element.143), channel_id=1, source_target_pairs={{0,4},{1,5},{4,8},{5,9},{8,12},{9,13},{12,14},{13,15},{14,10},{15,... | collective-permute-start | bytes 2451464 | tf_op jit(solution)/shard_map/ppermute | solution.py:62
  172.3 54.6 %collective-permute-start.26 = (bf16[128,256]{1,0:T(8,128)(2,1)S(1)}, bf16[128,256]{1,0:T(8,128)(2,1)S(1)}, u32[]{:S(2)}, u32[]{:S(2)}) collective-permute-start(bf16[128,256]{1,0:T(8,128)(2,1)S(1)} %add_convert_fusion.15), channel_id=1, source_target_pairs={{0,4},{1,5},{4,8},{5,9},{8,12},{9,13},{12,14},{13,15},{14,10},{15,... | collective-permute-start | bytes 196616 | tf_op jit(solution)/shard_map/ppermute | solution.py:62
  173.9 48.6 %collective-permute-start.35 = (bf16[456,896]{1,0:T(8,128)(2,1)S(1)}, bf16[456,896]{1,0:T(8,128)(2,1)S(1)}, u32[]{:S(2)}, u32[]{:S(2)}) collective-permute-start(bf16[456,896]{1,0:T(8,128)(2,1)S(1)} %copy-done.9), channel_id=1, source_target_pairs={{0,2},{1,3},{4,0},{5,1},{8,4},{9,5},{12,8},{13,9},{14,12},{15,13},... | collective-permute-start | bytes 2451464 | tf_op jit(solution)/shard_map/ppermute | solution.py:62
  198.4 24.2 %collective-permute-start.34 = (bf16[456,896]{1,0:T(8,128)(2,1)}, bf16[456,896]{1,0:T(8,128)(2,1)S(1)}, u32[]{:S(2)}, u32[]{:S(2)}) collective-permute-start(bf16[456,896]{1,0:T(8,128)(2,1)} %shard_map.203), channel_id=1, source_target_pairs={{0,4},{1,5},{4,8},{5,9},{8,12},{9,13},{12,14},{13,15},{14,10},{15,... | collective-permute-start | bytes 2451464 | tf_op jit(solution)/shard_map/ppermute | solution.py:62
  230.0 23.3 %collective-permute-start.48 = (bf16[520,896]{1,0:T(8,128)(2,1)}, bf16[520,896]{1,0:T(8,128)(2,1)S(1)}, u32[]{:S(2)}, u32[]{:S(2)}) collective-permute-start(bf16[520,896]{1,0:T(8,128)(2,1)} %shard_map.206.refs_0_), channel_id=1, source_target_pairs={{0,4},{1,5},{4,8},{5,9},{8,12},{9,13},{12,14},{13,15},{14,10},{15,... | collective-permute-start | bytes 2795528 | tf_op jit(solution)/shard_map/ppermute | solution.py:62
  231.2 23.0 %collective-permute-start.49 = (bf16[520,896]{1,0:T(8,128)(2,1)}, bf16[520,896]{1,0:T(8,128)(2,1)S(1)}, u32[]{:S(2)}, u32[]{:S(2)}) collective-permute-start(bf16[520,896]{1,0:T(8,128)(2,1)} %shard_map.206.refs_0_), channel_id=1, source_target_pairs={{0,2},{1,3},{4,0},{5,1},{8,4},{9,5},{12,8},{13,9},{14,12},{15,13},... | collective-permute-start | bytes 2795528 | tf_op jit(solution)/shard_map/ppermute | solution.py:62
  255.1 26.5 %collective-permute-start.50 = (bf16[520,896]{1,0:T(8,128)(2,1)}, bf16[520,896]{1,0:T(8,128)(2,1)S(1)}, u32[]{:S(2)}, u32[]{:S(2)}) collective-permute-start(bf16[520,896]{1,0:T(8,128)(2,1)} %get-tuple-element.160.refs_0_), channel_id=1, source_target_pairs={{0,1},{1,0},{2,3},{3,2},{4,5},{5,4},{6,7},{7,6},{8,9},{9,8},{10,11... | collective-permute-start | bytes 2795528 | tf_op jit(solution)/shard_map/ppermute | solution.py:50
  255.1 26.5 %collective-permute-start.51 = (bf16[520,896]{1,0:T(8,128)(2,1)}, bf16[520,896]{1,0:T(8,128)(2,1)}, u32[]{:S(2)}, u32[]{:S(2)}) collective-permute-start(bf16[520,896]{1,0:T(8,128)(2,1)} %get-tuple-element.161.refs_2_), channel_id=1, source_target_pairs={{0,1},{1,0},{2,3},{3,2},{4,5},{5,4},{6,7},{7,6},{8,9},{9,8},{10,11... | collective-permute-start | bytes 2795528 | tf_op jit(solution)/shard_map/ppermute | solution.py:50
  255.6 32.9 %collective-permute-start.54 = (bf16[520,896]{1,0:T(8,128)(2,1)}, bf16[520,896]{1,0:T(8,128)(2,1)S(1)}, u32[]{:S(2)}, u32[]{:S(2)}) collective-permute-start(bf16[520,896]{1,0:T(8,128)(2,1)} %get-tuple-element.160.refs_0_), channel_id=1, source_target_pairs={{0,4},{1,5},{4,8},{5,9},{8,12},{9,13},{12,14},{13,15},{14,10},{15,... | collective-permute-start | bytes 2795528 | tf_op jit(solution)/shard_map/ppermute | solution.py:62
  256.2 32.3 %collective-permute-start.55 = (bf16[520,896]{1,0:T(8,128)(2,1)}, bf16[520,896]{1,0:T(8,128)(2,1)S(1)}, u32[]{:S(2)}, u32[]{:S(2)}) collective-permute-start(bf16[520,896]{1,0:T(8,128)(2,1)} %get-tuple-element.161.refs_2_), channel_id=1, source_target_pairs={{0,2},{1,3},{4,0},{5,1},{8,4},{9,5},{12,8},{13,9},{14,12},{15,13},... | collective-permute-start | bytes 2795528 | tf_op jit(solution)/shard_map/ppermute | solution.py:62
  289.8 26.5 %collective-permute-start.56 = (bf16[520,896]{1,0:T(8,128)(2,1)}, bf16[520,896]{1,0:T(8,128)(2,1)S(1)}, u32[]{:S(2)}, u32[]{:S(2)}) collective-permute-start(bf16[520,896]{1,0:T(8,128)(2,1)} %get-tuple-element.168.refs_0_), channel_id=1, source_target_pairs={{0,1},{1,0},{2,3},{3,2},{4,5},{5,4},{6,7},{7,6},{8,9},{9,8},{10,11... | collective-permute-start | bytes 2795528 | tf_op jit(solution)/shard_map/ppermute | solution.py:50
  289.8 26.5 %collective-permute-start.57 = (bf16[520,896]{1,0:T(8,128)(2,1)}, bf16[520,896]{1,0:T(8,128)(2,1)S(1)}, u32[]{:S(2)}, u32[]{:S(2)}) collective-permute-start(bf16[520,896]{1,0:T(8,128)(2,1)} %get-tuple-element.169.refs_2_), channel_id=1, source_target_pairs={{0,1},{1,0},{2,3},{3,2},{4,5},{5,4},{6,7},{7,6},{8,9},{9,8},{10,11... | collective-permute-start | bytes 2795528 | tf_op jit(solution)/shard_map/ppermute | solution.py:50
  290.3 33.2 %collective-permute-start.59 = (bf16[520,896]{1,0:T(8,128)(2,1)}, bf16[520,896]{1,0:T(8,128)(2,1)S(1)}, u32[]{:S(2)}, u32[]{:S(2)}) collective-permute-start(bf16[520,896]{1,0:T(8,128)(2,1)} %get-tuple-element.168.refs_0_), channel_id=1, source_target_pairs={{0,4},{1,5},{4,8},{5,9},{8,12},{9,13},{12,14},{13,15},{14,10},{15,... | collective-permute-start | bytes 2795528 | tf_op jit(solution)/shard_map/ppermute | solution.py:62
  290.3 33.2 %collective-permute-start.60 = (bf16[520,896]{1,0:T(8,128)(2,1)}, bf16[520,896]{1,0:T(8,128)(2,1)S(1)}, u32[]{:S(2)}, u32[]{:S(2)}) collective-permute-start(bf16[520,896]{1,0:T(8,128)(2,1)} %get-tuple-element.169.refs_2_), channel_id=1, source_target_pairs={{0,2},{1,3},{4,0},{5,1},{8,4},{9,5},{12,8},{13,9},{14,12},{15,13},... | collective-permute-start | bytes 2795528 | tf_op jit(solution)/shard_map/ppermute | solution.py:62
  292.3 23.3 %collective-permute-start.58 = (bf16[232,256]{1,0:T(8,128)(2,1)S(1)}, bf16[232,256]{1,0:T(8,128)(2,1)S(1)}, u32[]{:S(2)}, u32[]{:S(2)}) collective-permute-start(bf16[232,256]{1,0:T(8,128)(2,1)S(1)} %copy-done.16), channel_id=1, source_target_pairs={{0,4},{1,5},{2,6},{3,7},{4,0},{5,1},{6,2},{7,3},{8,12},{9,13},{10,... | collective-permute-start | bytes 356360 | tf_op jit(solution)/shard_map/ppermute | solution.py:173
  324.8 24.3 %collective-permute-start.63 = (bf16[520,896]{1,0:T(8,128)(2,1)}, bf16[520,896]{1,0:T(8,128)(2,1)S(1)}, u32[]{:S(2)}, u32[]{:S(2)}) collective-permute-start(bf16[520,896]{1,0:T(8,128)(2,1)} %get-tuple-element.176.refs_0_), channel_id=1, source_target_pairs={{0,1},{1,0},{2,3},{3,2},{4,5},{5,4},{6,7},{7,6},{8,9},{9,8},{10,11... | collective-permute-start | bytes 2795528 | tf_op jit(solution)/shard_map/ppermute | solution.py:50
  324.8 24.4 %collective-permute-start.64 = (bf16[520,896]{1,0:T(8,128)(2,1)}, bf16[520,896]{1,0:T(8,128)(2,1)S(1)}, u32[]{:S(2)}, u32[]{:S(2)}) collective-permute-start(bf16[520,896]{1,0:T(8,128)(2,1)} %get-tuple-element.177.refs_2_), channel_id=1, source_target_pairs={{0,1},{1,0},{2,3},{3,2},{4,5},{5,4},{6,7},{7,6},{8,9},{9,8},{10,11... | collective-permute-start | bytes 2795528 | tf_op jit(solution)/shard_map/ppermute | solution.py:50
  327.1 29.1 %collective-permute-start.61 = (bf16[264,896]{1,0:T(8,128)(2,1)}, bf16[264,896]{1,0:T(8,128)(2,1)S(1)}, u32[]{:S(2)}, u32[]{:S(2)}) collective-permute-start(bf16[264,896]{1,0:T(8,128)(2,1)} %slice.103), channel_id=1, source_target_pairs={{0,4},{1,5},{4,8},{5,9},{8,12},{9,13},{12,14},{13,15},{14,10},{15,... | collective-permute-start | bytes 1419272 | tf_op jit(solution)/shard_map/ppermute | solution.py:62
  329.2 27.1 %collective-permute-start.62 = (bf16[256,896]{1,0:T(8,128)(2,1)}, bf16[256,896]{1,0:T(8,128)(2,1)}, u32[]{:S(2)}, u32[]{:S(2)}) collective-permute-start(bf16[256,896]{1,0:T(8,128)(2,1)} %slice.104), channel_id=1, source_target_pairs={{0,2},{1,3},{4,0},{5,1},{8,4},{9,5},{12,8},{13,9},{14,12},{15,13},... | collective-permute-start | bytes 1376264 | tf_op jit(solution)/shard_map/ppermute | solution.py:62
  (107 other events, 850.0 us)

commit v13 on v12

--- a/solution.py
+++ b/solution.py
@@ -167,13 +167,11 @@
 
         x = add(x, self.swap(x))
         x = lax.dynamic_slice(x, (self.core * half, 0), (half, x.shape[1]))
-        marks = [x]
         bit = 1
         while bit < self.chips:
             x = add(x, lax.ppermute(x, "ctx", [(i, i ^ (2 * bit)) for i in range(self.ctx)]))
-            marks.append(x)
             bit *= 2
-        return x, marks
+        return x
 
     def ring_sum(self, terms, between):
         half = self.chips // 2
@@ -1230,7 +1228,7 @@
             smem=1,
             scratch=[pltpu.VMEM((D, chip_rows), bf16)],
         )[0]
-        grad_pair, steps = net.exchange_sum(part_pair)
+        grad_pair = net.exchange_sum(part_pair)
         pair_halves = (grad_pair, net.swap(grad_pair))
         sums = jnp.where(core == 1, *pair_halves)[-SUM_ROWS:]
         small = sums.reshape(-1)[: 2 * D + qkv_cols].astype(f32)
@@ -1239,7 +1237,7 @@
             block,
             lambda slots, pairs, old, rest=None: place_all(spots, slots, pairs, old, sizes, rest),
             pair_halves,
-            [[part_pair], [steps[1]], [steps[2]]],
+            [[part_pair], [], []],
         )
     else:
         gathered = jnp.concatenate(near, 0).reshape(2 * net.dp, 3, rows, D)

time: 369 us -> 350 us (0.949)
  waiting for transfers between devices: 149 us -> 130 us
    ppermute x3, waiting for transfers between devices: 59.5 us -> 15 us  [exchange_sum(): lax.ppermute(x, 'ctx', [(i, i ^ 2 * bit) for i in range(self.ctx)])]
    ppermute x39, waiting for transfers between devices: 67.3 us -> 91.7 us  [hop(): return lax.ppermute(x, 'ctx', perm)]
    unnamed x140 -> x136, local copies, waits for them, and re-layouts: 19.8 us -> 19.4 us
  transfers between devices with their start and end apart: 68 -> 68, of which waited for: 27 -> 30; matrix products, arithmetic and copies ran while one was open for 11% -> 11% of each run, Pallas kernels for 20% -> 21%
where the time goes in v13:
time: 350 us; the launch traced here: 349 us
  waiting for transfers between devices  130 us (37%)
  Pallas kernels  100 us (29%)
  starting transfers between devices  57.3 us (16%)
  local copies, waits for them, and re-layouts  39.3 us (11%)
  other arithmetic  20.1 us (6%)
    ppermute x39, waiting for transfers between devices, hop(): return lax.ppermute(x, 'ctx', perm)  91.7 us
    pallas_call x10, Pallas kernels, call(): pl.pallas_call(body, out_shape=list(outs), in_specs=specs, out_specs=[pl....  48 us
    ppermute x39, starting transfers between devices, hop(): return lax.ppermute(x, 'ctx', perm)  37.8 us
    pallas_call x5, Pallas kernels, place_all(): pl.pallas_call(kernel, out_shape=[jax.ShapeDtypeStruct((D, ff_loc), f32),...  26.1 us
    unnamed x136, local copies, waits for them, and re-layouts  19.4 us
    ppermute x8, waiting for transfers between devices, shift(): return lax.ppermute(x, 'dp', [(i, (i + step) % n) for i in range(n)])  16.9 us
    pallas_call x1, Pallas kernels, feed_forward(): pl.pallas_call(lambda *refs: mlp_kernel(half, *refs), out_shape=[jax.Shap...  16.2 us
    ppermute x3, waiting for transfers between devices, exchange_sum(): lax.ppermute(x, 'ctx', [(i, i ^ 2 * bit) for i in range(self.ctx)])  15 us
  transfers between devices with their start and end apart: 68, of which 30 were waited for; matrix products, arithmetic and copies ran while one was open for 11% of the time, Pallas kernels for 21%

profile of v13, /device:TPU:0, one launch (start us, length us, event | category | flops | bytes accessed | tf_op | source)
XLA Modules:
  0.0 349.0 jit_solution(3515716358466864886)
XLA Ops:
  11.8 4.7 %collective-permute-done = bf16[224,1152]{1,0:T(8,128)(2,1)S(1)} collective-permute-done((bf16[224,1152]{1,0:T(8,128)(2,1)S(1)}, bf16[224,1152]{1,0:T(8,128)(2,1)S(1)}, u32[]{:S(2)}, u32[]{:S(2)}) %collective-permute-start) | collective-permute-done | bytes 516128 | tf_op jit(solution)/shard_map/ppermute | solution.py:54
  20.4 3.2 shard_map.195
  49.6 10.4 %shard_map.196 = (bf16[128,896]{1,0:T(8,128)(2,1)}, f32[2,896,128]{2,1,0:T(8,128)}, f32[2,2,8,448]{3,2,1,0:T(8,128)}, bf16[2,896,128]{2,1,0:T(8,128)(2,1)}, bf16...) custom-call(s32[17]{0:T(128)} %pad_add_fusion.refs_0_, ...), custom_call_target="tpu_custom_call" | custom-call | flops 1879048192 | bytes 6516292 | tf_op jit(solution)/shard_map/pallas_call | solution.py:236
  62.6 5.1 %collective-permute-done.13 = bf16[128,896]{1,0:T(8,128)(2,1)S(1)} collective-permute-done((bf16[128,896]{1,0:T(8,128)(2,1)}, bf16[128,896]{1,0:T(8,128)(2,1)S(1)}, u32[]{:S(2)}, u32[]{:S(2)}) %collective-permute-start.13) | collective-permute-done | bytes 229408 | tf_op jit(solution)/shard_map/ppermute | solution.py:54
  70.7 16.2 %shard_map.197 = (bf16[896,512]{1,0:T(8,128)(2,1)}, bf16[1280,512]{1,0:T(8,128)(2,1)}, bf16[512,1280]{1,0:T(8,128)(2,1)}, bf16[512,1280]{1,0:T(8,128)(2,1)}, f32...) custom-call(s32[20]{0:T(128)} %concatenate.63.refs_0_.meta_ref, bf16[256,896]{1,0:T(8,128)(2,1)} %copy-done.15, ...), custom_call_target="tpu_custom_call" | custom-call | flops 7046430720 | bytes 6881280 | tf_op jit(solution)/shard_map/pallas_call | solution.py:660
  94.1 10.1 %shard_map.198 = (bf16[456,896]{1,0:T(8,128)(2,1)}, bf16[456,896]{1,0:T(8,128)(2,1)}, bf16[456,896]{1,0:T(8,128)(2,1)}, bf16[456,896]{1,0:T(8,128)(2,1)}, bf16[4...) custom-call(s32[20]{0:T(128)} %concatenate.63.refs_0_.meta_ref, ...), custom_call_target="tpu_custom_call" | custom-call | flops 3523215360 | bytes 13074432 | tf_op jit(solution)/shard_map/pallas_call | solution.py:746
  107.1 14.8 %shard_map.199 = (f32[128,896]{1,0:T(8,128)}, bf16[128,896]{1,0:T(8,128)(2,1)}, f32[1,896]{1,0:T(1,128)}, bf16[128,896]{1,0:T(8,128)(2,1)}, f32[1024,256]{1,0:T(8,128)}, /*index=5*/bf16[1024,256]{1,0:T(8,128)(2,1)}) custom-call(s32[17]{0:T(128)} %pad_add_fusion.refs_0_, f32[128,896]{1,0:T(8,128)} %slice_add_fusion.refs_1_, ...), custom_call_target="tpu_custom_call" | custom-call | flops 4697620480 | bytes 8680516 | tf_op jit(solution)/shard_map/pallas_call | solution.py:236
  143.6 13.1 %collective-permute-done.27.refs_1_ = bf16[64,256]{1,0:T(8,128)(2,1)S(1)} collective-permute-done((bf16[64,256]{1,0:T(8,128)(2,1)S(1)}, bf16[64,256]{1,0:T(8,128)(2,1)S(1)}, u32[]{:S(2)}, u32[]{:S(2)}) %collective-permute-start.27) | collective-permute-done | bytes 32800 | tf_op jit(solution)/shard_map/ppermute | solution.py:62
  165.5 4.2 %shard_map.205 = (bf16[64,896]{1,0:T(8,128)(2,1)}, bf16[64,896]{1,0:T(8,128)(2,1)}, bf16[64,896]{1,0:T(8,128)(2,1)}, bf16[64,896]{1,0:T(8,128)(2,1)}, bf16[64,89...) custom-call(s32[20]{0:T(128)} %concatenate.63.refs_0_.meta_ref, ...), custom_call_target="tpu_custom_call" | custom-call | flops 1879048192 | bytes 5505104 | tf_op jit(solution)/shard_map/pallas_call | solution.py:236
  176.0 7.4 %collective-permute-done.38 = bf16[32,896]{1,0:T(8,128)(2,1)S(1)} collective-permute-done((bf16[32,896]{1,0:T(8,128)(2,1)S(1)}, bf16[32,896]{1,0:T(8,128)(2,1)S(1)}, u32[]{:S(2)}, u32[]{:S(2)}) %collective-permute-start.38) | collective-permute-done | bytes 57376 | tf_op jit(solution)/shard_map/ppermute | solution.py:62
  184.7 7.6 %collective-permute-done.42 = bf16[32,896]{1,0:T(8,128)(2,1)S(1)} collective-permute-done((bf16[32,896]{1,0:T(8,128)(2,1)S(1)}, bf16[32,896]{1,0:T(8,128)(2,1)S(1)}, u32[]{:S(2)}, u32[]{:S(2)}) %collective-permute-start.42) | collective-permute-done | bytes 57376 | tf_op jit(solution)/shard_map/ppermute | solution.py:62
  199.4 16.0 %collective-permute-done.40 = bf16[64,896]{1,0:T(8,128)(2,1)S(1)} collective-permute-done((bf16[64,896]{1,0:T(8,128)(2,1)S(1)}, bf16[64,896]{1,0:T(8,128)(2,1)S(1)}, u32[]{:S(2)}, u32[]{:S(2)}) %collective-permute-start.40) | collective-permute-done | bytes 114720 | tf_op jit(solution)/shard_map/ppermute | solution.py:62
  215.6 4.7 %collective-permute-done.44 = bf16[64,896]{1,0:T(8,128)(2,1)S(1)} collective-permute-done((bf16[64,896]{1,0:T(8,128)(2,1)S(1)}, bf16[64,896]{1,0:T(8,128)(2,1)S(1)}, u32[]{:S(2)}, u32[]{:S(2)}) %collective-permute-start.44) | collective-permute-done | bytes 114720 | tf_op jit(solution)/shard_map/ppermute | solution.py:62
  232.0 3.6 %shard_map.201 = (bf16[160,256]{1,0:T(8,128)(2,1)}, f32[128,896]{1,0:T(8,128)}, f32[1,896]{1,0:T(1,128)}, f32[1,1152]{1,0:T(1,128)}) custom-call(bf16[128,896]{1,0:T(8,128)(2,1)} %get-tuple-element.123.refs_0_, bf16[128,896]{1,0:T(8,128)(2,1)} %bitcast.17, f32[1,896]{1,0:T(1,128)} %broadcast_in_dim.22.refs_1_.refs_2_, ...), custom_call_target="tpu_custom_call" | custom-call | bytes 3931136 | tf_op jit(solution)/shard_map/pallas_call | solution.py:236
  237.0 3.2 collective-permute-done.47.refs_3_
  244.1 4.1 %shard_map.207 = (f32[896,2432]{1,0:T(8,128)}, f32[896,2432]{1,0:T(8,128)}, f32[2432,896]{1,0:T(8,128)}, f32[448,1152]{1,0:T(8,128)}, f32[448,896]{1,0:T(8,128)}, /*index=5*/f32[8,128]{1,0:T(8,128)}) custom-call(s32[20]{0:T(128)} %concatenate.63.refs_0_.meta_ref, bf16[520,896]{1,0:T(8,128)(2,1)} %shard_map.206.refs_0_, bf16[520,896]{1,0:T(8,128)(2,1)} %copy-done.16), custom_call_target="tpu_custom_call" | custom-call | bytes 7454720 | tf_op jit(solution)/shard_map/pallas_call | solution.py:902
  248.2 5.0 %collective-permute-done.48.refs_2_ = bf16[520,896]{1,0:T(8,128)(2,1)S(1)} collective-permute-done((bf16[520,896]{1,0:T(8,128)(2,1)}, bf16[520,896]{1,0:T(8,128)(2,1)S(1)}, u32[]{:S(2)}, u32[]{:S(2)}) %collective-permute-start.48) | collective-permute-done | bytes 931872 | tf_op jit(solution)/shard_map/ppermute | solution.py:62
  260.2 5.9 %shard_map.210 = (f32[896,2432]{1,0:T(8,128)}, f32[896,2432]{1,0:T(8,128)}, f32[2432,896]{1,0:T(8,128)}, f32[448,1152]{1,0:T(8,128)}, f32[448,896]{1,0:T(8,128)}, /*index=5*/f32[8,128]{1,0:T(8,128)}) custom-call(s32[20]{0:T(128)} %concatenate.63.refs_0_.meta_ref, ...), custom_call_target="tpu_custom_call", output_to_operand_aliasing={{0}: (5, {}), {1}: (6, {}), {2}: (7, {}), {3}: (8, {}), {4}... | custom-call | bytes 14909440 | tf_op jit(solution)/shard_map/pallas_call | solution.py:902
  266.1 12.3 %collective-permute-done.52.refs_1_ = bf16[520,896]{1,0:T(8,128)(2,1)S(1)} collective-permute-done((bf16[520,896]{1,0:T(8,128)(2,1)}, bf16[520,896]{1,0:T(8,128)(2,1)S(1)}, u32[]{:S(2)}, u32[]{:S(2)}) %collective-permute-start.52) | collective-permute-done | bytes 931872 | tf_op jit(solution)/shard_map/ppermute | solution.py:62
  286.3 5.9 %shard_map.212 = (f32[896,2432]{1,0:T(8,128)}, f32[896,2432]{1,0:T(8,128)}, f32[2432,896]{1,0:T(8,128)}, f32[448,1152]{1,0:T(8,128)}, f32[448,896]{1,0:T(8,128)}, /*index=5*/f32[8,128]{1,0:T(8,128)}) custom-call(s32[20]{0:T(128)} %concatenate.63.refs_0_.meta_ref, ...), custom_call_target="tpu_custom_call", output_to_operand_aliasing={{0}: (5, {}), {1}: (6, {}), {2}: (7, {}), {3}: (8, {}), {4}... | custom-call | bytes 14909440 | tf_op jit(solution)/shard_map/pallas_call | solution.py:902
  292.2 11.7 %collective-permute-done.56.refs_1_ = bf16[520,896]{1,0:T(8,128)(2,1)S(1)} collective-permute-done((bf16[520,896]{1,0:T(8,128)(2,1)}, bf16[520,896]{1,0:T(8,128)(2,1)S(1)}, u32[]{:S(2)}, u32[]{:S(2)}) %collective-permute-start.56) | collective-permute-done | bytes 931872 | tf_op jit(solution)/shard_map/ppermute | solution.py:62
  314.3 15.0 %collective-permute-done.66 = bf16[232,256]{1,0:T(8,128)(2,1)S(1)} collective-permute-done((bf16[232,256]{1,0:T(8,128)(2,1)S(1)}, bf16[232,256]{1,0:T(8,128)(2,1)S(1)}, u32[]{:S(2)}, u32[]{:S(2)}) %collective-permute-start.66) | collective-permute-done | bytes 118816 | tf_op jit(solution)/shard_map/ppermute | solution.py:172
  332.1 5.8 %shard_map.214 = (f32[896,2432]{1,0:T(8,128)}, f32[896,2432]{1,0:T(8,128)}, f32[2432,896]{1,0:T(8,128)}, f32[448,1152]{1,0:T(8,128)}, f32[448,896]{1,0:T(8,128)}, /*index=5*/f32[8,128]{1,0:T(8,128)}) custom-call(s32[20]{0:T(128)} %concatenate.63.refs_0_.meta_ref, ...), custom_call_target="tpu_custom_call", output_to_operand_aliasing={{0}: (5, {}), {1}: (6, {}), {2}: (7, {}), {3}: (8, {}), {4}... | custom-call | bytes 14909440 | tf_op jit(solution)/shard_map/pallas_call | solution.py:902
  344.6 4.3 %shard_map.216 = (f32[896,2432]{1,0:T(8,128)}, f32[896,2432]{1,0:T(8,128)}, f32[2432,896]{1,0:T(8,128)}, f32[448,1152]{1,0:T(8,128)}, f32[448,896]{1,0:T(8,128)}, /*index=5*/f32[8,128]{1,0:T(8,128)}) custom-call(s32[20]{0:T(128)} %concatenate.63.refs_0_.meta_ref, ...), custom_call_target="tpu_custom_call", output_to_operand_aliasing={{0}: (5, {}), {1}: (6, {}), {2}: (7, {}), {3}: (8, {}), {4}... | custom-call | bytes 7454720 | tf_op jit(solution)/shard_map/pallas_call | solution.py:902
  (343 shorter events, 153.1 us)
Async XLA Ops:
  28.5 18.0 %collective-permute-start.15 = (bf16[128,1792]{1,0:T(8,128)(2,1)S(1)}, bf16[128,1792]{1,0:T(8,128)(2,1)S(1)}, u32[]{:S(2)}, u32[]{:S(2)}) collective-permute-start(bf16[128,1792]{1,0:T(8,128)(2,1)S(1)} %constant_dynamic-update-slice_fusion.11), channel_id=1, source_target_pairs={{0,16},{16,0},{1,17},{17,1},{2,18},{18,2},{3,19},{19,3},{4,20},{20... | collective-permute-start | bytes 1376264 | tf_op jit(solution)/shard_map/ppermute | solution.py:54
  46.5 22.5 %collective-permute-start.16 = (bf16[256,1792]{1,0:T(8,128)(2,1)S(1)}, bf16[256,1792]{1,0:T(8,128)(2,1)S(1)}, u32[]{:S(2)}, u32[]{:S(2)}) collective-permute-start(bf16[256,1792]{1,0:T(8,128)(2,1)S(1)} %pad_maximum_fusion.3.refs_3_.refs_2_.refs_1_), channel_id=1, source_target_pairs={{0,1},{1,0},{2,3},{3,2},{4,5},{5,4},{6,7},{7,6},{8,9},{9,8},{10,11... | collective-permute-start | bytes 2752520 | tf_op jit(solution)/shard_map/ppermute | solution.py:50
  104.2 22.1 %collective-permute-start.21 = (bf16[456,896]{1,0:T(8,128)(2,1)}, bf16[456,896]{1,0:T(8,128)(2,1)S(1)}, u32[]{:S(2)}, u32[]{:S(2)}) collective-permute-start(bf16[456,896]{1,0:T(8,128)(2,1)} %get-tuple-element.128), channel_id=1, source_target_pairs={{0,4},{1,5},{4,8},{5,9},{8,12},{9,13},{12,14},{13,15},{14,10},{15,... | collective-permute-start | bytes 2451464 | tf_op jit(solution)/shard_map/ppermute | solution.py:62
  105.8 21.5 %collective-permute-start.22 = (bf16[456,896]{1,0:T(8,128)(2,1)}, bf16[456,896]{1,0:T(8,128)(2,1)S(1)}, u32[]{:S(2)}, u32[]{:S(2)}) collective-permute-start(bf16[456,896]{1,0:T(8,128)(2,1)} %get-tuple-element.130), channel_id=1, source_target_pairs={{0,2},{1,3},{4,0},{5,1},{8,4},{9,5},{12,8},{13,9},{14,12},{15,13},... | collective-permute-start | bytes 2451464 | tf_op jit(solution)/shard_map/ppermute | solution.py:62
  134.8 26.9 %collective-permute-start.31 = (bf16[456,896]{1,0:T(8,128)(2,1)S(1)}, bf16[456,896]{1,0:T(8,128)(2,1)S(1)}, u32[]{:S(2)}, u32[]{:S(2)}) collective-permute-start(bf16[456,896]{1,0:T(8,128)(2,1)S(1)} %copy-done.7), channel_id=1, source_target_pairs={{0,4},{1,5},{4,8},{5,9},{8,12},{9,13},{12,14},{13,15},{14,10},{15,... | collective-permute-start | bytes 2451464 | tf_op jit(solution)/shard_map/ppermute | solution.py:62
  136.3 26.4 %collective-permute-start.32 = (bf16[456,896]{1,0:T(8,128)(2,1)S(1)}, bf16[456,896]{1,0:T(8,128)(2,1)S(1)}, u32[]{:S(2)}, u32[]{:S(2)}) collective-permute-start(bf16[456,896]{1,0:T(8,128)(2,1)S(1)} %copy-done.8), channel_id=1, source_target_pairs={{0,2},{1,3},{4,0},{5,1},{8,4},{9,5},{12,8},{13,9},{14,12},{15,13},... | collective-permute-start | bytes 2451464 | tf_op jit(solution)/shard_map/ppermute | solution.py:62
  137.6 19.2 %collective-permute-start.27 = (bf16[64,256]{1,0:T(8,128)(2,1)S(1)}, bf16[64,256]{1,0:T(8,128)(2,1)S(1)}, u32[]{:S(2)}, u32[]{:S(2)}) collective-permute-start(bf16[64,256]{1,0:T(8,128)(2,1)S(1)} %get-tuple-element.206), channel_id=1, source_target_pairs={{0,2},{1,3},{4,0},{5,1},{8,4},{9,5},{12,8},{13,9},{14,12},{15,13},... | collective-permute-start | bytes 98312 | tf_op jit(solution)/shard_map/ppermute | solution.py:62
  142.0 23.5 %collective-permute-start.37 = (bf16[768,896]{1,0:T(8,128)(2,1)}, bf16[768,896]{1,0:T(8,128)(2,1)}, u32[]{:S(2)}, u32[]{:S(2)}) collective-permute-start(bf16[768,896]{1,0:T(8,128)(2,1)} %constant_dynamic-update-slice_fusion.13.refs_3_), channel_id=1, source_target_pairs={{0,1},{1,0},{2,3},{3,2},{4,5},{5,4},{6,7},{7,6},{8,9},{9,8},{10,11... | collective-permute-start | bytes 4128776 | tf_op jit(solution)/shard_map/ppermute | solution.py:50
  161.1 59.6 %collective-permute-start.29 = (bf16[128,256]{1,0:T(8,128)(2,1)S(1)}, bf16[128,256]{1,0:T(8,128)(2,1)S(1)}, u32[]{:S(2)}, u32[]{:S(2)}) collective-permute-start(bf16[128,256]{1,0:T(8,128)(2,1)S(1)} %add_convert_fusion.14), channel_id=1, source_target_pairs={{0,2},{1,3},{4,0},{5,1},{8,4},{9,5},{12,8},{13,9},{14,12},{15,13},... | collective-permute-start | bytes 196616 | tf_op jit(solution)/shard_map/ppermute | solution.py:62
  163.9 29.8 %collective-permute-start.33 = (bf16[456,896]{1,0:T(8,128)(2,1)}, bf16[456,896]{1,0:T(8,128)(2,1)S(1)}, u32[]{:S(2)}, u32[]{:S(2)}) collective-permute-start(bf16[456,896]{1,0:T(8,128)(2,1)} %get-tuple-element.143), channel_id=1, source_target_pairs={{0,4},{1,5},{4,8},{5,9},{8,12},{9,13},{12,14},{13,15},{14,10},{15,... | collective-permute-start | bytes 2451464 | tf_op jit(solution)/shard_map/ppermute | solution.py:62
  172.3 54.6 %collective-permute-start.26 = (bf16[128,256]{1,0:T(8,128)(2,1)S(1)}, bf16[128,256]{1,0:T(8,128)(2,1)S(1)}, u32[]{:S(2)}, u32[]{:S(2)}) collective-permute-start(bf16[128,256]{1,0:T(8,128)(2,1)S(1)} %add_convert_fusion.15), channel_id=1, source_target_pairs={{0,4},{1,5},{4,8},{5,9},{8,12},{9,13},{12,14},{13,15},{14,10},{15,... | collective-permute-start | bytes 196616 | tf_op jit(solution)/shard_map/ppermute | solution.py:62
  173.8 48.6 %collective-permute-start.35 = (bf16[456,896]{1,0:T(8,128)(2,1)S(1)}, bf16[456,896]{1,0:T(8,128)(2,1)S(1)}, u32[]{:S(2)}, u32[]{:S(2)}) collective-permute-start(bf16[456,896]{1,0:T(8,128)(2,1)S(1)} %copy-done.9), channel_id=1, source_target_pairs={{0,2},{1,3},{4,0},{5,1},{8,4},{9,5},{12,8},{13,9},{14,12},{15,13},... | collective-permute-start | bytes 2451464 | tf_op jit(solution)/shard_map/ppermute | solution.py:62
  198.4 24.2 %collective-permute-start.34 = (bf16[456,896]{1,0:T(8,128)(2,1)}, bf16[456,896]{1,0:T(8,128)(2,1)S(1)}, u32[]{:S(2)}, u32[]{:S(2)}) collective-permute-start(bf16[456,896]{1,0:T(8,128)(2,1)} %shard_map.203), channel_id=1, source_target_pairs={{0,4},{1,5},{4,8},{5,9},{8,12},{9,13},{12,14},{13,15},{14,10},{15,... | collective-permute-start | bytes 2451464 | tf_op jit(solution)/shard_map/ppermute | solution.py:62
  229.9 23.3 %collective-permute-start.48 = (bf16[520,896]{1,0:T(8,128)(2,1)}, bf16[520,896]{1,0:T(8,128)(2,1)S(1)}, u32[]{:S(2)}, u32[]{:S(2)}) collective-permute-start(bf16[520,896]{1,0:T(8,128)(2,1)} %shard_map.206.refs_0_), channel_id=1, source_target_pairs={{0,4},{1,5},{4,8},{5,9},{8,12},{9,13},{12,14},{13,15},{14,10},{15,... | collective-permute-start | bytes 2795528 | tf_op jit(solution)/shard_map/ppermute | solution.py:62
  231.1 23.0 %collective-permute-start.49 = (bf16[520,896]{1,0:T(8,128)(2,1)}, bf16[520,896]{1,0:T(8,128)(2,1)S(1)}, u32[]{:S(2)}, u32[]{:S(2)}) collective-permute-start(bf16[520,896]{1,0:T(8,128)(2,1)} %shard_map.206.refs_0_), channel_id=1, source_target_pairs={{0,2},{1,3},{4,0},{5,1},{8,4},{9,5},{12,8},{13,9},{14,12},{15,13},... | collective-permute-start | bytes 2795528 | tf_op jit(solution)/shard_map/ppermute | solution.py:62
  255.6 22.8 %collective-permute-start.52 = (bf16[520,896]{1,0:T(8,128)(2,1)}, bf16[520,896]{1,0:T(8,128)(2,1)S(1)}, u32[]{:S(2)}, u32[]{:S(2)}) collective-permute-start(bf16[520,896]{1,0:T(8,128)(2,1)} %get-tuple-element.160.refs_0_), channel_id=1, source_target_pairs={{0,4},{1,5},{4,8},{5,9},{8,12},{9,13},{12,14},{13,15},{14,10},{15,... | collective-permute-start | bytes 2795528 | tf_op jit(solution)/shard_map/ppermute | solution.py:62
  256.2 22.5 %collective-permute-start.53 = (bf16[520,896]{1,0:T(8,128)(2,1)}, bf16[520,896]{1,0:T(8,128)(2,1)S(1)}, u32[]{:S(2)}, u32[]{:S(2)}) collective-permute-start(bf16[520,896]{1,0:T(8,128)(2,1)} %get-tuple-element.161.refs_2_), channel_id=1, source_target_pairs={{0,2},{1,3},{4,0},{5,1},{8,4},{9,5},{12,8},{13,9},{14,12},{15,13},... | collective-permute-start | bytes 2795528 | tf_op jit(solution)/shard_map/ppermute | solution.py:62
  280.2 23.7 %collective-permute-start.56 = (bf16[520,896]{1,0:T(8,128)(2,1)}, bf16[520,896]{1,0:T(8,128)(2,1)S(1)}, u32[]{:S(2)}, u32[]{:S(2)}) collective-permute-start(bf16[520,896]{1,0:T(8,128)(2,1)} %get-tuple-element.168.refs_0_), channel_id=1, source_target_pairs={{0,4},{1,5},{4,8},{5,9},{8,12},{9,13},{12,14},{13,15},{14,10},{15,... | collective-permute-start | bytes 2795528 | tf_op jit(solution)/shard_map/ppermute | solution.py:62
  280.8 23.1 %collective-permute-start.57 = (bf16[520,896]{1,0:T(8,128)(2,1)}, bf16[520,896]{1,0:T(8,128)(2,1)S(1)}, u32[]{:S(2)}, u32[]{:S(2)}) collective-permute-start(bf16[520,896]{1,0:T(8,128)(2,1)} %get-tuple-element.169.refs_2_), channel_id=1, source_target_pairs={{0,2},{1,3},{4,0},{5,1},{8,4},{9,5},{12,8},{13,9},{14,12},{15,13},... | collective-permute-start | bytes 2795528 | tf_op jit(solution)/shard_map/ppermute | solution.py:62
  283.9 21.8 %collective-permute-start.64 = (bf16[232,256]{1,0:T(8,128)(2,1)S(1)}, bf16[232,256]{1,0:T(8,128)(2,1)S(1)}, u32[]{:S(2)}, u32[]{:S(2)}) collective-permute-start(bf16[232,256]{1,0:T(8,128)(2,1)S(1)} %add_convert_fusion.8), channel_id=1, source_target_pairs={{0,2},{1,3},{2,0},{3,1},{4,6},{5,7},{6,4},{7,5},{8,10},{9,11},{10,... | collective-permute-start | bytes 356360 | tf_op jit(solution)/shard_map/ppermute | solution.py:172
  305.2 25.6 %collective-permute-start.60 = (bf16[520,896]{1,0:T(8,128)(2,1)}, bf16[520,896]{1,0:T(8,128)(2,1)S(1)}, u32[]{:S(2)}, u32[]{:S(2)}) collective-permute-start(bf16[520,896]{1,0:T(8,128)(2,1)} %get-tuple-element.176.refs_0_), channel_id=1, source_target_pairs={{0,1},{1,0},{2,3},{3,2},{4,5},{5,4},{6,7},{7,6},{8,9},{9,8},{10,11... | collective-permute-start | bytes 2795528 | tf_op jit(solution)/shard_map/ppermute | solution.py:50
  305.2 25.7 %collective-permute-start.61 = (bf16[520,896]{1,0:T(8,128)(2,1)}, bf16[520,896]{1,0:T(8,128)(2,1)S(1)}, u32[]{:S(2)}, u32[]{:S(2)}) collective-permute-start(bf16[520,896]{1,0:T(8,128)(2,1)} %get-tuple-element.177.refs_2_), channel_id=1, source_target_pairs={{0,1},{1,0},{2,3},{3,2},{4,5},{5,4},{6,7},{7,6},{8,9},{9,8},{10,11... | collective-permute-start | bytes 2795528 | tf_op jit(solution)/shard_map/ppermute | solution.py:50
  309.5 28.5 %collective-permute-start.58 = (bf16[264,896]{1,0:T(8,128)(2,1)}, bf16[264,896]{1,0:T(8,128)(2,1)S(1)}, u32[]{:S(2)}, u32[]{:S(2)}) collective-permute-start(bf16[264,896]{1,0:T(8,128)(2,1)} %slice.103), channel_id=1, source_target_pairs={{0,4},{1,5},{4,8},{5,9},{8,12},{9,13},{12,14},{13,15},{14,10},{15,... | collective-permute-start | bytes 1419272 | tf_op jit(solution)/shard_map/ppermute | solution.py:62
  311.5 26.5 %collective-permute-start.59 = (bf16[256,896]{1,0:T(8,128)(2,1)}, bf16[256,896]{1,0:T(8,128)(2,1)}, u32[]{:S(2)}, u32[]{:S(2)}) collective-permute-start(bf16[256,896]{1,0:T(8,128)(2,1)} %slice.104), channel_id=1, source_target_pairs={{0,2},{1,3},{4,0},{5,1},{8,4},{9,5},{12,8},{13,9},{14,12},{15,13},... | collective-permute-start | bytes 1376264 | tf_op jit(solution)/shard_map/ppermute | solution.py:62
  (105 other events, 765.9 us)

commit v14 on v13

--- a/solution.py
+++ b/solution.py
@@ -30,6 +30,10 @@
 def half_cut(rows):
     cut = (rows // 2 + 7) // 8 * 8
     return cut if cut < rows else rows // 2
+
+
+def add_low(a, b):
+    return (a.astype(f32) + b.astype(f32)).astype(bf16)
 
 
 class Net:
@@ -159,19 +163,18 @@
             marks.append((fwd, back))
         return [local[0], fwd, back], marks
 
-    def exchange_sum(self, x):
+    def exchange_start(self, x):
         half = x.shape[0] // 2
-
-        def add(a, b):
-            return (a.astype(f32) + b.astype(f32)).astype(bf16)
-
-        x = add(x, self.swap(x))
+        x = add_low(x, self.swap(x))
         x = lax.dynamic_slice(x, (self.core * half, 0), (half, x.shape[1]))
         bit = 1
-        while bit < self.chips:
-            x = add(x, lax.ppermute(x, "ctx", [(i, i ^ (2 * bit)) for i in range(self.ctx)]))
+        while 2 * bit < self.chips:
+            x = self.exchange(x, bit)
             bit *= 2
         return x
+
+    def exchange(self, x, bit):
+        return add_low(x, lax.ppermute(x, "ctx", [(i, i ^ (2 * bit)) for i in range(self.ctx)]))
 
     def ring_sum(self, terms, between):
         half = self.chips // 2
@@ -211,7 +214,10 @@
                 fwd, back = self.hop(fwd[:cut], 1), self.hop(back[cut:], -1)
         placed, token = place(*waiting, placed)
         far = join(fwd, back, token)
-        return place([half], [(far, self.swap(far))], placed, rest)[0]
+        rest = gate([token], [rest])[0]
+        rest = self.exchange(rest, half)
+        halves = (rest, self.swap(rest))
+        return place([half], [(far, self.swap(far))], placed, halves)[0], halves
 
 
 VMEM_BYTES = 56 * 1024 * 1024
@@ -1228,17 +1234,16 @@
             smem=1,
             scratch=[pltpu.VMEM((D, chip_rows), bf16)],
         )[0]
-        grad_pair = net.exchange_sum(part_pair)
-        pair_halves = (grad_pair, net.swap(grad_pair))
+        sizes = (main, ff_loc, q_rows, qkv_cols, down_rows, chips)
+        placed, pair_halves = net.gather_placed(
+            block,
+            lambda slots, pairs, old, rest=None: place_all(spots, slots, pairs, old, sizes, rest),
+            net.exchange_start(part_pair),
+            [[part_pair], [], []],
+        )
+        grad_gate, grad_up, grad_down, grad_joint, grad_out_proj = placed
         sums = jnp.where(core == 1, *pair_halves)[-SUM_ROWS:]
         small = sums.reshape(-1)[: 2 * D + qkv_cols].astype(f32)
-        sizes = (main, ff_loc, q_rows, qkv_cols, down_rows, chips)
-        grad_gate, grad_up, grad_down, grad_joint, grad_out_proj = net.gather_placed(
-            block,
-            lambda slots, pairs, old, rest=None: place_all(spots, slots, pairs, old, sizes, rest),
-            pair_halves,
-            [[part_pair], [], []],
-        )
     else:
         gathered = jnp.concatenate(near, 0).reshape(2 * net.dp, 3, rows, D)
         grad_attn_group = gathered[:, 0].reshape(2 * net.dp * rows, D)

time: 350 us -> 348 us (level)
    ppermute x3, waiting for transfers between devices: 15 us -> 10.7 us  [exchange(): lax.ppermute(x, 'ctx', [(i, i ^ 2 * bit) for i in range(self.ctx)])]
    unnamed x136 -> x140, local copies, waits for them, and re-layouts: 19.4 us -> 19.3 us
  transfers between devices with their start and end apart: 68 -> 68, of which waited for: 30 -> 34; matrix products, arithmetic and copies ran while one was open for 11% -> 11% of each run, Pallas kernels for 21% -> 21%
where the time goes in v14:
time: 348 us; the launch traced here: 347 us
  waiting for transfers between devices  127 us (36%)
  Pallas kernels  100 us (29%)
  starting transfers between devices  58 us (17%)
  local copies, waits for them, and re-layouts  39.4 us (11%)
  other arithmetic  21 us (6%)
    ppermute x39, waiting for transfers between devices, hop(): return lax.ppermute(x, 'ctx', perm)  92.7 us
    pallas_call x10, Pallas kernels, call(): pl.pallas_call(body, out_shape=list(outs), in_specs=specs, out_specs=[pl....  47.9 us
    ppermute x39, starting transfers between devices, hop(): return lax.ppermute(x, 'ctx', perm)  38.9 us
    pallas_call x5, Pallas kernels, place_all(): pl.pallas_call(kernel, out_shape=[jax.ShapeDtypeStruct((D, ff_loc), f32),...  26.1 us
    unnamed x140, local copies, waits for them, and re-layouts  19.3 us
    ppermute x8, waiting for transfers between devices, shift(): return lax.ppermute(x, 'dp', [(i, (i + step) % n) for i in range(n)])  16.7 us
    pallas_call x1, Pallas kernels, feed_forward(): pl.pallas_call(lambda *refs: mlp_kernel(half, *refs), out_shape=[jax.Shap...  16.2 us
    ppermute x8, starting transfers between devices, shift(): return lax.ppermute(x, 'dp', [(i, (i + step) % n) for i in range(n)])  12.2 us
  transfers between devices with their start and end apart: 68, of which 34 were waited for; matrix products, arithmetic and copies ran while one was open for 11% of the time, Pallas kernels for 21%

profile of v14, /device:TPU:0, one launch (start us, length us, event | category | flops | bytes accessed | tf_op | source)
XLA Modules:
  0.0 346.9 jit_solution(12685516283247941655)
XLA Ops:
  12.0 4.5 %collective-permute-done = bf16[224,1152]{1,0:T(8,128)(2,1)S(1)} collective-permute-done((bf16[224,1152]{1,0:T(8,128)(2,1)S(1)}, bf16[224,1152]{1,0:T(8,128)(2,1)S(1)}, u32[]{:S(2)}, u32[]{:S(2)}) %collective-permute-start) | collective-permute-done | bytes 516128 | tf_op jit(solution)/shard_map/ppermute | solution.py:58
  20.4 3.2 shard_map.195
  49.5 10.3 %shard_map.196 = (bf16[128,896]{1,0:T(8,128)(2,1)}, f32[2,896,128]{2,1,0:T(8,128)}, f32[2,2,8,448]{3,2,1,0:T(8,128)}, bf16[2,896,128]{2,1,0:T(8,128)(2,1)}, bf16...) custom-call(s32[17]{0:T(128)} %pad_add_fusion.refs_0_, ...), custom_call_target="tpu_custom_call" | custom-call | flops 1879048192 | bytes 6516292 | tf_op jit(solution)/shard_map/pallas_call | solution.py:242
  62.6 5.1 %collective-permute-done.13 = bf16[128,896]{1,0:T(8,128)(2,1)S(1)} collective-permute-done((bf16[128,896]{1,0:T(8,128)(2,1)}, bf16[128,896]{1,0:T(8,128)(2,1)S(1)}, u32[]{:S(2)}, u32[]{:S(2)}) %collective-permute-start.13) | collective-permute-done | bytes 229408 | tf_op jit(solution)/shard_map/ppermute | solution.py:58
  70.9 16.2 %shard_map.197 = (bf16[896,512]{1,0:T(8,128)(2,1)}, bf16[1280,512]{1,0:T(8,128)(2,1)}, bf16[512,1280]{1,0:T(8,128)(2,1)}, bf16[512,1280]{1,0:T(8,128)(2,1)}, f32...) custom-call(s32[20]{0:T(128)} %concatenate.63.refs_0_.meta_ref, bf16[256,896]{1,0:T(8,128)(2,1)} %copy-done.16, ...), custom_call_target="tpu_custom_call" | custom-call | flops 7046430720 | bytes 6881280 | tf_op jit(solution)/shard_map/pallas_call | solution.py:666
  94.4 10.1 %shard_map.198 = (bf16[456,896]{1,0:T(8,128)(2,1)}, bf16[456,896]{1,0:T(8,128)(2,1)}, bf16[456,896]{1,0:T(8,128)(2,1)}, bf16[456,896]{1,0:T(8,128)(2,1)}, bf16[4...) custom-call(s32[20]{0:T(128)} %concatenate.63.refs_0_.meta_ref, ...), custom_call_target="tpu_custom_call" | custom-call | flops 3523215360 | bytes 13074432 | tf_op jit(solution)/shard_map/pallas_call | solution.py:752
  107.3 14.9 %shard_map.199 = (f32[128,896]{1,0:T(8,128)}, bf16[128,896]{1,0:T(8,128)(2,1)}, f32[1,896]{1,0:T(1,128)}, bf16[128,896]{1,0:T(8,128)(2,1)}, f32[1024,256]{1,0:T(8,128)}, /*index=5*/bf16[1024,256]{1,0:T(8,128)(2,1)}) custom-call(s32[17]{0:T(128)} %pad_add_fusion.refs_0_, f32[128,896]{1,0:T(8,128)} %slice_add_fusion.refs_1_, ...), custom_call_target="tpu_custom_call" | custom-call | flops 4697620480 | bytes 8680516 | tf_op jit(solution)/shard_map/pallas_call | solution.py:242
  143.9 13.1 %collective-permute-done.27.refs_1_ = bf16[64,256]{1,0:T(8,128)(2,1)S(1)} collective-permute-done((bf16[64,256]{1,0:T(8,128)(2,1)S(1)}, bf16[64,256]{1,0:T(8,128)(2,1)S(1)}, u32[]{:S(2)}, u32[]{:S(2)}) %collective-permute-start.27) | collective-permute-done | bytes 32800 | tf_op jit(solution)/shard_map/ppermute | solution.py:66
  165.7 4.2 %shard_map.205 = (bf16[64,896]{1,0:T(8,128)(2,1)}, bf16[64,896]{1,0:T(8,128)(2,1)}, bf16[64,896]{1,0:T(8,128)(2,1)}, bf16[64,896]{1,0:T(8,128)(2,1)}, bf16[64,89...) custom-call(s32[20]{0:T(128)} %concatenate.63.refs_0_.meta_ref, ...), custom_call_target="tpu_custom_call" | custom-call | flops 1879048192 | bytes 5505104 | tf_op jit(solution)/shard_map/pallas_call | solution.py:242
  176.2 7.4 %collective-permute-done.38 = bf16[32,896]{1,0:T(8,128)(2,1)S(1)} collective-permute-done((bf16[32,896]{1,0:T(8,128)(2,1)S(1)}, bf16[32,896]{1,0:T(8,128)(2,1)S(1)}, u32[]{:S(2)}, u32[]{:S(2)}) %collective-permute-start.38) | collective-permute-done | bytes 57376 | tf_op jit(solution)/shard_map/ppermute | solution.py:66
  184.9 7.6 %collective-permute-done.42 = bf16[32,896]{1,0:T(8,128)(2,1)S(1)} collective-permute-done((bf16[32,896]{1,0:T(8,128)(2,1)S(1)}, bf16[32,896]{1,0:T(8,128)(2,1)S(1)}, u32[]{:S(2)}, u32[]{:S(2)}) %collective-permute-start.42) | collective-permute-done | bytes 57376 | tf_op jit(solution)/shard_map/ppermute | solution.py:66
  199.7 16.0 %collective-permute-done.40 = bf16[64,896]{1,0:T(8,128)(2,1)S(1)} collective-permute-done((bf16[64,896]{1,0:T(8,128)(2,1)S(1)}, bf16[64,896]{1,0:T(8,128)(2,1)S(1)}, u32[]{:S(2)}, u32[]{:S(2)}) %collective-permute-start.40) | collective-permute-done | bytes 114720 | tf_op jit(solution)/shard_map/ppermute | solution.py:66
  215.8 4.7 %collective-permute-done.44 = bf16[64,896]{1,0:T(8,128)(2,1)S(1)} collective-permute-done((bf16[64,896]{1,0:T(8,128)(2,1)S(1)}, bf16[64,896]{1,0:T(8,128)(2,1)S(1)}, u32[]{:S(2)}, u32[]{:S(2)}) %collective-permute-start.44) | collective-permute-done | bytes 114720 | tf_op jit(solution)/shard_map/ppermute | solution.py:66
  232.2 3.6 %shard_map.201 = (bf16[160,256]{1,0:T(8,128)(2,1)}, f32[128,896]{1,0:T(8,128)}, f32[1,896]{1,0:T(1,128)}, f32[1,1152]{1,0:T(1,128)}) custom-call(bf16[128,896]{1,0:T(8,128)(2,1)} %get-tuple-element.123.refs_0_, bf16[128,896]{1,0:T(8,128)(2,1)} %bitcast.17, f32[1,896]{1,0:T(1,128)} %broadcast_in_dim.22.refs_1_.refs_2_, ...), custom_call_target="tpu_custom_call" | custom-call | bytes 3931136 | tf_op jit(solution)/shard_map/pallas_call | solution.py:242
  237.2 3.2 collective-permute-done.47.refs_3_
  244.3 4.1 %shard_map.207 = (f32[896,2432]{1,0:T(8,128)}, f32[896,2432]{1,0:T(8,128)}, f32[2432,896]{1,0:T(8,128)}, f32[448,1152]{1,0:T(8,128)}, f32[448,896]{1,0:T(8,128)}, /*index=5*/f32[8,128]{1,0:T(8,128)}) custom-call(s32[20]{0:T(128)} %concatenate.63.refs_0_.meta_ref, bf16[520,896]{1,0:T(8,128)(2,1)} %shard_map.206.refs_0_, bf16[520,896]{1,0:T(8,128)(2,1)} %copy-done.17), custom_call_target="tpu_custom_call" | custom-call | bytes 7454720 | tf_op jit(solution)/shard_map/pallas_call | solution.py:908
  248.4 5.0 %collective-permute-done.48.refs_2_ = bf16[520,896]{1,0:T(8,128)(2,1)S(1)} collective-permute-done((bf16[520,896]{1,0:T(8,128)(2,1)}, bf16[520,896]{1,0:T(8,128)(2,1)S(1)}, u32[]{:S(2)}, u32[]{:S(2)}) %collective-permute-start.48) | collective-permute-done | bytes 931872 | tf_op jit(solution)/shard_map/ppermute | solution.py:66
  260.3 5.9 %shard_map.210 = (f32[896,2432]{1,0:T(8,128)}, f32[896,2432]{1,0:T(8,128)}, f32[2432,896]{1,0:T(8,128)}, f32[448,1152]{1,0:T(8,128)}, f32[448,896]{1,0:T(8,128)}, /*index=5*/f32[8,128]{1,0:T(8,128)}) custom-call(s32[20]{0:T(128)} %concatenate.63.refs_0_.meta_ref, ...), custom_call_target="tpu_custom_call", output_to_operand_aliasing={{0}: (5, {}), {1}: (6, {}), {2}: (7, {}), {3}: (8, {}), {4}... | custom-call | bytes 14909440 | tf_op jit(solution)/shard_map/pallas_call | solution.py:908
  266.3 12.3 %collective-permute-done.52.refs_1_ = bf16[520,896]{1,0:T(8,128)(2,1)S(1)} collective-permute-done((bf16[520,896]{1,0:T(8,128)(2,1)}, bf16[520,896]{1,0:T(8,128)(2,1)S(1)}, u32[]{:S(2)}, u32[]{:S(2)}) %collective-permute-start.52) | collective-permute-done | bytes 931872 | tf_op jit(solution)/shard_map/ppermute | solution.py:66
  284.8 5.9 %shard_map.212 = (f32[896,2432]{1,0:T(8,128)}, f32[896,2432]{1,0:T(8,128)}, f32[2432,896]{1,0:T(8,128)}, f32[448,1152]{1,0:T(8,128)}, f32[448,896]{1,0:T(8,128)}, /*index=5*/f32[8,128]{1,0:T(8,128)}) custom-call(s32[20]{0:T(128)} %concatenate.63.refs_0_.meta_ref, ...), custom_call_target="tpu_custom_call", output_to_operand_aliasing={{0}: (5, {}), {1}: (6, {}), {2}: (7, {}), {3}: (8, {}), {4}... | custom-call | bytes 14909440 | tf_op jit(solution)/shard_map/pallas_call | solution.py:908
  290.8 12.4 %collective-permute-done.56.refs_1_ = bf16[520,896]{1,0:T(8,128)(2,1)S(1)} collective-permute-done((bf16[520,896]{1,0:T(8,128)(2,1)}, bf16[520,896]{1,0:T(8,128)(2,1)S(1)}, u32[]{:S(2)}, u32[]{:S(2)}) %collective-permute-start.56) | collective-permute-done | bytes 931872 | tf_op jit(solution)/shard_map/ppermute | solution.py:66
  314.9 7.5 %collective-permute-done.65 = bf16[232,256]{1,0:T(8,128)(2,1)S(1)} collective-permute-done((bf16[232,256]{1,0:T(8,128)(2,1)S(1)}, bf16[232,256]{1,0:T(8,128)(2,1)S(1)}, u32[]{:S(2)}, u32[]{:S(2)}) %collective-permute-start.65) | collective-permute-done | bytes 118816 | tf_op jit(solution)/shard_map/ppermute | solution.py:177
  324.4 5.9 %shard_map.214 = (f32[896,2432]{1,0:T(8,128)}, f32[896,2432]{1,0:T(8,128)}, f32[2432,896]{1,0:T(8,128)}, f32[448,1152]{1,0:T(8,128)}, f32[448,896]{1,0:T(8,128)}, /*index=5*/f32[8,128]{1,0:T(8,128)}) custom-call(s32[20]{0:T(128)} %concatenate.63.refs_0_.meta_ref, ...), custom_call_target="tpu_custom_call", output_to_operand_aliasing={{0}: (5, {}), {1}: (6, {}), {2}: (7, {}), {3}: (8, {}), {4}... | custom-call | bytes 14909440 | tf_op jit(solution)/shard_map/pallas_call | solution.py:908
  342.5 4.3 %shard_map.217 = (f32[896,2432]{1,0:T(8,128)}, f32[896,2432]{1,0:T(8,128)}, f32[2432,896]{1,0:T(8,128)}, f32[448,1152]{1,0:T(8,128)}, f32[448,896]{1,0:T(8,128)}, /*index=5*/f32[8,128]{1,0:T(8,128)}) custom-call(s32[20]{0:T(128)} %concatenate.63.refs_0_.meta_ref, ...), custom_call_target="tpu_custom_call", output_to_operand_aliasing={{0}: (5, {}), {1}: (6, {}), {2}: (7, {}), {3}: (8, {}), {4}... | custom-call | bytes 7454720 | tf_op jit(solution)/shard_map/pallas_call | solution.py:908
  (348 shorter events, 158.0 us)
Async XLA Ops:
  28.5 18.0 %collective-permute-start.15 = (bf16[128,1792]{1,0:T(8,128)(2,1)S(1)}, bf16[128,1792]{1,0:T(8,128)(2,1)S(1)}, u32[]{:S(2)}, u32[]{:S(2)}) collective-permute-start(bf16[128,1792]{1,0:T(8,128)(2,1)S(1)} %constant_dynamic-update-slice_fusion.11), channel_id=1, source_target_pairs={{0,16},{16,0},{1,17},{17,1},{2,18},{18,2},{3,19},{19,3},{4,20},{20... | collective-permute-start | bytes 1376264 | tf_op jit(solution)/shard_map/ppermute | solution.py:58
  46.5 22.7 %collective-permute-start.16 = (bf16[256,1792]{1,0:T(8,128)(2,1)S(1)}, bf16[256,1792]{1,0:T(8,128)(2,1)S(1)}, u32[]{:S(2)}, u32[]{:S(2)}) collective-permute-start(bf16[256,1792]{1,0:T(8,128)(2,1)S(1)} %pad_maximum_fusion.3.refs_3_.refs_2_.refs_1_), channel_id=1, source_target_pairs={{0,1},{1,0},{2,3},{3,2},{4,5},{5,4},{6,7},{7,6},{8,9},{9,8},{10,11... | collective-permute-start | bytes 2752520 | tf_op jit(solution)/shard_map/ppermute | solution.py:54
  104.4 22.1 %collective-permute-start.21 = (bf16[456,896]{1,0:T(8,128)(2,1)}, bf16[456,896]{1,0:T(8,128)(2,1)S(1)}, u32[]{:S(2)}, u32[]{:S(2)}) collective-permute-start(bf16[456,896]{1,0:T(8,128)(2,1)} %get-tuple-element.128), channel_id=1, source_target_pairs={{0,4},{1,5},{4,8},{5,9},{8,12},{9,13},{12,14},{13,15},{14,10},{15,... | collective-permute-start | bytes 2451464 | tf_op jit(solution)/shard_map/ppermute | solution.py:66
  106.1 21.6 %collective-permute-start.22 = (bf16[456,896]{1,0:T(8,128)(2,1)}, bf16[456,896]{1,0:T(8,128)(2,1)S(1)}, u32[]{:S(2)}, u32[]{:S(2)}) collective-permute-start(bf16[456,896]{1,0:T(8,128)(2,1)} %get-tuple-element.130), channel_id=1, source_target_pairs={{0,2},{1,3},{4,0},{5,1},{8,4},{9,5},{12,8},{13,9},{14,12},{15,13},... | collective-permute-start | bytes 2451464 | tf_op jit(solution)/shard_map/ppermute | solution.py:66
  135.0 26.9 %collective-permute-start.31 = (bf16[456,896]{1,0:T(8,128)(2,1)S(1)}, bf16[456,896]{1,0:T(8,128)(2,1)S(1)}, u32[]{:S(2)}, u32[]{:S(2)}) collective-permute-start(bf16[456,896]{1,0:T(8,128)(2,1)S(1)} %copy-done.7), channel_id=1, source_target_pairs={{0,4},{1,5},{4,8},{5,9},{8,12},{9,13},{12,14},{13,15},{14,10},{15,... | collective-permute-start | bytes 2451464 | tf_op jit(solution)/shard_map/ppermute | solution.py:66
  136.6 26.3 %collective-permute-start.32 = (bf16[456,896]{1,0:T(8,128)(2,1)S(1)}, bf16[456,896]{1,0:T(8,128)(2,1)S(1)}, u32[]{:S(2)}, u32[]{:S(2)}) collective-permute-start(bf16[456,896]{1,0:T(8,128)(2,1)S(1)} %copy-done.8), channel_id=1, source_target_pairs={{0,2},{1,3},{4,0},{5,1},{8,4},{9,5},{12,8},{13,9},{14,12},{15,13},... | collective-permute-start | bytes 2451464 | tf_op jit(solution)/shard_map/ppermute | solution.py:66
  137.8 19.2 %collective-permute-start.27 = (bf16[64,256]{1,0:T(8,128)(2,1)S(1)}, bf16[64,256]{1,0:T(8,128)(2,1)S(1)}, u32[]{:S(2)}, u32[]{:S(2)}) collective-permute-start(bf16[64,256]{1,0:T(8,128)(2,1)S(1)} %get-tuple-element.206), channel_id=1, source_target_pairs={{0,2},{1,3},{4,0},{5,1},{8,4},{9,5},{12,8},{13,9},{14,12},{15,13},... | collective-permute-start | bytes 98312 | tf_op jit(solution)/shard_map/ppermute | solution.py:66
  142.2 23.5 %collective-permute-start.37 = (bf16[768,896]{1,0:T(8,128)(2,1)}, bf16[768,896]{1,0:T(8,128)(2,1)}, u32[]{:S(2)}, u32[]{:S(2)}) collective-permute-start(bf16[768,896]{1,0:T(8,128)(2,1)} %constant_dynamic-update-slice_fusion.13.refs_3_), channel_id=1, source_target_pairs={{0,1},{1,0},{2,3},{3,2},{4,5},{5,4},{6,7},{7,6},{8,9},{9,8},{10,11... | collective-permute-start | bytes 4128776 | tf_op jit(solution)/shard_map/ppermute | solution.py:54
  161.4 59.7 %collective-permute-start.29 = (bf16[128,256]{1,0:T(8,128)(2,1)S(1)}, bf16[128,256]{1,0:T(8,128)(2,1)S(1)}, u32[]{:S(2)}, u32[]{:S(2)}) collective-permute-start(bf16[128,256]{1,0:T(8,128)(2,1)S(1)} %add_convert_fusion.14), channel_id=1, source_target_pairs={{0,2},{1,3},{4,0},{5,1},{8,4},{9,5},{12,8},{13,9},{14,12},{15,13},... | collective-permute-start | bytes 196616 | tf_op jit(solution)/shard_map/ppermute | solution.py:66
  164.1 29.8 %collective-permute-start.33 = (bf16[456,896]{1,0:T(8,128)(2,1)}, bf16[456,896]{1,0:T(8,128)(2,1)S(1)}, u32[]{:S(2)}, u32[]{:S(2)}) collective-permute-start(bf16[456,896]{1,0:T(8,128)(2,1)} %get-tuple-element.143), channel_id=1, source_target_pairs={{0,4},{1,5},{4,8},{5,9},{8,12},{9,13},{12,14},{13,15},{14,10},{15,... | collective-permute-start | bytes 2451464 | tf_op jit(solution)/shard_map/ppermute | solution.py:66
  172.5 54.6 %collective-permute-start.26 = (bf16[128,256]{1,0:T(8,128)(2,1)S(1)}, bf16[128,256]{1,0:T(8,128)(2,1)S(1)}, u32[]{:S(2)}, u32[]{:S(2)}) collective-permute-start(bf16[128,256]{1,0:T(8,128)(2,1)S(1)} %add_convert_fusion.15), channel_id=1, source_target_pairs={{0,4},{1,5},{4,8},{5,9},{8,12},{9,13},{12,14},{13,15},{14,10},{15,... | collective-permute-start | bytes 196616 | tf_op jit(solution)/shard_map/ppermute | solution.py:66
  174.1 48.6 %collective-permute-start.35 = (bf16[456,896]{1,0:T(8,128)(2,1)S(1)}, bf16[456,896]{1,0:T(8,128)(2,1)S(1)}, u32[]{:S(2)}, u32[]{:S(2)}) collective-permute-start(bf16[456,896]{1,0:T(8,128)(2,1)S(1)} %copy-done.9), channel_id=1, source_target_pairs={{0,2},{1,3},{4,0},{5,1},{8,4},{9,5},{12,8},{13,9},{14,12},{15,13},... | collective-permute-start | bytes 2451464 | tf_op jit(solution)/shard_map/ppermute | solution.py:66
  198.6 24.2 %collective-permute-start.34 = (bf16[456,896]{1,0:T(8,128)(2,1)}, bf16[456,896]{1,0:T(8,128)(2,1)S(1)}, u32[]{:S(2)}, u32[]{:S(2)}) collective-permute-start(bf16[456,896]{1,0:T(8,128)(2,1)} %shard_map.203), channel_id=1, source_target_pairs={{0,4},{1,5},{4,8},{5,9},{8,12},{9,13},{12,14},{13,15},{14,10},{15,... | collective-permute-start | bytes 2451464 | tf_op jit(solution)/shard_map/ppermute | solution.py:66
  230.1 23.3 %collective-permute-start.48 = (bf16[520,896]{1,0:T(8,128)(2,1)}, bf16[520,896]{1,0:T(8,128)(2,1)S(1)}, u32[]{:S(2)}, u32[]{:S(2)}) collective-permute-start(bf16[520,896]{1,0:T(8,128)(2,1)} %shard_map.206.refs_0_), channel_id=1, source_target_pairs={{0,4},{1,5},{4,8},{5,9},{8,12},{9,13},{12,14},{13,15},{14,10},{15,... | collective-permute-start | bytes 2795528 | tf_op jit(solution)/shard_map/ppermute | solution.py:66
  231.3 23.0 %collective-permute-start.49 = (bf16[520,896]{1,0:T(8,128)(2,1)}, bf16[520,896]{1,0:T(8,128)(2,1)S(1)}, u32[]{:S(2)}, u32[]{:S(2)}) collective-permute-start(bf16[520,896]{1,0:T(8,128)(2,1)} %shard_map.206.refs_0_), channel_id=1, source_target_pairs={{0,2},{1,3},{4,0},{5,1},{8,4},{9,5},{12,8},{13,9},{14,12},{15,13},... | collective-permute-start | bytes 2795528 | tf_op jit(solution)/shard_map/ppermute | solution.py:66
  255.8 22.8 %collective-permute-start.52 = (bf16[520,896]{1,0:T(8,128)(2,1)}, bf16[520,896]{1,0:T(8,128)(2,1)S(1)}, u32[]{:S(2)}, u32[]{:S(2)}) collective-permute-start(bf16[520,896]{1,0:T(8,128)(2,1)} %get-tuple-element.160.refs_0_), channel_id=1, source_target_pairs={{0,4},{1,5},{4,8},{5,9},{8,12},{9,13},{12,14},{13,15},{14,10},{15,... | collective-permute-start | bytes 2795528 | tf_op jit(solution)/shard_map/ppermute | solution.py:66
  256.4 22.5 %collective-permute-start.53 = (bf16[520,896]{1,0:T(8,128)(2,1)}, bf16[520,896]{1,0:T(8,128)(2,1)S(1)}, u32[]{:S(2)}, u32[]{:S(2)}) collective-permute-start(bf16[520,896]{1,0:T(8,128)(2,1)} %get-tuple-element.161.refs_2_), channel_id=1, source_target_pairs={{0,2},{1,3},{4,0},{5,1},{8,4},{9,5},{12,8},{13,9},{14,12},{15,13},... | collective-permute-start | bytes 2795528 | tf_op jit(solution)/shard_map/ppermute | solution.py:66
  280.4 22.8 %collective-permute-start.56 = (bf16[520,896]{1,0:T(8,128)(2,1)}, bf16[520,896]{1,0:T(8,128)(2,1)S(1)}, u32[]{:S(2)}, u32[]{:S(2)}) collective-permute-start(bf16[520,896]{1,0:T(8,128)(2,1)} %get-tuple-element.168.refs_0_), channel_id=1, source_target_pairs={{0,4},{1,5},{4,8},{5,9},{8,12},{9,13},{12,14},{13,15},{14,10},{15,... | collective-permute-start | bytes 2795528 | tf_op jit(solution)/shard_map/ppermute | solution.py:66
  281.0 22.5 %collective-permute-start.57 = (bf16[520,896]{1,0:T(8,128)(2,1)}, bf16[520,896]{1,0:T(8,128)(2,1)S(1)}, u32[]{:S(2)}, u32[]{:S(2)}) collective-permute-start(bf16[520,896]{1,0:T(8,128)(2,1)} %get-tuple-element.169.refs_2_), channel_id=1, source_target_pairs={{0,2},{1,3},{4,0},{5,1},{8,4},{9,5},{12,8},{13,9},{14,12},{15,13},... | collective-permute-start | bytes 2795528 | tf_op jit(solution)/shard_map/ppermute | solution.py:66
  282.4 22.6 %collective-permute-start.63 = (bf16[464,256]{1,0:T(8,128)(2,1)S(1)}, bf16[464,256]{1,0:T(8,128)(2,1)S(1)}, u32[]{:S(2)}, u32[]{:S(2)}) collective-permute-start(bf16[464,256]{1,0:T(8,128)(2,1)S(1)} %copy-done.14), channel_id=1, source_target_pairs={{0,1},{1,0},{2,3},{3,2},{4,5},{5,4},{6,7},{7,6},{8,9},{9,8},{10,11... | collective-permute-start | bytes 712712 | tf_op jit(solution)/shard_map/ppermute | solution.py:54
  304.5 18.6 %collective-permute-start.60 = (bf16[520,896]{1,0:T(8,128)(2,1)}, bf16[520,896]{1,0:T(8,128)(2,1)S(1)}, u32[]{:S(2)}, u32[]{:S(2)}) collective-permute-start(bf16[520,896]{1,0:T(8,128)(2,1)} %get-tuple-element.176.refs_0_), channel_id=1, source_target_pairs={{0,1},{1,0},{2,3},{3,2},{4,5},{5,4},{6,7},{7,6},{8,9},{9,8},{10,11... | collective-permute-start | bytes 2795528 | tf_op jit(solution)/shard_map/ppermute | solution.py:54
  304.5 18.6 %collective-permute-start.61 = (bf16[520,896]{1,0:T(8,128)(2,1)}, bf16[520,896]{1,0:T(8,128)(2,1)S(1)}, u32[]{:S(2)}, u32[]{:S(2)}) collective-permute-start(bf16[520,896]{1,0:T(8,128)(2,1)} %get-tuple-element.177.refs_2_), channel_id=1, source_target_pairs={{0,1},{1,0},{2,3},{3,2},{4,5},{5,4},{6,7},{7,6},{8,9},{9,8},{10,11... | collective-permute-start | bytes 2795528 | tf_op jit(solution)/shard_map/ppermute | solution.py:54
  308.3 24.9 %collective-permute-start.58 = (bf16[264,896]{1,0:T(8,128)(2,1)}, bf16[264,896]{1,0:T(8,128)(2,1)S(1)}, u32[]{:S(2)}, u32[]{:S(2)}) collective-permute-start(bf16[264,896]{1,0:T(8,128)(2,1)} %slice.103), channel_id=1, source_target_pairs={{0,4},{1,5},{4,8},{5,9},{8,12},{9,13},{12,14},{13,15},{14,10},{15,... | collective-permute-start | bytes 1419272 | tf_op jit(solution)/shard_map/ppermute | solution.py:66
  313.2 20.1 %collective-permute-start.59 = (bf16[256,896]{1,0:T(8,128)(2,1)}, bf16[256,896]{1,0:T(8,128)(2,1)}, u32[]{:S(2)}, u32[]{:S(2)}) collective-permute-start(bf16[256,896]{1,0:T(8,128)(2,1)} %slice.104), channel_id=1, source_target_pairs={{0,2},{1,3},{4,0},{5,1},{8,4},{9,5},{12,8},{13,9},{14,12},{15,13},... | collective-permute-start | bytes 1376264 | tf_op jit(solution)/shard_map/ppermute | solution.py:66
  (107 other events, 754.1 us)

commit v15 on v14

--- a/solution.py
+++ b/solution.py
@@ -166,12 +166,7 @@
     def exchange_start(self, x):
         half = x.shape[0] // 2
         x = add_low(x, self.swap(x))
-        x = lax.dynamic_slice(x, (self.core * half, 0), (half, x.shape[1]))
-        bit = 1
-        while 2 * bit < self.chips:
-            x = self.exchange(x, bit)
-            bit *= 2
-        return x
+        return lax.dynamic_slice(x, (self.core * half, 0), (half, x.shape[1]))
 
     def exchange(self, x, bit):
         return add_low(x, lax.ppermute(x, "ctx", [(i, i ^ (2 * bit)) for i in range(self.ctx)]))
@@ -205,7 +200,12 @@
         for s in range(1, half + 1):
             if s > 1:
                 placed, token = place(*waiting, placed)
-                fwd, back = gate([token] + marks[s - 2], [fwd, back])
+                before = [token] + marks[s - 2]
+                if s > half - 2:
+                    rest = self.exchange(gate([token], [rest])[0], 1 << (s - half + 1))
+                    if s == half:
+                        before.append(rest)
+                fwd, back = gate(before, [fwd, back])
                 waiting = ([s - 1, n - s + 1], [(fwd, self.swap(fwd)), (back, self.swap(back))])
             if s < half:
                 fwd, back = self.hop(fwd, 1), self.hop(back, -1)

time: 348 us -> 354 us (1.017)
  waiting for transfers between devices: 127 us -> 131 us
    ppermute x3, waiting for transfers between devices: 10.7 us -> 27.1 us  [exchange(): lax.ppermute(x, 'ctx', [(i, i ^ 2 * bit) for i in range(self.ctx)])]
    ppermute x39, waiting for transfers between devices: 92.7 us -> 80.9 us  [hop(): return lax.ppermute(x, 'ctx', perm)]
  transfers between devices with their start and end apart: 68 -> 68, of which waited for: 34 -> 32; matrix products, arithmetic and copies ran while one was open for 11% -> 12% of each run, Pallas kernels for 21% -> 21%
where the time goes in v15:
time: 354 us; the launch traced here: 352 us
  waiting for transfers between devices  131 us (37%)
  Pallas kernels  100 us (28%)
  starting transfers between devices  55.3 us (16%)
  local copies, waits for them, and re-layouts  39.4 us (11%)
  other arithmetic  24.1 us (7%)
    ppermute x39, waiting for transfers between devices, hop(): return lax.ppermute(x, 'ctx', perm)  80.9 us
    pallas_call x10, Pallas kernels, call(): pl.pallas_call(body, out_shape=list(outs), in_specs=specs, out_specs=[pl....  47.9 us
    ppermute x39, starting transfers between devices, hop(): return lax.ppermute(x, 'ctx', perm)  38 us
    ppermute x3, waiting for transfers between devices, exchange(): lax.ppermute(x, 'ctx', [(i, i ^ 2 * bit) for i in range(self.ctx)])  27.1 us
    pallas_call x5, Pallas kernels, place_all(): pl.pallas_call(kernel, out_shape=[jax.ShapeDtypeStruct((D, ff_loc), f32),...  26.1 us
    unnamed x140, local copies, waits for them, and re-layouts  21 us
    ppermute x8, waiting for transfers between devices, shift(): return lax.ppermute(x, 'dp', [(i, (i + step) % n) for i in range(n)])  16.7 us
    pallas_call x1, Pallas kernels, feed_forward(): pl.pallas_call(lambda *refs: mlp_kernel(half, *refs), out_shape=[jax.Shap...  16.2 us
  transfers between devices with their start and end apart: 68, of which 32 were waited for; matrix products, arithmetic and copies ran while one was open for 12% of the time, Pallas kernels for 21%

profile of v15, /device:TPU:0, one launch (start us, length us, event | category | flops | bytes accessed | tf_op | source)
XLA Modules:
  0.0 352.2 jit_solution(15289350874764576510)
XLA Ops:
  12.0 4.5 %collective-permute-done = bf16[224,1152]{1,0:T(8,128)(2,1)S(1)} collective-permute-done((bf16[224,1152]{1,0:T(8,128)(2,1)S(1)}, bf16[224,1152]{1,0:T(8,128)(2,1)S(1)}, u32[]{:S(2)}, u32[]{:S(2)}) %collective-permute-start) | collective-permute-done | bytes 516128 | tf_op jit(solution)/shard_map/ppermute | solution.py:58
  20.4 3.2 shard_map.195
  49.5 10.3 %shard_map.196 = (bf16[128,896]{1,0:T(8,128)(2,1)}, f32[2,896,128]{2,1,0:T(8,128)}, f32[2,2,8,448]{3,2,1,0:T(8,128)}, bf16[2,896,128]{2,1,0:T(8,128)(2,1)}, bf16...) custom-call(s32[17]{0:T(128)} %pad_add_fusion.refs_0_, ...), custom_call_target="tpu_custom_call" | custom-call | flops 1879048192 | bytes 6516292 | tf_op jit(solution)/shard_map/pallas_call | solution.py:242
  62.6 5.1 %collective-permute-done.13 = bf16[128,896]{1,0:T(8,128)(2,1)S(1)} collective-permute-done((bf16[128,896]{1,0:T(8,128)(2,1)}, bf16[128,896]{1,0:T(8,128)(2,1)S(1)}, u32[]{:S(2)}, u32[]{:S(2)}) %collective-permute-start.13) | collective-permute-done | bytes 229408 | tf_op jit(solution)/shard_map/ppermute | solution.py:58
  70.9 16.2 %shard_map.197 = (bf16[896,512]{1,0:T(8,128)(2,1)}, bf16[1280,512]{1,0:T(8,128)(2,1)}, bf16[512,1280]{1,0:T(8,128)(2,1)}, bf16[512,1280]{1,0:T(8,128)(2,1)}, f32...) custom-call(s32[20]{0:T(128)} %concatenate.63.refs_0_.meta_ref, bf16[256,896]{1,0:T(8,128)(2,1)} %copy-done.16, ...), custom_call_target="tpu_custom_call" | custom-call | flops 7046430720 | bytes 6881280 | tf_op jit(solution)/shard_map/pallas_call | solution.py:666
  94.4 10.1 %shard_map.198 = (bf16[456,896]{1,0:T(8,128)(2,1)}, bf16[456,896]{1,0:T(8,128)(2,1)}, bf16[456,896]{1,0:T(8,128)(2,1)}, bf16[456,896]{1,0:T(8,128)(2,1)}, bf16[4...) custom-call(s32[20]{0:T(128)} %concatenate.63.refs_0_.meta_ref, ...), custom_call_target="tpu_custom_call" | custom-call | flops 3523215360 | bytes 13074432 | tf_op jit(solution)/shard_map/pallas_call | solution.py:752
  107.3 14.9 %shard_map.199 = (f32[128,896]{1,0:T(8,128)}, bf16[128,896]{1,0:T(8,128)(2,1)}, f32[1,896]{1,0:T(1,128)}, bf16[128,896]{1,0:T(8,128)(2,1)}, f32[1024,256]{1,0:T(8,128)}, /*index=5*/bf16[1024,256]{1,0:T(8,128)(2,1)}) custom-call(s32[17]{0:T(128)} %pad_add_fusion.refs_0_, f32[128,896]{1,0:T(8,128)} %slice_add_fusion.refs_1_, ...), custom_call_target="tpu_custom_call" | custom-call | flops 4697620480 | bytes 8680516 | tf_op jit(solution)/shard_map/pallas_call | solution.py:242
  143.9 13.1 %collective-permute-done.27.refs_1_ = bf16[64,256]{1,0:T(8,128)(2,1)S(1)} collective-permute-done((bf16[64,256]{1,0:T(8,128)(2,1)S(1)}, bf16[64,256]{1,0:T(8,128)(2,1)S(1)}, u32[]{:S(2)}, u32[]{:S(2)}) %collective-permute-start.27) | collective-permute-done | bytes 32800 | tf_op jit(solution)/shard_map/ppermute | solution.py:66
  165.7 4.2 %shard_map.205 = (bf16[64,896]{1,0:T(8,128)(2,1)}, bf16[64,896]{1,0:T(8,128)(2,1)}, bf16[64,896]{1,0:T(8,128)(2,1)}, bf16[64,896]{1,0:T(8,128)(2,1)}, bf16[64,89...) custom-call(s32[20]{0:T(128)} %concatenate.63.refs_0_.meta_ref, ...), custom_call_target="tpu_custom_call" | custom-call | flops 1879048192 | bytes 5505104 | tf_op jit(solution)/shard_map/pallas_call | solution.py:242
  176.2 7.4 %collective-permute-done.38 = bf16[32,896]{1,0:T(8,128)(2,1)S(1)} collective-permute-done((bf16[32,896]{1,0:T(8,128)(2,1)S(1)}, bf16[32,896]{1,0:T(8,128)(2,1)S(1)}, u32[]{:S(2)}, u32[]{:S(2)}) %collective-permute-start.38) | collective-permute-done | bytes 57376 | tf_op jit(solution)/shard_map/ppermute | solution.py:66
  184.9 7.6 %collective-permute-done.42 = bf16[32,896]{1,0:T(8,128)(2,1)S(1)} collective-permute-done((bf16[32,896]{1,0:T(8,128)(2,1)S(1)}, bf16[32,896]{1,0:T(8,128)(2,1)S(1)}, u32[]{:S(2)}, u32[]{:S(2)}) %collective-permute-start.42) | collective-permute-done | bytes 57376 | tf_op jit(solution)/shard_map/ppermute | solution.py:66
  199.7 16.0 %collective-permute-done.40 = bf16[64,896]{1,0:T(8,128)(2,1)S(1)} collective-permute-done((bf16[64,896]{1,0:T(8,128)(2,1)S(1)}, bf16[64,896]{1,0:T(8,128)(2,1)S(1)}, u32[]{:S(2)}, u32[]{:S(2)}) %collective-permute-start.40) | collective-permute-done | bytes 114720 | tf_op jit(solution)/shard_map/ppermute | solution.py:66
  215.8 4.7 %collective-permute-done.44 = bf16[64,896]{1,0:T(8,128)(2,1)S(1)} collective-permute-done((bf16[64,896]{1,0:T(8,128)(2,1)S(1)}, bf16[64,896]{1,0:T(8,128)(2,1)S(1)}, u32[]{:S(2)}, u32[]{:S(2)}) %collective-permute-start.44) | collective-permute-done | bytes 114720 | tf_op jit(solution)/shard_map/ppermute | solution.py:66
  232.2 3.6 %shard_map.201 = (bf16[160,256]{1,0:T(8,128)(2,1)}, f32[128,896]{1,0:T(8,128)}, f32[1,896]{1,0:T(1,128)}, f32[1,1152]{1,0:T(1,128)}) custom-call(bf16[128,896]{1,0:T(8,128)(2,1)} %get-tuple-element.123.refs_0_, bf16[128,896]{1,0:T(8,128)(2,1)} %bitcast.17, f32[1,896]{1,0:T(1,128)} %broadcast_in_dim.22.refs_1_.refs_2_, ...), custom_call_target="tpu_custom_call" | custom-call | bytes 3931136 | tf_op jit(solution)/shard_map/pallas_call | solution.py:242
  237.2 3.2 collective-permute-done.47.refs_3_
  244.3 4.1 %shard_map.207 = (f32[896,2432]{1,0:T(8,128)}, f32[896,2432]{1,0:T(8,128)}, f32[2432,896]{1,0:T(8,128)}, f32[448,1152]{1,0:T(8,128)}, f32[448,896]{1,0:T(8,128)}, /*index=5*/f32[8,128]{1,0:T(8,128)}) custom-call(s32[20]{0:T(128)} %concatenate.63.refs_0_.meta_ref, bf16[520,896]{1,0:T(8,128)(2,1)} %shard_map.206.refs_0_, bf16[520,896]{1,0:T(8,128)(2,1)} %copy-done.17), custom_call_target="tpu_custom_call" | custom-call | bytes 7454720 | tf_op jit(solution)/shard_map/pallas_call | solution.py:908
  248.4 5.0 %collective-permute-done.48.refs_2_ = bf16[520,896]{1,0:T(8,128)(2,1)S(1)} collective-permute-done((bf16[520,896]{1,0:T(8,128)(2,1)}, bf16[520,896]{1,0:T(8,128)(2,1)S(1)}, u32[]{:S(2)}, u32[]{:S(2)}) %collective-permute-start.48) | collective-permute-done | bytes 931872 | tf_op jit(solution)/shard_map/ppermute | solution.py:66
  260.3 5.9 %shard_map.210 = (f32[896,2432]{1,0:T(8,128)}, f32[896,2432]{1,0:T(8,128)}, f32[2432,896]{1,0:T(8,128)}, f32[448,1152]{1,0:T(8,128)}, f32[448,896]{1,0:T(8,128)}, /*index=5*/f32[8,128]{1,0:T(8,128)}) custom-call(s32[20]{0:T(128)} %concatenate.63.refs_0_.meta_ref, ...), custom_call_target="tpu_custom_call", output_to_operand_aliasing={{0}: (5, {}), {1}: (6, {}), {2}: (7, {}), {3}: (8, {}), {4}... | custom-call | bytes 14909440 | tf_op jit(solution)/shard_map/pallas_call | solution.py:908
  266.3 12.3 %collective-permute-done.52.refs_1_ = bf16[520,896]{1,0:T(8,128)(2,1)S(1)} collective-permute-done((bf16[520,896]{1,0:T(8,128)(2,1)}, bf16[520,896]{1,0:T(8,128)(2,1)S(1)}, u32[]{:S(2)}, u32[]{:S(2)}) %collective-permute-start.52) | collective-permute-done | bytes 931872 | tf_op jit(solution)/shard_map/ppermute | solution.py:66
  286.1 20.2 %collective-permute-done.57 = bf16[232,256]{1,0:T(8,128)(2,1)S(1)} collective-permute-done((bf16[232,256]{1,0:T(8,128)(2,1)}, bf16[232,256]{1,0:T(8,128)(2,1)S(1)}, u32[]{:S(2)}, u32[]{:S(2)}) %collective-permute-start.57) | collective-permute-done | bytes 118816 | tf_op jit(solution)/shard_map/ppermute | solution.py:172
  308.7 5.9 %shard_map.212 = (f32[896,2432]{1,0:T(8,128)}, f32[896,2432]{1,0:T(8,128)}, f32[2432,896]{1,0:T(8,128)}, f32[448,1152]{1,0:T(8,128)}, f32[448,896]{1,0:T(8,128)}, /*index=5*/f32[8,128]{1,0:T(8,128)}) custom-call(s32[20]{0:T(128)} %concatenate.63.refs_0_.meta_ref, ...), custom_call_target="tpu_custom_call", output_to_operand_aliasing={{0}: (5, {}), {1}: (6, {}), {2}: (7, {}), {3}: (8, {}), {4}... | custom-call | bytes 14909440 | tf_op jit(solution)/shard_map/pallas_call | solution.py:908
  314.8 5.1 %collective-permute-done.58 = bf16[232,256]{1,0:T(8,128)(2,1)S(1)} collective-permute-done((bf16[232,256]{1,0:T(8,128)(2,1)}, bf16[232,256]{1,0:T(8,128)(2,1)S(1)}, u32[]{:S(2)}, u32[]{:S(2)}) %collective-permute-start.58) | collective-permute-done | bytes 118816 | tf_op jit(solution)/shard_map/ppermute | solution.py:172
  329.4 5.9 %shard_map.216 = (f32[896,2432]{1,0:T(8,128)}, f32[896,2432]{1,0:T(8,128)}, f32[2432,896]{1,0:T(8,128)}, f32[448,1152]{1,0:T(8,128)}, f32[448,896]{1,0:T(8,128)}, /*index=5*/f32[8,128]{1,0:T(8,128)}) custom-call(s32[20]{0:T(128)} %concatenate.63.refs_0_.meta_ref, ...), custom_call_target="tpu_custom_call", output_to_operand_aliasing={{0}: (5, {}), {1}: (6, {}), {2}: (7, {}), {3}: (8, {}), {4}... | custom-call | bytes 14909440 | tf_op jit(solution)/shard_map/pallas_call | solution.py:908
  347.8 4.2 %shard_map.219 = (f32[896,2432]{1,0:T(8,128)}, f32[896,2432]{1,0:T(8,128)}, f32[2432,896]{1,0:T(8,128)}, f32[448,1152]{1,0:T(8,128)}, f32[448,896]{1,0:T(8,128)}, /*index=5*/f32[8,128]{1,0:T(8,128)}) custom-call(s32[20]{0:T(128)} %concatenate.63.refs_0_.meta_ref, ...), custom_call_target="tpu_custom_call", output_to_operand_aliasing={{0}: (5, {}), {1}: (6, {}), {2}: (7, {}), {3}: (8, {}), {4}... | custom-call | bytes 7454720 | tf_op jit(solution)/shard_map/pallas_call | solution.py:908
  (350 shorter events, 157.9 us)
Async XLA Ops:
  25.7 17.8 %collective-permute-start.11 = (bf16[224,896]{1,0:T(8,128)(2,1)S(1)}, bf16[224,896]{1,0:T(8,128)(2,1)S(1)}, u32[]{:S(2)}, u32[]{:S(2)}) collective-permute-start(bf16[224,896]{1,0:T(8,128)(2,1)S(1)} %constant_dynamic-slice_fusion), channel_id=1, source_target_pairs={{0,16},{16,0},{1,17},{17,1},{2,18},{18,2},{3,19},{19,3},{4,20},{20... | collective-permute-start | bytes 1204232 | tf_op jit(solution)/shard_map/ppermute | solution.py:58
  28.5 18.0 %collective-permute-start.15 = (bf16[128,1792]{1,0:T(8,128)(2,1)S(1)}, bf16[128,1792]{1,0:T(8,128)(2,1)S(1)}, u32[]{:S(2)}, u32[]{:S(2)}) collective-permute-start(bf16[128,1792]{1,0:T(8,128)(2,1)S(1)} %constant_dynamic-update-slice_fusion.11), channel_id=1, source_target_pairs={{0,16},{16,0},{1,17},{17,1},{2,18},{18,2},{3,19},{19,3},{4,20},{20... | collective-permute-start | bytes 1376264 | tf_op jit(solution)/shard_map/ppermute | solution.py:58
  46.5 22.7 %collective-permute-start.16 = (bf16[256,1792]{1,0:T(8,128)(2,1)S(1)}, bf16[256,1792]{1,0:T(8,128)(2,1)S(1)}, u32[]{:S(2)}, u32[]{:S(2)}) collective-permute-start(bf16[256,1792]{1,0:T(8,128)(2,1)S(1)} %pad_maximum_fusion.3.refs_3_.refs_2_.refs_1_), channel_id=1, source_target_pairs={{0,1},{1,0},{2,3},{3,2},{4,5},{5,4},{6,7},{7,6},{8,9},{9,8},{10,11... | collective-permute-start | bytes 2752520 | tf_op jit(solution)/shard_map/ppermute | solution.py:54
  104.4 22.1 %collective-permute-start.21 = (bf16[456,896]{1,0:T(8,128)(2,1)}, bf16[456,896]{1,0:T(8,128)(2,1)S(1)}, u32[]{:S(2)}, u32[]{:S(2)}) collective-permute-start(bf16[456,896]{1,0:T(8,128)(2,1)} %get-tuple-element.128), channel_id=1, source_target_pairs={{0,4},{1,5},{4,8},{5,9},{8,12},{9,13},{12,14},{13,15},{14,10},{15,... | collective-permute-start | bytes 2451464 | tf_op jit(solution)/shard_map/ppermute | solution.py:66
  106.1 21.6 %collective-permute-start.22 = (bf16[456,896]{1,0:T(8,128)(2,1)}, bf16[456,896]{1,0:T(8,128)(2,1)S(1)}, u32[]{:S(2)}, u32[]{:S(2)}) collective-permute-start(bf16[456,896]{1,0:T(8,128)(2,1)} %get-tuple-element.130), channel_id=1, source_target_pairs={{0,2},{1,3},{4,0},{5,1},{8,4},{9,5},{12,8},{13,9},{14,12},{15,13},... | collective-permute-start | bytes 2451464 | tf_op jit(solution)/shard_map/ppermute | solution.py:66
  123.5 17.8 %collective-permute-start.36 = (bf16[384,896]{1,0:T(8,128)(2,1)S(1)}, bf16[384,896]{1,0:T(8,128)(2,1)S(1)}, u32[]{:S(2)}, u32[]{:S(2)}) collective-permute-start(bf16[384,896]{1,0:T(8,128)(2,1)S(1)} %pad_maximum_fusion.5), channel_id=1, source_target_pairs={{0,16},{16,0},{1,17},{17,1},{2,18},{18,2},{3,19},{19,3},{4,20},{20... | collective-permute-start | bytes 2064392 | tf_op jit(solution)/shard_map/ppermute | solution.py:58
  135.0 26.9 %collective-permute-start.31 = (bf16[456,896]{1,0:T(8,128)(2,1)S(1)}, bf16[456,896]{1,0:T(8,128)(2,1)S(1)}, u32[]{:S(2)}, u32[]{:S(2)}) collective-permute-start(bf16[456,896]{1,0:T(8,128)(2,1)S(1)} %copy-done.7), channel_id=1, source_target_pairs={{0,4},{1,5},{4,8},{5,9},{8,12},{9,13},{12,14},{13,15},{14,10},{15,... | collective-permute-start | bytes 2451464 | tf_op jit(solution)/shard_map/ppermute | solution.py:66
  136.6 26.3 %collective-permute-start.32 = (bf16[456,896]{1,0:T(8,128)(2,1)S(1)}, bf16[456,896]{1,0:T(8,128)(2,1)S(1)}, u32[]{:S(2)}, u32[]{:S(2)}) collective-permute-start(bf16[456,896]{1,0:T(8,128)(2,1)S(1)} %copy-done.8), channel_id=1, source_target_pairs={{0,2},{1,3},{4,0},{5,1},{8,4},{9,5},{12,8},{13,9},{14,12},{15,13},... | collective-permute-start | bytes 2451464 | tf_op jit(solution)/shard_map/ppermute | solution.py:66
  137.8 19.2 %collective-permute-start.27 = (bf16[64,256]{1,0:T(8,128)(2,1)S(1)}, bf16[64,256]{1,0:T(8,128)(2,1)S(1)}, u32[]{:S(2)}, u32[]{:S(2)}) collective-permute-start(bf16[64,256]{1,0:T(8,128)(2,1)S(1)} %get-tuple-element.206), channel_id=1, source_target_pairs={{0,2},{1,3},{4,0},{5,1},{8,4},{9,5},{12,8},{13,9},{14,12},{15,13},... | collective-permute-start | bytes 98312 | tf_op jit(solution)/shard_map/ppermute | solution.py:66
  142.2 23.5 %collective-permute-start.37 = (bf16[768,896]{1,0:T(8,128)(2,1)}, bf16[768,896]{1,0:T(8,128)(2,1)}, u32[]{:S(2)}, u32[]{:S(2)}) collective-permute-start(bf16[768,896]{1,0:T(8,128)(2,1)} %constant_dynamic-update-slice_fusion.13.refs_3_), channel_id=1, source_target_pairs={{0,1},{1,0},{2,3},{3,2},{4,5},{5,4},{6,7},{7,6},{8,9},{9,8},{10,11... | collective-permute-start | bytes 4128776 | tf_op jit(solution)/shard_map/ppermute | solution.py:54
  161.4 59.7 %collective-permute-start.29 = (bf16[128,256]{1,0:T(8,128)(2,1)S(1)}, bf16[128,256]{1,0:T(8,128)(2,1)S(1)}, u32[]{:S(2)}, u32[]{:S(2)}) collective-permute-start(bf16[128,256]{1,0:T(8,128)(2,1)S(1)} %add_convert_fusion.14), channel_id=1, source_target_pairs={{0,2},{1,3},{4,0},{5,1},{8,4},{9,5},{12,8},{13,9},{14,12},{15,13},... | collective-permute-start | bytes 196616 | tf_op jit(solution)/shard_map/ppermute | solution.py:66
  164.1 29.8 %collective-permute-start.33 = (bf16[456,896]{1,0:T(8,128)(2,1)}, bf16[456,896]{1,0:T(8,128)(2,1)S(1)}, u32[]{:S(2)}, u32[]{:S(2)}) collective-permute-start(bf16[456,896]{1,0:T(8,128)(2,1)} %get-tuple-element.143), channel_id=1, source_target_pairs={{0,4},{1,5},{4,8},{5,9},{8,12},{9,13},{12,14},{13,15},{14,10},{15,... | collective-permute-start | bytes 2451464 | tf_op jit(solution)/shard_map/ppermute | solution.py:66
  172.5 54.6 %collective-permute-start.26 = (bf16[128,256]{1,0:T(8,128)(2,1)S(1)}, bf16[128,256]{1,0:T(8,128)(2,1)S(1)}, u32[]{:S(2)}, u32[]{:S(2)}) collective-permute-start(bf16[128,256]{1,0:T(8,128)(2,1)S(1)} %add_convert_fusion.15), channel_id=1, source_target_pairs={{0,4},{1,5},{4,8},{5,9},{8,12},{9,13},{12,14},{13,15},{14,10},{15,... | collective-permute-start | bytes 196616 | tf_op jit(solution)/shard_map/ppermute | solution.py:66
  174.1 48.6 %collective-permute-start.35 = (bf16[456,896]{1,0:T(8,128)(2,1)S(1)}, bf16[456,896]{1,0:T(8,128)(2,1)S(1)}, u32[]{:S(2)}, u32[]{:S(2)}) collective-permute-start(bf16[456,896]{1,0:T(8,128)(2,1)S(1)} %copy-done.9), channel_id=1, source_target_pairs={{0,2},{1,3},{4,0},{5,1},{8,4},{9,5},{12,8},{13,9},{14,12},{15,13},... | collective-permute-start | bytes 2451464 | tf_op jit(solution)/shard_map/ppermute | solution.py:66
  198.6 24.2 %collective-permute-start.34 = (bf16[456,896]{1,0:T(8,128)(2,1)}, bf16[456,896]{1,0:T(8,128)(2,1)S(1)}, u32[]{:S(2)}, u32[]{:S(2)}) collective-permute-start(bf16[456,896]{1,0:T(8,128)(2,1)} %shard_map.203), channel_id=1, source_target_pairs={{0,4},{1,5},{4,8},{5,9},{8,12},{9,13},{12,14},{13,15},{14,10},{15,... | collective-permute-start | bytes 2451464 | tf_op jit(solution)/shard_map/ppermute | solution.py:66
  230.1 23.3 %collective-permute-start.48 = (bf16[520,896]{1,0:T(8,128)(2,1)}, bf16[520,896]{1,0:T(8,128)(2,1)S(1)}, u32[]{:S(2)}, u32[]{:S(2)}) collective-permute-start(bf16[520,896]{1,0:T(8,128)(2,1)} %shard_map.206.refs_0_), channel_id=1, source_target_pairs={{0,4},{1,5},{4,8},{5,9},{8,12},{9,13},{12,14},{13,15},{14,10},{15,... | collective-permute-start | bytes 2795528 | tf_op jit(solution)/shard_map/ppermute | solution.py:66
  231.3 23.0 %collective-permute-start.49 = (bf16[520,896]{1,0:T(8,128)(2,1)}, bf16[520,896]{1,0:T(8,128)(2,1)S(1)}, u32[]{:S(2)}, u32[]{:S(2)}) collective-permute-start(bf16[520,896]{1,0:T(8,128)(2,1)} %shard_map.206.refs_0_), channel_id=1, source_target_pairs={{0,2},{1,3},{4,0},{5,1},{8,4},{9,5},{12,8},{13,9},{14,12},{15,13},... | collective-permute-start | bytes 2795528 | tf_op jit(solution)/shard_map/ppermute | solution.py:66
  255.8 22.8 %collective-permute-start.52 = (bf16[520,896]{1,0:T(8,128)(2,1)}, bf16[520,896]{1,0:T(8,128)(2,1)S(1)}, u32[]{:S(2)}, u32[]{:S(2)}) collective-permute-start(bf16[520,896]{1,0:T(8,128)(2,1)} %get-tuple-element.160.refs_0_), channel_id=1, source_target_pairs={{0,4},{1,5},{4,8},{5,9},{8,12},{9,13},{12,14},{13,15},{14,10},{15,... | collective-permute-start | bytes 2795528 | tf_op jit(solution)/shard_map/ppermute | solution.py:66
  256.4 22.5 %collective-permute-start.53 = (bf16[520,896]{1,0:T(8,128)(2,1)}, bf16[520,896]{1,0:T(8,128)(2,1)S(1)}, u32[]{:S(2)}, u32[]{:S(2)}) collective-permute-start(bf16[520,896]{1,0:T(8,128)(2,1)} %get-tuple-element.161.refs_2_), channel_id=1, source_target_pairs={{0,2},{1,3},{4,0},{5,1},{8,4},{9,5},{12,8},{13,9},{14,12},{15,13},... | collective-permute-start | bytes 2795528 | tf_op jit(solution)/shard_map/ppermute | solution.py:66
  279.9 27.9 %collective-permute-start.54 = (bf16[520,896]{1,0:T(8,128)(2,1)}, bf16[520,896]{1,0:T(8,128)(2,1)S(1)}, u32[]{:S(2)}, u32[]{:S(2)}) collective-permute-start(bf16[520,896]{1,0:T(8,128)(2,1)} %get-tuple-element.168.refs_0_), channel_id=1, source_target_pairs={{0,1},{1,0},{2,3},{3,2},{4,5},{5,4},{6,7},{7,6},{8,9},{9,8},{10,11... | collective-permute-start | bytes 2795528 | tf_op jit(solution)/shard_map/ppermute | solution.py:54
  279.9 27.9 %collective-permute-start.55 = (bf16[520,896]{1,0:T(8,128)(2,1)}, bf16[520,896]{1,0:T(8,128)(2,1)}, u32[]{:S(2)}, u32[]{:S(2)}) collective-permute-start(bf16[520,896]{1,0:T(8,128)(2,1)} %get-tuple-element.169.refs_2_), channel_id=1, source_target_pairs={{0,1},{1,0},{2,3},{3,2},{4,5},{5,4},{6,7},{7,6},{8,9},{9,8},{10,11... | collective-permute-start | bytes 2795528 | tf_op jit(solution)/shard_map/ppermute | solution.py:54
  280.4 41.0 %collective-permute-start.59 = (bf16[520,896]{1,0:T(8,128)(2,1)}, bf16[520,896]{1,0:T(8,128)(2,1)S(1)}, u32[]{:S(2)}, u32[]{:S(2)}) collective-permute-start(bf16[520,896]{1,0:T(8,128)(2,1)} %get-tuple-element.168.refs_0_), channel_id=1, source_target_pairs={{0,4},{1,5},{4,8},{5,9},{8,12},{9,13},{12,14},{13,15},{14,10},{15,... | collective-permute-start | bytes 2795528 | tf_op jit(solution)/shard_map/ppermute | solution.py:66
  281.0 40.4 %collective-permute-start.60 = (bf16[520,896]{1,0:T(8,128)(2,1)}, bf16[520,896]{1,0:T(8,128)(2,1)S(1)}, u32[]{:S(2)}, u32[]{:S(2)}) collective-permute-start(bf16[520,896]{1,0:T(8,128)(2,1)} %get-tuple-element.169.refs_2_), channel_id=1, source_target_pairs={{0,2},{1,3},{4,0},{5,1},{8,4},{9,5},{12,8},{13,9},{14,12},{15,13},... | collective-permute-start | bytes 2795528 | tf_op jit(solution)/shard_map/ppermute | solution.py:66
  284.7 21.5 %collective-permute-start.57 = (bf16[232,256]{1,0:T(8,128)(2,1)}, bf16[232,256]{1,0:T(8,128)(2,1)S(1)}, u32[]{:S(2)}, u32[]{:S(2)}) collective-permute-start(bf16[232,256]{1,0:T(8,128)(2,1)} %shard_map.213), channel_id=1, source_target_pairs={{0,2},{1,3},{2,0},{3,1},{4,6},{5,7},{6,4},{7,5},{8,10},{9,11},{10,... | collective-permute-start | bytes 356360 | tf_op jit(solution)/shard_map/ppermute | solution.py:172
  (107 other events, 736.6 us)
